TPU v7x, 32 devices: a whole 2x2x4 slice. The times are simulated.
32 devices in a mesh: section: 2 (over x), lon: 4 (over z), lat: 4 (over y, core).
Axes of the slice: x: 2, y: 2, z: 4, core: 2. Of those that a mesh axis runs over, the one named last changes fastest.
Arguments:
- inputs: bfloat16 [2, 2, 24, 48, 512], P('section', None, 'lat', 'lon'), may hold values from -6 to 6
- cotangent: bfloat16 [2, 2, 24, 48, 512], P('section', None, 'lat', 'lon'), may hold values from -6 to 6
- land_sea: int32 [24, 48], P('lat', 'lon'), may hold values 0 or 1
- gains: float32 [2, 512], P('section'), may hold values from 0.5 to 1.5
- qkv_weight: bfloat16 [2, 512, 1536], P('section'), may hold values from -0.25 to 0.25
- out_weight: bfloat16 [2, 512, 512], P('section'), may hold values from -0.25 to 0.25
- land_bias: float32 [2, 16], P('section'), may hold values from -2 to 2
Outputs:
- input_grads: float32 [2, 2, 24, 48, 512], P('section', None, 'lat', 'lon')
- qkv_grad: float32 [2, 512, 1536], P('section')
- out_grad: float32 [2, 512, 512], P('section')
- gain_grad: float32 [2, 512], P('section')
- bias_grad: float32 [2, 16], P('section')
All inputs are finite; a program needn't handle non-finite values. No bound on the sum of `land_sea` on one device may be relied on, other than what follows from the above.
Results may differ from a plain program's by a relative error of at most 0.011.
Values may be sent and summed in bfloat16 or wider, within the bound.
No kernel may reach another device: no remote copies, remote signals or barrier semaphores. Data moves between devices by JAX's collectives and lax.ppermute only.
A program may use at most 64 MiB of HBM per device.

v0:
```python
import jax
import jax.numpy as jnp
from jax import lax
from jax.sharding import PartitionSpec as P

WLAT = 6
WLON = 12
SHIFT = 6


EPSILON = 1e-05


def from_behind(value, axis, by):
    count = lax.axis_size(axis)
    return lax.ppermute(value, axis, [(i, (i + by) % count) for i in range(count)])


def passed_along(block, axis, distance):
    devices = range(lax.axis_size(axis))
    route = [(i - distance, i) for i in devices if i - distance in devices]
    return lax.ppermute(block, axis, route)


def contract_last(left, right):
    return lax.dot_general(
        left, right, (((1,), (1,)), ((), ())), preferred_element_type=jnp.float32
    )


def contract_first(left, right):
    return lax.dot_general(
        left, right, (((0,), (0,)), ((), ())), preferred_element_type=jnp.float32
    )


def to_windows(grid, lat_span, lon_span):
    levels, rows, cols, width = grid.shape
    blocks = grid.reshape(levels, rows // lat_span, lat_span, cols // lon_span, lon_span, width)
    blocks = blocks.transpose(1, 3, 0, 2, 4, 5)
    return blocks.reshape(-1, levels * lat_span * lon_span, width)


def from_windows(windows, levels, rows, cols, lat_span, lon_span):
    width = windows.shape[-1]
    blocks = windows.reshape(rows // lat_span, cols // lon_span, levels, lat_span, lon_span, width)
    return blocks.transpose(2, 0, 3, 1, 4, 5).reshape(levels, rows, cols, width)


def land_windows(land, levels, lat_span, lon_span):
    rows, cols = land.shape
    blocks = land.reshape(rows // lat_span, lat_span, cols // lon_span, lon_span).transpose(
        0, 2, 1, 3
    )
    return jnp.tile(blocks.reshape(-1, lat_span * lon_span), (1, levels))


def window_forward(tokens_win, land_win, gain, qkv_weight, land_bias):
    batch, count, width = tokens_win.shape
    heads = land_bias.shape[0]
    head_size = width // heads
    values32 = tokens_win.astype(jnp.float32)
    centred = values32 - jnp.mean(values32, axis=-1, keepdims=True)
    inverse = lax.rsqrt(jnp.mean(centred * centred, axis=-1, keepdims=True) + EPSILON)
    normed = centred * inverse
    normed_b = (normed * gain).astype(jnp.bfloat16).reshape(batch * count, width)
    projected = jnp.dot(normed_b, qkv_weight, preferred_element_type=jnp.float32).astype(
        jnp.bfloat16
    )
    projected = projected.reshape(batch, count, 3, heads, head_size)
    queries = projected[:, :, 0]
    keys_win = projected[:, :, 1]
    values_win = projected[:, :, 2]
    scale = head_size ** (-0.5)
    scores = (
        jnp.einsum("bihd,bjhd->bhij", queries, keys_win, preferred_element_type=jnp.float32) * scale
    )
    scores = scores + land_bias[None, :, None, None] * land_win[:, None, None, :]
    weights = jax.nn.softmax(scores, axis=-1)
    weights_b = weights.astype(jnp.bfloat16)
    attended = jnp.einsum(
        "bhij,bjhd->bihd", weights_b, values_win, preferred_element_type=jnp.float32
    )
    attended = attended.astype(jnp.bfloat16).reshape(batch * count, width)
    return (
        normed.reshape(batch * count, width),
        inverse.reshape(batch * count, 1),
        normed_b,
        queries,
        keys_win,
        values_win,
        weights,
        weights_b,
        attended,
    )


def window_backward(cache, grad_out, land_win, gain, qkv_weight, out_weight, want_weights):
    normed, inverse, normed_b, queries, keys_win, values_win, weights, weights_b, attended = cache
    batch, count, heads, head_size = queries.shape
    width = heads * head_size
    scale = head_size ** (-0.5)
    grad_att = (
        contract_last(grad_out, out_weight)
        .astype(jnp.bfloat16)
        .reshape(batch, count, heads, head_size)
    )
    grad_weights = jnp.einsum(
        "bihd,bjhd->bhij", grad_att, values_win, preferred_element_type=jnp.float32
    )
    grad_values = jnp.einsum(
        "bhij,bihd->bjhd", weights_b, grad_att, preferred_element_type=jnp.float32
    )
    inner = jnp.sum(weights * grad_weights, axis=-1, keepdims=True)
    grad_scores = weights * (grad_weights - inner)
    scaled_b = (grad_scores * scale).astype(jnp.bfloat16)
    grad_queries = jnp.einsum(
        "bhij,bjhd->bihd", scaled_b, keys_win, preferred_element_type=jnp.float32
    )
    grad_keys = jnp.einsum("bhij,bihd->bjhd", scaled_b, queries, preferred_element_type=jnp.float32)
    grad_proj = jnp.stack([grad_queries, grad_keys, grad_values], axis=2).astype(jnp.bfloat16)
    grad_proj = grad_proj.reshape(batch * count, 3 * width)
    grad_normed = contract_last(grad_proj, qkv_weight)
    scaled = grad_normed * gain
    grad_tokens = inverse * (
        scaled
        - jnp.mean(scaled, axis=-1, keepdims=True)
        - normed * jnp.mean(scaled * normed, axis=-1, keepdims=True)
    )
    if want_weights:
        grad_bias = jnp.sum(grad_scores * land_win[:, None, None, :], axis=(0, 2, 3))
        grad_gain = jnp.sum(grad_normed * normed, axis=0)
        grad_qkv = contract_first(normed_b, grad_proj)
        grad_outw = contract_first(attended, grad_out)
        return (grad_tokens, (grad_qkv, grad_outw, grad_gain, grad_bias))
    return (grad_tokens, None)


def body(inputs, cotangent, land_sea, gains, qkv_weight, out_weight, land_bias):
    tokens = inputs[0]
    own_cot = cotangent[0]
    gain = gains[0]
    weight_qkv = qkv_weight[0]
    weight_out = out_weight[0]
    bias = land_bias[0]
    levels, rows, cols, width = tokens.shape
    heads = bias.shape[0]
    land_b = land_sea.astype(jnp.bfloat16)
    rim_tokens, rim_land = from_behind((tokens[:, :, :SHIFT], land_b[:, :SHIFT]), "lon", -1)
    shifted = jnp.concatenate([tokens[:, :, SHIFT:], rim_tokens], axis=2)
    land_shift = jnp.concatenate([land_b[:, SHIFT:], rim_land], axis=1).astype(jnp.float32)
    land_win = land_windows(land_shift, levels, WLAT, WLON)
    cache = window_forward(to_windows(shifted, WLAT, WLON), land_win, gain, weight_qkv, bias)
    count = levels * WLAT * WLON

    def input_grad(cot_grid, want_weights):
        rim_cot = from_behind(cot_grid[:, :, :SHIFT], "lon", -1)
        grad_shift = jnp.concatenate([cot_grid[:, :, SHIFT:], rim_cot], axis=2)
        grad_win = to_windows(grad_shift, WLAT, WLON).reshape(-1, width)
        grad_tokens, sums = window_backward(
            cache, grad_win, land_win, gain, weight_qkv, weight_out, want_weights
        )
        grid = from_windows(grad_tokens.reshape(-1, count, width), levels, rows, cols, WLAT, WLON)
        rim_back = from_behind(grid[:, :, cols - SHIFT :].astype(jnp.bfloat16), "lon", 1).astype(
            jnp.float32
        )
        rolled = jnp.concatenate([rim_back, grid[:, :, : cols - SHIFT]], axis=2)
        return (rolled + cot_grid.astype(jnp.float32), sums)

    first_grad, unused = input_grad(own_cot, False)
    skip_grad = passed_along(first_grad, "section", -1)
    total_cot = (own_cot.astype(jnp.float32) + skip_grad).astype(jnp.bfloat16)
    final_grad, sums = input_grad(total_cot, True)
    grad_qkv, grad_outw, grad_gain, grad_bias = sums
    entries = 2 * (4 * width * width + width + heads)
    grad_qkv, grad_outw, grad_gain, grad_bias = lax.psum(
        (grad_qkv, grad_outw, grad_gain, grad_bias), ("lon", "lat")
    )
    square = (
        jnp.sum(grad_qkv * grad_qkv)
        + jnp.sum(grad_outw * grad_outw)
        + jnp.sum(grad_gain * grad_gain)
        + jnp.sum(grad_bias * grad_bias)
    )
    square = lax.psum(square, "section")
    factor = jnp.minimum(1.0, lax.rsqrt(square / entries + 1e-06))
    grad_qkv = grad_qkv * factor
    grad_outw = grad_outw * factor
    grad_gain = grad_gain * factor
    grad_bias = grad_bias * factor
    return (final_grad[None], grad_qkv[None], grad_outw[None], grad_gain[None], grad_bias[None])


def solution(mesh):
    placed = (
        P("section", None, "lat", "lon", None),
        P("section", None, "lat", "lon", None),
        P("lat", "lon"),
        P("section", None),
        P("section", None, None),
        P("section", None, None),
        P("section", None),
    )
    return jax.shard_map(
        body,
        mesh=mesh,
        in_specs=placed,
        out_specs=(
            P("section", None, "lat", "lon", None),
            P("section", None, None),
            P("section", None, None),
            P("section", None),
            P("section", None),
        ),
        check_vma=False,
    )
```

profile of v0, /device:TPU:0, one launch (start us, length us, event | category | flops | bytes accessed | tf_op | source)
XLA Modules:
  0.0 227.2 jit_solution(11110739381999844899)
XLA Ops:
  7.2 1.1 fusion.69
  8.4 5.1 %collective-permute-start = (bf16[2,6,6,512]{3,0,2,1:T(2,128)(2,1)S(1)}, bf16[2,6,6,512]{3,0,2,1:T(2,128)(2,1)S(1)}, u32[]{:S(2)}, u32[]{:S(2)}) collective-permute-start(bf16[2,6,6,512]{3,0,2,1:T(2,128)(2,1)S(1)} %get-tuple-element.29), channel_id=1, source_target_pairs={{0,12},{4,0},{8,4},{12,8},{1,13},{5,1},{9,5},{13,9},{2,14},{6,2},{... | collective-permute-start | bytes 221192 | tf_op jit(solution)/shard_map/ppermute | solution.py:16
  13.5 0.7 convert_element_type.164
  14.2 0.4 collective-permute-start.1
  14.7 0.9 copy.77
  15.7 0.5 collective-permute-start.2
  16.2 1.7 collective-permute-done.1
  18.0 0.1 mul.217
  18.1 0.7 broadcast_multiply_fusion.1
  18.8 0.2 maximum_convert_fusion
  19.1 0.2 fusion.65
  19.3 0.1 copy.49
  19.6 0.2 multiply_reduce_fusion.8
  19.8 0.5 collective-permute-done.2
  20.5 0.3 convolution_convert_fusion.7
  20.8 0.8 copy.54
  21.7 0.1 copy.50
  21.8 0.3 multiply_convert_fusion.4
  22.2 1.2 convolution_convert_fusion
  23.4 1.3 copy.52
  24.7 2.4 %fusion.71 = (f32[16,144]{1,0:T(8,128)S(1)}, f32[16,144,144]{1,2,0:T(8,128)}) fusion(f32[16,144]{1,0:T(8,128)S(1)} %broadcast_multiply_fusion.1, bf16[1,144,3,16,32]{1,4,3,2,0:T(8,128)(2,1)S(1)} %bitcast.134), kind=kOutput, calls=%fused_computation.107 | convolution fusion | flops 22560912 | bytes 1876992 | tf_op jit(solution)/shard_map/sub | solution.py:79
  27.1 3.0 %fusion.54 = f32[16,144,144]{1,2,0:T(8,128)} fusion(bf16[144,16,32]{0,2,1:T(8,128)(2,1)} %bitcast.142, bf16[1,144,3,16,32]{1,4,3,2,0:T(8,128)(2,1)S(1)} %bitcast.135), kind=kOutput, calls=%fused_computation.77 | convolution fusion | flops 21233664 | bytes 1736704 | tf_op jit(solution)/shard_map/bihd,bjhd->bhij/dot_general | solution.py:108
  30.1 1.2 fusion.40
  31.3 5.3 %fusion.34 = bf16[1,144,1,16,32]{1,4,3,2,0:T(8,128)(2,1)} fusion(f32[16,144,144]{1,2,0:T(8,128)} %fusion.54, bf16[1,144,3,16,32]{1,4,3,2,0:T(8,128)(2,1)S(1)} %bitcast.136, f32[16,144,144]{1,2,0:T(8,128)} %get-tuple-element.33, f32[16,144]{1,0:T(8,128)S(1)} %get-tuple-element.32), kind=kOutput, calls=%fused_computation.37 | convolution fusion | flops 23632272 | bytes 9879552 | tf_op jit(solution)/shard_map/bhij,bihd->bjhd/dot_general | solution.py:120
  36.7 5.4 %fusion.37 = bf16[1,144,1,16,32]{1,4,3,2,0:T(8,128)(2,1)} fusion(f32[16,144,144]{1,2,0:T(8,128)} %fusion.54, bf16[1,144,3,16,32]{1,4,3,2,0:T(8,128)(2,1)S(1)} %bitcast.137, f32[16,144,144]{1,2,0:T(8,128)} %get-tuple-element.33, f32[16,144]{1,0:T(8,128)S(1)} %get-tuple-element.32), kind=kOutput, calls=%fused_computation.38 | convolution fusion | flops 23632272 | bytes 9879552 | tf_op jit(solution)/shard_map/bhij,bjhd->bihd/dot_general | solution.py:117
  42.1 1.3 pad_maximum_fusion
  43.4 0.8 fusion.66
  44.2 0.9 subtract_multiply_fusion.2
  45.1 1.7 reshape_transpose_reshape_reshape.6
  46.8 1.2 slice.101
  48.0 1.6 collective-permute-start.3
  49.6 0.9 slice.70
  50.6 3.9 %collective-permute-done.3 = bf16[2,6,6,512]{3,2,1,0:T(8,128)(2,1)S(1)} collective-permute-done((bf16[2,6,6,512]{3,2,1,0:T(8,128)(2,1)S(1)}, bf16[2,6,6,512]{3,2,1,0:T(8,128)(2,1)S(1)}, u32[]{:S(2)}, u32[]{:S(2)}) %collective-permute-start.3) | collective-permute-done | bytes 73760 | tf_op jit(solution)/shard_map/ppermute | solution.py:16
  54.6 1.3 collective-permute-start.4
  55.9 8.6 %collective-permute-done.4 = f32[2,6,12,512]{3,2,1,0:T(8,128)S(1)} collective-permute-done((f32[2,6,12,512]{3,2,1,0:T(8,128)S(1)}, f32[2,6,12,512]{3,2,1,0:T(8,128)S(1)}, u32[]{:S(2)}, u32[]{:S(2)}) %collective-permute-start.4) | collective-permute-done | bytes 294944 | tf_op jit(solution)/shard_map/ppermute | solution.py:22
  64.5 1.0 fusion.46
  65.5 0.5 collective-permute-start.5
  66.0 1.0 convolution_convert_fusion.1
  67.0 3.1 %collective-permute-done.5 = bf16[2,6,6,512]{3,2,1,0:T(8,128)(2,1)S(1)} collective-permute-done((bf16[2,6,6,512]{3,2,1,0:T(8,128)(2,1)S(1)}, bf16[2,6,6,512]{3,2,1,0:T(8,128)(2,1)S(1)}, u32[]{:S(2)}, u32[]{:S(2)}) %collective-permute-start.5) | collective-permute-done | bytes 73760 | tf_op jit(solution)/shard_map/ppermute | solution.py:16
  70.1 0.7 pad_maximum_fusion.3
  70.9 1.6 reshape_reshape_transpose_reshape.7
  72.5 1.9 convolution_convert_fusion.6
  74.4 1.0 copy.59
  75.4 2.9 %fusion.43 = bf16[1,144,1,16,32]{1,4,3,2,0:T(8,128)(2,1)} fusion(bf16[144,16,32]{0,2,1:T(8,128)(2,1)S(1)} %bitcast.145, f32[16,144,144]{1,2,0:T(8,128)} %get-tuple-element.33, f32[16,144]{1,0:T(8,128)S(1)} %get-tuple-element.32), kind=kOutput, calls=%fused_computation.42 | convolution fusion | flops 21970944 | bytes 1631232 | tf_op jit(solution)/shard_map/bhij,bihd->bjhd/dot_general | solution.py:111
  78.3 4.9 %multiply_reduce_fusion.1 = (f32[16]{0:T(128)S(1)}, f32[16,144,144]{1,2,0:T(8,128)}) fusion(f32[144]{0:T(256)S(1)} %mul.217, bf16[144,16,32]{0,2,1:T(8,128)(2,1)S(1)} %bitcast.146, bf16[1,144,3,16,32]{1,4,3,2,0:T(8,128)(2,1)S(1)} %bitcast.139, f32[16,144,144]{1,2,0:T(8,128)} %get-tuple-element.33, f32[16,144]{1,0:T(8,128)} %copy-done.12), kind=kOutput, calls=%fused_computation.6 | convolution fusion | flops 44792192 | bytes 6668928 | tf_op jit(solution)/shard_map/sub | solution.py:115
  83.2 2.3 %fusion.42 = bf16[1,144,1,16,32]{1,4,3,2,0:T(8,128)(2,1)S(1)} fusion(f32[16,144,144]{1,2,0:T(8,128)} %get-tuple-element.37, bf16[1,144,3,16,32]{1,4,3,2,0:T(8,128)(2,1)S(1)} %bitcast.140), kind=kOutput, calls=%fused_computation.41 | convolution fusion | flops 21970944 | bytes 1736704 | tf_op jit(solution)/shard_map/bhij,bihd->bjhd/dot_general | solution.py:120
  85.6 0.3 fusion.41
  85.9 0.2 pad_maximum_fusion.1
  86.1 2.3 %fusion.72 = f32[512,1536]{1,0:T(8,128)} fusion(bf16[144,512]{1,0:T(8,128)(2,1)S(1)} %convert_element_type.162, bf16[144,1536]{0,1:T(8,128)(2,1)S(1)} %bitcast.131), kind=kOutput, calls=%fused_computation.108 | convolution fusion | flops 226492416 | bytes 3735552 | tf_op jit(solution)/shard_map/dot_general | solution.py:32
  88.4 1.2 fusion.73
  89.7 0.8 multiply_reduce_fusion.5
  90.6 0.2 subtract_multiply_fusion.1
  90.9 30.8 %all-reduce = (f32[512]{0:T(512)S(1)}, f32[16]{0:T(128)S(1)}) all-reduce(f32[512]{0:T(512)S(1)} %get-tuple-element.15, f32[16]{0:T(128)S(1)} %get-tuple-element.36), channel_id=1, replica_groups=mesh['section'=2,'lon'=4,'lat'=4] {'lon','lat'}, use_global_device_ids=true, to_apply=%region_15.0 | all-reduce | flops 528 | bytes 4224 | tf_op jit(solution)/shard_map/psum | solution.py:176
  121.6 0.6 multiply_reduce_fusion.10
  122.2 0.6 multiply_reduce_fusion.11
  123.0 77.6 %all-reduce.4.cloned.1.call-done = (f32[512,1536]{1,0:T(8,128)}, f32[512,512]{1,0:T(8,128)}) async-done(((f32[512,1536]{1,0:T(8,128)}, f32[512,512]{1,0:T(8,128)}), (f32[512,1536]{1,0:T(8,128)}, f32[512,512]{1,0:T(8,128)})) %all-reduce.4.cloned.1.call-update) | async-done | bytes 4194320 | tf_op jit(solution)/shard_map/psum | solution.py:176
  200.6 3.4 %multiply_reduce_fusion = f32[]{:T(128)} fusion(f32[512,1536]{1,0:T(8,128)} %get-tuple-element.22), kind=kLoop, calls=%fused_computation.4 | loop fusion | flops 1572863 | bytes 3145732 | tf_op jit(solution)/shard_map/reduce_sum | solution.py:180
  204.0 0.9 multiply_reduce_fusion.4
  207.4 0.9 copy.64
  208.3 5.4 %psum.39 = f32[]{:T(128)} all-reduce(f32[]{:T(128)S(6)} %add.66), channel_id=1, replica_groups=mesh['section'=2,'lon'=4,'lat'=4] {'section'}, use_global_device_ids=true, to_apply=%region_20.0 | all-reduce | flops 1 | bytes 8 | tf_op jit(solution)/shard_map/psum | solution.py:185
  214.5 3.8 %multiply_bitcast_fusion = f32[1,512,1536]{2,1,0:T(8,128)} fusion(f32[512,1536]{1,0:T(8,128)} %get-tuple-element.22, f32[]{:T(128)S(6)} %min_shard_map.3), kind=kLoop, calls=%fused_computation.3 | loop fusion | flops 786432 | bytes 6291460 | tf_op jit(solution)/shard_map/broadcast_in_dim | solution.py:191
  218.2 1.1 multiply_bitcast_fusion.1
  219.3 0.6 broadcast_multiply_fusion.2
  219.9 0.5 multiply_bitcast_fusion.2
  (58 shorter events, 1.3 us)
Async XLA Ops:
  7.2 15.1 %copy-start = (bf16[1,512,1536]{2,1,0:T(8,128)(2,1)S(1)}, bf16[1,512,1536]{2,1,0:T(8,128)(2,1)}, u32[]{:S(2)}) copy-start(bf16[1,512,1536]{2,1,0:T(8,128)(2,1)} %param.11) | copy-start | bytes 4718596
  7.2 193.4 %all-reduce.4.cloned.1.call-start = ((), (), s32[]{:S(2)}) async-start(), calls=%async_computation | async-start | bytes 8388608 | tf_op jit(solution)/shard_map/psum | solution.py:176
  8.4 12.1 %copy-start.3 = (bf16[1,512,512]{2,1,0:T(8,128)(2,1)S(1)}, bf16[1,512,512]{2,1,0:T(8,128)(2,1)}, u32[]{:S(2)}) copy-start(bf16[1,512,512]{2,1,0:T(8,128)(2,1)} %param.12) | copy-start | bytes 1572868
  8.4 10.5 %collective-permute-start = (bf16[2,6,6,512]{3,0,2,1:T(2,128)(2,1)S(1)}, bf16[2,6,6,512]{3,0,2,1:T(2,128)(2,1)S(1)}, u32[]{:S(2)}, u32[]{:S(2)}) collective-permute-start(bf16[2,6,6,512]{3,0,2,1:T(2,128)(2,1)S(1)} %get-tuple-element.29), channel_id=1, source_target_pairs={{0,12},{4,0},{8,4},{12,8},{1,13},{5,1},{9,5},{13,9},{2,14},{6,2},{... | collective-permute-start | bytes 221192 | tf_op jit(solution)/shard_map/ppermute | solution.py:16
  14.2 3.6 %collective-permute-start.1 = (bf16[6,6]{1,0:T(8,128)(2,1)S(1)}, bf16[6,6]{1,0:T(8,128)(2,1)S(1)}, u32[]{:S(2)}, u32[]{:S(2)}) collective-permute-start(bf16[6,6]{1,0:T(8,128)(2,1)S(1)} %get-tuple-element.31), channel_id=1, source_target_pairs={{0,12},{4,0},{8,4},{12,8},{1,13},{5,1},{9,5},{13,9},{2,14},{6,2},{... | collective-permute-start | bytes 224 | tf_op jit(solution)/shard_map/ppermute | solution.py:16
  15.7 4.7 %collective-permute-start.2 = (bf16[2,6,6,512]{3,2,1,0:T(8,128)(2,1)S(1)}, bf16[2,6,6,512]{3,2,1,0:T(8,128)(2,1)S(1)}, u32[]{:S(2)}, u32[]{:S(2)}) collective-permute-start(bf16[2,6,6,512]{3,2,1,0:T(8,128)(2,1)S(1)} %get-tuple-element.27), channel_id=1, source_target_pairs={{0,12},{4,0},{8,4},{12,8},{1,13},{5,1},{9,5},{13,9},{2,14},{6,2},{... | collective-permute-start | bytes 221192 | tf_op jit(solution)/shard_map/ppermute | solution.py:16
  19.0 2.8 %copy-start.9 = (f32[1,512]{1,0:T(1,128)S(1)}, f32[1,512]{1,0:T(1,128)}, u32[]{:S(2)}) copy-start(f32[1,512]{1,0:T(1,128)} %param.10) | copy-start | bytes 6148
  27.1 48.4 %copy-start.12 = (f32[16,144]{1,0:T(8,128)}, f32[16,144]{1,0:T(8,128)S(1)}, u32[]{:S(2)}) copy-start(f32[16,144]{1,0:T(8,128)S(1)} %get-tuple-element.32) | copy-start | bytes 27652
  27.1 3.0 %copy-start.6 = (bf16[144,512]{0,1:T(8,128)(2,1)S(1)}, bf16[144,512]{0,1:T(8,128)(2,1)}, u32[]{:S(2)}) copy-start(bf16[144,512]{0,1:T(8,128)(2,1)} %copy.54) | copy-start | bytes 442372
  27.1 3.0 %copy-start.10 = (f32[16,144,144]{1,2,0:T(8,128)S(1)}, f32[16,144,144]{1,2,0:T(8,128)}, u32[]{:S(2)}) copy-start(f32[16,144,144]{1,2,0:T(8,128)} %get-tuple-element.33) | copy-start | bytes 3981316
  43.4 11.1 %copy-start.4 = (bf16[1,2,6,12,512]{4,1,3,2,0:T(2,128)(2,1)S(1)}, bf16[1,2,6,12,512]{4,1,3,2,0:T(2,128)(2,1)}, u32[]{:S(2)}) copy-start(bf16[1,2,6,12,512]{4,1,3,2,0:T(2,128)(2,1)} %param.8) | copy-start | bytes 442372
  46.8 19.2 %copy-start.11 = (f32[16,144,144]{1,2,0:T(8,128)S(1)}, f32[16,144,144]{1,2,0:T(8,128)}, u32[]{:S(2)}) copy-start(f32[16,144,144]{1,2,0:T(8,128)} %get-tuple-element.33) | copy-start | bytes 3981316
  48.0 6.5 %collective-permute-start.3 = (bf16[2,6,6,512]{3,2,1,0:T(8,128)(2,1)S(1)}, bf16[2,6,6,512]{3,2,1,0:T(8,128)(2,1)S(1)}, u32[]{:S(2)}, u32[]{:S(2)}) collective-permute-start(bf16[2,6,6,512]{3,2,1,0:T(8,128)(2,1)S(1)} %slice.101), channel_id=1, source_target_pairs={{0,4},{4,8},{8,12},{12,0},{1,5},{5,9},{9,13},{13,1},{2,6},{6,10},{... | collective-permute-start | bytes 221192 | tf_op jit(solution)/shard_map/ppermute | solution.py:16
  54.6 9.9 %collective-permute-start.4 = (f32[2,6,12,512]{3,2,1,0:T(8,128)S(1)}, f32[2,6,12,512]{3,2,1,0:T(8,128)S(1)}, u32[]{:S(2)}, u32[]{:S(2)}) collective-permute-start(f32[2,6,12,512]{3,2,1,0:T(8,128)S(1)} %convert_add_fusion.1), channel_id=1, source_target_pairs={{16,0},{17,1},{18,2},{19,3},{20,4},{21,5},{22,6},{23,7},{24,8},{25... | collective-permute-start | bytes 884744 | tf_op jit(solution)/shard_map/ppermute | solution.py:22
  65.5 4.7 %collective-permute-start.5 = (bf16[2,6,6,512]{3,2,1,0:T(8,128)(2,1)S(1)}, bf16[2,6,6,512]{3,2,1,0:T(8,128)(2,1)S(1)}, u32[]{:S(2)}, u32[]{:S(2)}) collective-permute-start(bf16[2,6,6,512]{3,2,1,0:T(8,128)(2,1)S(1)} %get-tuple-element.25), channel_id=1, source_target_pairs={{0,12},{4,0},{8,4},{12,8},{1,13},{5,1},{9,5},{13,9},{2,14},{6,2},{... | collective-permute-start | bytes 221192 | tf_op jit(solution)/shard_map/ppermute | solution.py:16
  83.2 2.4 %copy-start.1 = (f32[16,144,144]{1,2,0:T(8,128)S(1)}, f32[16,144,144]{1,2,0:T(8,128)}, u32[]{:S(2)}) copy-start(f32[16,144,144]{1,2,0:T(8,128)} %get-tuple-element.37) | copy-start | bytes 3981316
  83.2 2.7 %copy-start.8 = (bf16[1,144,1,16,32]{1,4,3,2,0:T(8,128)(2,1)S(1)}, bf16[1,144,1,16,32]{1,4,3,2,0:T(8,128)(2,1)}, u32[]{:S(2)}) copy-start(bf16[1,144,1,16,32]{1,4,3,2,0:T(8,128)(2,1)} %fusion.43) | copy-start | bytes 442372
  86.1 2.3 %copy-start.5 = (bf16[144,512]{1,0:T(8,128)(2,1)S(1)}, bf16[144,512]{1,0:T(8,128)(2,1)}, u32[]{:S(2)}) copy-start(bf16[144,512]{1,0:T(8,128)(2,1)} %reshape_reshape_transpose_reshape.7) | copy-start | bytes 442372
  86.1 2.3 %copy-start.7 = (bf16[16,32,144]{2,1,0:T(8,128)(2,1)S(1)}, bf16[16,32,144]{2,1,0:T(8,128)(2,1)}, u32[]{:S(2)}) copy-start(bf16[16,32,144]{2,1,0:T(8,128)(2,1)} %convolution_convert_fusion.1) | copy-start | bytes 442372
  90.8 32.0 %collective-permute-start.6 = (bf16[2,6,6,512]{3,2,1,0:T(8,128)(2,1)S(1)}, bf16[2,6,6,512]{3,2,1,0:T(8,128)(2,1)S(1)}, u32[]{:S(2)}, u32[]{:S(2)}) collective-permute-start(bf16[2,6,6,512]{3,2,1,0:T(8,128)(2,1)S(1)} %slice.100), channel_id=1, source_target_pairs={{0,4},{4,8},{8,12},{12,0},{1,5},{5,9},{9,13},{13,1},{2,6},{6,10},{... | collective-permute-start | bytes 221192 | tf_op jit(solution)/shard_map/ppermute | solution.py:16
  200.6 3.4 %copy-start.2 = (f32[512,512]{1,0:T(8,128)S(1)}, f32[512,512]{1,0:T(8,128)}, u32[]{:S(2)}) copy-start(f32[512,512]{1,0:T(8,128)} %get-tuple-element.23) | copy-start | bytes 3145732
Sparse Core Ops, SparseCore 0:
  89.8 110.6 all-reduce.3
where the time goes:
time: 228 us; the launch traced here: 227 us
  waiting for transfers between devices  95.4 us (42%)
  matrix products  37.3 us (16%)
  blocking collectives  36.2 us (16%)
  other arithmetic  18.2 us (8%)
  between operations  17.6 us (8%)
  local copies, waits for them, and re-layouts  12.8 us (6%)
  starting transfers between devices  9.59 us (4%)
    psum x1, waiting for transfers between devices, body(): lax.psum((grad_qkv, grad_outw, grad_gain, grad_bias), ('lon', 'lat'))  77.6 us
    psum x1, blocking collectives, body(): lax.psum((grad_qkv, grad_outw, grad_gain, grad_bias), ('lon', 'lat'))  30.8 us
    ppermute x6, waiting for transfers between devices, from_behind(): lax.ppermute(value, axis, [(i, (i + by) % count) for i in range(count)])  9.22 us
    ppermute x1, waiting for transfers between devices, passed_along(): return lax.ppermute(block, axis, route)  8.59 us
    ppermute x6, starting transfers between devices, from_behind(): lax.ppermute(value, axis, [(i, (i + by) % count) for i in range(count)])  8.26 us
    dot_general x2, matrix products, window_backward(): jnp.einsum('bhij,bihd->bjhd', scaled_b, queries, preferred_element_type=j...  7.65 us
    dot_general x2, matrix products, window_backward(): jnp.einsum('bhij,bjhd->bihd', scaled_b, keys_win, preferred_element_type=...  5.7 us
    psum x1, blocking collectives, body(): square = lax.psum(square, 'section')  5.42 us
  transfers between devices with their start and end apart: 8, of which 6 were waited for; matrix products, arithmetic and copies ran while one was open for 4% of the time, Pallas kernels for 0%

commit v1 on v0

--- a/solution.py
+++ b/solution.py
@@ -136,6 +136,59 @@
     return (grad_tokens, None)
 
 
+def swapped(value, axis, bit):
+    count = lax.axis_size(axis)
+    return lax.ppermute(value, axis, [(i, i ^ bit) for i in range(count)])
+
+
+def halved(block, axis, bit):
+    mine = (lax.axis_index(axis) // bit) % 2
+    pair = block.reshape(2, block.shape[0] // 2, -1)
+    give = lax.dynamic_index_in_dim(pair, 1 - mine, 0, keepdims=False).astype(jnp.bfloat16)
+    keep = lax.dynamic_index_in_dim(pair, mine, 0, keepdims=False)
+    return keep + swapped(give, axis, bit).astype(jnp.float32)
+
+
+def scattered(block, axis):
+    count = lax.axis_size(axis)
+    mine = lax.axis_index(axis)
+    pieces = block.reshape(count, block.shape[0] // count, -1)
+    total = lax.dynamic_index_in_dim(pieces, mine, 0, keepdims=False)
+    for by in range(1, count):
+        give = lax.dynamic_index_in_dim(pieces, (mine + by) % count, 0, keepdims=False)
+        total = total + from_behind(give.astype(jnp.bfloat16), axis, by).astype(jnp.float32)
+    return total
+
+
+def doubled(block, axis, bit):
+    mine = (lax.axis_index(axis) // bit) % 2
+    other = swapped(block, axis, bit)
+    low = jnp.where(mine == 0, block, other)
+    high = jnp.where(mine == 0, other, block)
+    return jnp.concatenate([low, high], axis=0)
+
+
+def gathered(block, axis):
+    count = lax.axis_size(axis)
+    mine = lax.axis_index(axis)
+    whole = jnp.zeros((count,) + block.shape, block.dtype)
+    whole = lax.dynamic_update_index_in_dim(whole, block, mine, 0)
+    for by in range(1, count):
+        whole = lax.dynamic_update_index_in_dim(
+            whole, from_behind(block, axis, by), (mine - by) % count, 0
+        )
+    return whole.reshape(count * block.shape[0], -1)
+
+
+def small_sum(value, axes):
+    for axis in axes:
+        bit = 1
+        while bit < lax.axis_size(axis):
+            value = value + swapped(value, axis, bit)
+            bit *= 2
+    return value
+
+
 def body(inputs, cotangent, land_sea, gains, qkv_weight, out_weight, land_bias):
     tokens = inputs[0]
     own_cot = cotangent[0]
@@ -147,48 +200,60 @@
     heads = bias.shape[0]
     land_b = land_sea.astype(jnp.bfloat16)
     rim_tokens, rim_land = from_behind((tokens[:, :, :SHIFT], land_b[:, :SHIFT]), "lon", -1)
+    rim_cot = from_behind(own_cot[:, :, :SHIFT], "lon", -1)
     shifted = jnp.concatenate([tokens[:, :, SHIFT:], rim_tokens], axis=2)
+    cot_shift = jnp.concatenate([own_cot[:, :, SHIFT:], rim_cot], axis=2)
     land_shift = jnp.concatenate([land_b[:, SHIFT:], rim_land], axis=1).astype(jnp.float32)
     land_win = land_windows(land_shift, levels, WLAT, WLON)
     cache = window_forward(to_windows(shifted, WLAT, WLON), land_win, gain, weight_qkv, bias)
+    normed_b, attended = cache[2], cache[8]
     count = levels * WLAT * WLON
-
-    def input_grad(cot_grid, want_weights):
-        rim_cot = from_behind(cot_grid[:, :, :SHIFT], "lon", -1)
-        grad_shift = jnp.concatenate([cot_grid[:, :, SHIFT:], rim_cot], axis=2)
-        grad_win = to_windows(grad_shift, WLAT, WLON).reshape(-1, width)
-        grad_tokens, sums = window_backward(
-            cache, grad_win, land_win, gain, weight_qkv, weight_out, want_weights
-        )
-        grid = from_windows(grad_tokens.reshape(-1, count, width), levels, rows, cols, WLAT, WLON)
-        rim_back = from_behind(grid[:, :, cols - SHIFT :].astype(jnp.bfloat16), "lon", 1).astype(
-            jnp.float32
-        )
-        rolled = jnp.concatenate([rim_back, grid[:, :, : cols - SHIFT]], axis=2)
-        return (rolled + cot_grid.astype(jnp.float32), sums)
-
-    first_grad, unused = input_grad(own_cot, False)
-    skip_grad = passed_along(first_grad, "section", -1)
-    total_cot = (own_cot.astype(jnp.float32) + skip_grad).astype(jnp.bfloat16)
-    final_grad, sums = input_grad(total_cot, True)
-    grad_qkv, grad_outw, grad_gain, grad_bias = sums
+    cot_win = to_windows(cot_shift, WLAT, WLON).reshape(-1, width)
+
+    first, unused = window_backward(
+        cache, cot_win, land_win, gain, weight_qkv, weight_out, False
+    )
+    skip = (first + cot_win.astype(jnp.float32)).astype(jnp.bfloat16)
+    skip = passed_along(skip, "section", -1)
+    total_cot = (cot_win.astype(jnp.float32) + skip.astype(jnp.float32)).astype(jnp.bfloat16)
+    second, sums = window_backward(
+        cache, total_cot, land_win, gain, weight_qkv, weight_out, True
+    )
+    final = (second + total_cot.astype(jnp.float32)).reshape(-1, count, width)
+    grid = from_windows(final, levels, rows, cols, WLAT, WLON)
+    rim_back = from_behind(grid[:, :, cols - SHIFT :].astype(jnp.bfloat16), "lon", 1)
+    final_grad = jnp.concatenate(
+        [rim_back.astype(jnp.float32), grid[:, :, : cols - SHIFT]], axis=2
+    )
+
+    grad_qkv, grad_outw, unused, grad_bias = sums
+    grad_bias = small_sum(grad_bias, ("lat", "lon"))
+    part_out = halved(scattered(halved(grad_outw, "lat", 1), "lon"), "lat", 2)
+    part_qkv = scattered(halved(halved(grad_qkv, "lat", 1), "lat", 2), "lon")
+    lat, lon = lax.axis_index("lat"), lax.axis_index("lon")
+    piece = part_qkv.shape[0]
+    start = ((lat % 2) * 2 + lat // 2) * (width // 4) + lon * piece
+    weight_rows = lax.dynamic_slice_in_dim(weight_qkv, start, piece, 0).astype(jnp.float32)
+    gain_rows = lax.dynamic_slice_in_dim(gain, start, piece, 0)
+    part_gain = jnp.sum(part_qkv * weight_rows, axis=1) / gain_rows
+    square = jnp.sum(part_qkv * part_qkv) + jnp.sum(part_out * part_out)
+    square = square + jnp.sum(part_gain * part_gain)
+    square = small_sum(square.reshape(1), ("section", "lat", "lon"))[0]
+    both_bias = jnp.sum(grad_bias * grad_bias).reshape(1)
+    square = square + small_sum(both_bias, ("section",))[0]
     entries = 2 * (4 * width * width + width + heads)
-    grad_qkv, grad_outw, grad_gain, grad_bias = lax.psum(
-        (grad_qkv, grad_outw, grad_gain, grad_bias), ("lon", "lat")
-    )
-    square = (
-        jnp.sum(grad_qkv * grad_qkv)
-        + jnp.sum(grad_outw * grad_outw)
-        + jnp.sum(grad_gain * grad_gain)
-        + jnp.sum(grad_bias * grad_bias)
-    )
-    square = lax.psum(square, "section")
     factor = jnp.minimum(1.0, lax.rsqrt(square / entries + 1e-06))
-    grad_qkv = grad_qkv * factor
-    grad_outw = grad_outw * factor
-    grad_gain = grad_gain * factor
+
+    part_out = part_out.astype(jnp.bfloat16)
+    part_qkv = part_qkv.astype(jnp.bfloat16)
+    all_out = doubled(gathered(doubled(part_out, "lat", 2), "lon"), "lat", 1)
+    all_qkv = doubled(doubled(gathered(part_qkv, "lon"), "lat", 2), "lat", 1)
+    all_out = all_out.astype(jnp.float32) * factor
+    all_qkv = all_qkv.astype(jnp.float32)
+    grad_gain = jnp.sum(all_qkv * weight_qkv.astype(jnp.float32), axis=1) / gain * factor
+    all_qkv = all_qkv * factor
     grad_bias = grad_bias * factor
-    return (final_grad[None], grad_qkv[None], grad_outw[None], grad_gain[None], grad_bias[None])
+    return (final_grad[None], all_qkv[None], all_out[None], grad_gain[None], grad_bias[None])
 
 
 def solution(mesh):

time: 228 us -> 164 us (0.72)
  waiting for transfers between devices: 95.4 us -> 47.5 us
  blocking collectives: 36.2 us -> 0 us
  starting transfers between devices: 9.59 us -> 40.8 us
  between operations: 17.6 us -> 7.23 us
    psum x1 -> x0, waiting for transfers between devices: 77.6 us -> none  [body(): lax.psum((grad_qkv, grad_outw, grad_gain, grad_bias), ('lon', 'lat'))]
    psum x2 -> x0, blocking collectives: 36.2 us -> none  [the longest x1 30.8 us: body(): lax.psum((grad_qkv, grad_outw, grad_gain, grad_bias), ('lon', 'lat'))]
    ppermute x0 -> x18, waiting for transfers between devices: none -> 25 us  [swapped(): return lax.ppermute(value, axis, [(i, i ^ bit) for i in range(count)])]
    ppermute x6 -> x16, starting transfers between devices: 8.26 us -> 26 us  [from_behind(): lax.ppermute(value, axis, [(i, (i + by) % count) for i in range(count)])]
    ppermute x0 -> x18, starting transfers between devices: none -> 13.5 us  [swapped(): return lax.ppermute(value, axis, [(i, i ^ bit) for i in range(count)])]
    ppermute x6 -> x16, waiting for transfers between devices: 9.22 us -> 19.3 us  [from_behind(): lax.ppermute(value, axis, [(i, (i + by) % count) for i in range(count)])]
    ppermute x1, waiting for transfers between devices: 8.59 us -> 3.16 us  [passed_along(): return lax.ppermute(block, axis, route)]
    broadcast_in_dim x2 -> x0, other arithmetic: 4.85 us -> none  [the longest x1 3.79 us: body(): grad_qkv[None]]
  transfers between devices with their start and end apart: 8 -> 35, of which waited for: 6 -> 19; matrix products, arithmetic and copies ran while one was open for 4% -> 13% of each run, Pallas kernels for 0% -> 0%
where the time goes in v1:
time: 164 us; the launch traced here: 163 us
  waiting for transfers between devices  47.5 us (29%)
  starting transfers between devices  40.8 us (25%)
  matrix products  35.6 us (22%)
  other arithmetic  18.7 us (11%)
  local copies, waits for them, and re-layouts  13.6 us (8%)
  between operations  7.23 us (4%)
    ppermute x16, starting transfers between devices, from_behind(): lax.ppermute(value, axis, [(i, (i + by) % count) for i in range(count)])  26 us
    ppermute x18, waiting for transfers between devices, swapped(): return lax.ppermute(value, axis, [(i, i ^ bit) for i in range(count)])  25 us
    ppermute x16, waiting for transfers between devices, from_behind(): lax.ppermute(value, axis, [(i, (i + by) % count) for i in range(count)])  19.3 us
    ppermute x18, starting transfers between devices, swapped(): return lax.ppermute(value, axis, [(i, i ^ bit) for i in range(count)])  13.5 us
    dot_general x2, matrix products, window_backward(): jnp.einsum('bhij,bihd->bjhd', scaled_b, queries, preferred_element_type=j...  7.59 us
    dot_general x2, matrix products, window_backward(): jnp.einsum('bhij,bihd->bjhd', weights_b, grad_att, preferred_element_type...  5.93 us
    dot_general x2, matrix products, window_backward(): jnp.einsum('bhij,bjhd->bihd', scaled_b, keys_win, preferred_element_type=...  5.63 us
    sub x1, matrix products, window_backward(): grad_scores = weights * (grad_weights - inner)  5 us
  transfers between devices with their start and end apart: 35, of which 19 were waited for; matrix products, arithmetic and copies ran while one was open for 13% of the time, Pallas kernels for 0%

profile of v1, /device:TPU:0, one launch (start us, length us, event | category | flops | bytes accessed | tf_op | source)
XLA Modules:
  0.0 163.4 jit_solution(18191004284503157141)
XLA Ops:
  1.5 5.0 %collective-permute-start.1 = (bf16[6,6]{1,0:T(8,128)(2,1)S(1)}, bf16[6,6]{1,0:T(8,128)(2,1)S(1)}, u32[]{:S(2)}, u32[]{:S(2)}) collective-permute-start(bf16[6,6]{1,0:T(8,128)(2,1)S(1)} %get-tuple-element.49), channel_id=1, source_target_pairs={{0,12},{4,0},{8,4},{12,8},{1,13},{5,1},{9,5},{13,9},{2,14},{6,2},{... | collective-permute-start | bytes 224 | tf_op jit(solution)/shard_map/ppermute | solution.py:16
  6.5 1.0 fusion.99
  8.1 1.0 fusion.100
  10.6 2.0 %collective-permute-done = bf16[2,6,6,512]{3,0,2,1:T(2,128)(2,1)S(1)} collective-permute-done((bf16[2,6,6,512]{3,0,2,1:T(2,128)(2,1)S(1)}, bf16[2,6,6,512]{3,0,2,1:T(2,128)(2,1)S(1)}, u32[]{:S(2)}, u32[]{:S(2)}) %collective-permute-start) | collective-permute-done | bytes 73760 | tf_op jit(solution)/shard_map/ppermute | solution.py:16
  15.7 1.2 convolution_convert_fusion
  16.9 1.3 copy.57
  18.2 2.9 %fusion.63 = f32[16,144,144]{1,2,0:T(8,128)} fusion(bf16[144,16,32]{0,2,1:T(8,128)(2,1)} %bitcast.245, bf16[1,144,3,16,32]{1,4,3,2,0:T(8,128)(2,1)S(1)} %bitcast.231), kind=kOutput, calls=%fused_computation.96 | convolution fusion | flops 21233664 | bytes 1736704 | tf_op jit(solution)/shard_map/bihd,bjhd->bhij/dot_general | solution.py:108
  21.1 2.4 %fusion.102 = (f32[16,144]{1,0:T(8,128)S(1)}, f32[16,144,144]{1,2,0:T(8,128)}) fusion(f32[16,144]{1,0:T(8,128)S(1)} %broadcast_multiply_fusion.1, bf16[1,144,3,16,32]{1,4,3,2,0:T(8,128)(2,1)S(1)} %bitcast.232), kind=kOutput, calls=%fused_computation.165 | convolution fusion | flops 22560912 | bytes 1876992 | tf_op jit(solution)/shard_map/sub | solution.py:79
  23.5 3.0 %fusion.43 = bf16[1,144,1,16,32]{1,4,3,2,0:T(8,128)(2,1)} fusion(bf16[144,16,32]{0,2,1:T(8,128)(2,1)} %bitcast.246, f32[16,144,144]{1,2,0:T(8,128)} %get-tuple-element.51, f32[16,144]{1,0:T(8,128)S(1)} %get-tuple-element.50), kind=kOutput, calls=%fused_computation.42 | convolution fusion | flops 21970944 | bytes 1631232 | tf_op jit(solution)/shard_map/bhij,bihd->bjhd/dot_general | solution.py:111
  26.4 5.3 %fusion.37 = bf16[1,144,1,16,32]{1,4,3,2,0:T(8,128)(2,1)} fusion(f32[16,144,144]{1,2,0:T(8,128)} %fusion.63, bf16[1,144,3,16,32]{1,4,3,2,0:T(8,128)(2,1)S(1)} %bitcast.233, f32[16,144,144]{1,2,0:T(8,128)} %get-tuple-element.51, f32[16,144]{1,0:T(8,128)S(1)} %get-tuple-element.50), kind=kOutput, calls=%fused_computation.40 | convolution fusion | flops 23632272 | bytes 9879552 | tf_op jit(solution)/shard_map/bhij,bihd->bjhd/dot_general | solution.py:120
  31.7 5.3 %fusion.40 = bf16[1,144,1,16,32]{1,4,3,2,0:T(8,128)(2,1)} fusion(f32[16,144,144]{1,2,0:T(8,128)} %fusion.63, bf16[1,144,3,16,32]{1,4,3,2,0:T(8,128)(2,1)S(1)} %bitcast.234, f32[16,144,144]{1,2,0:T(8,128)} %get-tuple-element.51, f32[16,144]{1,0:T(8,128)S(1)} %get-tuple-element.50), kind=kOutput, calls=%fused_computation.41 | convolution fusion | flops 23632272 | bytes 9879552 | tf_op jit(solution)/shard_map/bhij,bjhd->bihd/dot_general | solution.py:117
  37.1 1.3 pad_maximum_fusion
  39.2 0.9 multiply_convert_fusion.4
  40.1 1.3 collective-permute-start.3
  41.4 1.1 convolution_convert_fusion.1
  42.4 1.7 %copy.71 = bf16[144,512]{1,0:T(8,128)(2,1)} copy(bf16[144,512]{0,1:T(8,128)(2,1)} %bitcast.253) | data formatting | bytes 294912 | tf_op jit(solution)/shard_map/reshape | solution.py:84
  44.2 3.2 %collective-permute-done.3 = bf16[144,512]{1,0:T(8,128)(2,1)S(1)} collective-permute-done((bf16[144,512]{1,0:T(8,128)(2,1)}, bf16[144,512]{1,0:T(8,128)(2,1)S(1)}, u32[]{:S(2)}, u32[]{:S(2)}) %collective-permute-start.3) | collective-permute-done | bytes 147488 | tf_op jit(solution)/shard_map/ppermute | solution.py:22
  47.3 1.0 convolution_convert_fusion.6
  48.3 1.7 %copy.64 = bf16[144,512]{0,1:T(8,128)(2,1)} copy(bf16[144,512]{1,0:T(8,128)(2,1)} %convolution_convert_fusion.6) | data formatting | bytes 294912 | tf_op jit(solution)/shard_map/convert_element_type | solution.py:105
  50.0 3.0 %fusion.46 = bf16[1,144,1,16,32]{1,4,3,2,0:T(8,128)(2,1)} fusion(bf16[144,16,32]{0,2,1:T(8,128)(2,1)} %bitcast.251, f32[16,144,144]{1,2,0:T(8,128)} %get-tuple-element.51, f32[16,144]{1,0:T(8,128)S(1)} %get-tuple-element.50), kind=kOutput, calls=%fused_computation.45 | convolution fusion | flops 21970944 | bytes 1631232 | tf_op jit(solution)/shard_map/bhij,bihd->bjhd/dot_general | solution.py:111
  53.0 5.0 %multiply_reduce_fusion.1 = (f32[16]{0:T(128)S(1)}, f32[16,144,144]{1,2,0:T(8,128)}) fusion(f32[144]{0:T(256)S(1)} %mul.238, bf16[144,16,32]{0,2,1:T(8,128)(2,1)} %bitcast.252, bf16[1,144,3,16,32]{1,4,3,2,0:T(8,128)(2,1)S(1)} %bitcast.236, f32[16,144,144]{1,2,0:T(8,128)} %get-tuple-element.51, f32[16,144]{1,0:T(8,128)S(1)} %get-tuple-element.50), kind=kOutput, calls=%fused_computation.6 | convolution fusion | flops 44792192 | bytes 7128128 | tf_op jit(solution)/shard_map/sub | solution.py:115
  58.0 2.3 %fusion.45 = bf16[1,144,1,16,32]{1,4,3,2,0:T(8,128)(2,1)S(1)} fusion(f32[16,144,144]{1,2,0:T(8,128)} %get-tuple-element.55, bf16[1,144,3,16,32]{1,4,3,2,0:T(8,128)(2,1)S(1)} %bitcast.237), kind=kOutput, calls=%fused_computation.44 | convolution fusion | flops 21970944 | bytes 1736704 | tf_op jit(solution)/shard_map/bhij,bihd->bjhd/dot_general | solution.py:120
  63.4 1.6 %copy-done.2 = f32[2,256,1536]{2,1,0:T(8,128)} copy-done((f32[2,256,1536]{2,1,0:T(8,128)}, f32[2,256,1536]{2,1,0:T(8,128)S(1)}, u32[]{:S(2)}) %copy-start.2) | copy-done | bytes 3145752
  65.1 1.0 fusion.47
  66.2 1.6 %collective-permute-start.16 = (bf16[64,512]{1,0:T(8,128)(2,1)S(1)}, bf16[64,512]{1,0:T(8,128)(2,1)S(1)}, u32[]{:S(2)}, u32[]{:S(2)}) collective-permute-start(bf16[64,512]{1,0:T(8,128)(2,1)S(1)} %get-tuple-element.35), channel_id=1, source_target_pairs={{0,4},{4,8},{8,12},{12,0},{1,5},{5,9},{9,13},{13,1},{2,6},{6,10},{... | collective-permute-start | bytes 196616 | tf_op jit(solution)/shard_map/ppermute | solution.py:16
  67.8 2.2 %collective-permute-start.18 = (bf16[64,512]{1,0:T(8,128)(2,1)S(1)}, bf16[64,512]{1,0:T(8,128)(2,1)S(1)}, u32[]{:S(2)}, u32[]{:S(2)}) collective-permute-start(bf16[64,512]{1,0:T(8,128)(2,1)S(1)} %get-tuple-element.36), channel_id=1, source_target_pairs={{0,12},{4,0},{8,4},{12,8},{1,13},{5,1},{9,5},{13,9},{2,14},{6,2},{... | collective-permute-start | bytes 196616 | tf_op jit(solution)/shard_map/ppermute | solution.py:16
  70.1 3.0 %collective-permute-done.16 = bf16[64,512]{1,0:T(8,128)(2,1)S(1)} collective-permute-done((bf16[64,512]{1,0:T(8,128)(2,1)S(1)}, bf16[64,512]{1,0:T(8,128)(2,1)S(1)}, u32[]{:S(2)}, u32[]{:S(2)}) %collective-permute-start.16) | collective-permute-done | bytes 65568 | tf_op jit(solution)/shard_map/ppermute | solution.py:16
  73.0 2.7 %collective-permute-done.17 = bf16[64,512]{1,0:T(8,128)(2,1)S(1)} collective-permute-done((bf16[64,512]{1,0:T(8,128)(2,1)S(1)}, bf16[64,512]{1,0:T(8,128)(2,1)S(1)}, u32[]{:S(2)}, u32[]{:S(2)}) %collective-permute-start.17) | collective-permute-done | bytes 65568 | tf_op jit(solution)/shard_map/ppermute | solution.py:16
  75.8 1.6 collective-permute-start.19
  77.4 0.9 convert_add_fusion.2
  78.3 1.0 reshape_transpose_reshape_reshape.3
  79.9 3.0 %collective-permute-done.26 = f32[16]{0:T(128)S(1)} collective-permute-done((f32[16]{0:T(128)S(1)}, f32[16]{0:T(128)S(1)}, u32[]{:S(2)}, u32[]{:S(2)}) %collective-permute-start.26) | collective-permute-done | bytes 96 | tf_op jit(solution)/shard_map/ppermute | solution.py:141
  82.9 2.0 %collective-permute-start.4 = (bf16[2,6,6,512]{3,2,1,0:T(8,128)(2,1)S(1)}, bf16[2,6,6,512]{3,2,1,0:T(8,128)(2,1)S(1)}, u32[]{:S(2)}, u32[]{:S(2)}) collective-permute-start(bf16[2,6,6,512]{3,2,1,0:T(8,128)(2,1)S(1)} %slice.78), channel_id=1, source_target_pairs={{0,4},{4,8},{8,12},{12,0},{1,5},{5,9},{9,13},{13,1},{2,6},{6,10},{... | collective-permute-start | bytes 221192 | tf_op jit(solution)/shard_map/ppermute | solution.py:16
  85.0 1.5 collective-permute-done.27
  87.0 1.5 fusion.79
  89.0 1.8 %bitcast_add_fusion = f32[256,1536]{1,0:T(8,128)S(1)} fusion(bf16[256,1536]{1,0:T(8,128)(2,1)} %collective-permute-done.5, f32[2,256,1536]{2,1,0:T(8,128)} %copy-done.2, s32[]{:T(128)S(6)} %select_n.184), kind=kLoop, calls=%fused_computation.19 | loop fusion | flops 786432 | bytes 3932164 | tf_op jit(solution)/shard_map/add | solution.py:149
  90.9 1.5 collective-permute-start.6
  93.1 3.8 %collective-permute-done.29 = f32[1]{0:T(128)} collective-permute-done((f32[1]{0:T(128)}, f32[1]{0:T(128)}, u32[]{:S(2)}, u32[]{:S(2)}) %collective-permute-start.29) | collective-permute-done | bytes 36 | tf_op jit(solution)/shard_map/ppermute | solution.py:141
  98.2 2.5 %collective-permute-start.32 = (bf16[64,512]{1,0:T(8,128)(2,1)S(1)}, bf16[64,512]{1,0:T(8,128)(2,1)S(1)}, u32[]{:S(2)}, u32[]{:S(2)}) collective-permute-start(bf16[64,512]{1,0:T(8,128)(2,1)S(1)} %pad_maximum_fusion.4), channel_id=1, source_target_pairs={{0,8},{4,12},{8,0},{12,4},{1,9},{5,13},{9,1},{13,5},{2,10},{6,14},... | collective-permute-start | bytes 196616 | tf_op jit(solution)/shard_map/ppermute | solution.py:16
  100.8 1.1 collective-permute-start.7
  101.9 2.8 %collective-permute-start.9 = (bf16[32,1536]{1,0:T(8,128)(2,1)S(1)}, bf16[32,1536]{1,0:T(8,128)(2,1)S(1)}, u32[]{:S(2)}, u32[]{:S(2)}) collective-permute-start(bf16[32,1536]{1,0:T(8,128)(2,1)S(1)} %get-tuple-element.31), channel_id=1, source_target_pairs={{0,12},{4,0},{8,4},{12,8},{1,13},{5,1},{9,5},{13,9},{2,14},{6,2},{... | collective-permute-start | bytes 294920 | tf_op jit(solution)/shard_map/ppermute | solution.py:16
  105.4 2.5 %collective-permute-done.7 = bf16[32,1536]{1,0:T(8,128)(2,1)S(1)} collective-permute-done((bf16[32,1536]{1,0:T(8,128)(2,1)S(1)}, bf16[32,1536]{1,0:T(8,128)(2,1)S(1)}, u32[]{:S(2)}, u32[]{:S(2)}) %collective-permute-start.7) | collective-permute-done | bytes 98336 | tf_op jit(solution)/shard_map/ppermute | solution.py:16
  107.9 2.2 %collective-permute-start.33 = (bf16[64,512]{1,0:T(8,128)(2,1)S(1)}, bf16[64,512]{1,0:T(8,128)(2,1)S(1)}, u32[]{:S(2)}, u32[]{:S(2)}) collective-permute-start(bf16[64,512]{1,0:T(8,128)(2,1)S(1)} %pad_maximum_fusion.4), channel_id=1, source_target_pairs={{0,12},{4,0},{8,4},{12,8},{1,13},{5,1},{9,5},{13,9},{2,14},{6,2},{... | collective-permute-start | bytes 196616 | tf_op jit(solution)/shard_map/ppermute | solution.py:16
  110.1 3.9 %collective-permute-done.8 = bf16[32,1536]{1,0:T(8,128)(2,1)S(1)} collective-permute-done((bf16[32,1536]{1,0:T(8,128)(2,1)S(1)}, bf16[32,1536]{1,0:T(8,128)(2,1)S(1)}, u32[]{:S(2)}, u32[]{:S(2)}) %collective-permute-start.8) | collective-permute-done | bytes 98336 | tf_op jit(solution)/shard_map/ppermute | solution.py:16
  114.8 1.2 collective-permute-start.10
  116.0 3.6 %collective-permute-start.11 = (bf16[32,1536]{1,0:T(8,128)(2,1)S(1)}, bf16[32,1536]{1,0:T(8,128)(2,1)S(1)}, u32[]{:S(2)}, u32[]{:S(2)}) collective-permute-start(bf16[32,1536]{1,0:T(8,128)(2,1)S(1)} %get-tuple-element.25), channel_id=1, source_target_pairs={{0,8},{4,12},{8,0},{12,4},{1,9},{5,13},{9,1},{13,5},{2,10},{6,14},... | collective-permute-start | bytes 294920 | tf_op jit(solution)/shard_map/ppermute | solution.py:16
  119.6 2.0 %collective-permute-done.10 = bf16[32,1536]{1,0:T(8,128)(2,1)S(1)} collective-permute-done((bf16[32,1536]{1,0:T(8,128)(2,1)S(1)}, bf16[32,1536]{1,0:T(8,128)(2,1)S(1)}, u32[]{:S(2)}, u32[]{:S(2)}) %collective-permute-start.10) | collective-permute-done | bytes 98336 | tf_op jit(solution)/shard_map/ppermute | solution.py:16
  121.6 2.1 %collective-permute-done.11 = bf16[32,1536]{1,0:T(8,128)(2,1)S(1)} collective-permute-done((bf16[32,1536]{1,0:T(8,128)(2,1)S(1)}, bf16[32,1536]{1,0:T(8,128)(2,1)S(1)}, u32[]{:S(2)}, u32[]{:S(2)}) %collective-permute-start.11) | collective-permute-done | bytes 98336 | tf_op jit(solution)/shard_map/ppermute | solution.py:16
  123.7 1.0 collective-permute-done.12
  124.9 7.6 %collective-permute-done.13 = bf16[128,1536]{1,0:T(8,128)(2,1)S(1)} collective-permute-done((bf16[128,1536]{1,0:T(8,128)(2,1)S(1)}, bf16[128,1536]{1,0:T(8,128)(2,1)S(1)}, u32[]{:S(2)}, u32[]{:S(2)}) %collective-permute-start.13) | collective-permute-done | bytes 393248 | tf_op jit(solution)/shard_map/ppermute | solution.py:141
  132.6 0.9 pad_maximum_fusion.2
  133.6 0.9 copy.73
  137.3 1.4 collective-permute-start.20
  138.6 2.3 %collective-permute-done.20 = f32[1]{0:T(128)} collective-permute-done((f32[1]{0:T(128)}, f32[1]{0:T(128)}, u32[]{:S(2)}, u32[]{:S(2)}) %collective-permute-start.20) | collective-permute-done | bytes 36 | tf_op jit(solution)/shard_map/ppermute | solution.py:141
  141.5 1.0 collective-permute-start.21
  143.4 1.4 collective-permute-start.22
  144.8 2.3 %collective-permute-done.22 = f32[1]{0:T(128)} collective-permute-done((f32[1]{0:T(128)}, f32[1]{0:T(128)}, u32[]{:S(2)}, u32[]{:S(2)}) %collective-permute-start.22) | collective-permute-done | bytes 36 | tf_op jit(solution)/shard_map/ppermute | solution.py:141
  147.7 1.9 %collective-permute-start.23 = (f32[1]{0:T(128)}, f32[1]{0:T(128)}, u32[]{:S(2)}, u32[]{:S(2)}) collective-permute-start(f32[1]{0:T(128)} %add.276), channel_id=1, source_target_pairs={{0,4},{4,0},{8,12},{12,8},{1,5},{5,1},{9,13},{13,9},{2,6},{6,2},{1... | collective-permute-start | bytes 20 | tf_op jit(solution)/shard_map/ppermute | solution.py:141
  149.6 1.8 %collective-permute-done.23 = f32[1]{0:T(128)} collective-permute-done((f32[1]{0:T(128)}, f32[1]{0:T(128)}, u32[]{:S(2)}, u32[]{:S(2)}) %collective-permute-start.23) | collective-permute-done | bytes 36 | tf_op jit(solution)/shard_map/ppermute | solution.py:141
  152.0 2.3 %collective-permute-start.24 = (f32[1]{0:T(128)}, f32[1]{0:T(128)}, u32[]{:S(2)}, u32[]{:S(2)}) collective-permute-start(f32[1]{0:T(128)} %add.277), channel_id=1, source_target_pairs={{0,8},{4,12},{8,0},{12,4},{1,9},{5,13},{9,1},{13,5},{2,10},{6,14},... | collective-permute-start | bytes 20 | tf_op jit(solution)/shard_map/ppermute | solution.py:141
  154.2 2.4 %collective-permute-done.24 = f32[1]{0:T(128)} collective-permute-done((f32[1]{0:T(128)}, f32[1]{0:T(128)}, u32[]{:S(2)}, u32[]{:S(2)}) %collective-permute-start.24) | collective-permute-done | bytes 36 | tf_op jit(solution)/shard_map/ppermute | solution.py:141
  157.2 1.1 convert_multiply_fusion.1
  158.8 1.4 broadcast_select_fusion.1
  161.3 2.1 %convert_multiply_fusion = f32[1,512,1536]{2,1,0:T(8,128)} fusion(bf16[1,256,1536]{2,1,0:T(8,128)(2,1)S(1)} %bitcast.225, bf16[1,256,1536]{2,1,0:T(8,128)(2,1)S(1)} %bitcast.224, f32[]{:T(128)} %bitcast.71), kind=kLoop, calls=%fused_computation.4 | loop fusion | flops 3932160 | bytes 4718596 | tf_op jit(solution)/shard_map/mul | solution.py:254
  (128 shorter events, 16.9 us)
Async XLA Ops:
  0.6 13.1 %copy-start = (bf16[1,512,512]{2,1,0:T(8,128)(2,1)S(1)}, bf16[1,512,512]{2,1,0:T(8,128)(2,1)}, u32[]{:S(2)}) copy-start(bf16[1,512,512]{2,1,0:T(8,128)(2,1)} %param.12) | copy-start | bytes 1572868
  1.5 8.1 %collective-permute-start.1 = (bf16[6,6]{1,0:T(8,128)(2,1)S(1)}, bf16[6,6]{1,0:T(8,128)(2,1)S(1)}, u32[]{:S(2)}, u32[]{:S(2)}) collective-permute-start(bf16[6,6]{1,0:T(8,128)(2,1)S(1)} %get-tuple-element.49), channel_id=1, source_target_pairs={{0,12},{4,0},{8,4},{12,8},{1,13},{5,1},{9,5},{13,9},{2,14},{6,2},{... | collective-permute-start | bytes 224 | tf_op jit(solution)/shard_map/ppermute | solution.py:16
  7.5 5.0 %collective-permute-start = (bf16[2,6,6,512]{3,0,2,1:T(2,128)(2,1)S(1)}, bf16[2,6,6,512]{3,0,2,1:T(2,128)(2,1)S(1)}, u32[]{:S(2)}, u32[]{:S(2)}) collective-permute-start(bf16[2,6,6,512]{3,0,2,1:T(2,128)(2,1)S(1)} %get-tuple-element.43), channel_id=1, source_target_pairs={{0,12},{4,0},{8,4},{12,8},{1,13},{5,1},{9,5},{13,9},{2,14},{6,2},{... | collective-permute-start | bytes 221192 | tf_op jit(solution)/shard_map/ppermute | solution.py:16
  9.1 4.4 %collective-permute-start.2 = (bf16[2,6,6,512]{3,0,2,1:T(2,128)(2,1)S(1)}, bf16[2,6,6,512]{3,0,2,1:T(2,128)(2,1)S(1)}, u32[]{:S(2)}, u32[]{:S(2)}) collective-permute-start(bf16[2,6,6,512]{3,0,2,1:T(2,128)(2,1)S(1)} %get-tuple-element.45), channel_id=1, source_target_pairs={{0,12},{4,0},{8,4},{12,8},{1,13},{5,1},{9,5},{13,9},{2,14},{6,2},{... | collective-permute-start | bytes 221192 | tf_op jit(solution)/shard_map/ppermute | solution.py:16
  13.0 2.4 %copy-start.9 = (f32[1,512]{1,0:T(1,128)S(1)}, f32[1,512]{1,0:T(1,128)}, u32[]{:S(2)}) copy-start(f32[1,512]{1,0:T(1,128)} %param.10) | copy-start | bytes 6148
  13.1 2.6 %copy-start.1 = (bf16[1,512,1536]{2,1,0:T(8,128)(2,1)S(1)}, bf16[1,512,1536]{2,1,0:T(8,128)(2,1)}, u32[]{:S(2)}) copy-start(bf16[1,512,1536]{2,1,0:T(8,128)(2,1)} %param.11) | copy-start | bytes 4718596
  38.3 3.0 %copy-start.10 = (f32[16,144,144]{1,2,0:T(8,128)S(1)}, f32[16,144,144]{1,2,0:T(8,128)}, u32[]{:S(2)}) copy-start(f32[16,144,144]{1,2,0:T(8,128)} %get-tuple-element.51) | copy-start | bytes 3981316
  40.1 7.2 %collective-permute-start.3 = (bf16[144,512]{1,0:T(8,128)(2,1)}, bf16[144,512]{1,0:T(8,128)(2,1)S(1)}, u32[]{:S(2)}, u32[]{:S(2)}) collective-permute-start(bf16[144,512]{1,0:T(8,128)(2,1)} %get-tuple-element.39), channel_id=1, source_target_pairs={{16,0},{17,1},{18,2},{19,3},{20,4},{21,5},{22,6},{23,7},{24,8},{25... | collective-permute-start | bytes 442376 | tf_op jit(solution)/shard_map/ppermute | solution.py:22
  58.0 2.4 %copy-start.3 = (f32[16,144,144]{1,2,0:T(8,128)S(1)}, f32[16,144,144]{1,2,0:T(8,128)}, u32[]{:S(2)}) copy-start(f32[16,144,144]{1,2,0:T(8,128)} %get-tuple-element.55) | copy-start | bytes 3981316
  58.0 2.8 %copy-start.8 = (bf16[1,144,1,16,32]{1,4,3,2,0:T(8,128)(2,1)S(1)}, bf16[1,144,1,16,32]{1,4,3,2,0:T(8,128)(2,1)}, u32[]{:S(2)}) copy-start(bf16[1,144,1,16,32]{1,4,3,2,0:T(8,128)(2,1)} %fusion.46) | copy-start | bytes 442372
  60.7 1.1 copy-start.5
  60.7 18.6 %collective-permute-start.25 = (f32[16]{0:T(128)S(1)}, f32[16]{0:T(128)S(1)}, u32[]{:S(2)}, u32[]{:S(2)}) collective-permute-start(f32[16]{0:T(128)S(1)} %get-tuple-element.54), channel_id=1, source_target_pairs={{0,1},{1,0},{2,3},{3,2},{4,5},{5,4},{6,7},{7,6},{8,9},{9,8},{10,11... | collective-permute-start | bytes 200 | tf_op jit(solution)/shard_map/ppermute | solution.py:141
  61.0 1.8 %copy-start.6 = (bf16[144,512]{1,0:T(8,128)(2,1)S(1)}, bf16[144,512]{1,0:T(8,128)(2,1)}, u32[]{:S(2)}) copy-start(bf16[144,512]{1,0:T(8,128)(2,1)} %get-tuple-element.38) | copy-start | bytes 442372
  62.2 3.8 %collective-permute-start.15 = (bf16[256,512]{1,0:T(8,128)(2,1)S(1)}, bf16[256,512]{1,0:T(8,128)(2,1)S(1)}, u32[]{:S(2)}, u32[]{:S(2)}) collective-permute-start(bf16[256,512]{1,0:T(8,128)(2,1)S(1)} %fusion.53), channel_id=1, source_target_pairs={{0,1},{1,0},{2,3},{3,2},{4,5},{5,4},{6,7},{7,6},{8,9},{9,8},{10,11... | collective-permute-start | bytes 786440 | tf_op jit(solution)/shard_map/ppermute | solution.py:141
  63.4 1.7 %copy-start.2 = (f32[2,256,1536]{2,1,0:T(8,128)}, f32[2,256,1536]{2,1,0:T(8,128)S(1)}, u32[]{:S(2)}) copy-start(f32[2,256,1536]{2,1,0:T(8,128)S(1)} %fusion.67) | copy-start | bytes 9437188
  66.2 6.9 %collective-permute-start.16 = (bf16[64,512]{1,0:T(8,128)(2,1)S(1)}, bf16[64,512]{1,0:T(8,128)(2,1)S(1)}, u32[]{:S(2)}, u32[]{:S(2)}) collective-permute-start(bf16[64,512]{1,0:T(8,128)(2,1)S(1)} %get-tuple-element.35), channel_id=1, source_target_pairs={{0,4},{4,8},{8,12},{12,0},{1,5},{5,9},{9,13},{13,1},{2,6},{6,10},{... | collective-permute-start | bytes 196616 | tf_op jit(solution)/shard_map/ppermute | solution.py:16
  67.8 5.2 %collective-permute-start.18 = (bf16[64,512]{1,0:T(8,128)(2,1)S(1)}, bf16[64,512]{1,0:T(8,128)(2,1)S(1)}, u32[]{:S(2)}, u32[]{:S(2)}) collective-permute-start(bf16[64,512]{1,0:T(8,128)(2,1)S(1)} %get-tuple-element.36), channel_id=1, source_target_pairs={{0,12},{4,0},{8,4},{12,8},{1,13},{5,1},{9,5},{13,9},{2,14},{6,2},{... | collective-permute-start | bytes 196616 | tf_op jit(solution)/shard_map/ppermute | solution.py:16
  70.1 5.7 %collective-permute-start.17 = (bf16[64,512]{1,0:T(8,128)(2,1)S(1)}, bf16[64,512]{1,0:T(8,128)(2,1)S(1)}, u32[]{:S(2)}, u32[]{:S(2)}) collective-permute-start(bf16[64,512]{1,0:T(8,128)(2,1)S(1)} %get-tuple-element.37), channel_id=1, source_target_pairs={{0,8},{4,12},{8,0},{12,4},{1,9},{5,13},{9,1},{13,5},{2,10},{6,14},... | collective-permute-start | bytes 196616 | tf_op jit(solution)/shard_map/ppermute | solution.py:16
  70.1 19.0 %collective-permute-start.5 = (bf16[256,1536]{1,0:T(8,128)(2,1)}, bf16[256,1536]{1,0:T(8,128)(2,1)}, u32[]{:S(2)}, u32[]{:S(2)}) collective-permute-start(bf16[256,1536]{1,0:T(8,128)(2,1)} %fusion.47), channel_id=1, source_target_pairs={{0,1},{1,0},{2,3},{3,2},{4,5},{5,4},{6,7},{7,6},{8,9},{9,8},{10,11... | collective-permute-start | bytes 2359304 | tf_op jit(solution)/shard_map/ppermute | solution.py:141
  75.8 1.6 copy-start.7
  75.8 11.2 %collective-permute-start.19 = (bf16[32,512]{1,0:T(8,128)(2,1)S(1)}, bf16[32,512]{1,0:T(8,128)(2,1)S(1)}, u32[]{:S(2)}, u32[]{:S(2)}) collective-permute-start(bf16[32,512]{1,0:T(8,128)(2,1)S(1)} %fusion.80), channel_id=1, source_target_pairs={{0,2},{1,3},{2,0},{3,1},{4,6},{5,7},{6,4},{7,5},{8,10},{9,11},{10,... | collective-permute-start | bytes 98312 | tf_op jit(solution)/shard_map/ppermute | solution.py:141
  79.2 11.7 %copy-start.4 = (f32[2,6,12,512]{3,2,1,0:T(8,128)}, f32[2,6,12,512]{3,2,1,0:T(8,128)S(1)}, u32[]{:S(2)}) copy-start(f32[2,6,12,512]{3,2,1,0:T(8,128)S(1)} %reshape_transpose_reshape_reshape.3) | copy-start | bytes 884740
  79.3 3.6 %collective-permute-start.26 = (f32[16]{0:T(128)S(1)}, f32[16]{0:T(128)S(1)}, u32[]{:S(2)}, u32[]{:S(2)}) collective-permute-start(f32[16]{0:T(128)S(1)} %add.279), channel_id=1, source_target_pairs={{0,2},{1,3},{2,0},{3,1},{4,6},{5,7},{6,4},{7,5},{8,10},{9,11},{10,... | collective-permute-start | bytes 200 | tf_op jit(solution)/shard_map/ppermute | solution.py:141
  82.9 3.5 %collective-permute-start.27 = (f32[16]{0:T(128)S(1)}, f32[16]{0:T(128)S(1)}, u32[]{:S(2)}, u32[]{:S(2)}) collective-permute-start(f32[16]{0:T(128)S(1)} %add.280), channel_id=1, source_target_pairs={{0,4},{4,0},{8,12},{12,8},{1,5},{5,1},{9,13},{13,9},{2,6},{6,2},{1... | collective-permute-start | bytes 200 | tf_op jit(solution)/shard_map/ppermute | solution.py:141
  82.9 15.1 %collective-permute-start.4 = (bf16[2,6,6,512]{3,2,1,0:T(8,128)(2,1)S(1)}, bf16[2,6,6,512]{3,2,1,0:T(8,128)(2,1)S(1)}, u32[]{:S(2)}, u32[]{:S(2)}) collective-permute-start(bf16[2,6,6,512]{3,2,1,0:T(8,128)(2,1)S(1)} %slice.78), channel_id=1, source_target_pairs={{0,4},{4,8},{8,12},{12,0},{1,5},{5,9},{9,13},{13,1},{2,6},{6,10},{... | collective-permute-start | bytes 221192 | tf_op jit(solution)/shard_map/ppermute | solution.py:16
  86.5 6.0 %collective-permute-start.28 = (f32[16]{0:T(128)S(1)}, f32[16]{0:T(128)S(1)}, u32[]{:S(2)}, u32[]{:S(2)}) collective-permute-start(f32[16]{0:T(128)S(1)} %add.281), channel_id=1, source_target_pairs={{0,8},{4,12},{8,0},{12,4},{1,9},{5,13},{9,1},{13,5},{2,10},{6,14},... | collective-permute-start | bytes 200 | tf_op jit(solution)/shard_map/ppermute | solution.py:141
  88.5 9.6 %collective-permute-start.30 = (bf16[32,512]{1,0:T(8,128)(2,1)S(1)}, bf16[32,512]{1,0:T(8,128)(2,1)S(1)}, u32[]{:S(2)}, u32[]{:S(2)}) collective-permute-start(bf16[32,512]{1,0:T(8,128)(2,1)S(1)} %get-tuple-element.40), channel_id=1, source_target_pairs={{0,2},{1,3},{2,0},{3,1},{4,6},{5,7},{6,4},{7,5},{8,10},{9,11},{10,... | collective-permute-start | bytes 98312 | tf_op jit(solution)/shard_map/ppermute | solution.py:141
  90.9 9.7 %collective-permute-start.6 = (bf16[128,1536]{1,0:T(8,128)(2,1)S(1)}, bf16[128,1536]{1,0:T(8,128)(2,1)S(1)}, u32[]{:S(2)}, u32[]{:S(2)}) collective-permute-start(bf16[128,1536]{1,0:T(8,128)(2,1)S(1)} %fusion.50), channel_id=1, source_target_pairs={{0,2},{1,3},{2,0},{3,1},{4,6},{5,7},{6,4},{7,5},{8,10},{9,11},{10,... | collective-permute-start | bytes 1179656 | tf_op jit(solution)/shard_map/ppermute | solution.py:141
  93.1 3.8 %collective-permute-start.29 = (f32[1]{0:T(128)}, f32[1]{0:T(128)}, u32[]{:S(2)}, u32[]{:S(2)}) collective-permute-start(f32[1]{0:T(128)} %bitcast.70), channel_id=1, source_target_pairs={{0,16},{16,0},{1,17},{17,1},{2,18},{18,2},{3,19},{19,3},{4,20},{20... | collective-permute-start | bytes 20 | tf_op jit(solution)/shard_map/ppermute | solution.py:141
  98.2 26.6 %collective-permute-start.32 = (bf16[64,512]{1,0:T(8,128)(2,1)S(1)}, bf16[64,512]{1,0:T(8,128)(2,1)S(1)}, u32[]{:S(2)}, u32[]{:S(2)}) collective-permute-start(bf16[64,512]{1,0:T(8,128)(2,1)S(1)} %pad_maximum_fusion.4), channel_id=1, source_target_pairs={{0,8},{4,12},{8,0},{12,4},{1,9},{5,13},{9,1},{13,5},{2,10},{6,14},... | collective-permute-start | bytes 196616 | tf_op jit(solution)/shard_map/ppermute | solution.py:16
  100.6 15.3 %collective-permute-start.31 = (bf16[64,512]{1,0:T(8,128)(2,1)S(1)}, bf16[64,512]{1,0:T(8,128)(2,1)S(1)}, u32[]{:S(2)}, u32[]{:S(2)}) collective-permute-start(bf16[64,512]{1,0:T(8,128)(2,1)S(1)} %pad_maximum_fusion.4), channel_id=1, source_target_pairs={{0,4},{4,8},{8,12},{12,0},{1,5},{5,9},{9,13},{13,1},{2,6},{6,10},{... | collective-permute-start | bytes 196616 | tf_op jit(solution)/shard_map/ppermute | solution.py:16
  100.8 7.1 %collective-permute-start.7 = (bf16[32,1536]{1,0:T(8,128)(2,1)S(1)}, bf16[32,1536]{1,0:T(8,128)(2,1)S(1)}, u32[]{:S(2)}, u32[]{:S(2)}) collective-permute-start(bf16[32,1536]{1,0:T(8,128)(2,1)S(1)} %get-tuple-element.30), channel_id=1, source_target_pairs={{0,4},{4,8},{8,12},{12,0},{1,5},{5,9},{9,13},{13,1},{2,6},{6,10},{... | collective-permute-start | bytes 294920 | tf_op jit(solution)/shard_map/ppermute | solution.py:16
  101.9 8.2 %collective-permute-start.9 = (bf16[32,1536]{1,0:T(8,128)(2,1)S(1)}, bf16[32,1536]{1,0:T(8,128)(2,1)S(1)}, u32[]{:S(2)}, u32[]{:S(2)}) collective-permute-start(bf16[32,1536]{1,0:T(8,128)(2,1)S(1)} %get-tuple-element.31), channel_id=1, source_target_pairs={{0,12},{4,0},{8,4},{12,8},{1,13},{5,1},{9,5},{13,9},{2,14},{6,2},{... | collective-permute-start | bytes 294920 | tf_op jit(solution)/shard_map/ppermute | solution.py:16
  104.7 9.4 %collective-permute-start.8 = (bf16[32,1536]{1,0:T(8,128)(2,1)S(1)}, bf16[32,1536]{1,0:T(8,128)(2,1)S(1)}, u32[]{:S(2)}, u32[]{:S(2)}) collective-permute-start(bf16[32,1536]{1,0:T(8,128)(2,1)S(1)} %get-tuple-element.32), channel_id=1, source_target_pairs={{0,8},{4,12},{8,0},{12,4},{1,9},{5,13},{9,1},{13,5},{2,10},{6,14},... | collective-permute-start | bytes 294920 | tf_op jit(solution)/shard_map/ppermute | solution.py:16
  107.9 16.9 %collective-permute-start.33 = (bf16[64,512]{1,0:T(8,128)(2,1)S(1)}, bf16[64,512]{1,0:T(8,128)(2,1)S(1)}, u32[]{:S(2)}, u32[]{:S(2)}) collective-permute-start(bf16[64,512]{1,0:T(8,128)(2,1)S(1)} %pad_maximum_fusion.4), channel_id=1, source_target_pairs={{0,12},{4,0},{8,4},{12,8},{1,13},{5,1},{9,5},{13,9},{2,14},{6,2},{... | collective-permute-start | bytes 196616 | tf_op jit(solution)/shard_map/ppermute | solution.py:16
  114.7 18.8 %slice-start = ((f32[2,6,12,512]{3,2,1,0:T(8,128)}), f32[2,6,6,512]{3,2,1,0:T(8,128)S(1)}, s32[]{:S(2)}) async-start(f32[2,6,12,512]{3,2,1,0:T(8,128)} %copy-done.4), calls=%async_computation | async-start | bytes 393216 | tf_op jit(solution)/shard_map/slice | solution.py:226
  114.8 6.8 %collective-permute-start.10 = (bf16[32,1536]{1,0:T(8,128)(2,1)S(1)}, bf16[32,1536]{1,0:T(8,128)(2,1)S(1)}, u32[]{:S(2)}, u32[]{:S(2)}) collective-permute-start(bf16[32,1536]{1,0:T(8,128)(2,1)S(1)} %get-tuple-element.25), channel_id=1, source_target_pairs={{0,4},{4,8},{8,12},{12,0},{1,5},{5,9},{9,13},{13,1},{2,6},{6,10},{... | collective-permute-start | bytes 294920 | tf_op jit(solution)/shard_map/ppermute | solution.py:16
  116.0 7.7 %collective-permute-start.11 = (bf16[32,1536]{1,0:T(8,128)(2,1)S(1)}, bf16[32,1536]{1,0:T(8,128)(2,1)S(1)}, u32[]{:S(2)}, u32[]{:S(2)}) collective-permute-start(bf16[32,1536]{1,0:T(8,128)(2,1)S(1)} %get-tuple-element.25), channel_id=1, source_target_pairs={{0,8},{4,12},{8,0},{12,4},{1,9},{5,13},{9,1},{13,5},{2,10},{6,14},... | collective-permute-start | bytes 294920 | tf_op jit(solution)/shard_map/ppermute | solution.py:16
  119.6 5.1 %collective-permute-start.12 = (bf16[32,1536]{1,0:T(8,128)(2,1)S(1)}, bf16[32,1536]{1,0:T(8,128)(2,1)S(1)}, u32[]{:S(2)}, u32[]{:S(2)}) collective-permute-start(bf16[32,1536]{1,0:T(8,128)(2,1)S(1)} %get-tuple-element.25), channel_id=1, source_target_pairs={{0,12},{4,0},{8,4},{12,8},{1,13},{5,1},{9,5},{13,9},{2,14},{6,2},{... | collective-permute-start | bytes 294920 | tf_op jit(solution)/shard_map/ppermute | solution.py:16
  124.7 7.8 %collective-permute-start.13 = (bf16[128,1536]{1,0:T(8,128)(2,1)S(1)}, bf16[128,1536]{1,0:T(8,128)(2,1)S(1)}, u32[]{:S(2)}, u32[]{:S(2)}) collective-permute-start(bf16[128,1536]{1,0:T(8,128)(2,1)S(1)} %bitcast.241), channel_id=1, source_target_pairs={{0,2},{1,3},{2,0},{3,1},{4,6},{5,7},{6,4},{7,5},{8,10},{9,11},{10,... | collective-permute-start | bytes 1179656 | tf_op jit(solution)/shard_map/ppermute | solution.py:141
  124.8 9.7 %collective-permute-start.34 = (bf16[256,512]{1,0:T(8,128)(2,1)S(1)}, bf16[256,512]{1,0:T(8,128)(2,1)S(1)}, u32[]{:S(2)}, u32[]{:S(2)}) collective-permute-start(bf16[256,512]{1,0:T(8,128)(2,1)S(1)} %bitcast.244), channel_id=1, source_target_pairs={{0,1},{1,0},{2,3},{3,2},{4,5},{5,4},{6,7},{7,6},{8,9},{9,8},{10,11... | collective-permute-start | bytes 786440 | tf_op jit(solution)/shard_map/ppermute | solution.py:141
  133.5 25.3 %collective-permute-start.14 = (bf16[256,1536]{1,0:T(8,128)(2,1)}, bf16[256,1536]{1,0:T(8,128)(2,1)}, u32[]{:S(2)}, u32[]{:S(2)}) collective-permute-start(bf16[256,1536]{1,0:T(8,128)(2,1)} %pad_maximum_fusion.2), channel_id=1, source_target_pairs={{0,1},{1,0},{2,3},{3,2},{4,5},{5,4},{6,7},{7,6},{8,9},{9,8},{10,11... | collective-permute-start | bytes 2359304 | tf_op jit(solution)/shard_map/ppermute | solution.py:141
  137.3 3.7 %collective-permute-start.20 = (f32[1]{0:T(128)}, f32[1]{0:T(128)}, u32[]{:S(2)}, u32[]{:S(2)}) collective-permute-start(f32[1]{0:T(128)} %bitcast.69), channel_id=1, source_target_pairs={{0,16},{16,0},{1,17},{17,1},{2,18},{18,2},{3,19},{19,3},{4,20},{20... | collective-permute-start | bytes 20 | tf_op jit(solution)/shard_map/ppermute | solution.py:141
  141.5 1.3 collective-permute-start.21
  143.4 3.7 %collective-permute-start.22 = (f32[1]{0:T(128)}, f32[1]{0:T(128)}, u32[]{:S(2)}, u32[]{:S(2)}) collective-permute-start(f32[1]{0:T(128)} %add.275), channel_id=1, source_target_pairs={{0,2},{1,3},{2,0},{3,1},{4,6},{5,7},{6,4},{7,5},{8,10},{9,11},{10,... | collective-permute-start | bytes 20 | tf_op jit(solution)/shard_map/ppermute | solution.py:141
  147.7 3.7 %collective-permute-start.23 = (f32[1]{0:T(128)}, f32[1]{0:T(128)}, u32[]{:S(2)}, u32[]{:S(2)}) collective-permute-start(f32[1]{0:T(128)} %add.276), channel_id=1, source_target_pairs={{0,4},{4,0},{8,12},{12,8},{1,5},{5,1},{9,13},{13,9},{2,6},{6,2},{1... | collective-permute-start | bytes 20 | tf_op jit(solution)/shard_map/ppermute | solution.py:141
  152.0 4.6 %collective-permute-start.24 = (f32[1]{0:T(128)}, f32[1]{0:T(128)}, u32[]{:S(2)}, u32[]{:S(2)}) collective-permute-start(f32[1]{0:T(128)} %add.277), channel_id=1, source_target_pairs={{0,8},{4,12},{8,0},{12,4},{1,9},{5,13},{9,1},{13,5},{2,10},{6,14},... | collective-permute-start | bytes 20 | tf_op jit(solution)/shard_map/ppermute | solution.py:141

commit v2 on v1

v2 whole, which is shorter than its diff:
```python
import functools

import jax
import jax.numpy as jnp
from jax import lax
from jax.experimental import pallas as pl
from jax.experimental.pallas import tpu as pltpu
from jax.sharding import PartitionSpec as P

SHIFT = 6
GROUP = 128
EPSILON = 1e-05
F32 = jnp.float32
BF16 = jnp.bfloat16


def from_behind(value, axis, by):
    count = lax.axis_size(axis)
    return lax.ppermute(value, axis, [(i, (i + by) % count) for i in range(count)])


def passed_along(block, axis, distance):
    devices = range(lax.axis_size(axis))
    route = [(i - distance, i) for i in devices if i - distance in devices]
    return lax.ppermute(block, axis, route)


def swapped(value, axis, bit):
    count = lax.axis_size(axis)
    return lax.ppermute(value, axis, [(i, i ^ bit) for i in range(count)])


def dot(left, right):
    return jnp.dot(left, right, preferred_element_type=F32)


def dot_last(left, right):
    return lax.dot_general(left, right, (((1,), (1,)), ((), ())), preferred_element_type=F32)


def call(kernel, outs, scratch=(), smem=(), operands=(), flops=10**8):
    moved = sum(o.size * o.dtype.itemsize for o in list(outs) + list(operands))
    return pl.pallas_call(
        kernel,
        out_shape=list(outs),
        in_specs=[
            pl.BlockSpec(memory_space=pltpu.SMEM if i in smem else pltpu.VMEM)
            for i in range(len(operands))
        ],
        out_specs=[pl.BlockSpec(memory_space=pltpu.VMEM) for _ in outs],
        scratch_shapes=list(scratch),
        compiler_params=pltpu.CompilerParams(vmem_limit_bytes=40 * 2**20),
        cost_estimate=pl.CostEstimate(flops=flops, bytes_accessed=moved, transcendentals=0),
    )(*operands)


def shape(dims, dtype):
    return jax.ShapeDtypeStruct(dims, dtype)


def pack_kernel(tokens, cot, land, own, rim, own32, rim32):
    levels, lats, cols, width = tokens.shape
    half = levels * lats * SHIFT
    rim32[2 * half :, :] = jnp.zeros((rim32.shape[0] - 2 * half, width), F32)
    for which, ref in enumerate((tokens, cot)):
        for level in range(levels):
            for lat in range(lats):
                base = which * half + (level * lats + lat) * SHIFT
                line = ref[level, lat].astype(F32)
                rim32[base : base + SHIFT, :] = line[:SHIFT]
                own32[base : base + SHIFT, :] = line[SHIFT:]
    rim32[2 * half : 2 * half + lats, :cols] = land[...].astype(F32)
    own[...] = own32[...].astype(BF16)
    rim[...] = rim32[...].astype(BF16)


def unpack_kernel(own, back, grid):
    levels, lats, cols, width = grid.shape
    came = back[...].astype(F32)
    for level in range(levels):
        for lat in range(lats):
            base = (level * lats + lat) * SHIFT
            grid[level, lat, :SHIFT, :] = came[base : base + SHIFT]
            grid[level, lat, SHIFT:, :] = own[base : base + SHIFT, :]


def land_column(land, rows, first):
    lats, cols = land.shape
    row = lax.broadcasted_iota(jnp.int32, (rows, lats), 0)
    lat = lax.rem(lax.div(row, SHIFT), lats)
    pick = (lat == lax.broadcasted_iota(jnp.int32, (rows, lats), 1)).astype(F32)
    lines = dot(pick.astype(BF16), land.astype(BF16))
    row = lax.broadcasted_iota(jnp.int32, (rows, cols), 0)
    column = lax.broadcasted_iota(jnp.int32, (rows, cols), 1)
    here = column == lax.rem(row, SHIFT) + first
    return jnp.sum(jnp.where(here, lines, 0.0), axis=1, keepdims=True)


def head_masks(dtype, size):
    lane = lax.broadcasted_iota(jnp.int32, (1, GROUP), 1)
    return [
        (lax.div(lane, size) == part).astype(F32).astype(dtype) for part in range(GROUP // size)
    ]


def stacked(block, masks):
    return jnp.concatenate([block * mask for mask in masks], axis=0)


def folded(block, masks):
    rows = block.shape[0] // len(masks)
    return sum(block[i * rows : (i + 1) * rows] * mask for i, mask in enumerate(masks))


def back_through(grad_out, probs, qkv, keys_t, weight_out, grad_proj, size, land):
    count, width = grad_out.shape
    per = GROUP // size
    scale = size ** (-0.5)
    masks_b, masks = head_masks(BF16, size), head_masks(F32, size)
    att_t = dot_last(weight_out[...], grad_out)
    grad_att = att_t.T.astype(BF16)
    att_t = att_t.astype(BF16)
    lane = lax.broadcasted_iota(jnp.int32, (1, GROUP), 1)
    bias_row = jnp.zeros((1, GROUP), F32)
    for group in range(width // GROUP):
        at = group * GROUP
        values = qkv[:, 2 * width + at : 2 * width + at + GROUP]
        grad_probs = dot(stacked(values, masks_b), att_t[at : at + GROUP, :])
        scores_b, probs_b, queries_t = [], [], []
        for part in range(per):
            head = group * per + part
            weights = probs[head * count : (head + 1) * count, :]
            grad_weights = grad_probs[part * count : (part + 1) * count]
            inner = jnp.sum(weights * grad_weights, axis=0, keepdims=True)
            grad_scores = weights * (grad_weights - inner)
            if land is not None:
                on_land = jnp.sum(grad_scores * land, axis=0, keepdims=True)
                on_land = jnp.sum(on_land, axis=1, keepdims=True)
                bias_row = bias_row + jnp.where(lane == head, on_land, 0.0)
            scaled_b = (grad_scores * scale).astype(BF16)
            scores_b.append(scaled_b)
            probs_b.append(weights.astype(BF16))
            queries_t.append(dot(keys_t[head * size : (head + 1) * size, :], scaled_b))
        queries = qkv[:, at : at + GROUP]
        grad_keys = dot(jnp.concatenate(scores_b, axis=0), queries)
        grad_values = dot(jnp.concatenate(probs_b, axis=0), grad_att[:, at : at + GROUP])
        grad_proj[:, at : at + GROUP] = jnp.concatenate(queries_t, axis=0).T.astype(BF16)
        grad_proj[:, width + at : width + at + GROUP] = folded(grad_keys, masks).astype(BF16)
        grad_proj[:, 2 * width + at : 2 * width + at + GROUP] = folded(grad_values, masks).astype(
            BF16
        )
    return bias_row


def through_norm(grad_proj, weight_qkv, gain, normed, inverse):
    scaled = dot_last(grad_proj, weight_qkv[...]) * gain[...]
    mean = jnp.mean(scaled, axis=-1, keepdims=True)
    along = jnp.mean(scaled * normed, axis=-1, keepdims=True)
    return inverse * (scaled - mean - normed * along)


def forward_kernel(
    bias, own, rim, land_own, gain, weight_qkv, weight_out,
    skip, cot, normed_out, inverse_out, normed_t, qkv, keys_t, probs, attended_t, land_out,
    grad_proj, values_t,
):
    width = gain.shape[1]
    heads = bias.shape[1]
    size = width // heads
    half = own.shape[0] // 2
    count = 2 * half
    per = GROUP // size
    scale = size ** (-0.5)
    masks_b = head_masks(BF16, size)
    mine = own[...].astype(F32)
    came = rim[...].astype(F32)
    lats, cols = land_own.shape
    land = jnp.concatenate(
        [
            land_column(land_own[...].astype(F32), half, SHIFT),
            land_column(came[2 * half : 2 * half + lats, :cols], half, 0),
        ],
        axis=0,
    )
    land_out[...] = jnp.broadcast_to(land, land_out.shape)
    values = jnp.concatenate([mine[:half], came[:half]], axis=0)
    centred = values - jnp.mean(values, axis=-1, keepdims=True)
    inverse = lax.rsqrt(jnp.mean(centred * centred, axis=-1, keepdims=True) + EPSILON)
    normed = centred * inverse
    normed_out[...] = normed
    inverse_out[...] = jnp.broadcast_to(inverse, inverse_out.shape)
    normed_b = (normed * gain[...]).astype(BF16)
    normed_t[...] = normed_b.T
    qkv[...] = dot(normed_b, weight_qkv[...]).astype(BF16)
    queries_t = qkv[:, :width].T
    keys_t[...] = qkv[:, width : 2 * width].T
    values_t[...] = qkv[:, 2 * width :].T
    for group in range(width // GROUP):
        at = group * GROUP
        keys = qkv[:, width + at : width + at + GROUP]
        scores = dot(stacked(keys, masks_b), queries_t[at : at + GROUP, :])
        for part in range(per):
            head = group * per + part
            block = scores[part * count : (part + 1) * count] * scale + bias[0, head] * land
            block = jnp.exp(block - jnp.max(block, axis=0, keepdims=True))
            weights = block * (1.0 / jnp.sum(block, axis=0, keepdims=True))
            probs[head * count : (head + 1) * count, :] = weights
            out = dot(values_t[head * size : (head + 1) * size, :], weights.astype(BF16))
            attended_t[head * size : (head + 1) * size, :] = out.astype(BF16)
    grad_out = jnp.concatenate([mine[half:], came[half : 2 * half]], axis=0)
    cot[...] = grad_out.astype(BF16)
    back_through(cot[...], probs, qkv, keys_t, weight_out, grad_proj, size, None)
    skip[...] = (
        through_norm(grad_proj[...], weight_qkv, gain, normed, inverse) + grad_out
    ).astype(BF16)


def backward_kernel(
    core, skip, cot, qkv, keys_t, probs, land, weight_out, normed_t, attended_t,
    total_out, grad_proj, bias_out, give_p, give_q,
    *, heads,
):
    count, width = cot.shape
    total_out[...] = (cot[...].astype(F32) + skip[...].astype(F32)).astype(BF16)
    bias_row = back_through(
        total_out[...], probs, qkv, keys_t, weight_out, grad_proj, width // heads, land[:, :1]
    )
    bias_out[...] = jnp.broadcast_to(bias_row, bias_out.shape)
    half = width // 2
    rows = pl.ds(pl.multiple_of((1 - core[0]) * half, half), half)
    weight_rows(rows, normed_t, attended_t, grad_proj, total_out, bias_row, give_p, give_q)


def weight_rows(rows, normed_t, attended_t, grad_proj, total, bias_row, out_p, out_q):
    width = normed_t.shape[0]
    tokens = normed_t[rows, :]
    out_p[:, : 2 * width] = dot(tokens, grad_proj[:, : 2 * width]).astype(out_p.dtype)
    out_p[:, 2 * width :] = jnp.broadcast_to(bias_row, (out_p.shape[0], GROUP)).astype(out_p.dtype)
    out_q[:, :width] = dot(tokens, grad_proj[:, 2 * width :]).astype(out_q.dtype)
    out_q[:, width:] = dot(attended_t[rows, :], total[...]).astype(out_q.dtype)


def finish_kernel(
    core, total, grad_proj, bias_row, normed_t, attended_t, normed, inverse, weight_qkv, gain,
    keep_p, keep_q, own, back,
):
    count, width = total.shape
    half = width // 2
    rows = pl.ds(pl.multiple_of(core[0] * half, half), half)
    bias_b = bias_row[:1, :].astype(BF16).astype(F32)
    weight_rows(rows, normed_t, attended_t, grad_proj, total, bias_b, keep_p, keep_q)
    final = through_norm(grad_proj[...], weight_qkv, gain, normed[...], inverse[:, :1])
    final = final + total[...].astype(F32)
    own[...] = final[: count // 2]
    back[...] = final[count // 2 :].astype(BF16)


def split_two(block, axis, bit):
    mine = (lax.axis_index(axis) // bit) % 2
    pair = block.reshape(2, block.shape[0] // 2, -1)
    give = lax.dynamic_index_in_dim(pair, 1 - mine, 0, keepdims=False).astype(BF16)
    return give, lax.dynamic_index_in_dim(pair, mine, 0, keepdims=False)


def halved(block, axis, bit):
    give, keep = split_two(block, axis, bit)
    return keep + swapped(give, axis, bit).astype(F32)


def scattered(block, axis):
    count = lax.axis_size(axis)
    mine = lax.axis_index(axis)
    pieces = block.reshape(count, block.shape[0] // count, -1)
    total = lax.dynamic_index_in_dim(pieces, mine, 0, keepdims=False)
    others = []
    for by in range(1, count):
        give = lax.dynamic_index_in_dim(pieces, (mine + by) % count, 0, keepdims=False)
        others.append(from_behind(give.astype(BF16), axis, by))
    for other in others:
        total = total + other.astype(F32)
    return total, others


def doubled(block, axis, bit):
    mine = (lax.axis_index(axis) // bit) % 2
    other = swapped(block, axis, bit)
    low = jnp.where(mine == 0, block, other)
    high = jnp.where(mine == 0, other, block)
    return jnp.concatenate([low, high], axis=0)


def gathered(block, axis):
    count = lax.axis_size(axis)
    mine = lax.axis_index(axis)
    whole = jnp.zeros((count,) + block.shape, block.dtype)
    whole = lax.dynamic_update_index_in_dim(whole, block, mine, 0)
    for by in range(1, count):
        whole = lax.dynamic_update_index_in_dim(
            whole, from_behind(block, axis, by), (mine - by) % count, 0
        )
    return whole.reshape(count * block.shape[0], -1)


def sum_squares(block):
    wide = block.astype(F32)
    return jnp.sum(wide * wide)


def body(inputs, cotangent, land_sea, gains, qkv_weight, out_weight, land_bias):
    tokens, own_cot = inputs[0], cotangent[0]
    weight_qkv, weight_out = qkv_weight[0], out_weight[0]
    levels, lats, cols, width = tokens.shape
    heads = land_bias.shape[1]
    half = levels * lats * SHIFT
    count = 2 * half
    packed = half * 2 + 16

    own, rim = call(
        pack_kernel,
        [shape((2 * half, width), BF16), shape((packed, width), BF16)],
        scratch=[pltpu.VMEM((2 * half, width), F32), pltpu.VMEM((packed, width), F32)],
        operands=(tokens, own_cot, land_sea),
    )
    rim = from_behind(rim, "lon", -1)
    skip, cot, normed, inverse, normed_t, qkv, keys_t, probs, attended_t, land = call(
        forward_kernel,
        [
            shape((count, width), BF16),
            shape((count, width), BF16),
            shape((count, width), F32),
            shape((count, GROUP), F32),
            shape((width, count), BF16),
            shape((count, 3 * width), BF16),
            shape((width, count), BF16),
            shape((heads * count, count), F32),
            shape((width, count), BF16),
            shape((count, GROUP), F32),
        ],
        scratch=[pltpu.VMEM((count, 3 * width), BF16), pltpu.VMEM((width, count), BF16)],
        smem=(0,),
        operands=(land_bias, own, rim, land_sea, gains, weight_qkv, weight_out),
        flops=10**9,
    )
    skip = passed_along(skip, "section", -1)
    lat, lon = lax.axis_index("lat"), lax.axis_index("lon")
    core = (lat % 2).astype(jnp.int32).reshape(1)
    total, grad_proj, bias_row, give_p, give_q = call(
        functools.partial(backward_kernel, heads=heads),
        [
            shape((count, width), BF16),
            shape((count, 3 * width), BF16),
            shape((8, GROUP), F32),
            shape((width // 2, 2 * width + GROUP), BF16),
            shape((width // 2, 2 * width), BF16),
        ],
        smem=(0,),
        operands=(core, skip, cot, qkv, keys_t, probs, land, weight_out, normed_t, attended_t),
        flops=10**9,
    )
    came_p = swapped(give_p, "lat", 1)
    came_q = swapped(give_q, "lat", 1)
    keep_p, keep_q, own_grad, back = call(
        finish_kernel,
        [
            shape((width // 2, 2 * width + GROUP), F32),
            shape((width // 2, 2 * width), F32),
            shape((half, width), F32),
            shape((half, width), BF16),
        ],
        smem=(0,),
        operands=(
            core, total, grad_proj, bias_row, normed_t, attended_t, normed, inverse,
            weight_qkv, gains,
        ),
        flops=5 * 10**8,
    )
    back = from_behind(back, "lon", 1)
    (final_grad,) = call(
        unpack_kernel, [shape(tokens.shape, F32)], operands=(own_grad, back)
    )

    part_p = keep_p + came_p.astype(F32)
    part_q = keep_q + came_q.astype(F32)
    give, keep = split_two(part_p, "lat", 2)
    came = swapped(give, "lat", 2).astype(F32)
    is_bias = lax.broadcasted_iota(jnp.int32, keep.shape, 1) >= 2 * width
    part_p = jnp.where(is_bias, lax.reduce_precision(keep, 8, 7), keep) + came
    bias_part = lax.reduce_precision(part_p[:1, 2 * width :], 8, 7)
    part_p, others = scattered(part_p, "lon")
    bias_parts = [bias_part] + [other[:1, 2 * width :].astype(F32) for other in others]
    bias_parts = jnp.concatenate(bias_parts[:1] + bias_parts[:0:-1], axis=0)
    grad_bias = jnp.sum(jnp.roll(bias_parts, lon, axis=0), axis=0)[:heads]
    part_q = halved(scattered(part_q, "lon")[0], "lat", 2)
    part_p = part_p[:, : 2 * width].astype(BF16)
    part_q = part_q.astype(BF16)
    half_p = doubled(gathered(part_p, "lon"), "lat", 2)
    half_q = gathered(doubled(part_q, "lat", 2), "lon")

    mine = lat % 2
    weight_half = lax.dynamic_slice_in_dim(weight_qkv, mine * (width // 2), width // 2, 0)
    gain_half = lax.dynamic_slice_in_dim(gains[0], mine * (width // 2), width // 2, 0)
    weight_half = weight_half.astype(F32)
    gain_half = (
        jnp.sum(half_p.astype(F32) * weight_half[:, : 2 * width], axis=1)
        + jnp.sum(half_q[:, :width].astype(F32) * weight_half[:, 2 * width :], axis=1)
    ) / gain_half
    square = sum_squares(half_p) + sum_squares(half_q) + sum_squares(gain_half)
    square = square + 0.5 * sum_squares(grad_bias)
    row = jnp.concatenate([gain_half, square.reshape(1), jnp.zeros((127,), F32)])
    row = row.reshape(1, -1)
    sections, lats_on = lax.axis_size("section"), lax.axis_size("lat")
    pairs = [
        (s * lats_on + i, (sections - 1 - s) * lats_on + (i ^ 1))
        for s in range(sections) for i in range(lats_on)
    ]
    row_other = swapped(row, "lat", 1)
    square = square + row_other[0, width // 2]
    square = square + (
        swapped(row[:, width // 2 :], "section", 1)[0, 0]
        + lax.ppermute(row[:, width // 2 :], ("section", "lat"), pairs)[0, 0]
    )
    entries = 2 * (4 * width * width + width + heads)
    factor = jnp.minimum(1.0, lax.rsqrt(square / entries + 1e-06))
    gain_other = row_other[0, : width // 2]
    grad_gain = jnp.concatenate(
        [
            jnp.where(mine == 0, gain_half, gain_other),
            jnp.where(mine == 0, gain_other, gain_half),
        ]
    )
    all_p = doubled(half_p, "lat", 1).astype(F32) * factor
    all_q = doubled(half_q, "lat", 1).astype(F32) * factor
    grad_qkv = jnp.concatenate([all_p, all_q[:, :width]], axis=1)
    grad_out = all_q[:, width:]
    return (
        final_grad[None],
        grad_qkv[None],
        grad_out[None],
        (grad_gain * factor)[None],
        (grad_bias * factor)[None],
    )


def solution(mesh):
    placed = (
        P("section", None, "lat", "lon", None),
        P("section", None, "lat", "lon", None),
        P("lat", "lon"),
        P("section", None),
        P("section", None, None),
        P("section", None, None),
        P("section", None),
    )
    return jax.shard_map(
        body,
        mesh=mesh,
        in_specs=placed,
        out_specs=(
            P("section", None, "lat", "lon", None),
            P("section", None, None),
            P("section", None, None),
            P("section", None),
            P("section", None),
        ),
        check_vma=False,
    )
```

time: 164 us -> 122 us (0.74)
  matrix products: 35.6 us -> 0 us
  Pallas kernels: 0 us -> 10.5 us
  starting transfers between devices: 40.8 us -> 33.4 us
  waiting for transfers between devices: 47.5 us -> 40.8 us
  other arithmetic: 18.7 us -> 12.2 us
  local copies, waits for them, and re-layouts: 13.6 us -> 20 us
  between operations: 7.23 us -> 4.51 us
    dot_general x15 -> x0, matrix products: 28.2 us -> none  [the longest x2 7.59 us: window_backward(): jnp.einsum('bhij,bihd->bjhd', scaled_b, queries, preferred_element_type=j...]
    ppermute x18 -> x10, waiting for transfers between devices: 25 us -> 10.7 us  [swapped(): return lax.ppermute(value, axis, [(i, i ^ bit) for i in range(count)])]
    unnamed x23 -> x55, local copies, waits for them, and re-layouts: 2.71 us -> 16.9 us
    pallas_call x0 -> x5, Pallas kernels: none -> 10.5 us  [call(): pl.pallas_call(kernel, out_shape=list(outs), in_specs=[pl.BlockSpec(memor...]
    sub x2 -> x0, matrix products: 7.4 us -> none  [the longest x1 5 us: window_backward(): grad_scores = weights * (grad_weights - inner)]
    ppermute x18 -> x10, starting transfers between devices: 13.5 us -> 7.95 us  [swapped(): return lax.ppermute(value, axis, [(i, i ^ bit) for i in range(count)])]
    convert_element_type x15 -> x4, local copies, waits for them, and re-layouts: 5.29 us -> 0.15 us  [the longest x2 0.09 us: scattered(): others.append(from_behind(give.astype(BF16), axis, by))]
    ppermute x16 -> x14, waiting for transfers between devices: 19.3 us -> 24.4 us  [from_behind(): lax.ppermute(value, axis, [(i, (i + by) % count) for i in range(count)])]
  transfers between devices with their start and end apart: 35 -> 26, of which waited for: 19 -> 12; matrix products, arithmetic and copies ran while one was open for 13% -> 11% of each run, Pallas kernels for 0% -> 1%
where the time goes in v2:
time: 122 us
  waiting for transfers between devices  40.8 us (33%)
  starting transfers between devices  33.4 us (27%)
  local copies, waits for them, and re-layouts  20 us (16%)
  other arithmetic  12.2 us (10%)
  Pallas kernels  10.5 us (9%)
  between operations  4.51 us (4%)
    ppermute x14, waiting for transfers between devices, from_behind(): lax.ppermute(value, axis, [(i, (i + by) % count) for i in range(count)])  24.4 us
    ppermute x14, starting transfers between devices, from_behind(): lax.ppermute(value, axis, [(i, (i + by) % count) for i in range(count)])  24.1 us
    unnamed x55, local copies, waits for them, and re-layouts  16.9 us
    ppermute x10, waiting for transfers between devices, swapped(): return lax.ppermute(value, axis, [(i, i ^ bit) for i in range(count)])  10.7 us
    pallas_call x5, Pallas kernels, call(): pl.pallas_call(kernel, out_shape=list(outs), in_specs=[pl.BlockSpec(memor...  10.5 us
    ppermute x10, starting transfers between devices, swapped(): return lax.ppermute(value, axis, [(i, i ^ bit) for i in range(count)])  7.95 us
    ppermute x1, waiting for transfers between devices, passed_along(): return lax.ppermute(block, axis, route)  5.72 us
  transfers between devices with their start and end apart: 26, of which 12 were waited for; matrix products, arithmetic and copies ran while one was open for 11% of the time, Pallas kernels for 1%

profile of v2, /device:TPU:0, one launch (start us, length us, event | category | flops | bytes accessed | tf_op | source)
XLA Modules:
  0.0 121.5 jit_solution(2308179172436511389)
XLA Ops:
  0.6 1.1 copy_bitcast_fusion
  1.8 0.7 copy-done.22
  2.5 5.1 %collective-permute-start = (bf16[160,512]{1,0:T(8,128)(2,1)S(1)}, bf16[160,512]{1,0:T(8,128)(2,1)S(1)}, u32[]{:S(2)}, u32[]{:S(2)}) collective-permute-start(bf16[160,512]{1,0:T(8,128)(2,1)S(1)} %get-tuple-element.27), channel_id=1, source_target_pairs={{0,12},{4,0},{8,4},{12,8},{1,13},{5,1},{9,5},{13,9},{2,14},{6,2},{... | collective-permute-start | bytes 491528 | tf_op jit(solution)/shard_map/ppermute | solution.py:19
  7.7 3.5 %collective-permute-done.rim = bf16[160,512]{1,0:T(8,128)(2,1)S(1)} collective-permute-done((bf16[160,512]{1,0:T(8,128)(2,1)S(1)}, bf16[160,512]{1,0:T(8,128)(2,1)S(1)}, u32[]{:S(2)}, u32[]{:S(2)}) %collective-permute-start) | collective-permute-done | bytes 163872 | tf_op jit(solution)/shard_map/ppermute | solution.py:19
  11.1 1.4 %copy-done = bf16[1,512,1536]{2,1,0:T(8,128)(2,1)S(1)} copy-done((bf16[1,512,1536]{2,1,0:T(8,128)(2,1)S(1)}, bf16[1,512,1536]{2,1,0:T(8,128)(2,1)}, u32[]{:S(2)}) %copy-start) | copy-done | bytes 1572888
  12.5 1.0 copy-done.4
  13.6 0.7 copy-done.20
  14.2 0.7 copy-done.23
  14.9 0.7 copy-done.25
  15.6 5.7 %shard_map.111 = (bf16[144,512]{1,0:T(8,128)(2,1)S(1)}, bf16[144,512]{1,0:T(8,128)(2,1)S(1)}, f32[144,512]{1,0:T(8,128)S(1)}, f32[144,128]{1,0:T(8,128)S(1)}, bf...) custom-call(f32[1,16]{1,0:T(1,128)S(1)} %copy-done.25, ...), custom_call_target="tpu_custom_call" | custom-call | flops 1000000000 | bytes 5359968 | tf_op jit(solution)/shard_map/pallas_call | solution.py:43
  21.3 1.4 %copy-done.2 = f32[2304,144]{1,0:T(8,128)} copy-done((f32[2304,144]{1,0:T(8,128)}, f32[2304,144]{1,0:T(8,128)S(1)}, u32[]{:S(2)}) %copy-start.2) | copy-done | bytes 1327128
  22.7 0.7 copy-done.8
  23.4 0.6 copy-done.16
  24.1 0.6 copy-done.18
  24.7 1.3 %collective-permute-start.1 = (bf16[144,512]{1,0:T(8,128)(2,1)S(1)}, bf16[144,512]{1,0:T(8,128)(2,1)S(1)}, u32[]{:S(2)}, u32[]{:S(2)}) collective-permute-start(bf16[144,512]{1,0:T(8,128)(2,1)S(1)} %get-tuple-element.28), channel_id=1, source_target_pairs={{16,0},{17,1},{18,2},{19,3},{20,4},{21,5},{22,6},{23,7},{24,8},{25... | collective-permute-start | bytes 442376 | tf_op jit(solution)/shard_map/ppermute | solution.py:25
  26.0 5.7 %collective-permute-done.1.skip = bf16[144,512]{1,0:T(8,128)(2,1)S(1)} collective-permute-done((bf16[144,512]{1,0:T(8,128)(2,1)S(1)}, bf16[144,512]{1,0:T(8,128)(2,1)S(1)}, u32[]{:S(2)}, u32[]{:S(2)}) %collective-permute-start.1) | collective-permute-done | bytes 147488 | tf_op jit(solution)/shard_map/ppermute | solution.py:25
  31.7 0.7 copy-done.12
  32.4 1.7 %copy-done.3 = f32[2304,144]{1,0:T(8,128)S(1)} copy-done((f32[2304,144]{1,0:T(8,128)S(1)}, f32[2304,144]{1,0:T(8,128)}, u32[]{:S(2)}) %copy-start.3) | copy-done | bytes 1327128
  34.1 0.9 copy-done.13
  35.0 0.9 copy-done.19
  35.9 3.7 %shard_map.112 = (bf16[144,512]{1,0:T(8,128)(2,1)S(1)}, bf16[144,1536]{1,0:T(8,128)(2,1)S(1)}, f32[8,128]{1,0:T(8,128)S(1)}, bf16[256,1152]{1,0:T(8,128)(2,1)}, bf16[256,1024]{1,0:T(8,128)(2,1)}) custom-call(s32[1]{0:T(128)} %bitcast.core, bf16[144,512]{1,0:T(8,128)(2,1)S(1)} %copy-done.13, bf16[144,512]{1,0:T(8,128)(2,1)S(1)} %get-tuple-element.29.cot, ...), custom_call_target="tpu_custom_call" | custom-call | flops 1000000000 | bytes 4812804 | tf_op jit(solution)/shard_map/pallas_call | solution.py:43
  39.5 0.8 copy-done.6
  40.3 0.7 copy-done.10
  41.1 1.3 %bitcast_convert_fusion = f32[256,1536]{1,0:T(8,128)} fusion(bf16[1,512,1536]{2,1,0:T(8,128)(2,1)S(1)} %copy-done.1, s32[]{:T(128)S(6)} %select_n.218), kind=kLoop, calls=%fused_computation.12 | loop fusion | flops 393216 | bytes 2359300 | tf_op jit(solution)/shard_map/convert_element_type | solution.py:402
  42.8 1.0 copy-done.9
  43.8 1.0 shard_map.113
  44.8 1.3 %convert_add_fusion.1 = f32[256,1024]{1,0:T(8,128)S(1)} fusion(f32[256,1024]{1,0:T(8,128)S(1)} %get-tuple-element.45, bf16[256,1024]{1,0:T(8,128)(2,1)} %collective-permute-done.13), kind=kLoop, calls=%fused_computation.10 | loop fusion | flops 524288 | bytes 2621440 | tf_op jit(solution)/shard_map/add | solution.py:383
  46.7 4.4 %collective-permute-start.15 = (bf16[64,1024]{1,0:T(8,128)(2,1)S(1)}, bf16[64,1024]{1,0:T(8,128)(2,1)S(1)}, u32[]{:S(2)}, u32[]{:S(2)}) collective-permute-start(bf16[64,1024]{1,0:T(8,128)(2,1)S(1)} %get-tuple-element.69), channel_id=1, source_target_pairs={{0,8},{4,12},{8,0},{12,4},{1,9},{5,13},{9,1},{13,5},{2,10},{6,14},... | collective-permute-start | bytes 393224 | tf_op jit(solution)/shard_map/ppermute | solution.py:19
  51.1 2.0 %collective-permute-start.2 = (bf16[72,512]{1,0:T(8,128)(2,1)}, bf16[72,512]{1,0:T(8,128)(2,1)S(1)}, u32[]{:S(2)}, u32[]{:S(2)}) collective-permute-start(bf16[72,512]{1,0:T(8,128)(2,1)} %copy-done.24), channel_id=1, source_target_pairs={{0,4},{4,8},{8,12},{12,0},{1,5},{5,9},{9,13},{13,1},{2,6},{6,10},{... | collective-permute-start | bytes 221192 | tf_op jit(solution)/shard_map/ppermute | solution.py:19
  53.1 8.5 %collective-permute-done.2.back = bf16[72,512]{1,0:T(8,128)(2,1)S(1)} collective-permute-done((bf16[72,512]{1,0:T(8,128)(2,1)}, bf16[72,512]{1,0:T(8,128)(2,1)S(1)}, u32[]{:S(2)}, u32[]{:S(2)}) %collective-permute-start.2) | collective-permute-done | bytes 73760 | tf_op jit(solution)/shard_map/ppermute | solution.py:19
  61.6 0.9 copy-done.15
  62.6 0.9 copy.14
  63.6 1.6 %collective-permute-start.17 = (bf16[32,1024]{1,0:T(8,128)(2,1)S(1)}, bf16[32,1024]{1,0:T(8,128)(2,1)S(1)}, u32[]{:S(2)}, u32[]{:S(2)}) collective-permute-start(bf16[32,1024]{1,0:T(8,128)(2,1)S(1)} %fusion.17), channel_id=1, source_target_pairs={{0,2},{1,3},{2,0},{3,1},{4,6},{5,7},{6,4},{7,5},{8,10},{9,11},{10,... | collective-permute-start | bytes 196616 | tf_op jit(solution)/shard_map/ppermute | solution.py:30
  65.2 1.2 convert_add_fusion
  66.4 1.6 %collective-permute-done.17 = bf16[32,1024]{1,0:T(8,128)(2,1)S(1)} collective-permute-done((bf16[32,1024]{1,0:T(8,128)(2,1)S(1)}, bf16[32,1024]{1,0:T(8,128)(2,1)S(1)}, u32[]{:S(2)}, u32[]{:S(2)}) %collective-permute-start.17) | collective-permute-done | bytes 65568 | tf_op jit(solution)/shard_map/ppermute | solution.py:30
  68.0 1.6 %collective-permute-start.18 = (bf16[32,1024]{1,0:T(8,128)(2,1)S(1)}, bf16[32,1024]{1,0:T(8,128)(2,1)S(1)}, u32[]{:S(2)}, u32[]{:S(2)}) collective-permute-start(bf16[32,1024]{1,0:T(8,128)(2,1)S(1)} %fusion.13), channel_id=1, source_target_pairs={{0,2},{1,3},{2,0},{3,1},{4,6},{5,7},{6,4},{7,5},{8,10},{9,11},{10,... | collective-permute-start | bytes 196616 | tf_op jit(solution)/shard_map/ppermute | solution.py:30
  69.6 0.6 collective-permute-start.4
  70.2 2.9 %collective-permute-done.18 = bf16[32,1024]{1,0:T(8,128)(2,1)S(1)} collective-permute-done((bf16[32,1024]{1,0:T(8,128)(2,1)S(1)}, bf16[32,1024]{1,0:T(8,128)(2,1)S(1)}, u32[]{:S(2)}, u32[]{:S(2)}) %collective-permute-start.18) | collective-permute-done | bytes 65568 | tf_op jit(solution)/shard_map/ppermute | solution.py:30
  73.1 1.3 %collective-permute-start.19 = (bf16[64,1024]{1,0:T(8,128)(2,1)S(1)}, bf16[64,1024]{1,0:T(8,128)(2,1)S(1)}, u32[]{:S(2)}, u32[]{:S(2)}) collective-permute-start(bf16[64,1024]{1,0:T(8,128)(2,1)S(1)} %pad_maximum_fusion.1), channel_id=1, source_target_pairs={{0,4},{4,8},{8,12},{12,0},{1,5},{5,9},{9,13},{13,1},{2,6},{6,10},{... | collective-permute-start | bytes 393224 | tf_op jit(solution)/shard_map/ppermute | solution.py:19
  74.4 0.7 collective-permute-start.20
  75.0 2.8 %collective-permute-start.21 = (bf16[64,1024]{1,0:T(8,128)(2,1)S(1)}, bf16[64,1024]{1,0:T(8,128)(2,1)S(1)}, u32[]{:S(2)}, u32[]{:S(2)}) collective-permute-start(bf16[64,1024]{1,0:T(8,128)(2,1)S(1)} %pad_maximum_fusion.1), channel_id=1, source_target_pairs={{0,12},{4,0},{8,4},{12,8},{1,13},{5,1},{9,5},{13,9},{2,14},{6,2},{... | collective-permute-start | bytes 393224 | tf_op jit(solution)/shard_map/ppermute | solution.py:19
  78.1 1.3 %collective-permute-start.5 = (bf16[32,1152]{1,0:T(8,128)(2,1)S(1)}, bf16[32,1152]{1,0:T(8,128)(2,1)S(1)}, u32[]{:S(2)}, u32[]{:S(2)}) collective-permute-start(bf16[32,1152]{1,0:T(8,128)(2,1)S(1)} %get-tuple-element.70), channel_id=1, source_target_pairs={{0,4},{4,8},{8,12},{12,0},{1,5},{5,9},{9,13},{13,1},{2,6},{6,10},{... | collective-permute-start | bytes 221192 | tf_op jit(solution)/shard_map/ppermute | solution.py:19
  79.6 0.7 collective-permute-done.19
  80.3 1.9 %collective-permute-start.7 = (bf16[32,1152]{1,0:T(8,128)(2,1)S(1)}, bf16[32,1152]{1,0:T(8,128)(2,1)S(1)}, u32[]{:S(2)}, u32[]{:S(2)}) collective-permute-start(bf16[32,1152]{1,0:T(8,128)(2,1)S(1)} %get-tuple-element.71), channel_id=1, source_target_pairs={{0,12},{4,0},{8,4},{12,8},{1,13},{5,1},{9,5},{13,9},{2,14},{6,2},{... | collective-permute-start | bytes 221192 | tf_op jit(solution)/shard_map/ppermute | solution.py:19
  82.3 5.2 %collective-permute-done.20 = bf16[64,1024]{1,0:T(8,128)(2,1)S(1)} collective-permute-done((bf16[64,1024]{1,0:T(8,128)(2,1)S(1)}, bf16[64,1024]{1,0:T(8,128)(2,1)S(1)}, u32[]{:S(2)}, u32[]{:S(2)}) %collective-permute-start.20) | collective-permute-done | bytes 131104 | tf_op jit(solution)/shard_map/ppermute | solution.py:19
  87.7 0.9 multiply_reduce_fusion
  88.6 2.1 %collective-permute-done.6 = bf16[32,1152]{1,0:T(8,128)(2,1)S(1)} collective-permute-done((bf16[32,1152]{1,0:T(8,128)(2,1)S(1)}, bf16[32,1152]{1,0:T(8,128)(2,1)S(1)}, u32[]{:S(2)}, u32[]{:S(2)}) %collective-permute-start.6) | collective-permute-done | bytes 73760 | tf_op jit(solution)/shard_map/ppermute | solution.py:19
  90.8 1.4 %collective-permute-start.8 = (bf16[32,1024]{1,0:T(8,128)(2,1)S(1)}, bf16[32,1024]{1,0:T(8,128)(2,1)S(1)}, u32[]{:S(2)}, u32[]{:S(2)}) collective-permute-start(bf16[32,1024]{1,0:T(8,128)(2,1)S(1)} %get-tuple-element.60), channel_id=1, source_target_pairs={{0,4},{4,8},{8,12},{12,0},{1,5},{5,9},{9,13},{13,1},{2,6},{6,10},{... | collective-permute-start | bytes 196616 | tf_op jit(solution)/shard_map/ppermute | solution.py:19
  92.2 1.3 %collective-permute-start.9 = (bf16[32,1024]{1,0:T(8,128)(2,1)S(1)}, bf16[32,1024]{1,0:T(8,128)(2,1)S(1)}, u32[]{:S(2)}, u32[]{:S(2)}) collective-permute-start(bf16[32,1024]{1,0:T(8,128)(2,1)S(1)} %get-tuple-element.60), channel_id=1, source_target_pairs={{0,8},{4,12},{8,0},{12,4},{1,9},{5,13},{9,1},{13,5},{2,10},{6,14},... | collective-permute-start | bytes 196616 | tf_op jit(solution)/shard_map/ppermute | solution.py:19
  93.5 1.2 collective-permute-start.10
  94.7 2.7 %collective-permute-done.8 = bf16[32,1024]{1,0:T(8,128)(2,1)S(1)} collective-permute-done((bf16[32,1024]{1,0:T(8,128)(2,1)S(1)}, bf16[32,1024]{1,0:T(8,128)(2,1)S(1)}, u32[]{:S(2)}, u32[]{:S(2)}) %collective-permute-start.8) | collective-permute-done | bytes 65568 | tf_op jit(solution)/shard_map/ppermute | solution.py:19
  97.4 1.7 %collective-permute-done.9 = bf16[32,1024]{1,0:T(8,128)(2,1)S(1)} collective-permute-done((bf16[32,1024]{1,0:T(8,128)(2,1)S(1)}, bf16[32,1024]{1,0:T(8,128)(2,1)S(1)}, u32[]{:S(2)}, u32[]{:S(2)}) %collective-permute-start.9) | collective-permute-done | bytes 65568 | tf_op jit(solution)/shard_map/ppermute | solution.py:19
  99.1 1.6 %collective-permute-start.11 = (bf16[128,1024]{1,0:T(8,128)(2,1)S(1)}, bf16[128,1024]{1,0:T(8,128)(2,1)S(1)}, u32[]{:S(2)}, u32[]{:S(2)}) collective-permute-start(bf16[128,1024]{1,0:T(8,128)(2,1)S(1)} %bitcast.93), channel_id=1, source_target_pairs={{0,2},{1,3},{2,0},{3,1},{4,6},{5,7},{6,4},{7,5},{8,10},{9,11},{10,... | collective-permute-start | bytes 786440 | tf_op jit(solution)/shard_map/ppermute | solution.py:30
  100.8 0.6 multiply_reduce_fusion.2
  102.0 4.9 %collective-permute-done.11 = bf16[128,1024]{1,0:T(8,128)(2,1)S(1)} collective-permute-done((bf16[128,1024]{1,0:T(8,128)(2,1)S(1)}, bf16[128,1024]{1,0:T(8,128)(2,1)S(1)}, u32[]{:S(2)}, u32[]{:S(2)}) %collective-permute-start.11) | collective-permute-done | bytes 262176 | tf_op jit(solution)/shard_map/ppermute | solution.py:30
  107.0 0.9 fusion.1
  109.2 0.6 multiply_reduce_fusion.1
  110.6 2.0 %collective-permute-start.22 = (f32[1,384]{1,0:T(1,128)S(1)}, f32[1,384]{1,0:T(1,128)S(1)}, u32[]{:S(2)}, u32[]{:S(2)}) collective-permute-start(f32[1,384]{1,0:T(1,128)S(1)} %reshape.92), channel_id=1, source_target_pairs={{0,1},{1,0},{2,3},{3,2},{4,5},{5,4},{6,7},{7,6},{8,9},{9,8},{10,11... | collective-permute-start | bytes 4616 | tf_op jit(solution)/shard_map/ppermute | solution.py:30
  112.8 1.3 %collective-permute-done.23 = f32[1,128]{1,0:T(1,128)S(1)} collective-permute-done((f32[1,128]{1,0:T(1,128)S(1)}, f32[1,128]{1,0:T(1,128)S(1)}, u32[]{:S(2)}, u32[]{:S(2)}) %collective-permute-start.23) | collective-permute-done | bytes 544 | tf_op jit(solution)/shard_map/ppermute | solution.py:30
  114.1 0.5 slice.77
  115.4 0.6 maximum_multiply_fusion
  116.5 1.1 broadcast_select_fusion.1
  117.9 1.2 slice_bitcast_fusion
  119.6 1.9 %maximum_bitcast_fusion = f32[1,512,1536]{2,1,0:T(8,128)} fusion(f32[512,512]{1,0:T(8,128)S(1)} %get-tuple-element.62, f32[512,1024]{1,0:T(8,128)S(1)} %convert_multiply_fusion.1), kind=kLoop, calls=%fused_computation | loop fusion | flops 786432 | bytes 6291456 | tf_op jit(solution)/shard_map/broadcast_in_dim | solution.py:437
  (102 shorter events, 3.9 us)
Async XLA Ops:
  0.6 31.8 %copy-start.5 = (bf16[1,512,512]{2,1,0:T(8,128)(2,1)S(1)}, bf16[1,512,512]{2,1,0:T(8,128)(2,1)}, u32[]{:S(2)}) copy-start(bf16[1,512,512]{2,1,0:T(8,128)(2,1)} %param.12) | copy-start | bytes 1572868
  1.7 0.7 copy-start.22
  2.5 8.6 %collective-permute-start = (bf16[160,512]{1,0:T(8,128)(2,1)S(1)}, bf16[160,512]{1,0:T(8,128)(2,1)S(1)}, u32[]{:S(2)}, u32[]{:S(2)}) collective-permute-start(bf16[160,512]{1,0:T(8,128)(2,1)S(1)} %get-tuple-element.27), channel_id=1, source_target_pairs={{0,12},{4,0},{8,4},{12,8},{1,13},{5,1},{9,5},{13,9},{2,14},{6,2},{... | collective-permute-start | bytes 491528 | tf_op jit(solution)/shard_map/ppermute | solution.py:19
  11.1 1.4 %copy-start = (bf16[1,512,1536]{2,1,0:T(8,128)(2,1)S(1)}, bf16[1,512,1536]{2,1,0:T(8,128)(2,1)}, u32[]{:S(2)}) copy-start(bf16[1,512,1536]{2,1,0:T(8,128)(2,1)} %param.11) | copy-start | bytes 4718596
  12.5 1.0 copy-start.4
  13.6 0.7 copy-start.20
  14.2 0.7 copy-start.23
  14.9 0.7 copy-start.25
  21.3 1.4 %copy-start.2 = (f32[2304,144]{1,0:T(8,128)}, f32[2304,144]{1,0:T(8,128)S(1)}, u32[]{:S(2)}) copy-start(f32[2304,144]{1,0:T(8,128)S(1)} %get-tuple-element.32.probs) | copy-start | bytes 3981316
  22.7 0.7 copy-start.8
  23.4 0.6 copy-start.16
  24.1 0.6 copy-start.18
  24.7 7.0 %collective-permute-start.1 = (bf16[144,512]{1,0:T(8,128)(2,1)S(1)}, bf16[144,512]{1,0:T(8,128)(2,1)S(1)}, u32[]{:S(2)}, u32[]{:S(2)}) collective-permute-start(bf16[144,512]{1,0:T(8,128)(2,1)S(1)} %get-tuple-element.28), channel_id=1, source_target_pairs={{16,0},{17,1},{18,2},{19,3},{20,4},{21,5},{22,6},{23,7},{24,8},{25... | collective-permute-start | bytes 442376 | tf_op jit(solution)/shard_map/ppermute | solution.py:25
  31.7 0.7 copy-start.12
  32.4 1.7 %copy-start.3 = (f32[2304,144]{1,0:T(8,128)S(1)}, f32[2304,144]{1,0:T(8,128)}, u32[]{:S(2)}) copy-start(f32[2304,144]{1,0:T(8,128)} %copy-done.2) | copy-start | bytes 3981316
  34.1 0.9 copy-start.13
  35.0 0.9 copy-start.19
  35.8 5.2 %copy-start.1 = (bf16[1,512,1536]{2,1,0:T(8,128)(2,1)S(1)}, bf16[1,512,1536]{2,1,0:T(8,128)(2,1)}, u32[]{:S(2)}) copy-start(bf16[1,512,1536]{2,1,0:T(8,128)(2,1)} %param.11) | copy-start | bytes 4718596
  39.5 0.8 copy-start.6
  40.3 0.7 copy-start.10
  41.0 1.9 %copy-start.17 = (f32[144,128]{1,0:T(8,128)S(1)}, f32[144,128]{1,0:T(8,128)}, u32[]{:S(2)}) copy-start(f32[144,128]{1,0:T(8,128)} %copy-done.16) | copy-start | bytes 221188
  41.0 1.9 %copy-start.21 = (f32[1,512]{1,0:T(1,128)S(1)}, f32[1,512]{1,0:T(1,128)}, u32[]{:S(2)}) copy-start(f32[1,512]{1,0:T(1,128)} %gain.3) | copy-start | bytes 6148
  41.0 1.9 %copy-start.11 = (bf16[144,512]{1,0:T(8,128)(2,1)S(1)}, bf16[144,512]{1,0:T(8,128)(2,1)}, u32[]{:S(2)}) copy-start(bf16[144,512]{1,0:T(8,128)(2,1)} %copy-done.10) | copy-start | bytes 442372
  41.0 3.8 %collective-permute-start.13 = (bf16[256,1024]{1,0:T(8,128)(2,1)}, bf16[256,1024]{1,0:T(8,128)(2,1)}, u32[]{:S(2)}, u32[]{:S(2)}) collective-permute-start(bf16[256,1024]{1,0:T(8,128)(2,1)} %get-tuple-element.46), channel_id=1, source_target_pairs={{0,1},{1,0},{2,3},{3,2},{4,5},{5,4},{6,7},{7,6},{8,9},{9,8},{10,11... | collective-permute-start | bytes 1572872 | tf_op jit(solution)/shard_map/ppermute | solution.py:30
  41.0 1.8 %copy-start.7 = (bf16[144,1536]{1,0:T(8,128)(2,1)S(1)}, bf16[144,1536]{1,0:T(8,128)(2,1)}, u32[]{:S(2)}) copy-start(bf16[144,1536]{1,0:T(8,128)(2,1)} %copy-done.6) | copy-start | bytes 1327108
  42.4 22.8 %collective-permute-start.3 = (bf16[256,1152]{1,0:T(8,128)(2,1)}, bf16[256,1152]{1,0:T(8,128)(2,1)}, u32[]{:S(2)}, u32[]{:S(2)}) collective-permute-start(bf16[256,1152]{1,0:T(8,128)(2,1)} %get-tuple-element.44), channel_id=1, source_target_pairs={{0,1},{1,0},{2,3},{3,2},{4,5},{5,4},{6,7},{7,6},{8,9},{9,8},{10,11... | collective-permute-start | bytes 1769480 | tf_op jit(solution)/shard_map/ppermute | solution.py:30
  42.8 1.0 copy-start.9
  44.8 1.3 %copy-start.14 = (f32[72,512]{1,0:T(8,128)}, f32[72,512]{1,0:T(8,128)S(1)}, u32[]{:S(2)}) copy-start(f32[72,512]{1,0:T(8,128)S(1)} %get-tuple-element.41.own) | copy-start | bytes 442372
  44.8 1.3 %copy-start.24 = (bf16[72,512]{1,0:T(8,128)(2,1)}, bf16[72,512]{1,0:T(8,128)(2,1)S(1)}, u32[]{:S(2)}) copy-start(bf16[72,512]{1,0:T(8,128)(2,1)S(1)} %get-tuple-element.42) | copy-start | bytes 221188
  46.2 17.3 %collective-permute-start.14 = (bf16[64,1024]{1,0:T(8,128)(2,1)S(1)}, bf16[64,1024]{1,0:T(8,128)(2,1)S(1)}, u32[]{:S(2)}, u32[]{:S(2)}) collective-permute-start(bf16[64,1024]{1,0:T(8,128)(2,1)S(1)} %get-tuple-element.67), channel_id=1, source_target_pairs={{0,4},{4,8},{8,12},{12,0},{1,5},{5,9},{9,13},{13,1},{2,6},{6,10},{... | collective-permute-start | bytes 393224 | tf_op jit(solution)/shard_map/ppermute | solution.py:19
  46.7 16.8 %collective-permute-start.15 = (bf16[64,1024]{1,0:T(8,128)(2,1)S(1)}, bf16[64,1024]{1,0:T(8,128)(2,1)S(1)}, u32[]{:S(2)}, u32[]{:S(2)}) collective-permute-start(bf16[64,1024]{1,0:T(8,128)(2,1)S(1)} %get-tuple-element.69), channel_id=1, source_target_pairs={{0,8},{4,12},{8,0},{12,4},{1,9},{5,13},{9,1},{13,5},{2,10},{6,14},... | collective-permute-start | bytes 393224 | tf_op jit(solution)/shard_map/ppermute | solution.py:19
  51.1 12.5 %collective-permute-start.16 = (bf16[64,1024]{1,0:T(8,128)(2,1)S(1)}, bf16[64,1024]{1,0:T(8,128)(2,1)S(1)}, u32[]{:S(2)}, u32[]{:S(2)}) collective-permute-start(bf16[64,1024]{1,0:T(8,128)(2,1)S(1)} %get-tuple-element.68), channel_id=1, source_target_pairs={{0,12},{4,0},{8,4},{12,8},{1,13},{5,1},{9,5},{13,9},{2,14},{6,2},{... | collective-permute-start | bytes 393224 | tf_op jit(solution)/shard_map/ppermute | solution.py:19
  51.1 10.5 %collective-permute-start.2 = (bf16[72,512]{1,0:T(8,128)(2,1)}, bf16[72,512]{1,0:T(8,128)(2,1)S(1)}, u32[]{:S(2)}, u32[]{:S(2)}) collective-permute-start(bf16[72,512]{1,0:T(8,128)(2,1)} %copy-done.24), channel_id=1, source_target_pairs={{0,4},{4,8},{8,12},{12,0},{1,5},{5,9},{9,13},{13,1},{2,6},{6,10},{... | collective-permute-start | bytes 221192 | tf_op jit(solution)/shard_map/ppermute | solution.py:19
  61.6 0.9 copy-start.15
  63.6 4.3 %collective-permute-start.17 = (bf16[32,1024]{1,0:T(8,128)(2,1)S(1)}, bf16[32,1024]{1,0:T(8,128)(2,1)S(1)}, u32[]{:S(2)}, u32[]{:S(2)}) collective-permute-start(bf16[32,1024]{1,0:T(8,128)(2,1)S(1)} %fusion.17), channel_id=1, source_target_pairs={{0,2},{1,3},{2,0},{3,1},{4,6},{5,7},{6,4},{7,5},{8,10},{9,11},{10,... | collective-permute-start | bytes 196616 | tf_op jit(solution)/shard_map/ppermute | solution.py:30
  68.0 5.1 %collective-permute-start.18 = (bf16[32,1024]{1,0:T(8,128)(2,1)S(1)}, bf16[32,1024]{1,0:T(8,128)(2,1)S(1)}, u32[]{:S(2)}, u32[]{:S(2)}) collective-permute-start(bf16[32,1024]{1,0:T(8,128)(2,1)S(1)} %fusion.13), channel_id=1, source_target_pairs={{0,2},{1,3},{2,0},{3,1},{4,6},{5,7},{6,4},{7,5},{8,10},{9,11},{10,... | collective-permute-start | bytes 196616 | tf_op jit(solution)/shard_map/ppermute | solution.py:30
  69.6 8.4 %collective-permute-start.4 = (bf16[128,1152]{1,0:T(8,128)(2,1)S(1)}, bf16[128,1152]{1,0:T(8,128)(2,1)S(1)}, u32[]{:S(2)}, u32[]{:S(2)}) collective-permute-start(bf16[128,1152]{1,0:T(8,128)(2,1)S(1)} %fusion.4), channel_id=1, source_target_pairs={{0,2},{1,3},{2,0},{3,1},{4,6},{5,7},{6,4},{7,5},{8,10},{9,11},{10,... | collective-permute-start | bytes 884744 | tf_op jit(solution)/shard_map/ppermute | solution.py:30
  73.1 14.5 %copy-start.26 = (f32[256,1536]{1,0:T(8,128)S(1)}, f32[256,1536]{1,0:T(8,128)}, u32[]{:S(2)}) copy-start(f32[256,1536]{1,0:T(8,128)} %bitcast_convert_fusion) | copy-start | bytes 4718596
  73.1 7.2 %collective-permute-start.19 = (bf16[64,1024]{1,0:T(8,128)(2,1)S(1)}, bf16[64,1024]{1,0:T(8,128)(2,1)S(1)}, u32[]{:S(2)}, u32[]{:S(2)}) collective-permute-start(bf16[64,1024]{1,0:T(8,128)(2,1)S(1)} %pad_maximum_fusion.1), channel_id=1, source_target_pairs={{0,4},{4,8},{8,12},{12,0},{1,5},{5,9},{9,13},{13,1},{2,6},{6,10},{... | collective-permute-start | bytes 393224 | tf_op jit(solution)/shard_map/ppermute | solution.py:19
  74.4 13.1 %collective-permute-start.20 = (bf16[64,1024]{1,0:T(8,128)(2,1)S(1)}, bf16[64,1024]{1,0:T(8,128)(2,1)S(1)}, u32[]{:S(2)}, u32[]{:S(2)}) collective-permute-start(bf16[64,1024]{1,0:T(8,128)(2,1)S(1)} %pad_maximum_fusion.1), channel_id=1, source_target_pairs={{0,8},{4,12},{8,0},{12,4},{1,9},{5,13},{9,1},{13,5},{2,10},{6,14},... | collective-permute-start | bytes 393224 | tf_op jit(solution)/shard_map/ppermute | solution.py:19
  75.0 12.5 %collective-permute-start.21 = (bf16[64,1024]{1,0:T(8,128)(2,1)S(1)}, bf16[64,1024]{1,0:T(8,128)(2,1)S(1)}, u32[]{:S(2)}, u32[]{:S(2)}) collective-permute-start(bf16[64,1024]{1,0:T(8,128)(2,1)S(1)} %pad_maximum_fusion.1), channel_id=1, source_target_pairs={{0,12},{4,0},{8,4},{12,8},{1,13},{5,1},{9,5},{13,9},{2,14},{6,2},{... | collective-permute-start | bytes 393224 | tf_op jit(solution)/shard_map/ppermute | solution.py:19
  78.1 10.5 %collective-permute-start.5 = (bf16[32,1152]{1,0:T(8,128)(2,1)S(1)}, bf16[32,1152]{1,0:T(8,128)(2,1)S(1)}, u32[]{:S(2)}, u32[]{:S(2)}) collective-permute-start(bf16[32,1152]{1,0:T(8,128)(2,1)S(1)} %get-tuple-element.70), channel_id=1, source_target_pairs={{0,4},{4,8},{8,12},{12,0},{1,5},{5,9},{9,13},{13,1},{2,6},{6,10},{... | collective-permute-start | bytes 221192 | tf_op jit(solution)/shard_map/ppermute | solution.py:19
  79.4 11.4 %collective-permute-start.6 = (bf16[32,1152]{1,0:T(8,128)(2,1)S(1)}, bf16[32,1152]{1,0:T(8,128)(2,1)S(1)}, u32[]{:S(2)}, u32[]{:S(2)}) collective-permute-start(bf16[32,1152]{1,0:T(8,128)(2,1)S(1)} %get-tuple-element.72), channel_id=1, source_target_pairs={{0,8},{4,12},{8,0},{12,4},{1,9},{5,13},{9,1},{13,5},{2,10},{6,14},... | collective-permute-start | bytes 221192 | tf_op jit(solution)/shard_map/ppermute | solution.py:19
  80.3 10.4 %collective-permute-start.7 = (bf16[32,1152]{1,0:T(8,128)(2,1)S(1)}, bf16[32,1152]{1,0:T(8,128)(2,1)S(1)}, u32[]{:S(2)}, u32[]{:S(2)}) collective-permute-start(bf16[32,1152]{1,0:T(8,128)(2,1)S(1)} %get-tuple-element.71), channel_id=1, source_target_pairs={{0,12},{4,0},{8,4},{12,8},{1,13},{5,1},{9,5},{13,9},{2,14},{6,2},{... | collective-permute-start | bytes 221192 | tf_op jit(solution)/shard_map/ppermute | solution.py:19
  87.5 29.0 %collective-permute-start.25 = (bf16[256,1024]{1,0:T(8,128)(2,1)S(1)}, bf16[256,1024]{1,0:T(8,128)(2,1)}, u32[]{:S(2)}, u32[]{:S(2)}) collective-permute-start(bf16[256,1024]{1,0:T(8,128)(2,1)S(1)} %bitcast.85), channel_id=1, source_target_pairs={{0,1},{1,0},{2,3},{3,2},{4,5},{5,4},{6,7},{7,6},{8,9},{9,8},{10,11... | collective-permute-start | bytes 1572872 | tf_op jit(solution)/shard_map/ppermute | solution.py:30
  90.8 6.5 %collective-permute-start.8 = (bf16[32,1024]{1,0:T(8,128)(2,1)S(1)}, bf16[32,1024]{1,0:T(8,128)(2,1)S(1)}, u32[]{:S(2)}, u32[]{:S(2)}) collective-permute-start(bf16[32,1024]{1,0:T(8,128)(2,1)S(1)} %get-tuple-element.60), channel_id=1, source_target_pairs={{0,4},{4,8},{8,12},{12,0},{1,5},{5,9},{9,13},{13,1},{2,6},{6,10},{... | collective-permute-start | bytes 196616 | tf_op jit(solution)/shard_map/ppermute | solution.py:19
  92.2 6.9 %collective-permute-start.9 = (bf16[32,1024]{1,0:T(8,128)(2,1)S(1)}, bf16[32,1024]{1,0:T(8,128)(2,1)S(1)}, u32[]{:S(2)}, u32[]{:S(2)}) collective-permute-start(bf16[32,1024]{1,0:T(8,128)(2,1)S(1)} %get-tuple-element.60), channel_id=1, source_target_pairs={{0,8},{4,12},{8,0},{12,4},{1,9},{5,13},{9,1},{13,5},{2,10},{6,14},... | collective-permute-start | bytes 196616 | tf_op jit(solution)/shard_map/ppermute | solution.py:19
  93.5 5.6 %collective-permute-start.10 = (bf16[32,1024]{1,0:T(8,128)(2,1)S(1)}, bf16[32,1024]{1,0:T(8,128)(2,1)S(1)}, u32[]{:S(2)}, u32[]{:S(2)}) collective-permute-start(bf16[32,1024]{1,0:T(8,128)(2,1)S(1)} %get-tuple-element.60), channel_id=1, source_target_pairs={{0,12},{4,0},{8,4},{12,8},{1,13},{5,1},{9,5},{13,9},{2,14},{6,2},{... | collective-permute-start | bytes 196616 | tf_op jit(solution)/shard_map/ppermute | solution.py:19
  99.1 7.8 %collective-permute-start.11 = (bf16[128,1024]{1,0:T(8,128)(2,1)S(1)}, bf16[128,1024]{1,0:T(8,128)(2,1)S(1)}, u32[]{:S(2)}, u32[]{:S(2)}) collective-permute-start(bf16[128,1024]{1,0:T(8,128)(2,1)S(1)} %bitcast.93), channel_id=1, source_target_pairs={{0,2},{1,3},{2,0},{3,1},{4,6},{5,7},{6,4},{7,5},{8,10},{9,11},{10,... | collective-permute-start | bytes 786440 | tf_op jit(solution)/shard_map/ppermute | solution.py:30
  110.5 3.6 %collective-permute-start.23 = (f32[1,128]{1,0:T(1,128)S(1)}, f32[1,128]{1,0:T(1,128)S(1)}, u32[]{:S(2)}, u32[]{:S(2)}) collective-permute-start(f32[1,128]{1,0:T(1,128)S(1)} %slice.78), channel_id=1, source_target_pairs={{0,16},{16,0},{1,17},{17,1},{2,18},{18,2},{3,19},{19,3},{4,20},{20... | collective-permute-start | bytes 1544 | tf_op jit(solution)/shard_map/ppermute | solution.py:30
  110.6 3.5 %collective-permute-start.24 = (f32[1,128]{1,0:T(1,128)S(1)}, f32[1,128]{1,0:T(1,128)S(1)}, u32[]{:S(2)}, u32[]{:S(2)}) collective-permute-start(f32[1,128]{1,0:T(1,128)S(1)} %slice.78), channel_id=1, source_target_pairs={{0,17},{1,16},{2,19},{3,18},{16,1},{17,0},{18,3},{19,2},{4,21},{5,... | collective-permute-start | bytes 1544 | tf_op jit(solution)/shard_map/ppermute | solution.py:420
  110.6 3.5 %collective-permute-start.22 = (f32[1,384]{1,0:T(1,128)S(1)}, f32[1,384]{1,0:T(1,128)S(1)}, u32[]{:S(2)}, u32[]{:S(2)}) collective-permute-start(f32[1,384]{1,0:T(1,128)S(1)} %reshape.92), channel_id=1, source_target_pairs={{0,1},{1,0},{2,3},{3,2},{4,5},{5,4},{6,7},{7,6},{8,9},{9,8},{10,11... | collective-permute-start | bytes 4616 | tf_op jit(solution)/shard_map/ppermute | solution.py:30
  112.7 6.3 %collective-permute-start.12 = (bf16[256,1024]{1,0:T(8,128)(2,1)S(1)}, bf16[256,1024]{1,0:T(8,128)(2,1)S(1)}, u32[]{:S(2)}, u32[]{:S(2)}) collective-permute-start(bf16[256,1024]{1,0:T(8,128)(2,1)S(1)} %pad_maximum_fusion), channel_id=1, source_target_pairs={{0,1},{1,0},{2,3},{3,2},{4,5},{5,4},{6,7},{7,6},{8,9},{9,8},{10,11... | collective-permute-start | bytes 1572872 | tf_op jit(solution)/shard_map/ppermute | solution.py:30

commit v3 on v2

--- a/solution.py
+++ b/solution.py
@@ -9,6 +9,7 @@
 
 SHIFT = 6
 GROUP = 128
+CUT = 1280
 EPSILON = 1e-05
 F32 = jnp.float32
 BF16 = jnp.bfloat16
@@ -38,7 +39,7 @@
     return lax.dot_general(left, right, (((1,), (1,)), ((), ())), preferred_element_type=F32)
 
 
-def call(kernel, outs, scratch=(), smem=(), operands=(), flops=10**8):
+def call(kernel, outs, scratch=(), smem=(), operands=(), flops=10**8, limit=12):
     moved = sum(o.size * o.dtype.itemsize for o in list(outs) + list(operands))
     return pl.pallas_call(
         kernel,
@@ -49,7 +50,7 @@
         ],
         out_specs=[pl.BlockSpec(memory_space=pltpu.VMEM) for _ in outs],
         scratch_shapes=list(scratch),
-        compiler_params=pltpu.CompilerParams(vmem_limit_bytes=40 * 2**20),
+        compiler_params=pltpu.CompilerParams(vmem_limit_bytes=limit * 2**20),
         cost_estimate=pl.CostEstimate(flops=flops, bytes_accessed=moved, transcendentals=0),
     )(*operands)
 
@@ -58,15 +59,19 @@
     return jax.ShapeDtypeStruct(dims, dtype)
 
 
+def aligned(start, size):
+    return pl.ds(pl.multiple_of(start, size), size)
+
+
 def pack_kernel(tokens, cot, land, own, rim, own32, rim32):
-    levels, lats, cols, width = tokens.shape
+    levels, lats, cols, width = tokens.shape[1:]
     half = levels * lats * SHIFT
     rim32[2 * half :, :] = jnp.zeros((rim32.shape[0] - 2 * half, width), F32)
     for which, ref in enumerate((tokens, cot)):
         for level in range(levels):
             for lat in range(lats):
                 base = which * half + (level * lats + lat) * SHIFT
-                line = ref[level, lat].astype(F32)
+                line = ref[0, level, lat].astype(F32)
                 rim32[base : base + SHIFT, :] = line[:SHIFT]
                 own32[base : base + SHIFT, :] = line[SHIFT:]
     rim32[2 * half : 2 * half + lats, :cols] = land[...].astype(F32)
@@ -75,13 +80,13 @@
 
 
 def unpack_kernel(own, back, grid):
-    levels, lats, cols, width = grid.shape
+    levels, lats, cols, width = grid.shape[1:]
     came = back[...].astype(F32)
     for level in range(levels):
         for lat in range(lats):
             base = (level * lats + lat) * SHIFT
-            grid[level, lat, :SHIFT, :] = came[base : base + SHIFT]
-            grid[level, lat, SHIFT:, :] = own[base : base + SHIFT, :]
+            grid[0, level, lat, :SHIFT, :] = came[base : base + SHIFT]
+            grid[0, level, lat, SHIFT:, :] = own[base : base + SHIFT, :]
 
 
 def land_column(land, rows, first):
@@ -217,7 +222,7 @@
 
 def backward_kernel(
     core, skip, cot, qkv, keys_t, probs, land, weight_out, normed_t, attended_t,
-    total_out, grad_proj, bias_out, give_p, give_q,
+    total_out, grad_proj, bias_out, give,
     *, heads,
 ):
     count, width = cot.shape
@@ -227,99 +232,180 @@
     )
     bias_out[...] = jnp.broadcast_to(bias_row, bias_out.shape)
     half = width // 2
-    rows = pl.ds(pl.multiple_of((1 - core[0]) * half, half), half)
-    weight_rows(rows, normed_t, attended_t, grad_proj, total_out, bias_row, give_p, give_q)
-
-
-def weight_rows(rows, normed_t, attended_t, grad_proj, total, bias_row, out_p, out_q):
-    width = normed_t.shape[0]
+    rows = aligned((1 - core[0]) * half, half)
+    weight_rows(rows, normed_t, attended_t, grad_proj, total_out, bias_row, give)
+
+
+def weight_rows(rows, normed_t, attended_t, grad_proj, total, bias_row, out):
     tokens = normed_t[rows, :]
-    out_p[:, : 2 * width] = dot(tokens, grad_proj[:, : 2 * width]).astype(out_p.dtype)
-    out_p[:, 2 * width :] = jnp.broadcast_to(bias_row, (out_p.shape[0], GROUP)).astype(out_p.dtype)
-    out_q[:, :width] = dot(tokens, grad_proj[:, 2 * width :]).astype(out_q.dtype)
-    out_q[:, width:] = dot(attended_t[rows, :], total[...]).astype(out_q.dtype)
+    three = grad_proj.shape[1]
+    out[:, :CUT] = dot(tokens, grad_proj[:, :CUT]).astype(out.dtype)
+    out[:, CUT : CUT + GROUP] = jnp.broadcast_to(bias_row, (out.shape[0], GROUP)).astype(out.dtype)
+    out[:, CUT + GROUP : three + GROUP] = dot(tokens, grad_proj[:, CUT:]).astype(out.dtype)
+    out[:, three + GROUP :] = dot(attended_t[rows, :], total[...]).astype(out.dtype)
 
 
 def finish_kernel(
     core, total, grad_proj, bias_row, normed_t, attended_t, normed, inverse, weight_qkv, gain,
-    keep_p, keep_q, own, back,
+    keep, own, back,
 ):
     count, width = total.shape
     half = width // 2
-    rows = pl.ds(pl.multiple_of(core[0] * half, half), half)
+    rows = aligned(core[0] * half, half)
     bias_b = bias_row[:1, :].astype(BF16).astype(F32)
-    weight_rows(rows, normed_t, attended_t, grad_proj, total, bias_b, keep_p, keep_q)
+    weight_rows(rows, normed_t, attended_t, grad_proj, total, bias_b, keep)
     final = through_norm(grad_proj[...], weight_qkv, gain, normed[...], inverse[:, :1])
     final = final + total[...].astype(F32)
     own[...] = final[: count // 2]
     back[...] = final[count // 2 :].astype(BF16)
 
 
-def split_two(block, axis, bit):
-    mine = (lax.axis_index(axis) // bit) % 2
-    pair = block.reshape(2, block.shape[0] // 2, -1)
-    give = lax.dynamic_index_in_dim(pair, 1 - mine, 0, keepdims=False).astype(BF16)
-    return give, lax.dynamic_index_in_dim(pair, mine, 0, keepdims=False)
-
-
-def halved(block, axis, bit):
-    give, keep = split_two(block, axis, bit)
-    return keep + swapped(give, axis, bit).astype(F32)
-
-
-def scattered(block, axis):
-    count = lax.axis_size(axis)
-    mine = lax.axis_index(axis)
-    pieces = block.reshape(count, block.shape[0] // count, -1)
-    total = lax.dynamic_index_in_dim(pieces, mine, 0, keepdims=False)
-    others = []
-    for by in range(1, count):
-        give = lax.dynamic_index_in_dim(pieces, (mine + by) % count, 0, keepdims=False)
-        others.append(from_behind(give.astype(BF16), axis, by))
-    for other in others:
-        total = total + other.astype(F32)
-    return total, others
-
-
-def doubled(block, axis, bit):
-    mine = (lax.axis_index(axis) // bit) % 2
-    other = swapped(block, axis, bit)
-    low = jnp.where(mine == 0, block, other)
-    high = jnp.where(mine == 0, other, block)
-    return jnp.concatenate([low, high], axis=0)
-
-
-def gathered(block, axis):
-    count = lax.axis_size(axis)
-    mine = lax.axis_index(axis)
-    whole = jnp.zeros((count,) + block.shape, block.dtype)
-    whole = lax.dynamic_update_index_in_dim(whole, block, mine, 0)
-    for by in range(1, count):
-        whole = lax.dynamic_update_index_in_dim(
-            whole, from_behind(block, axis, by), (mine - by) % count, 0
-        )
-    return whole.reshape(count * block.shape[0], -1)
-
-
-def sum_squares(block):
-    wide = block.astype(F32)
-    return jnp.sum(wide * wide)
+def first_kernel(place, keep, came, give_p, kept_p, kept_q, *rest):
+    *give_q, total = rest
+    wide_p = give_p.shape[1]
+    half = keep.shape[0] // 2
+    total[...] = keep[...] + came[...].astype(F32)
+    give_p[...] = total[aligned((1 - place[1]) * half, half), :wide_p].astype(BF16)
+    mine = aligned(place[1] * half, half)
+    kept_p[:, :CUT] = total[mine, :CUT]
+    kept_p[:, CUT:] = total[mine, CUT:wide_p].astype(BF16).astype(F32)
+    piece, count = kept_q.shape[0], len(give_q) + 1
+    kept_q[...] = total[aligned(place[2] * piece, piece), wide_p:]
+    for by, give in enumerate(give_q, 1):
+        owner = lax.rem(place[2] + by, count)
+        give[...] = total[aligned(owner * piece, piece), wide_p:].astype(BF16)
+
+
+def second_kernel(place, kept_p, came_p, kept_q, *rest):
+    count = (len(rest) - 5) // 2 + 1
+    came_q, (give_q, left_q, left_p), rest = rest[: count - 1], rest[count - 1 : count + 2], rest[count + 2 :]
+    *give_p, total_p, total_q = rest
+    total_p[...] = kept_p[...] + came_p[...].astype(F32)
+    piece = left_p.shape[0]
+    mine = aligned(place[2] * piece, piece)
+    left_p[:, :CUT] = total_p[mine, :CUT]
+    left_p[:, CUT:] = total_p[mine, CUT:].astype(BF16).astype(F32)
+    for by, give in enumerate(give_p, 1):
+        owner = lax.rem(place[2] + by, count)
+        give[...] = total_p[aligned(owner * piece, piece), :].astype(BF16)
+    total = kept_q[...]
+    for came in came_q:
+        total = total + came[...].astype(F32)
+    total_q[...] = total
+    half = give_q.shape[0]
+    give_q[...] = total_q[aligned((1 - place[1]) * half, half), :].astype(BF16)
+    left_q[...] = total_q[aligned(place[1] * half, half), :]
+
+
+def third_kernel(place, left_p, left_q, came_q, *rest):
+    *came_p, piece_p, piece_q, bias = rest
+    count = len(came_p) + 1
+    total = left_p[:, :CUT]
+    for came in came_p:
+        total = total + came[:, :CUT].astype(F32)
+    piece_p[...] = total.astype(BF16)
+    piece_q[...] = (left_q[...] + came_q[...].astype(F32)).astype(BF16)
+    terms = [left_p[:8, CUT:]] + [came[...].astype(F32)[:8, CUT:] for came in came_p]
+    total = jnp.zeros_like(terms[0])
+    for source in range(count):
+        for by, term in enumerate(terms):
+            here = lax.rem(place[2] - by + count, count) == source
+            total = total + jnp.where(here, term, 0.0)
+    bias[...] = total
+
+
+def fourth_kernel(place, piece_p, piece_q, other_q, *rest):
+    *others_p, block_p, block_q = rest
+    count = len(others_p) + 1
+    piece = piece_p.shape[0]
+    for by, part in enumerate((piece_p, *others_p)):
+        source = lax.rem(place[2] - by + count, count)
+        block_p[aligned(source * piece, piece), :] = part[...]
+    piece = piece_q.shape[0]
+    block_q[aligned(place[1] * piece, piece), :] = piece_q[...]
+    block_q[aligned((1 - place[1]) * piece, piece), :] = other_q[...]
+
+
+def fifth_kernel(place, weight_qkv, gain, bias, block_p, other_p, block_q, *rest):
+    *others_q, half, row = rest
+    count = len(others_q) + 1
+    rows, width = half.shape[0], weight_qkv.shape[0]
+    piece = block_p.shape[0]
+    half[aligned(place[1] * piece, piece), :CUT] = block_p[...]
+    half[aligned((1 - place[1]) * piece, piece), :CUT] = other_p[...]
+    piece = block_q.shape[0]
+    for by, part in enumerate((block_q, *others_q)):
+        source = lax.rem(place[2] - by + count, count)
+        half[aligned(source * piece, piece), CUT:] = part[...]
+    three = weight_qkv.shape[1]
+    wide = half[:, :three].astype(F32)
+    mine = aligned(place[0] * rows, rows)
+    gain_half = jnp.sum(wide * weight_qkv[mine, :].astype(F32), axis=1, keepdims=True)
+    gain_half = jnp.broadcast_to(gain_half, (rows, GROUP)).T[:8]
+    core = place[0].astype(F32)
+    own_gain = gain[:, :rows] * (1.0 - core) + gain[:, rows:] * core
+    gain_half = gain_half / own_gain
+    out = half[:, three:].astype(F32)
+    square = jnp.sum(jnp.sum(wide * wide, axis=0, keepdims=True), axis=1, keepdims=True)
+    square = square + jnp.sum(jnp.sum(out * out, axis=0, keepdims=True), axis=1, keepdims=True)
+    square = square + jnp.sum(gain_half[:1] * gain_half[:1], axis=1, keepdims=True)
+    square = square + 0.5 * jnp.sum(bias[:1, :] * bias[:1, :], axis=1, keepdims=True)
+    row[:, :rows] = gain_half
+    row[:, rows:] = jnp.broadcast_to(square, (8, GROUP))
+
+
+def last_kernel(
+    place, half, other, row, row_core, row_section, row_both, bias,
+    grad_qkv, grad_out, grad_gain, grad_bias,
+    *, entries,
+):
+    rows, three = half.shape[0], grad_qkv.shape[1]
+    square = row[:1, rows : rows + 1] + row_core[:1, rows : rows + 1]
+    square = square + (row_section[:1, rows : rows + 1] + row_both[:1, rows : rows + 1])
+    factor = jnp.minimum(1.0, lax.rsqrt(square / entries + 1e-06))
+    step = pl.program_id(0)
+    piece = grad_qkv.shape[0]
+    per = rows // piece
+    at = aligned(lax.rem(step, per) * piece, piece)
+    own = lax.div(step, per) == place[0]
+
+    @pl.when(own)
+    def _():
+        grad_qkv[...] = half[at, :three].astype(F32) * factor
+        grad_out[...] = half[at, three:].astype(F32) * factor
+
+    @pl.when(jnp.logical_not(own))
+    def _():
+        grad_qkv[...] = other[at, :three].astype(F32) * factor
+        grad_out[...] = other[at, three:].astype(F32) * factor
+
+    core = place[0].astype(F32)
+    mine, its = row[:1, :rows] * factor, row_core[:1, :rows] * factor
+    grad_gain[:, :rows] = mine * (1.0 - core) + its * core
+    grad_gain[:, rows:] = mine * core + its * (1.0 - core)
+    grad_bias[...] = bias[:1, : grad_bias.shape[1]] * factor
+
+
+def pieces_sent(pieces, axis):
+    return [from_behind(piece, axis, by) for by, piece in enumerate(pieces, 1)]
 
 
 def body(inputs, cotangent, land_sea, gains, qkv_weight, out_weight, land_bias):
-    tokens, own_cot = inputs[0], cotangent[0]
     weight_qkv, weight_out = qkv_weight[0], out_weight[0]
-    levels, lats, cols, width = tokens.shape
+    levels, lats, cols, width = inputs.shape[1:]
     heads = land_bias.shape[1]
     half = levels * lats * SHIFT
     count = 2 * half
     packed = half * 2 + 16
+    lons = lax.axis_size("lon")
+    lat, lon = lax.axis_index("lat"), lax.axis_index("lon")
+    place = jnp.stack([lat % 2, lat // 2, lon]).astype(jnp.int32)
 
     own, rim = call(
         pack_kernel,
         [shape((2 * half, width), BF16), shape((packed, width), BF16)],
         scratch=[pltpu.VMEM((2 * half, width), F32), pltpu.VMEM((packed, width), F32)],
-        operands=(tokens, own_cot, land_sea),
+        operands=(inputs, cotangent, land_sea),
     )
     rim = from_behind(rim, "lon", -1)
     skip, cot, normed, inverse, normed_t, qkv, keys_t, probs, attended_t, land = call(
@@ -342,103 +428,219 @@
         flops=10**9,
     )
     skip = passed_along(skip, "section", -1)
-    lat, lon = lax.axis_index("lat"), lax.axis_index("lon")
-    core = (lat % 2).astype(jnp.int32).reshape(1)
-    total, grad_proj, bias_row, give_p, give_q = call(
+    rows, wide = width // 2, 4 * width + GROUP
+    total, grad_proj, bias_row, give = call(
         functools.partial(backward_kernel, heads=heads),
         [
             shape((count, width), BF16),
             shape((count, 3 * width), BF16),
             shape((8, GROUP), F32),
-            shape((width // 2, 2 * width + GROUP), BF16),
-            shape((width // 2, 2 * width), BF16),
-        ],
-        smem=(0,),
-        operands=(core, skip, cot, qkv, keys_t, probs, land, weight_out, normed_t, attended_t),
+            shape((rows, wide), BF16),
+        ],
+        smem=(0,),
+        operands=(place, skip, cot, qkv, keys_t, probs, land, weight_out, normed_t, attended_t),
         flops=10**9,
     )
-    came_p = swapped(give_p, "lat", 1)
-    came_q = swapped(give_q, "lat", 1)
-    keep_p, keep_q, own_grad, back = call(
+    came = swapped(give, "lat", 1)
+    keep, own_grad, back = call(
         finish_kernel,
         [
-            shape((width // 2, 2 * width + GROUP), F32),
-            shape((width // 2, 2 * width), F32),
+            shape((rows, wide), F32),
             shape((half, width), F32),
             shape((half, width), BF16),
         ],
         smem=(0,),
         operands=(
-            core, total, grad_proj, bias_row, normed_t, attended_t, normed, inverse,
+            place, total, grad_proj, bias_row, normed_t, attended_t, normed, inverse,
             weight_qkv, gains,
         ),
         flops=5 * 10**8,
     )
     back = from_behind(back, "lon", 1)
+    entries = 2 * (4 * width * width + width + heads)
+    if rows // 2 // lons % 16 == 0:
+        grads, mark = staged(place, keep, came, weight_qkv, gains, lons, heads, entries)
+    else:
+        grads, mark = plain(keep, came, weight_qkv, gains, heads, entries)
+    own_grad, back, _ = lax.optimization_barrier((own_grad, back, mark))
     (final_grad,) = call(
-        unpack_kernel, [shape(tokens.shape, F32)], operands=(own_grad, back)
-    )
-
-    part_p = keep_p + came_p.astype(F32)
-    part_q = keep_q + came_q.astype(F32)
-    give, keep = split_two(part_p, "lat", 2)
+        unpack_kernel, [shape(inputs.shape, F32)], operands=(own_grad, back)
+    )
+    return (final_grad, *(grad[None] for grad in grads))
+
+
+def staged(place, keep, came, weight_qkv, gains, lons, heads, entries):
+    rows, wide = keep.shape
+    width = 2 * rows
+    wide_p = CUT + GROUP
+    wide_q = wide - wide_p
+    some = range(lons - 1)
+    give_p, kept_p, kept_q, *give_q = call(
+        first_kernel,
+        [
+            shape((rows // 2, wide_p), BF16),
+            shape((rows // 2, wide_p), F32),
+            shape((rows // lons, wide_q), F32),
+            *(shape((rows // lons, wide_q), BF16) for _ in some),
+        ],
+        scratch=[pltpu.VMEM((rows, wide), F32)],
+        smem=(0,),
+        operands=(place, keep, came),
+    )
+    came_p = swapped(give_p, "lat", 2)
+    came_q = pieces_sent(give_q, "lon")
+    piece = rows // 2 // lons
+    give_q, left_q, left_p, *give_p = call(
+        second_kernel,
+        [
+            shape((piece, wide_q), BF16),
+            shape((piece, wide_q), F32),
+            shape((piece, wide_p), F32),
+            *(shape((piece, wide_p), BF16) for _ in some),
+        ],
+        scratch=[pltpu.VMEM((rows // 2, wide_p), F32), pltpu.VMEM((rows // lons, wide_q), F32)],
+        smem=(0,),
+        operands=(place, kept_p, came_p, kept_q, *came_q),
+    )
+    came_p = pieces_sent(give_p, "lon")
+    came_q = swapped(give_q, "lat", 2)
+    piece_p, piece_q, bias = call(
+        third_kernel,
+        [
+            shape((piece, CUT), BF16),
+            shape((piece, wide_q), BF16),
+            shape((8, GROUP), F32),
+        ],
+        smem=(0,),
+        operands=(place, left_p, left_q, came_q, *came_p),
+    )
+    others_p = pieces_sent([piece_p for _ in some], "lon")
+    other_q = swapped(piece_q, "lat", 2)
+    block_p, block_q = call(
+        fourth_kernel,
+        [shape((rows // 2, CUT), BF16), shape((rows // lons, wide_q), BF16)],
+        smem=(0,),
+        operands=(place, piece_p, piece_q, other_q, *others_p),
+    )
+    other_p = swapped(block_p, "lat", 2)
+    others_q = pieces_sent([block_q for _ in some], "lon")
+    half, row = call(
+        fifth_kernel,
+        [shape((rows, 4 * width), BF16), shape((8, rows + GROUP), F32)],
+        smem=(0,),
+        operands=(place, weight_qkv, gains, bias, block_p, other_p, block_q, *others_q),
+    )
+    row_section = swapped(row, "section", 1)
+    row_both = lax.ppermute(row, ("section", "lat"), across())
+    row_core = swapped(row, "lat", 1)
+    other = swapped(half, "lat", 1)
+    steps = 8
+    vmem = pl.BlockSpec(memory_space=pltpu.VMEM)
+    grads = pl.pallas_call(
+        functools.partial(last_kernel, entries=entries),
+        grid=(steps,),
+        out_shape=[
+            shape((width, 3 * width), F32),
+            shape((width, width), F32),
+            shape((1, width), F32),
+            shape((1, heads), F32),
+        ],
+        in_specs=[pl.BlockSpec(memory_space=pltpu.SMEM)] + [vmem] * 7,
+        out_specs=[
+            pl.BlockSpec((width // steps, 3 * width), lambda i: (i, 0)),
+            pl.BlockSpec((width // steps, width), lambda i: (i, 0)),
+            pl.BlockSpec((1, width), lambda i: (0, 0)),
+            pl.BlockSpec((1, heads), lambda i: (0, 0)),
+        ],
+        compiler_params=pltpu.CompilerParams(vmem_limit_bytes=12 * 2**20),
+    )(place, half, other, row, row_core, row_section, row_both, bias)
+    return (grads[0], grads[1], grads[2][0], grads[3][0]), bias
+
+
+def across():
+    sections, lats = lax.axis_size("section"), lax.axis_size("lat")
+    return [
+        (s * lats + i, (sections - 1 - s) * lats + (i ^ 1))
+        for s in range(sections)
+        for i in range(lats)
+    ]
+
+
+def split_two(block, axis, bit):
+    mine = (lax.axis_index(axis) // bit) % 2
+    pair = block.reshape(2, block.shape[0] // 2, -1)
+    give = lax.dynamic_index_in_dim(pair, 1 - mine, 0, keepdims=False).astype(BF16)
+    return give, lax.dynamic_index_in_dim(pair, mine, 0, keepdims=False)
+
+
+def doubled(block, axis, bit):
+    mine = (lax.axis_index(axis) // bit) % 2
+    other = swapped(block, axis, bit)
+    low = jnp.where(mine == 0, block, other)
+    high = jnp.where(mine == 0, other, block)
+    return jnp.concatenate([low, high], axis=0)
+
+
+def scattered(block, axis):
+    count = lax.axis_size(axis)
+    mine = lax.axis_index(axis)
+    pieces = block.reshape(count, block.shape[0] // count, -1)
+    total = lax.dynamic_index_in_dim(pieces, mine, 0, keepdims=False)
+    others = []
+    for by in range(1, count):
+        give = lax.dynamic_index_in_dim(pieces, (mine + by) % count, 0, keepdims=False)
+        others.append(from_behind(give.astype(BF16), axis, by))
+    for other in others:
+        total = total + other.astype(F32)
+    return total, others
+
+
+def gathered(block, axis):
+    count = lax.axis_size(axis)
+    mine = lax.axis_index(axis)
+    whole = jnp.zeros((count,) + block.shape, block.dtype)
+    whole = lax.dynamic_update_index_in_dim(whole, block, mine, 0)
+    for by in range(1, count):
+        whole = lax.dynamic_update_index_in_dim(
+            whole, from_behind(block, axis, by), (mine - by) % count, 0
+        )
+    return whole.reshape(count * block.shape[0], -1)
+
+
+def sum_squares(block):
+    wide = block.astype(F32)
+    return jnp.sum(wide * wide)
+
+
+def plain(keep, came, weight_qkv, gains, heads, entries):
+    width = gains.shape[1]
+    lat, lon = lax.axis_index("lat"), lax.axis_index("lon")
+    part = keep + came.astype(F32)
+    give, keep = split_two(part, "lat", 2)
     came = swapped(give, "lat", 2).astype(F32)
-    is_bias = lax.broadcasted_iota(jnp.int32, keep.shape, 1) >= 2 * width
-    part_p = jnp.where(is_bias, lax.reduce_precision(keep, 8, 7), keep) + came
-    bias_part = lax.reduce_precision(part_p[:1, 2 * width :], 8, 7)
-    part_p, others = scattered(part_p, "lon")
-    bias_parts = [bias_part] + [other[:1, 2 * width :].astype(F32) for other in others]
-    bias_parts = jnp.concatenate(bias_parts[:1] + bias_parts[:0:-1], axis=0)
-    grad_bias = jnp.sum(jnp.roll(bias_parts, lon, axis=0), axis=0)[:heads]
-    part_q = halved(scattered(part_q, "lon")[0], "lat", 2)
-    part_p = part_p[:, : 2 * width].astype(BF16)
-    part_q = part_q.astype(BF16)
-    half_p = doubled(gathered(part_p, "lon"), "lat", 2)
-    half_q = gathered(doubled(part_q, "lat", 2), "lon")
-
+    column = lax.broadcasted_iota(jnp.int32, keep.shape, 1)
+    is_bias = (column >= CUT) & (column < CUT + GROUP)
+    part = jnp.where(is_bias, lax.reduce_precision(keep, 8, 7), keep) + came
+    bias_part = lax.reduce_precision(part[:1, CUT : CUT + GROUP], 8, 7)
+    part, others = scattered(part, "lon")
+    terms = [bias_part] + [other[:1, CUT : CUT + GROUP].astype(F32) for other in others]
+    terms = jnp.concatenate(terms[:1] + terms[:0:-1], axis=0)
+    bias = jnp.sum(jnp.roll(terms, lon, axis=0), axis=0)[:heads]
+    part = jnp.concatenate([part[:, :CUT], part[:, CUT + GROUP :]], axis=1).astype(BF16)
+    half = doubled(gathered(part, "lon"), "lat", 2)
     mine = lat % 2
     weight_half = lax.dynamic_slice_in_dim(weight_qkv, mine * (width // 2), width // 2, 0)
     gain_half = lax.dynamic_slice_in_dim(gains[0], mine * (width // 2), width // 2, 0)
-    weight_half = weight_half.astype(F32)
-    gain_half = (
-        jnp.sum(half_p.astype(F32) * weight_half[:, : 2 * width], axis=1)
-        + jnp.sum(half_q[:, :width].astype(F32) * weight_half[:, 2 * width :], axis=1)
-    ) / gain_half
-    square = sum_squares(half_p) + sum_squares(half_q) + sum_squares(gain_half)
-    square = square + 0.5 * sum_squares(grad_bias)
-    row = jnp.concatenate([gain_half, square.reshape(1), jnp.zeros((127,), F32)])
-    row = row.reshape(1, -1)
-    sections, lats_on = lax.axis_size("section"), lax.axis_size("lat")
-    pairs = [
-        (s * lats_on + i, (sections - 1 - s) * lats_on + (i ^ 1))
-        for s in range(sections) for i in range(lats_on)
-    ]
-    row_other = swapped(row, "lat", 1)
-    square = square + row_other[0, width // 2]
-    square = square + (
-        swapped(row[:, width // 2 :], "section", 1)[0, 0]
-        + lax.ppermute(row[:, width // 2 :], ("section", "lat"), pairs)[0, 0]
-    )
-    entries = 2 * (4 * width * width + width + heads)
-    factor = jnp.minimum(1.0, lax.rsqrt(square / entries + 1e-06))
-    gain_other = row_other[0, : width // 2]
-    grad_gain = jnp.concatenate(
-        [
-            jnp.where(mine == 0, gain_half, gain_other),
-            jnp.where(mine == 0, gain_other, gain_half),
-        ]
-    )
-    all_p = doubled(half_p, "lat", 1).astype(F32) * factor
-    all_q = doubled(half_q, "lat", 1).astype(F32) * factor
-    grad_qkv = jnp.concatenate([all_p, all_q[:, :width]], axis=1)
-    grad_out = all_q[:, width:]
-    return (
-        final_grad[None],
-        grad_qkv[None],
-        grad_out[None],
-        (grad_gain * factor)[None],
-        (grad_bias * factor)[None],
-    )
+    weighed = half[:, : 3 * width].astype(F32) * weight_half.astype(F32)
+    gain_half = jnp.sum(weighed, axis=1) / gain_half
+    square = sum_squares(half) + sum_squares(gain_half) + 0.5 * sum_squares(bias)
+    square = square.reshape(1)
+    square = square + swapped(square, "lat", 1)
+    square = square + swapped(square, "section", 1)
+    factor = jnp.minimum(1.0, lax.rsqrt(square[0] / entries + 1e-06))
+    grads = doubled(half, "lat", 1).astype(F32) * factor
+    gain = doubled(gain_half.reshape(-1, 1), "lat", 1)[:, 0] * factor
+    return (grads[:, : 3 * width], grads[:, 3 * width :], gain, bias * factor), bias
 
 
 def solution(mesh):

time: 122 us -> 103 us (0.84)
  other arithmetic: 12.2 us -> 0.08 us
  Pallas kernels: 10.5 us -> 20.3 us
  local copies, waits for them, and re-layouts: 20 us -> 14.3 us
  waiting for transfers between devices: 40.8 us -> 35.7 us
  between operations: 4.51 us -> 0.83 us
  starting transfers between devices: 33.4 us -> 31.7 us
    pallas_call x5 -> x10, Pallas kernels: 10.5 us -> 15.8 us  [call(): pl.pallas_call(kernel, out_shape=list(outs), in_specs=[pl.BlockSpec(memor...]
    ppermute x10 -> x8, starting transfers between devices: 7.95 us -> 3.45 us  [swapped(): return lax.ppermute(value, axis, [(i, i ^ bit) for i in range(count)])]
    pallas_call x0 -> x1, Pallas kernels: none -> 4.46 us  [staged(): pl.pallas_call(functools.partial(last_kernel, entries=entries), grid=(ste...]
    reduce_sum x6 -> x0, other arithmetic: 3.13 us -> none  [the longest x3 2.08 us: sum_squares(): return jnp.sum(wide * wide)]
    ppermute x14, waiting for transfers between devices: 24.4 us -> 21.4 us  [from_behind(): lax.ppermute(value, axis, [(i, (i + by) % count) for i in range(count)])]
    unnamed x55 -> x41, local copies, waits for them, and re-layouts: 16.9 us -> 14.3 us
    add x4 -> x0, other arithmetic: 2.57 us -> none  [the longest x1 1.26 us: body(): part_q = keep_q + came_q.astype(F32)]
    broadcast_in_dim x2 -> x0, other arithmetic: 2.44 us -> none  [the longest x1 1.93 us: body(): grad_qkv[None]]
  transfers between devices with their start and end apart: 26 -> 24, of which waited for: 12 -> 12; matrix products, arithmetic and copies ran while one was open for 11% -> 1% of each run, Pallas kernels for 1% -> 2%
where the time goes in v3:
time: 103 us
  waiting for transfers between devices  35.7 us (35%)
  starting transfers between devices  31.7 us (31%)
  Pallas kernels  20.3 us (20%)
  local copies, waits for them, and re-layouts  14.3 us (14%)
    ppermute x14, starting transfers between devices, from_behind(): lax.ppermute(value, axis, [(i, (i + by) % count) for i in range(count)])  25.3 us
    ppermute x14, waiting for transfers between devices, from_behind(): lax.ppermute(value, axis, [(i, (i + by) % count) for i in range(count)])  21.4 us
    pallas_call x10, Pallas kernels, call(): pl.pallas_call(kernel, out_shape=list(outs), in_specs=[pl.BlockSpec(memor...  15.8 us
    unnamed x41, local copies, waits for them, and re-layouts  14.3 us
    ppermute x8, waiting for transfers between devices, swapped(): return lax.ppermute(value, axis, [(i, i ^ bit) for i in range(count)])  8.33 us
    ppermute x1, waiting for transfers between devices, passed_along(): return lax.ppermute(block, axis, route)  5.96 us
    pallas_call x1, Pallas kernels, staged(): pl.pallas_call(functools.partial(last_kernel, entries=entries), grid=(ste...  4.46 us
    ppermute x8, starting transfers between devices, swapped(): return lax.ppermute(value, axis, [(i, i ^ bit) for i in range(count)])  3.45 us
  transfers between devices with their start and end apart: 24, of which 12 were waited for; matrix products, arithmetic and copies ran while one was open for 1% of the time, Pallas kernels for 2%

profile of v3, /device:TPU:0, one launch (start us, length us, event | category | flops | bytes accessed | tf_op | source)
XLA Modules:
  0.0 103.0 jit_solution(12580894657538461428)
XLA Ops:
  0.6 0.9 copy.12.tokens
  1.6 0.0 copy-start.3
  1.6 1.0 copy.13.cot
  2.6 0.7 copy-done.16
  3.3 0.1 shard_map.110
  3.4 5.1 %collective-permute-start = (bf16[160,512]{1,0:T(8,128)(2,1)S(1)}, bf16[160,512]{1,0:T(8,128)(2,1)S(1)}, u32[]{:S(2)}, u32[]{:S(2)}) collective-permute-start(bf16[160,512]{1,0:T(8,128)(2,1)S(1)} %get-tuple-element.50), channel_id=1, source_target_pairs={{0,12},{4,0},{8,4},{12,8},{1,13},{5,1},{9,5},{13,9},{2,14},{6,2},{... | collective-permute-start | bytes 491528 | tf_op jit(solution)/shard_map/ppermute | solution.py:20
  8.5 3.5 %collective-permute-done.rim = bf16[160,512]{1,0:T(8,128)(2,1)S(1)} collective-permute-done((bf16[160,512]{1,0:T(8,128)(2,1)S(1)}, bf16[160,512]{1,0:T(8,128)(2,1)S(1)}, u32[]{:S(2)}, u32[]{:S(2)}) %collective-permute-start) | collective-permute-done | bytes 163872 | tf_op jit(solution)/shard_map/ppermute | solution.py:20
  11.9 1.4 %copy-done = bf16[1,512,1536]{2,1,0:T(8,128)(2,1)S(1)} copy-done((bf16[1,512,1536]{2,1,0:T(8,128)(2,1)S(1)}, bf16[1,512,1536]{2,1,0:T(8,128)(2,1)}, u32[]{:S(2)}) %copy-start) | copy-done | bytes 1572888
  13.4 1.0 %copy-done.2 = bf16[1,512,512]{2,1,0:T(8,128)(2,1)S(1)} copy-done((bf16[1,512,512]{2,1,0:T(8,128)(2,1)S(1)}, bf16[1,512,512]{2,1,0:T(8,128)(2,1)}, u32[]{:S(2)}) %copy-start.2) | copy-done | bytes 524312
  14.4 0.7 copy-done.14
  15.1 0.7 copy-done.17
  15.8 0.7 copy-done.18
  16.4 6.4 %shard_map.111 = (bf16[144,512]{1,0:T(8,128)(2,1)}, bf16[144,512]{1,0:T(8,128)(2,1)S(1)}, f32[144,512]{1,0:T(8,128)S(1)}, f32[144,128]{1,0:T(8,128)S(1)}, bf16[5...) custom-call(f32[1,16]{1,0:T(1,128)S(1)} %copy-done.18, ...), custom_call_target="tpu_custom_call" | custom-call | flops 1000000000 | bytes 5359968 | tf_op jit(solution)/shard_map/pallas_call | solution.py:44
  22.8 0.8 copy-done.4
  23.5 0.7 copy-done.6
  24.3 0.7 copy-done.8
  25.0 0.6 copy-done.10
  25.6 0.6 copy-done.12
  26.2 1.3 %collective-permute-start.1 = (bf16[144,512]{1,0:T(8,128)(2,1)}, bf16[144,512]{1,0:T(8,128)(2,1)}, u32[]{:S(2)}, u32[]{:S(2)}) collective-permute-start(bf16[144,512]{1,0:T(8,128)(2,1)} %get-tuple-element.51), channel_id=1, source_target_pairs={{16,0},{17,1},{18,2},{19,3},{20,4},{21,5},{22,6},{23,7},{24,8},{25... | collective-permute-start | bytes 442376 | tf_op jit(solution)/shard_map/ppermute | solution.py:26
  27.5 0.1 pad_add_fusion.core.place
  27.6 6.0 %collective-permute-done.1.skip = bf16[144,512]{1,0:T(8,128)(2,1)} collective-permute-done((bf16[144,512]{1,0:T(8,128)(2,1)}, bf16[144,512]{1,0:T(8,128)(2,1)}, u32[]{:S(2)}, u32[]{:S(2)}) %collective-permute-start.1) | collective-permute-done | bytes 147488 | tf_op jit(solution)/shard_map/ppermute | solution.py:26
  33.6 1.0 copy-done.5
  34.6 0.9 copy-done.9
  35.5 0.9 copy-done.13
  36.4 3.8 %shard_map.112 = (bf16[144,512]{1,0:T(8,128)(2,1)S(1)}, bf16[144,1536]{1,0:T(8,128)(2,1)S(1)}, f32[8,128]{1,0:T(8,128)S(1)}, bf16[256,2176]{1,0:T(8,128)(2,1)S(1)}) custom-call(s32[3]{0:T(128)S(1)} %pad_add_fusion.core.place, bf16[144,512]{1,0:T(8,128)(2,1)} %collective-permute-done.1.skip, bf16[144,512]{1,0:T(8,128)(2,1)S(1)} %get-tuple-element.52.cot, ...), custom_call_target="tpu_custom_call" | custom-call | flops 1000000000 | bytes 4812812 | tf_op jit(solution)/shard_map/pallas_call | solution.py:44
  40.3 0.1 collective-permute-start.3
  40.4 1.5 %shard_map.113 = (f32[256,2176]{1,0:T(8,128)S(1)}, f32[72,512]{1,0:T(8,128)S(1)}, bf16[72,512]{1,0:T(8,128)(2,1)S(1)}) custom-call(s32[3]{0:T(128)S(1)} %pad_add_fusion.core.place, bf16[144,512]{1,0:T(8,128)(2,1)S(1)} %get-tuple-element.59.total, bf16[144,1536]{1,0:T(8,128)(2,1)S(1)} %get-tuple-element.60.grad_proj, ...), custom_call_target="tpu_custom_call" | custom-call | flops 500000000 | bytes 5281804 | tf_op jit(solution)/shard_map/pallas_call | solution.py:44
  41.9 1.2 %collective-permute-done.3.came = bf16[256,2176]{1,0:T(8,128)(2,1)S(1)} collective-permute-done((bf16[256,2176]{1,0:T(8,128)(2,1)S(1)}, bf16[256,2176]{1,0:T(8,128)(2,1)S(1)}, u32[]{:S(2)}, u32[]{:S(2)}) %collective-permute-start.3) | collective-permute-done | bytes 1114144 | tf_op jit(solution)/shard_map/ppermute | solution.py:31
  43.1 0.9 shard_map.114
  44.0 1.6 %collective-permute-start.4 = (bf16[128,1408]{1,0:T(8,128)(2,1)S(1)}, bf16[128,1408]{1,0:T(8,128)(2,1)S(1)}, u32[]{:S(2)}, u32[]{:S(2)}) collective-permute-start(bf16[128,1408]{1,0:T(8,128)(2,1)S(1)} %get-tuple-element.69), channel_id=1, source_target_pairs={{0,2},{1,3},{2,0},{3,1},{4,6},{5,7},{6,4},{7,5},{8,10},{9,11},{10,... | collective-permute-start | bytes 1081352 | tf_op jit(solution)/shard_map/ppermute | solution.py:31
  45.6 0.5 collective-permute-start.5
  46.1 4.4 %collective-permute-start.6 = (bf16[64,768]{1,0:T(8,128)(2,1)S(1)}, bf16[64,768]{1,0:T(8,128)(2,1)S(1)}, u32[]{:S(2)}, u32[]{:S(2)}) collective-permute-start(bf16[64,768]{1,0:T(8,128)(2,1)S(1)} %get-tuple-element.72), channel_id=1, source_target_pairs={{0,8},{4,12},{8,0},{12,4},{1,9},{5,13},{9,1},{13,5},{2,10},{6,14},... | collective-permute-start | bytes 294920 | tf_op jit(solution)/shard_map/ppermute | solution.py:20
  50.4 3.1 %collective-permute-done.5.rest_0_ = bf16[64,768]{1,0:T(8,128)(2,1)S(1)} collective-permute-done((bf16[64,768]{1,0:T(8,128)(2,1)S(1)}, bf16[64,768]{1,0:T(8,128)(2,1)S(1)}, u32[]{:S(2)}, u32[]{:S(2)}) %collective-permute-start.5) | collective-permute-done | bytes 98336 | tf_op jit(solution)/shard_map/ppermute | solution.py:20
  53.6 3.5 %collective-permute-done.6.rest_1_ = bf16[64,768]{1,0:T(8,128)(2,1)S(1)} collective-permute-done((bf16[64,768]{1,0:T(8,128)(2,1)S(1)}, bf16[64,768]{1,0:T(8,128)(2,1)S(1)}, u32[]{:S(2)}, u32[]{:S(2)}) %collective-permute-start.6) | collective-permute-done | bytes 98336 | tf_op jit(solution)/shard_map/ppermute | solution.py:20
  57.0 0.0 collective-permute-done.7.rest_2_
  57.1 0.7 shard_map.115
  57.8 1.6 %collective-permute-start.10 = (bf16[32,1408]{1,0:T(8,128)(2,1)S(1)}, bf16[32,1408]{1,0:T(8,128)(2,1)S(1)}, u32[]{:S(2)}, u32[]{:S(2)}) collective-permute-start(bf16[32,1408]{1,0:T(8,128)(2,1)S(1)} %get-tuple-element.78), channel_id=1, source_target_pairs={{0,8},{4,12},{8,0},{12,4},{1,9},{5,13},{9,1},{13,5},{2,10},{6,14},... | collective-permute-start | bytes 270344 | tf_op jit(solution)/shard_map/ppermute | solution.py:20
  59.4 3.4 %collective-permute-start.11 = (bf16[32,1408]{1,0:T(8,128)(2,1)S(1)}, bf16[32,1408]{1,0:T(8,128)(2,1)S(1)}, u32[]{:S(2)}, u32[]{:S(2)}) collective-permute-start(bf16[32,1408]{1,0:T(8,128)(2,1)S(1)} %get-tuple-element.79), channel_id=1, source_target_pairs={{0,12},{4,0},{8,4},{12,8},{1,13},{5,1},{9,5},{13,9},{2,14},{6,2},{... | collective-permute-start | bytes 270344 | tf_op jit(solution)/shard_map/ppermute | solution.py:20
  62.8 0.5 collective-permute-start.8
  63.3 3.6 %collective-permute-done.8.came_q = bf16[32,768]{1,0:T(8,128)(2,1)S(1)} collective-permute-done((bf16[32,768]{1,0:T(8,128)(2,1)S(1)}, bf16[32,768]{1,0:T(8,128)(2,1)S(1)}, u32[]{:S(2)}, u32[]{:S(2)}) %collective-permute-start.8) | collective-permute-done | bytes 49184 | tf_op jit(solution)/shard_map/ppermute | solution.py:31
  66.9 2.3 %collective-permute-done.9.rest_0_ = bf16[32,1408]{1,0:T(8,128)(2,1)S(1)} collective-permute-done((bf16[32,1408]{1,0:T(8,128)(2,1)S(1)}, bf16[32,1408]{1,0:T(8,128)(2,1)S(1)}, u32[]{:S(2)}, u32[]{:S(2)}) %collective-permute-start.9) | collective-permute-done | bytes 90144 | tf_op jit(solution)/shard_map/ppermute | solution.py:20
  69.2 0.6 shard_map.116
  69.8 0.1 collective-permute-start.13
  69.9 2.1 %collective-permute-start.14 = (bf16[32,1280]{1,0:T(8,128)(2,1)S(1)}, bf16[32,1280]{1,0:T(8,128)(2,1)S(1)}, u32[]{:S(2)}, u32[]{:S(2)}) collective-permute-start(bf16[32,1280]{1,0:T(8,128)(2,1)S(1)} %get-tuple-element.83.piece_p), channel_id=1, source_target_pairs={{0,8},{4,12},{8,0},{12,4},{1,9},{5,13},{9,1},{13,5},{2,10},{6,14},... | collective-permute-start | bytes 245768 | tf_op jit(solution)/shard_map/ppermute | solution.py:20
  72.0 2.2 %collective-permute-start.15 = (bf16[32,1280]{1,0:T(8,128)(2,1)S(1)}, bf16[32,1280]{1,0:T(8,128)(2,1)S(1)}, u32[]{:S(2)}, u32[]{:S(2)}) collective-permute-start(bf16[32,1280]{1,0:T(8,128)(2,1)S(1)} %get-tuple-element.83.piece_p), channel_id=1, source_target_pairs={{0,12},{4,0},{8,4},{12,8},{1,13},{5,1},{9,5},{13,9},{2,14},{6,2},{... | collective-permute-start | bytes 245768 | tf_op jit(solution)/shard_map/ppermute | solution.py:20
  74.1 0.5 collective-permute-start.12
  74.6 3.6 %collective-permute-done.12.other_q = bf16[32,768]{1,0:T(8,128)(2,1)S(1)} collective-permute-done((bf16[32,768]{1,0:T(8,128)(2,1)S(1)}, bf16[32,768]{1,0:T(8,128)(2,1)S(1)}, u32[]{:S(2)}, u32[]{:S(2)}) %collective-permute-start.12) | collective-permute-done | bytes 49184 | tf_op jit(solution)/shard_map/ppermute | solution.py:31
  78.2 0.5 collective-permute-done.14.rest_1_
  78.7 0.6 shard_map.118
  79.3 0.6 collective-permute-start.16
  79.9 1.5 %collective-permute-start.17 = (bf16[64,768]{1,0:T(8,128)(2,1)S(1)}, bf16[64,768]{1,0:T(8,128)(2,1)S(1)}, u32[]{:S(2)}, u32[]{:S(2)}) collective-permute-start(bf16[64,768]{1,0:T(8,128)(2,1)S(1)} %get-tuple-element.86.block_q), channel_id=1, source_target_pairs={{0,4},{4,8},{8,12},{12,0},{1,5},{5,9},{9,13},{13,1},{2,6},{6,10},{... | collective-permute-start | bytes 294920 | tf_op jit(solution)/shard_map/ppermute | solution.py:20
  81.4 2.1 %collective-permute-start.18 = (bf16[64,768]{1,0:T(8,128)(2,1)S(1)}, bf16[64,768]{1,0:T(8,128)(2,1)S(1)}, u32[]{:S(2)}, u32[]{:S(2)}) collective-permute-start(bf16[64,768]{1,0:T(8,128)(2,1)S(1)} %get-tuple-element.86.block_q), channel_id=1, source_target_pairs={{0,8},{4,12},{8,0},{12,4},{1,9},{5,13},{9,1},{13,5},{2,10},{6,14},... | collective-permute-start | bytes 294920 | tf_op jit(solution)/shard_map/ppermute | solution.py:20
  83.5 0.5 collective-permute-start.19
  83.9 3.3 %collective-permute-done.17.rest_0_ = bf16[64,768]{1,0:T(8,128)(2,1)S(1)} collective-permute-done((bf16[64,768]{1,0:T(8,128)(2,1)S(1)}, bf16[64,768]{1,0:T(8,128)(2,1)S(1)}, u32[]{:S(2)}, u32[]{:S(2)}) %collective-permute-start.17) | collective-permute-done | bytes 98336 | tf_op jit(solution)/shard_map/ppermute | solution.py:20
  87.2 2.7 %collective-permute-done.18.rest_1_ = bf16[64,768]{1,0:T(8,128)(2,1)S(1)} collective-permute-done((bf16[64,768]{1,0:T(8,128)(2,1)S(1)}, bf16[64,768]{1,0:T(8,128)(2,1)S(1)}, u32[]{:S(2)}, u32[]{:S(2)}) %collective-permute-start.18) | collective-permute-done | bytes 98336 | tf_op jit(solution)/shard_map/ppermute | solution.py:20
  89.9 1.1 %shard_map.119 = (bf16[256,2048]{1,0:T(8,128)(2,1)S(1)}, f32[8,384]{1,0:T(8,128)S(1)}) custom-call(s32[3]{0:T(128)S(1)} %pad_add_fusion.core.place, bf16[512,1536]{1,0:T(8,128)(2,1)S(1)} %bitcast.9, f32[1,512]{1,0:T(1,128)S(1)} %copy-done.15, f32[8,128]{1,0:T(8,128)S(1)} %get-tuple-element.80.bias, bf16[128,1280]{1,0:T(8,128)(2,1)S(1)} %get-tuple-element.85.block_p, ...), custom_call_target="tpu_custom_call" | custom-call | flops 100000000 | bytes 3688460 | tf_op jit(solution)/shard_map/pallas_call | solution.py:44
  91.0 0.0 collective-permute-start.20
  91.0 2.1 %collective-permute-start.2 = (bf16[72,512]{1,0:T(8,128)(2,1)S(1)}, bf16[72,512]{1,0:T(8,128)(2,1)S(1)}, u32[]{:S(2)}, u32[]{:S(2)}) collective-permute-start(bf16[72,512]{1,0:T(8,128)(2,1)S(1)} %get-tuple-element.65), channel_id=1, source_target_pairs={{0,4},{4,8},{8,12},{12,0},{1,5},{5,9},{9,13},{13,1},{2,6},{6,10},{... | collective-permute-start | bytes 221192 | tf_op jit(solution)/shard_map/ppermute | solution.py:20
  93.1 0.2 collective-permute-start.21
  93.3 1.7 %collective-permute-start.23 = (f32[8,384]{1,0:T(8,128)S(1)}, f32[8,384]{1,0:T(8,128)S(1)}, u32[]{:S(2)}, u32[]{:S(2)}) collective-permute-start(f32[8,384]{1,0:T(8,128)S(1)} %get-tuple-element.88.row), channel_id=1, source_target_pairs={{0,17},{1,16},{2,19},{3,18},{16,1},{17,0},{18,3},{19,2},{4,21},{5,... | collective-permute-start | bytes 36872 | tf_op jit(solution)/shard_map/ppermute | solution.py:534
  95.0 2.5 %collective-permute-done.2.back = bf16[72,512]{1,0:T(8,128)(2,1)S(1)} collective-permute-done((bf16[72,512]{1,0:T(8,128)(2,1)S(1)}, bf16[72,512]{1,0:T(8,128)(2,1)S(1)}, u32[]{:S(2)}, u32[]{:S(2)}) %collective-permute-start.2) | collective-permute-done | bytes 73760 | tf_op jit(solution)/shard_map/ppermute | solution.py:20
  97.5 0.1 shard_map.117
  97.5 0.9 copy.14
  98.5 4.5 %shard_map.120 = (f32[512,1536]{1,0:T(8,128)}, f32[512,512]{1,0:T(8,128)}, f32[1,512]{1,0:T(1,128)}, f32[1,16]{1,0:T(1,128)}) custom-call(s32[3]{0:T(128)S(1)} %pad_add_fusion.core.place, bf16[256,2048]{1,0:T(8,128)(2,1)S(1)} %get-tuple-element.87.half, bf16[256,2048]{1,0:T(8,128)(2,1)S(1)} %collective-permute-done.20.other, ...), custom_call_target="tpu_custom_call" | custom-call | tf_op jit(solution)/shard_map/pallas_call | solution.py:539
  (37 shorter events, 0.1 us)
Async XLA Ops:
  1.6 32.0 %copy-start.3 = (bf16[1,512,512]{2,1,0:T(8,128)(2,1)S(1)}, bf16[1,512,512]{2,1,0:T(8,128)(2,1)}, u32[]{:S(2)}) copy-start(bf16[1,512,512]{2,1,0:T(8,128)(2,1)} %param.12) | copy-start | bytes 1572868
  2.6 0.7 copy-start.16
  3.4 8.6 %collective-permute-start = (bf16[160,512]{1,0:T(8,128)(2,1)S(1)}, bf16[160,512]{1,0:T(8,128)(2,1)S(1)}, u32[]{:S(2)}, u32[]{:S(2)}) collective-permute-start(bf16[160,512]{1,0:T(8,128)(2,1)S(1)} %get-tuple-element.50), channel_id=1, source_target_pairs={{0,12},{4,0},{8,4},{12,8},{1,13},{5,1},{9,5},{13,9},{2,14},{6,2},{... | collective-permute-start | bytes 491528 | tf_op jit(solution)/shard_map/ppermute | solution.py:20
  11.9 1.4 %copy-start = (bf16[1,512,1536]{2,1,0:T(8,128)(2,1)S(1)}, bf16[1,512,1536]{2,1,0:T(8,128)(2,1)}, u32[]{:S(2)}) copy-start(bf16[1,512,1536]{2,1,0:T(8,128)(2,1)} %param.11) | copy-start | bytes 4718596
  13.4 1.0 %copy-start.2 = (bf16[1,512,512]{2,1,0:T(8,128)(2,1)S(1)}, bf16[1,512,512]{2,1,0:T(8,128)(2,1)}, u32[]{:S(2)}) copy-start(bf16[1,512,512]{2,1,0:T(8,128)(2,1)} %param.12) | copy-start | bytes 1572868
  14.4 0.7 copy-start.14
  15.1 0.7 copy-start.17
  15.8 0.7 copy-start.18
  22.8 0.8 copy-start.4
  23.5 0.7 copy-start.6
  24.3 0.7 copy-start.8
  25.0 0.6 copy-start.10
  25.6 0.6 copy-start.12
  26.2 7.3 %collective-permute-start.1 = (bf16[144,512]{1,0:T(8,128)(2,1)}, bf16[144,512]{1,0:T(8,128)(2,1)}, u32[]{:S(2)}, u32[]{:S(2)}) collective-permute-start(bf16[144,512]{1,0:T(8,128)(2,1)} %get-tuple-element.51), channel_id=1, source_target_pairs={{16,0},{17,1},{18,2},{19,3},{20,4},{21,5},{22,6},{23,7},{24,8},{25... | collective-permute-start | bytes 442376 | tf_op jit(solution)/shard_map/ppermute | solution.py:26
  33.6 1.0 copy-start.5
  34.6 0.9 copy-start.9
  35.5 0.9 copy-start.13
  36.4 3.9 %copy-start.1 = (bf16[1,512,1536]{2,1,0:T(8,128)(2,1)S(1)}, bf16[1,512,1536]{2,1,0:T(8,128)(2,1)}, u32[]{:S(2)}) copy-start(bf16[1,512,1536]{2,1,0:T(8,128)(2,1)} %param.11) | copy-start | bytes 4718596
  36.4 3.9 %copy-start.7 = (f32[144,512]{1,0:T(8,128)S(1)}, f32[144,512]{1,0:T(8,128)}, u32[]{:S(2)}) copy-start(f32[144,512]{1,0:T(8,128)} %copy-done.6) | copy-start | bytes 884740
  36.4 4.0 %copy-start.11 = (f32[144,128]{1,0:T(8,128)S(1)}, f32[144,128]{1,0:T(8,128)}, u32[]{:S(2)}) copy-start(f32[144,128]{1,0:T(8,128)} %copy-done.10) | copy-start | bytes 221188
  36.4 4.0 %copy-start.15 = (f32[1,512]{1,0:T(1,128)S(1)}, f32[1,512]{1,0:T(1,128)}, u32[]{:S(2)}) copy-start(f32[1,512]{1,0:T(1,128)} %gain.5) | copy-start | bytes 6148
  40.3 2.8 %collective-permute-start.3 = (bf16[256,2176]{1,0:T(8,128)(2,1)S(1)}, bf16[256,2176]{1,0:T(8,128)(2,1)S(1)}, u32[]{:S(2)}, u32[]{:S(2)}) collective-permute-start(bf16[256,2176]{1,0:T(8,128)(2,1)S(1)} %get-tuple-element.67), channel_id=1, source_target_pairs={{0,1},{1,0},{2,3},{3,2},{4,5},{5,4},{6,7},{7,6},{8,9},{9,8},{10,11... | collective-permute-start | bytes 3342344 | tf_op jit(solution)/shard_map/ppermute | solution.py:31
  44.0 13.1 %collective-permute-start.4 = (bf16[128,1408]{1,0:T(8,128)(2,1)S(1)}, bf16[128,1408]{1,0:T(8,128)(2,1)S(1)}, u32[]{:S(2)}, u32[]{:S(2)}) collective-permute-start(bf16[128,1408]{1,0:T(8,128)(2,1)S(1)} %get-tuple-element.69), channel_id=1, source_target_pairs={{0,2},{1,3},{2,0},{3,1},{4,6},{5,7},{6,4},{7,5},{8,10},{9,11},{10,... | collective-permute-start | bytes 1081352 | tf_op jit(solution)/shard_map/ppermute | solution.py:31
  45.6 8.0 %collective-permute-start.5 = (bf16[64,768]{1,0:T(8,128)(2,1)S(1)}, bf16[64,768]{1,0:T(8,128)(2,1)S(1)}, u32[]{:S(2)}, u32[]{:S(2)}) collective-permute-start(bf16[64,768]{1,0:T(8,128)(2,1)S(1)} %get-tuple-element.71), channel_id=1, source_target_pairs={{0,4},{4,8},{8,12},{12,0},{1,5},{5,9},{9,13},{13,1},{2,6},{6,10},{... | collective-permute-start | bytes 294920 | tf_op jit(solution)/shard_map/ppermute | solution.py:20
  46.1 11.0 %collective-permute-start.6 = (bf16[64,768]{1,0:T(8,128)(2,1)S(1)}, bf16[64,768]{1,0:T(8,128)(2,1)S(1)}, u32[]{:S(2)}, u32[]{:S(2)}) collective-permute-start(bf16[64,768]{1,0:T(8,128)(2,1)S(1)} %get-tuple-element.72), channel_id=1, source_target_pairs={{0,8},{4,12},{8,0},{12,4},{1,9},{5,13},{9,1},{13,5},{2,10},{6,14},... | collective-permute-start | bytes 294920 | tf_op jit(solution)/shard_map/ppermute | solution.py:20
  50.4 6.6 %collective-permute-start.7 = (bf16[64,768]{1,0:T(8,128)(2,1)S(1)}, bf16[64,768]{1,0:T(8,128)(2,1)S(1)}, u32[]{:S(2)}, u32[]{:S(2)}) collective-permute-start(bf16[64,768]{1,0:T(8,128)(2,1)S(1)} %get-tuple-element.73), channel_id=1, source_target_pairs={{0,12},{4,0},{8,4},{12,8},{1,13},{5,1},{9,5},{13,9},{2,14},{6,2},{... | collective-permute-start | bytes 294920 | tf_op jit(solution)/shard_map/ppermute | solution.py:20
  57.8 9.1 %collective-permute-start.10 = (bf16[32,1408]{1,0:T(8,128)(2,1)S(1)}, bf16[32,1408]{1,0:T(8,128)(2,1)S(1)}, u32[]{:S(2)}, u32[]{:S(2)}) collective-permute-start(bf16[32,1408]{1,0:T(8,128)(2,1)S(1)} %get-tuple-element.78), channel_id=1, source_target_pairs={{0,8},{4,12},{8,0},{12,4},{1,9},{5,13},{9,1},{13,5},{2,10},{6,14},... | collective-permute-start | bytes 270344 | tf_op jit(solution)/shard_map/ppermute | solution.py:20
  59.4 7.5 %collective-permute-start.11 = (bf16[32,1408]{1,0:T(8,128)(2,1)S(1)}, bf16[32,1408]{1,0:T(8,128)(2,1)S(1)}, u32[]{:S(2)}, u32[]{:S(2)}) collective-permute-start(bf16[32,1408]{1,0:T(8,128)(2,1)S(1)} %get-tuple-element.79), channel_id=1, source_target_pairs={{0,12},{4,0},{8,4},{12,8},{1,13},{5,1},{9,5},{13,9},{2,14},{6,2},{... | collective-permute-start | bytes 270344 | tf_op jit(solution)/shard_map/ppermute | solution.py:20
  62.8 6.4 %collective-permute-start.9 = (bf16[32,1408]{1,0:T(8,128)(2,1)S(1)}, bf16[32,1408]{1,0:T(8,128)(2,1)S(1)}, u32[]{:S(2)}, u32[]{:S(2)}) collective-permute-start(bf16[32,1408]{1,0:T(8,128)(2,1)S(1)} %get-tuple-element.77), channel_id=1, source_target_pairs={{0,4},{4,8},{8,12},{12,0},{1,5},{5,9},{9,13},{13,1},{2,6},{6,10},{... | collective-permute-start | bytes 270344 | tf_op jit(solution)/shard_map/ppermute | solution.py:20
  62.8 4.1 %collective-permute-start.8 = (bf16[32,768]{1,0:T(8,128)(2,1)S(1)}, bf16[32,768]{1,0:T(8,128)(2,1)S(1)}, u32[]{:S(2)}, u32[]{:S(2)}) collective-permute-start(bf16[32,768]{1,0:T(8,128)(2,1)S(1)} %get-tuple-element.76), channel_id=1, source_target_pairs={{0,2},{1,3},{2,0},{3,1},{4,6},{5,7},{6,4},{7,5},{8,10},{9,11},{10,... | collective-permute-start | bytes 147464 | tf_op jit(solution)/shard_map/ppermute | solution.py:31
  69.8 8.4 %collective-permute-start.13 = (bf16[32,1280]{1,0:T(8,128)(2,1)S(1)}, bf16[32,1280]{1,0:T(8,128)(2,1)S(1)}, u32[]{:S(2)}, u32[]{:S(2)}) collective-permute-start(bf16[32,1280]{1,0:T(8,128)(2,1)S(1)} %get-tuple-element.83.piece_p), channel_id=1, source_target_pairs={{0,4},{4,8},{8,12},{12,0},{1,5},{5,9},{9,13},{13,1},{2,6},{6,10},{... | collective-permute-start | bytes 245768 | tf_op jit(solution)/shard_map/ppermute | solution.py:20
  69.9 8.8 %collective-permute-start.14 = (bf16[32,1280]{1,0:T(8,128)(2,1)S(1)}, bf16[32,1280]{1,0:T(8,128)(2,1)S(1)}, u32[]{:S(2)}, u32[]{:S(2)}) collective-permute-start(bf16[32,1280]{1,0:T(8,128)(2,1)S(1)} %get-tuple-element.83.piece_p), channel_id=1, source_target_pairs={{0,8},{4,12},{8,0},{12,4},{1,9},{5,13},{9,1},{13,5},{2,10},{6,14},... | collective-permute-start | bytes 245768 | tf_op jit(solution)/shard_map/ppermute | solution.py:20
  72.0 6.8 %collective-permute-start.15 = (bf16[32,1280]{1,0:T(8,128)(2,1)S(1)}, bf16[32,1280]{1,0:T(8,128)(2,1)S(1)}, u32[]{:S(2)}, u32[]{:S(2)}) collective-permute-start(bf16[32,1280]{1,0:T(8,128)(2,1)S(1)} %get-tuple-element.83.piece_p), channel_id=1, source_target_pairs={{0,12},{4,0},{8,4},{12,8},{1,13},{5,1},{9,5},{13,9},{2,14},{6,2},{... | collective-permute-start | bytes 245768 | tf_op jit(solution)/shard_map/ppermute | solution.py:20
  74.1 4.1 %collective-permute-start.12 = (bf16[32,768]{1,0:T(8,128)(2,1)S(1)}, bf16[32,768]{1,0:T(8,128)(2,1)S(1)}, u32[]{:S(2)}, u32[]{:S(2)}) collective-permute-start(bf16[32,768]{1,0:T(8,128)(2,1)S(1)} %get-tuple-element.84.piece_q), channel_id=1, source_target_pairs={{0,2},{1,3},{2,0},{3,1},{4,6},{5,7},{6,4},{7,5},{8,10},{9,11},{10,... | collective-permute-start | bytes 147464 | tf_op jit(solution)/shard_map/ppermute | solution.py:31
  79.3 10.6 %collective-permute-start.16 = (bf16[128,1280]{1,0:T(8,128)(2,1)S(1)}, bf16[128,1280]{1,0:T(8,128)(2,1)S(1)}, u32[]{:S(2)}, u32[]{:S(2)}) collective-permute-start(bf16[128,1280]{1,0:T(8,128)(2,1)S(1)} %get-tuple-element.85.block_p), channel_id=1, source_target_pairs={{0,2},{1,3},{2,0},{3,1},{4,6},{5,7},{6,4},{7,5},{8,10},{9,11},{10,... | collective-permute-start | bytes 983048 | tf_op jit(solution)/shard_map/ppermute | solution.py:31
  79.9 7.3 %collective-permute-start.17 = (bf16[64,768]{1,0:T(8,128)(2,1)S(1)}, bf16[64,768]{1,0:T(8,128)(2,1)S(1)}, u32[]{:S(2)}, u32[]{:S(2)}) collective-permute-start(bf16[64,768]{1,0:T(8,128)(2,1)S(1)} %get-tuple-element.86.block_q), channel_id=1, source_target_pairs={{0,4},{4,8},{8,12},{12,0},{1,5},{5,9},{9,13},{13,1},{2,6},{6,10},{... | collective-permute-start | bytes 294920 | tf_op jit(solution)/shard_map/ppermute | solution.py:20
  81.4 8.5 %collective-permute-start.18 = (bf16[64,768]{1,0:T(8,128)(2,1)S(1)}, bf16[64,768]{1,0:T(8,128)(2,1)S(1)}, u32[]{:S(2)}, u32[]{:S(2)}) collective-permute-start(bf16[64,768]{1,0:T(8,128)(2,1)S(1)} %get-tuple-element.86.block_q), channel_id=1, source_target_pairs={{0,8},{4,12},{8,0},{12,4},{1,9},{5,13},{9,1},{13,5},{2,10},{6,14},... | collective-permute-start | bytes 294920 | tf_op jit(solution)/shard_map/ppermute | solution.py:20
  83.5 6.4 %collective-permute-start.19 = (bf16[64,768]{1,0:T(8,128)(2,1)S(1)}, bf16[64,768]{1,0:T(8,128)(2,1)S(1)}, u32[]{:S(2)}, u32[]{:S(2)}) collective-permute-start(bf16[64,768]{1,0:T(8,128)(2,1)S(1)} %get-tuple-element.86.block_q), channel_id=1, source_target_pairs={{0,12},{4,0},{8,4},{12,8},{1,13},{5,1},{9,5},{13,9},{2,14},{6,2},{... | collective-permute-start | bytes 294920 | tf_op jit(solution)/shard_map/ppermute | solution.py:20
  91.0 7.5 %collective-permute-start.20 = (bf16[256,2048]{1,0:T(8,128)(2,1)S(1)}, bf16[256,2048]{1,0:T(8,128)(2,1)S(1)}, u32[]{:S(2)}, u32[]{:S(2)}) collective-permute-start(bf16[256,2048]{1,0:T(8,128)(2,1)S(1)} %get-tuple-element.87.half), channel_id=1, source_target_pairs={{0,1},{1,0},{2,3},{3,2},{4,5},{5,4},{6,7},{7,6},{8,9},{9,8},{10,11... | collective-permute-start | bytes 3145736 | tf_op jit(solution)/shard_map/ppermute | solution.py:31
  91.0 6.5 %collective-permute-start.2 = (bf16[72,512]{1,0:T(8,128)(2,1)S(1)}, bf16[72,512]{1,0:T(8,128)(2,1)S(1)}, u32[]{:S(2)}, u32[]{:S(2)}) collective-permute-start(bf16[72,512]{1,0:T(8,128)(2,1)S(1)} %get-tuple-element.65), channel_id=1, source_target_pairs={{0,4},{4,8},{8,12},{12,0},{1,5},{5,9},{9,13},{13,1},{2,6},{6,10},{... | collective-permute-start | bytes 221192 | tf_op jit(solution)/shard_map/ppermute | solution.py:20
  93.1 5.4 %collective-permute-start.21 = (f32[8,384]{1,0:T(8,128)S(1)}, f32[8,384]{1,0:T(8,128)S(1)}, u32[]{:S(2)}, u32[]{:S(2)}) collective-permute-start(f32[8,384]{1,0:T(8,128)S(1)} %get-tuple-element.88.row), channel_id=1, source_target_pairs={{0,1},{1,0},{2,3},{3,2},{4,5},{5,4},{6,7},{7,6},{8,9},{9,8},{10,11... | collective-permute-start | bytes 36872 | tf_op jit(solution)/shard_map/ppermute | solution.py:31
  93.3 5.2 %collective-permute-start.22 = (f32[8,384]{1,0:T(8,128)S(1)}, f32[8,384]{1,0:T(8,128)S(1)}, u32[]{:S(2)}, u32[]{:S(2)}) collective-permute-start(f32[8,384]{1,0:T(8,128)S(1)} %get-tuple-element.88.row), channel_id=1, source_target_pairs={{0,16},{16,0},{1,17},{17,1},{2,18},{18,2},{3,19},{19,3},{4,20},{20... | collective-permute-start | bytes 36872 | tf_op jit(solution)/shard_map/ppermute | solution.py:31
  93.3 5.2 %collective-permute-start.23 = (f32[8,384]{1,0:T(8,128)S(1)}, f32[8,384]{1,0:T(8,128)S(1)}, u32[]{:S(2)}, u32[]{:S(2)}) collective-permute-start(f32[8,384]{1,0:T(8,128)S(1)} %get-tuple-element.88.row), channel_id=1, source_target_pairs={{0,17},{1,16},{2,19},{3,18},{16,1},{17,0},{18,3},{19,2},{4,21},{5,... | collective-permute-start | bytes 36872 | tf_op jit(solution)/shard_map/ppermute | solution.py:534

commit v4 on v3

--- a/solution.py
+++ b/solution.py
@@ -39,22 +39,28 @@
     return lax.dot_general(left, right, (((1,), (1,)), ((), ())), preferred_element_type=F32)
 
 
-def call(kernel, outs, scratch=(), smem=(), operands=(), flops=10**8, limit=12):
+def call(kernel, outs, scratch=(), places="", out_places="", operands=(), flops=10**8, limit=12):
+    spaces = {"v": pltpu.VMEM, "s": pltpu.SMEM, "a": pl.ANY}
+    places = places or "v" * len(operands)
+    out_places = out_places or "v" * len(outs)
     moved = sum(o.size * o.dtype.itemsize for o in list(outs) + list(operands))
     return pl.pallas_call(
         kernel,
         out_shape=list(outs),
-        in_specs=[
-            pl.BlockSpec(memory_space=pltpu.SMEM if i in smem else pltpu.VMEM)
-            for i in range(len(operands))
-        ],
-        out_specs=[pl.BlockSpec(memory_space=pltpu.VMEM) for _ in outs],
+        in_specs=[pl.BlockSpec(memory_space=spaces[letter]) for letter in places],
+        out_specs=[pl.BlockSpec(memory_space=spaces[letter]) for letter in out_places],
         scratch_shapes=list(scratch),
         compiler_params=pltpu.CompilerParams(vmem_limit_bytes=limit * 2**20),
         cost_estimate=pl.CostEstimate(flops=flops, bytes_accessed=moved, transcendentals=0),
     )(*operands)
 
 
+def started(source, target, semaphores, index):
+    copy = pltpu.make_async_copy(source, target, semaphores.at[index])
+    copy.start()
+    return copy
+
+
 def shape(dims, dtype):
     return jax.ShapeDtypeStruct(dims, dtype)
 
@@ -63,30 +69,35 @@
     return pl.ds(pl.multiple_of(start, size), size)
 
 
-def pack_kernel(tokens, cot, land, own, rim, own32, rim32):
+def pack_kernel(tokens, cot, land, own, rim, tokens_v, cot_v, land_v, own32, rim32, sems):
+    arrays = ((tokens, tokens_v), (cot, cot_v), (land, land_v))
+    copies = [started(source, target, sems, i) for i, (source, target) in enumerate(arrays)]
     levels, lats, cols, width = tokens.shape[1:]
     half = levels * lats * SHIFT
     rim32[2 * half :, :] = jnp.zeros((rim32.shape[0] - 2 * half, width), F32)
-    for which, ref in enumerate((tokens, cot)):
+    for which, ref in enumerate((tokens_v, cot_v)):
+        copies[which].wait()
         for level in range(levels):
             for lat in range(lats):
                 base = which * half + (level * lats + lat) * SHIFT
                 line = ref[0, level, lat].astype(F32)
                 rim32[base : base + SHIFT, :] = line[:SHIFT]
                 own32[base : base + SHIFT, :] = line[SHIFT:]
-    rim32[2 * half : 2 * half + lats, :cols] = land[...].astype(F32)
+    copies[2].wait()
+    rim32[2 * half : 2 * half + lats, :cols] = land_v[...].astype(F32)
     own[...] = own32[...].astype(BF16)
     rim[...] = rim32[...].astype(BF16)
 
 
-def unpack_kernel(own, back, grid):
+def unpack_kernel(own, back, grid, grid_v, sems):
     levels, lats, cols, width = grid.shape[1:]
     came = back[...].astype(F32)
     for level in range(levels):
         for lat in range(lats):
             base = (level * lats + lat) * SHIFT
-            grid[0, level, lat, :SHIFT, :] = came[base : base + SHIFT]
-            grid[0, level, lat, SHIFT:, :] = own[base : base + SHIFT, :]
+            grid_v[0, level, lat, :SHIFT, :] = came[base : base + SHIFT]
+            grid_v[0, level, lat, SHIFT:, :] = own[base : base + SHIFT, :]
+    started(grid_v, grid, sems, 0).wait()
 
 
 def land_column(land, rows, first):
@@ -117,7 +128,7 @@
     return sum(block[i * rows : (i + 1) * rows] * mask for i, mask in enumerate(masks))
 
 
-def back_through(grad_out, probs, qkv, keys_t, weight_out, grad_proj, size, land):
+def back_through(grad_out, probs, qkv, keys_t, weight_out, grad_proj, size, land, ready=None):
     count, width = grad_out.shape
     per = GROUP // size
     scale = size ** (-0.5)
@@ -129,6 +140,8 @@
     bias_row = jnp.zeros((1, GROUP), F32)
     for group in range(width // GROUP):
         at = group * GROUP
+        if ready is not None:
+            ready[group].wait()
         values = qkv[:, 2 * width + at : 2 * width + at + GROUP]
         grad_probs = dot(stacked(values, masks_b), att_t[at : at + GROUP, :])
         scores_b, probs_b, queries_t = [], [], []
@@ -166,8 +179,10 @@
 
 def forward_kernel(
     bias, own, rim, land_own, gain, weight_qkv, weight_out,
-    skip, cot, normed_out, inverse_out, normed_t, qkv, keys_t, probs, attended_t, land_out,
-    grad_proj, values_t,
+    skip, cot, normed_out, normed_t_out, qkv_out, probs_out, attended_t_out, extra_out,
+    bias_v, land_v, gain_v, qkv_v, out_v,
+    normed_v, normed_t, qkv, probs, attended_t, extra, queries_t, keys_t, values_t, grad_proj,
+    sems_in, sems_out,
 ):
     width = gain.shape[1]
     heads = bias.shape[1]
@@ -176,63 +191,116 @@
     count = 2 * half
     per = GROUP // size
     scale = size ** (-0.5)
+    got = [
+        started(source, target, sems_in, i)
+        for i, (source, target) in enumerate(
+            [
+                (gain, gain_v),
+                (land_own, land_v),
+                (bias, bias_v),
+                (weight_qkv.at[:, :width], qkv_v.at[:, :width]),
+                (weight_qkv.at[:, width : 2 * width], qkv_v.at[:, width : 2 * width]),
+                (weight_qkv.at[:, 2 * width :], qkv_v.at[:, 2 * width :]),
+                (weight_out, out_v),
+            ]
+        )
+    ]
+    sent = []
     masks_b = head_masks(BF16, size)
     mine = own[...].astype(F32)
     came = rim[...].astype(F32)
     lats, cols = land_own.shape
-    land = jnp.concatenate(
-        [
-            land_column(land_own[...].astype(F32), half, SHIFT),
-            land_column(came[2 * half : 2 * half + lats, :cols], half, 0),
-        ],
-        axis=0,
-    )
-    land_out[...] = jnp.broadcast_to(land, land_out.shape)
     values = jnp.concatenate([mine[:half], came[:half]], axis=0)
     centred = values - jnp.mean(values, axis=-1, keepdims=True)
     inverse = lax.rsqrt(jnp.mean(centred * centred, axis=-1, keepdims=True) + EPSILON)
     normed = centred * inverse
-    normed_out[...] = normed
-    inverse_out[...] = jnp.broadcast_to(inverse, inverse_out.shape)
-    normed_b = (normed * gain[...]).astype(BF16)
+    normed_v[...] = normed
+    sent.append(started(normed_v, normed_out, sems_out, 0))
+    for copy in got[:3]:
+        copy.wait()
+    normed_b = (normed * gain_v[...]).astype(BF16)
     normed_t[...] = normed_b.T
-    qkv[...] = dot(normed_b, weight_qkv[...]).astype(BF16)
-    queries_t = qkv[:, :width].T
-    keys_t[...] = qkv[:, width : 2 * width].T
-    values_t[...] = qkv[:, 2 * width :].T
+    sent.append(started(normed_t, normed_t_out, sems_out, 1))
+    land = jnp.concatenate(
+        [
+            land_column(land_v[...].astype(F32), half, SHIFT),
+            land_column(came[2 * half : 2 * half + lats, :cols], half, 0),
+        ],
+        axis=0,
+    )
+    extra[:, :GROUP] = jnp.broadcast_to(land, (count, GROUP))
+    extra[:, GROUP:] = jnp.broadcast_to(inverse, (count, GROUP))
+    sent.append(started(extra, extra_out, sems_out, 2))
+    for part, turned in enumerate((queries_t, keys_t, values_t)):
+        got[3 + part].wait()
+        columns = slice(part * width, (part + 1) * width)
+        qkv[:, columns] = dot(normed_b, qkv_v[:, columns]).astype(BF16)
+        turned[...] = qkv[:, columns].T
+    sent.append(started(qkv, qkv_out, sems_out, 3))
     for group in range(width // GROUP):
         at = group * GROUP
         keys = qkv[:, width + at : width + at + GROUP]
         scores = dot(stacked(keys, masks_b), queries_t[at : at + GROUP, :])
         for part in range(per):
             head = group * per + part
-            block = scores[part * count : (part + 1) * count] * scale + bias[0, head] * land
+            block = scores[part * count : (part + 1) * count] * scale
+            block = block + bias_v[:, head : head + 1] * land
             block = jnp.exp(block - jnp.max(block, axis=0, keepdims=True))
             weights = block * (1.0 / jnp.sum(block, axis=0, keepdims=True))
             probs[head * count : (head + 1) * count, :] = weights
             out = dot(values_t[head * size : (head + 1) * size, :], weights.astype(BF16))
             attended_t[head * size : (head + 1) * size, :] = out.astype(BF16)
+        rows = pl.ds(group * per * count, per * count)
+        sent.append(started(probs.at[rows, :], probs_out.at[rows, :], sems_out, 4 + group))
+    sent.append(started(attended_t, attended_t_out, sems_out, 4 + width // GROUP))
     grad_out = jnp.concatenate([mine[half:], came[half : 2 * half]], axis=0)
     cot[...] = grad_out.astype(BF16)
-    back_through(cot[...], probs, qkv, keys_t, weight_out, grad_proj, size, None)
+    got[6].wait()
+    back_through(cot[...], probs, qkv, keys_t, out_v, grad_proj, size, None)
     skip[...] = (
-        through_norm(grad_proj[...], weight_qkv, gain, normed, inverse) + grad_out
+        through_norm(grad_proj[...], qkv_v, gain_v, normed, inverse) + grad_out
     ).astype(BF16)
+    for copy in sent:
+        copy.wait()
 
 
 def backward_kernel(
-    core, skip, cot, qkv, keys_t, probs, land, weight_out, normed_t, attended_t,
+    place, skip, cot, qkv_in, probs_in, weight_out, extra_in, normed_t_in, attended_t_in,
     total_out, grad_proj, bias_out, give,
+    qkv, probs, out_v, extra, normed_t, attended_t, keys_t, sems,
     *, heads,
 ):
     count, width = cot.shape
+    per = probs.shape[0] * GROUP // width
+    got = [
+        started(source, target, sems, i)
+        for i, (source, target) in enumerate(
+            [
+                (weight_out, out_v),
+                (qkv_in, qkv),
+                (extra_in, extra),
+                (normed_t_in, normed_t),
+                (attended_t_in, attended_t),
+            ]
+        )
+    ]
+    groups = []
+    for group in range(width // GROUP):
+        rows = pl.ds(group * per, per)
+        groups.append(started(probs_in.at[rows, :], probs.at[rows, :], sems, len(got) + group))
     total_out[...] = (cot[...].astype(F32) + skip[...].astype(F32)).astype(BF16)
+    got[1].wait()
+    keys_t[...] = qkv[:, width : 2 * width].T
+    got[2].wait()
+    got[0].wait()
     bias_row = back_through(
-        total_out[...], probs, qkv, keys_t, weight_out, grad_proj, width // heads, land[:, :1]
+        total_out[...], probs, qkv, keys_t, out_v, grad_proj, width // heads, extra[:, :1], groups
     )
     bias_out[...] = jnp.broadcast_to(bias_row, bias_out.shape)
     half = width // 2
-    rows = aligned((1 - core[0]) * half, half)
+    got[3].wait()
+    got[4].wait()
+    rows = aligned((1 - place[0]) * half, half)
     weight_rows(rows, normed_t, attended_t, grad_proj, total_out, bias_row, give)
 
 
@@ -246,22 +314,41 @@
 
 
 def finish_kernel(
-    core, total, grad_proj, bias_row, normed_t, attended_t, normed, inverse, weight_qkv, gain,
+    place, total, grad_proj, bias_row, normed_t_in, attended_t_in, normed_in, extra_in,
+    weight_qkv, gain,
     keep, own, back,
+    normed_t, attended_t, normed, extra, qkv_v, gain_v, sems,
 ):
     count, width = total.shape
     half = width // 2
-    rows = aligned(core[0] * half, half)
+    got = [
+        started(source, target, sems, i)
+        for i, (source, target) in enumerate(
+            [
+                (normed_t_in, normed_t),
+                (attended_t_in, attended_t),
+                (weight_qkv.at[:half, :], qkv_v.at[:half, :]),
+                (weight_qkv.at[half:, :], qkv_v.at[half:, :]),
+                (normed_in, normed),
+                (extra_in, extra),
+                (gain, gain_v),
+            ]
+        )
+    ]
+    got[0].wait()
+    got[1].wait()
+    rows = aligned(place[0] * half, half)
     bias_b = bias_row[:1, :].astype(BF16).astype(F32)
     weight_rows(rows, normed_t, attended_t, grad_proj, total, bias_b, keep)
-    final = through_norm(grad_proj[...], weight_qkv, gain, normed[...], inverse[:, :1])
+    for copy in got[2:]:
+        copy.wait()
+    final = through_norm(grad_proj[...], qkv_v, gain_v, normed[...], extra[:, GROUP : GROUP + 1])
     final = final + total[...].astype(F32)
     own[...] = final[: count // 2]
     back[...] = final[count // 2 :].astype(BF16)
 
 
-def first_kernel(place, keep, came, give_p, kept_p, kept_q, *rest):
-    *give_q, total = rest
+def first_kernel(place, keep, came, give_p, kept_p, give_q, total):
     wide_p = give_p.shape[1]
     half = keep.shape[0] // 2
     total[...] = keep[...] + came[...].astype(F32)
@@ -269,74 +356,47 @@
     mine = aligned(place[1] * half, half)
     kept_p[:, :CUT] = total[mine, :CUT]
     kept_p[:, CUT:] = total[mine, CUT:wide_p].astype(BF16).astype(F32)
-    piece, count = kept_q.shape[0], len(give_q) + 1
-    kept_q[...] = total[aligned(place[2] * piece, piece), wide_p:]
-    for by, give in enumerate(give_q, 1):
-        owner = lax.rem(place[2] + by, count)
-        give[...] = total[aligned(owner * piece, piece), wide_p:].astype(BF16)
-
-
-def second_kernel(place, kept_p, came_p, kept_q, *rest):
-    count = (len(rest) - 5) // 2 + 1
-    came_q, (give_q, left_q, left_p), rest = rest[: count - 1], rest[count - 1 : count + 2], rest[count + 2 :]
-    *give_p, total_p, total_q = rest
-    total_p[...] = kept_p[...] + came_p[...].astype(F32)
-    piece = left_p.shape[0]
-    mine = aligned(place[2] * piece, piece)
-    left_p[:, :CUT] = total_p[mine, :CUT]
-    left_p[:, CUT:] = total_p[mine, CUT:].astype(BF16).astype(F32)
-    for by, give in enumerate(give_p, 1):
-        owner = lax.rem(place[2] + by, count)
-        give[...] = total_p[aligned(owner * piece, piece), :].astype(BF16)
-    total = kept_q[...]
-    for came in came_q:
-        total = total + came[...].astype(F32)
-    total_q[...] = total
+    give_q[...] = total[:, wide_p:].astype(BF16).reshape(give_q.shape)
+
+
+def added(pieces):
+    total = pieces[0].astype(F32)
+    for other in range(1, pieces.shape[0]):
+        total = total + pieces[other].astype(F32)
+    return total
+
+
+def second_kernel(place, kept_p, came_p, came_q, give_q, left_q, give_p, total_q):
+    give_p[...] = (kept_p[...] + came_p[...].astype(F32)).astype(BF16).reshape(give_p.shape)
+    total_q[...] = added(came_q)
     half = give_q.shape[0]
     give_q[...] = total_q[aligned((1 - place[1]) * half, half), :].astype(BF16)
     left_q[...] = total_q[aligned(place[1] * half, half), :]
 
 
-def third_kernel(place, left_p, left_q, came_q, *rest):
-    *came_p, piece_p, piece_q, bias = rest
-    count = len(came_p) + 1
-    total = left_p[:, :CUT]
-    for came in came_p:
-        total = total + came[:, :CUT].astype(F32)
-    piece_p[...] = total.astype(BF16)
+def third_kernel(left_q, came_q, came_p, pieces_p, piece_q, bias):
+    total = added(came_p)
+    piece = total[:, :CUT].astype(BF16)
+    for other in range(pieces_p.shape[0]):
+        pieces_p[other] = piece
     piece_q[...] = (left_q[...] + came_q[...].astype(F32)).astype(BF16)
-    terms = [left_p[:8, CUT:]] + [came[...].astype(F32)[:8, CUT:] for came in came_p]
-    total = jnp.zeros_like(terms[0])
-    for source in range(count):
-        for by, term in enumerate(terms):
-            here = lax.rem(place[2] - by + count, count) == source
-            total = total + jnp.where(here, term, 0.0)
-    bias[...] = total
-
-
-def fourth_kernel(place, piece_p, piece_q, other_q, *rest):
-    *others_p, block_p, block_q = rest
-    count = len(others_p) + 1
-    piece = piece_p.shape[0]
-    for by, part in enumerate((piece_p, *others_p)):
-        source = lax.rem(place[2] - by + count, count)
-        block_p[aligned(source * piece, piece), :] = part[...]
+    bias[...] = total[:8, CUT:]
+
+
+def fourth_kernel(place, pieces_p, piece_q, other_q, block_p, blocks_q):
+    block_p[...] = pieces_p[...].reshape(block_p.shape)
     piece = piece_q.shape[0]
-    block_q[aligned(place[1] * piece, piece), :] = piece_q[...]
-    block_q[aligned((1 - place[1]) * piece, piece), :] = other_q[...]
-
-
-def fifth_kernel(place, weight_qkv, gain, bias, block_p, other_p, block_q, *rest):
-    *others_q, half, row = rest
-    count = len(others_q) + 1
+    for other in range(blocks_q.shape[0]):
+        blocks_q[other, aligned(place[1] * piece, piece), :] = piece_q[...]
+        blocks_q[other, aligned((1 - place[1]) * piece, piece), :] = other_q[...]
+
+
+def fifth_kernel(place, weight_qkv, gain, bias, block_p, other_p, blocks_q, half, row):
     rows, width = half.shape[0], weight_qkv.shape[0]
     piece = block_p.shape[0]
     half[aligned(place[1] * piece, piece), :CUT] = block_p[...]
     half[aligned((1 - place[1]) * piece, piece), :CUT] = other_p[...]
-    piece = block_q.shape[0]
-    for by, part in enumerate((block_q, *others_q)):
-        source = lax.rem(place[2] - by + count, count)
-        half[aligned(source * piece, piece), CUT:] = part[...]
+    half[:, CUT:] = blocks_q[...].reshape(rows, half.shape[1] - CUT)
     three = weight_qkv.shape[1]
     wide = half[:, :three].astype(F32)
     mine = aligned(place[0] * rows, rows)
@@ -357,37 +417,46 @@
 def last_kernel(
     place, half, other, row, row_core, row_section, row_both, bias,
     grad_qkv, grad_out, grad_gain, grad_bias,
+    qkv_v, out_v, gain_v, bias_v, sems,
     *, entries,
 ):
     rows, three = half.shape[0], grad_qkv.shape[1]
     square = row[:1, rows : rows + 1] + row_core[:1, rows : rows + 1]
     square = square + (row_section[:1, rows : rows + 1] + row_both[:1, rows : rows + 1])
     factor = jnp.minimum(1.0, lax.rsqrt(square / entries + 1e-06))
-    step = pl.program_id(0)
-    piece = grad_qkv.shape[0]
-    per = rows // piece
-    at = aligned(lax.rem(step, per) * piece, piece)
-    own = lax.div(step, per) == place[0]
-
-    @pl.when(own)
-    def _():
-        grad_qkv[...] = half[at, :three].astype(F32) * factor
-        grad_out[...] = half[at, three:].astype(F32) * factor
-
-    @pl.when(jnp.logical_not(own))
-    def _():
-        grad_qkv[...] = other[at, :three].astype(F32) * factor
-        grad_out[...] = other[at, three:].astype(F32) * factor
-
+    sent = []
+    piece = 64
+    for which, ref in enumerate((half, other)):
+        base = place[0] * rows if which == 0 else (1 - place[0]) * rows
+        for part in range(rows // piece):
+            here = slice(part * piece, (part + 1) * piece)
+            at = aligned(base + part * piece, piece)
+            slot = slice(which * rows + part * piece, which * rows + (part + 1) * piece)
+            qkv_v[slot, :] = ref[here, :three].astype(F32) * factor
+            sent.append(started(qkv_v.at[slot, :], grad_qkv.at[at, :], sems, len(sent)))
+            out_v[slot, :] = ref[here, three:].astype(F32) * factor
+            sent.append(started(out_v.at[slot, :], grad_out.at[at, :], sems, len(sent)))
     core = place[0].astype(F32)
     mine, its = row[:1, :rows] * factor, row_core[:1, :rows] * factor
-    grad_gain[:, :rows] = mine * (1.0 - core) + its * core
-    grad_gain[:, rows:] = mine * core + its * (1.0 - core)
-    grad_bias[...] = bias[:1, : grad_bias.shape[1]] * factor
-
-
-def pieces_sent(pieces, axis):
-    return [from_behind(piece, axis, by) for by, piece in enumerate(pieces, 1)]
+    gain_v[:, :rows] = mine * (1.0 - core) + its * core
+    gain_v[:, rows:] = mine * core + its * (1.0 - core)
+    bias_v[...] = bias[:1, : bias_v.shape[1]] * factor
+    sent.append(started(gain_v, grad_gain, sems, len(sent)))
+    sent.append(started(bias_v, grad_bias, sems, len(sent)))
+    for copy in sent:
+        copy.wait()
+
+
+def exchanged(pieces, axis):
+    return lax.all_to_all(pieces, axis, 0, 0, tiled=True)
+
+
+def vmem(dims, dtype):
+    return pltpu.VMEM(dims, dtype)
+
+
+def copies(number):
+    return pltpu.SemaphoreType.DMA((number,))
 
 
 def body(inputs, cotangent, land_sea, gains, qkv_weight, out_weight, land_bias):
@@ -404,28 +473,49 @@
     own, rim = call(
         pack_kernel,
         [shape((2 * half, width), BF16), shape((packed, width), BF16)],
-        scratch=[pltpu.VMEM((2 * half, width), F32), pltpu.VMEM((packed, width), F32)],
+        scratch=[
+            vmem(inputs.shape, BF16),
+            vmem(inputs.shape, BF16),
+            vmem(land_sea.shape, jnp.int32),
+            vmem((2 * half, width), F32),
+            vmem((packed, width), F32),
+            copies(3),
+        ],
+        places="aaa",
         operands=(inputs, cotangent, land_sea),
     )
     rim = from_behind(rim, "lon", -1)
-    skip, cot, normed, inverse, normed_t, qkv, keys_t, probs, attended_t, land = call(
+    groups = width // GROUP
+    state = [
+        shape((count, width), F32),
+        shape((width, count), BF16),
+        shape((count, 3 * width), BF16),
+        shape((heads * count, count), F32),
+        shape((width, count), BF16),
+        shape((count, 2 * GROUP), F32),
+    ]
+    skip, cot, normed, normed_t, qkv, probs, attended_t, extra = call(
         forward_kernel,
-        [
-            shape((count, width), BF16),
-            shape((count, width), BF16),
-            shape((count, width), F32),
-            shape((count, GROUP), F32),
-            shape((width, count), BF16),
-            shape((count, 3 * width), BF16),
-            shape((width, count), BF16),
-            shape((heads * count, count), F32),
-            shape((width, count), BF16),
-            shape((count, GROUP), F32),
-        ],
-        scratch=[pltpu.VMEM((count, 3 * width), BF16), pltpu.VMEM((width, count), BF16)],
-        smem=(0,),
+        [shape((count, width), BF16), shape((count, width), BF16), *state],
+        scratch=[
+            vmem(land_bias.shape, F32),
+            vmem(land_sea.shape, jnp.int32),
+            vmem(gains.shape, F32),
+            vmem(weight_qkv.shape, BF16),
+            vmem(weight_out.shape, BF16),
+            *(vmem(kept.shape, kept.dtype) for kept in state),
+            vmem((width, count), BF16),
+            vmem((width, count), BF16),
+            vmem((width, count), BF16),
+            vmem((count, 3 * width), BF16),
+            copies(7),
+            copies(5 + groups),
+        ],
+        places="avvaaaa",
+        out_places="vvaaaaaa",
         operands=(land_bias, own, rim, land_sea, gains, weight_qkv, weight_out),
         flops=10**9,
+        limit=20,
     )
     skip = passed_along(skip, "section", -1)
     rows, wide = width // 2, 4 * width + GROUP
@@ -437,9 +527,20 @@
             shape((8, GROUP), F32),
             shape((rows, wide), BF16),
         ],
-        smem=(0,),
-        operands=(place, skip, cot, qkv, keys_t, probs, land, weight_out, normed_t, attended_t),
+        scratch=[
+            vmem(qkv.shape, BF16),
+            vmem(probs.shape, F32),
+            vmem(weight_out.shape, BF16),
+            vmem(extra.shape, F32),
+            vmem(normed_t.shape, BF16),
+            vmem(attended_t.shape, BF16),
+            vmem((width, count), BF16),
+            copies(5 + groups),
+        ],
+        places="svvaaaaaa",
+        operands=(place, skip, cot, qkv, probs, weight_out, extra, normed_t, attended_t),
         flops=10**9,
+        limit=20,
     )
     came = swapped(give, "lat", 1)
     keep, own_grad, back = call(
@@ -449,9 +550,18 @@
             shape((half, width), F32),
             shape((half, width), BF16),
         ],
-        smem=(0,),
+        scratch=[
+            vmem(normed_t.shape, BF16),
+            vmem(attended_t.shape, BF16),
+            vmem(normed.shape, F32),
+            vmem(extra.shape, F32),
+            vmem(weight_qkv.shape, BF16),
+            vmem(gains.shape, F32),
+            copies(7),
+        ],
+        places="svvvaaaaaa",
         operands=(
-            place, total, grad_proj, bias_row, normed_t, attended_t, normed, inverse,
+            place, total, grad_proj, bias_row, normed_t, attended_t, normed, extra,
             weight_qkv, gains,
         ),
         flops=5 * 10**8,
@@ -464,7 +574,11 @@
         grads, mark = plain(keep, came, weight_qkv, gains, heads, entries)
     own_grad, back, _ = lax.optimization_barrier((own_grad, back, mark))
     (final_grad,) = call(
-        unpack_kernel, [shape(inputs.shape, F32)], operands=(own_grad, back)
+        unpack_kernel,
+        [shape(inputs.shape, F32)],
+        scratch=[vmem(inputs.shape, F32), copies(1)],
+        out_places="a",
+        operands=(own_grad, back),
     )
     return (final_grad, *(grad[None] for grad in grads))
 
@@ -474,87 +588,82 @@
     width = 2 * rows
     wide_p = CUT + GROUP
     wide_q = wide - wide_p
-    some = range(lons - 1)
-    give_p, kept_p, kept_q, *give_q = call(
+    give_p, kept_p, give_q = call(
         first_kernel,
         [
             shape((rows // 2, wide_p), BF16),
             shape((rows // 2, wide_p), F32),
-            shape((rows // lons, wide_q), F32),
-            *(shape((rows // lons, wide_q), BF16) for _ in some),
-        ],
-        scratch=[pltpu.VMEM((rows, wide), F32)],
-        smem=(0,),
+            shape((lons, rows // lons, wide_q), BF16),
+        ],
+        scratch=[vmem((rows, wide), F32)],
+        places="svv",
         operands=(place, keep, came),
     )
     came_p = swapped(give_p, "lat", 2)
-    came_q = pieces_sent(give_q, "lon")
+    came_q = exchanged(give_q, "lon")
     piece = rows // 2 // lons
-    give_q, left_q, left_p, *give_p = call(
+    give_q, left_q, give_p = call(
         second_kernel,
         [
             shape((piece, wide_q), BF16),
             shape((piece, wide_q), F32),
-            shape((piece, wide_p), F32),
-            *(shape((piece, wide_p), BF16) for _ in some),
-        ],
-        scratch=[pltpu.VMEM((rows // 2, wide_p), F32), pltpu.VMEM((rows // lons, wide_q), F32)],
-        smem=(0,),
-        operands=(place, kept_p, came_p, kept_q, *came_q),
-    )
-    came_p = pieces_sent(give_p, "lon")
+            shape((lons, piece, wide_p), BF16),
+        ],
+        scratch=[vmem((rows // lons, wide_q), F32)],
+        places="svvv",
+        operands=(place, kept_p, came_p, came_q),
+    )
     came_q = swapped(give_q, "lat", 2)
-    piece_p, piece_q, bias = call(
+    came_p = exchanged(give_p, "lon")
+    pieces_p, piece_q, bias = call(
         third_kernel,
         [
-            shape((piece, CUT), BF16),
+            shape((lons, piece, CUT), BF16),
             shape((piece, wide_q), BF16),
             shape((8, GROUP), F32),
         ],
-        smem=(0,),
-        operands=(place, left_p, left_q, came_q, *came_p),
-    )
-    others_p = pieces_sent([piece_p for _ in some], "lon")
+        operands=(left_q, came_q, came_p),
+    )
     other_q = swapped(piece_q, "lat", 2)
-    block_p, block_q = call(
+    pieces_p = exchanged(pieces_p, "lon")
+    block_p, blocks_q = call(
         fourth_kernel,
-        [shape((rows // 2, CUT), BF16), shape((rows // lons, wide_q), BF16)],
-        smem=(0,),
-        operands=(place, piece_p, piece_q, other_q, *others_p),
+        [shape((rows // 2, CUT), BF16), shape((lons, rows // lons, wide_q), BF16)],
+        places="svvv",
+        operands=(place, pieces_p, piece_q, other_q),
     )
     other_p = swapped(block_p, "lat", 2)
-    others_q = pieces_sent([block_q for _ in some], "lon")
+    blocks_q = exchanged(blocks_q, "lon")
     half, row = call(
         fifth_kernel,
         [shape((rows, 4 * width), BF16), shape((8, rows + GROUP), F32)],
-        smem=(0,),
-        operands=(place, weight_qkv, gains, bias, block_p, other_p, block_q, *others_q),
+        places="svvvvvv",
+        operands=(place, weight_qkv, gains, bias, block_p, other_p, blocks_q),
     )
     row_section = swapped(row, "section", 1)
     row_both = lax.ppermute(row, ("section", "lat"), across())
     row_core = swapped(row, "lat", 1)
     other = swapped(half, "lat", 1)
-    steps = 8
-    vmem = pl.BlockSpec(memory_space=pltpu.VMEM)
-    grads = pl.pallas_call(
+    grads = call(
         functools.partial(last_kernel, entries=entries),
-        grid=(steps,),
-        out_shape=[
+        [
             shape((width, 3 * width), F32),
             shape((width, width), F32),
             shape((1, width), F32),
             shape((1, heads), F32),
         ],
-        in_specs=[pl.BlockSpec(memory_space=pltpu.SMEM)] + [vmem] * 7,
-        out_specs=[
-            pl.BlockSpec((width // steps, 3 * width), lambda i: (i, 0)),
-            pl.BlockSpec((width // steps, width), lambda i: (i, 0)),
-            pl.BlockSpec((1, width), lambda i: (0, 0)),
-            pl.BlockSpec((1, heads), lambda i: (0, 0)),
-        ],
-        compiler_params=pltpu.CompilerParams(vmem_limit_bytes=12 * 2**20),
-    )(place, half, other, row, row_core, row_section, row_both, bias)
-    return (grads[0], grads[1], grads[2][0], grads[3][0]), bias
+        scratch=[
+            vmem((width, 3 * width), F32),
+            vmem((width, width), F32),
+            vmem((1, width), F32),
+            vmem((1, heads), F32),
+            copies(4 * rows // 64 + 2),
+        ],
+        places="svvvvvvv",
+        out_places="aaaa",
+        operands=(place, half, other, row, row_core, row_section, row_both, bias),
+    )
+    return (grads[0], grads[1], grads[2][0], grads[3][0]), left_q
 
 
 def across():

time: 103 us -> 121 us (1.17)
  waiting for transfers between devices: 35.7 us -> 48.4 us
  Pallas kernels: 20.3 us -> 26.5 us
    ppermute x14 -> x2, starting transfers between devices: 25.3 us -> 5.16 us  [from_behind(): lax.ppermute(value, axis, [(i, (i + by) % count) for i in range(count)])]
    all_to_all x0 -> x4, starting transfers between devices: none -> 15.9 us  [exchanged(): return lax.all_to_all(pieces, axis, 0, 0, tiled=True)]
    all_to_all x0 -> x4, waiting for transfers between devices: none -> 14.6 us  [exchanged(): return lax.all_to_all(pieces, axis, 0, 0, tiled=True)]
    ppermute x14 -> x2, waiting for transfers between devices: 21.4 us -> 7.79 us  [from_behind(): lax.ppermute(value, axis, [(i, (i + by) % count) for i in range(count)])]
    ppermute x8, waiting for transfers between devices: 8.33 us -> 20.1 us  [swapped(): return lax.ppermute(value, axis, [(i, i ^ bit) for i in range(count)])]
    pallas_call x10 -> x11, Pallas kernels: 15.8 us -> 26.5 us  [call(): pl.pallas_call(kernel, out_shape=list(outs), in_specs=[pl.BlockSpec(memor...]
    ppermute x8, starting transfers between devices: 3.45 us -> 8.37 us  [swapped(): return lax.ppermute(value, axis, [(i, i ^ bit) for i in range(count)])]
    pallas_call x1 -> x0, Pallas kernels: 4.46 us -> none  [staged(): pl.pallas_call(functools.partial(last_kernel, entries=entries), grid=(ste...]
  transfers between devices with their start and end apart: 24 -> 16, of which waited for: 12 -> 12; matrix products, arithmetic and copies ran while one was open for 1% -> 1% of each run, Pallas kernels for 2% -> 2%
where the time goes in v4:
time: 121 us; the launch traced here: 120 us
  waiting for transfers between devices  48.4 us (40%)
  starting transfers between devices  30.9 us (26%)
  Pallas kernels  26.5 us (22%)
  local copies, waits for them, and re-layouts  13.4 us (11%)
    pallas_call x11, Pallas kernels, call(): pl.pallas_call(kernel, out_shape=list(outs), in_specs=[pl.BlockSpec(memor...  26.5 us
    ppermute x8, waiting for transfers between devices, swapped(): return lax.ppermute(value, axis, [(i, i ^ bit) for i in range(count)])  20.1 us
    all_to_all x4, starting transfers between devices, exchanged(): return lax.all_to_all(pieces, axis, 0, 0, tiled=True)  15.9 us
    all_to_all x4, waiting for transfers between devices, exchanged(): return lax.all_to_all(pieces, axis, 0, 0, tiled=True)  14.6 us
    unnamed x31, local copies, waits for them, and re-layouts  13.4 us
    ppermute x8, starting transfers between devices, swapped(): return lax.ppermute(value, axis, [(i, i ^ bit) for i in range(count)])  8.37 us
    ppermute x2, waiting for transfers between devices, from_behind(): lax.ppermute(value, axis, [(i, (i + by) % count) for i in range(count)])  7.79 us
    ppermute x1, waiting for transfers between devices, passed_along(): return lax.ppermute(block, axis, route)  5.96 us
  transfers between devices with their start and end apart: 16, of which 12 were waited for; matrix products, arithmetic and copies ran while one was open for 1% of the time, Pallas kernels for 2%

profile of v4, /device:TPU:0, one launch (start us, length us, event | category | flops | bytes accessed | tf_op | source)
XLA Modules:
  0.0 120.2 jit_solution(5015450631416284402)
XLA Ops:
  0.6 0.9 copy.12.tokens
  1.6 0.0 copy-start.5
  1.6 1.0 copy.13.cot
  2.6 0.0 copy-start.10
  2.6 0.7 copy-done.10
  3.3 0.6 shard_map.110
  3.9 5.1 %collective-permute-start = (bf16[160,512]{1,0:T(8,128)(2,1)S(1)}, bf16[160,512]{1,0:T(8,128)(2,1)S(1)}, u32[]{:S(2)}, u32[]{:S(2)}) collective-permute-start(bf16[160,512]{1,0:T(8,128)(2,1)S(1)} %get-tuple-element.42), channel_id=1, source_target_pairs={{0,12},{4,0},{8,4},{12,8},{1,13},{5,1},{9,5},{13,9},{2,14},{6,2},{... | collective-permute-start | bytes 491528 | tf_op jit(solution)/shard_map/ppermute | solution.py:20
  9.0 3.5 %collective-permute-done.rim = bf16[160,512]{1,0:T(8,128)(2,1)S(1)} collective-permute-done((bf16[160,512]{1,0:T(8,128)(2,1)S(1)}, bf16[160,512]{1,0:T(8,128)(2,1)S(1)}, u32[]{:S(2)}, u32[]{:S(2)}) %collective-permute-start) | collective-permute-done | bytes 163872 | tf_op jit(solution)/shard_map/ppermute | solution.py:20
  12.5 1.4 %copy-done = bf16[1,512,1536]{2,1,0:T(8,128)(2,1)S(1)} copy-done((bf16[1,512,1536]{2,1,0:T(8,128)(2,1)S(1)}, bf16[1,512,1536]{2,1,0:T(8,128)(2,1)}, u32[]{:S(2)}) %copy-start) | copy-done | bytes 1572888
  13.9 1.0 copy-done.4
  14.9 0.7 copy-done.8
  15.6 0.7 copy-done.11
  16.3 0.7 copy-done.13
  16.9 8.7 %shard_map.111 = (bf16[144,512]{1,0:T(8,128)(2,1)}, bf16[144,512]{1,0:T(8,128)(2,1)S(1)}, f32[144,512]{1,0:T(8,128)S(1)}, bf16[512,144]{1,0:T(8,128)(2,1)S(1)}, ...) custom-call(f32[1,16]{1,0:T(1,128)S(1)} %copy-done.13, ...), custom_call_target="tpu_custom_call" | custom-call | flops 1000000000 | bytes 5212512 | tf_op jit(solution)/shard_map/pallas_call | solution.py:47
  25.6 0.0 copy-start.2
  25.6 1.4 %copy-done.2 = f32[2304,144]{1,0:T(8,128)} copy-done((f32[2304,144]{1,0:T(8,128)}, f32[2304,144]{1,0:T(8,128)S(1)}, u32[]{:S(2)}) %copy-start.2) | copy-done | bytes 1327128
  27.0 0.7 copy-done.6
  27.7 1.4 %collective-permute-start.1 = (bf16[144,512]{1,0:T(8,128)(2,1)}, bf16[144,512]{1,0:T(8,128)(2,1)}, u32[]{:S(2)}, u32[]{:S(2)}) collective-permute-start(bf16[144,512]{1,0:T(8,128)(2,1)} %get-tuple-element.43), channel_id=1, source_target_pairs={{16,0},{17,1},{18,2},{19,3},{20,4},{21,5},{22,6},{23,7},{24,8},{25... | collective-permute-start | bytes 442376 | tf_op jit(solution)/shard_map/ppermute | solution.py:26
  29.1 0.1 pad_add_fusion.place
  29.2 6.0 %collective-permute-done.1.skip = bf16[144,512]{1,0:T(8,128)(2,1)} collective-permute-done((bf16[144,512]{1,0:T(8,128)(2,1)}, bf16[144,512]{1,0:T(8,128)(2,1)}, u32[]{:S(2)}, u32[]{:S(2)}) %collective-permute-start.1) | collective-permute-done | bytes 147488 | tf_op jit(solution)/shard_map/ppermute | solution.py:26
  35.2 0.0 copy-done.5
  35.2 1.7 %copy-done.3 = f32[2304,144]{1,0:T(8,128)S(1)} copy-done((f32[2304,144]{1,0:T(8,128)S(1)}, f32[2304,144]{1,0:T(8,128)}, u32[]{:S(2)}) %copy-start.3) | copy-done | bytes 1327128
  36.9 0.9 copy-done.7
  37.8 5.8 %shard_map.112 = (bf16[144,512]{1,0:T(8,128)(2,1)S(1)}, bf16[144,1536]{1,0:T(8,128)(2,1)S(1)}, f32[8,128]{1,0:T(8,128)S(1)}, bf16[256,2176]{1,0:T(8,128)(2,1)S(1)}) custom-call(s32[3]{0:T(128)S(1)} %pad_add_fusion.place, bf16[144,512]{1,0:T(8,128)(2,1)} %collective-permute-done.1.skip, bf16[144,512]{1,0:T(8,128)(2,1)S(1)} %copy-done.7, ...), custom_call_target="tpu_custom_call" | custom-call | flops 1000000000 | bytes 4739084 | tf_op jit(solution)/shard_map/pallas_call | solution.py:47
  43.5 0.1 collective-permute-start.3
  43.6 0.0 copy-done.9
  43.6 0.0 copy-done.1
  43.6 2.2 %shard_map.113 = (f32[256,2176]{1,0:T(8,128)S(1)}, f32[72,512]{1,0:T(8,128)S(1)}, bf16[72,512]{1,0:T(8,128)(2,1)S(1)}) custom-call(s32[3]{0:T(128)S(1)} %pad_add_fusion.place, bf16[144,512]{1,0:T(8,128)(2,1)S(1)} %get-tuple-element.50.total, bf16[144,1536]{1,0:T(8,128)(2,1)S(1)} %get-tuple-element.51.grad_proj, f32[8,128]{1,0:T(8,128)S(1)} %get-tuple-element.52.bias_row, ...), custom_call_target="tpu_custom_call" | custom-call | flops 500000000 | bytes 5355532 | tf_op jit(solution)/shard_map/pallas_call | solution.py:47
  45.8 0.5 collective-permute-done.3.came
  46.3 1.7 %shard_map.114 = (bf16[128,1408]{1,0:T(8,128)(2,1)S(1)}, f32[128,1408]{1,0:T(8,128)S(1)}, bf16[4,64,768]{2,1,0:T(8,128)(2,1)}) custom-call(s32[3]{0:T(128)S(1)} %pad_add_fusion.place, f32[256,2176]{1,0:T(8,128)S(1)} %get-tuple-element.56.keep, bf16[256,2176]{1,0:T(8,128)(2,1)S(1)} %collective-permute-done.3.came), custom_call_target="tpu_custom_call" | custom-call | flops 100000000 | bytes 4816908 | tf_op jit(solution)/shard_map/pallas_call | solution.py:47
  48.0 0.7 copy-done.12
  48.7 5.5 %all-to-all-start = ((bf16[4,64,768]{2,1,0:T(8,128)(2,1)}), bf16[4,64,768]{2,1,0:T(8,128)(2,1)S(1)}, u32[]{:S(2)}, u32[]{:S(2)}) async-start(bf16[4,64,768]{2,1,0:T(8,128)(2,1)} %get-tuple-element.60), calls=%async_computation | async-start | bytes 786432 | tf_op jit(solution)/shard_map/all_to_all | solution.py:451
  54.3 1.5 %collective-permute-start.4 = (bf16[128,1408]{1,0:T(8,128)(2,1)}, bf16[128,1408]{1,0:T(8,128)(2,1)S(1)}, u32[]{:S(2)}, u32[]{:S(2)}) collective-permute-start(bf16[128,1408]{1,0:T(8,128)(2,1)} %copy-done.12), channel_id=1, source_target_pairs={{0,2},{1,3},{2,0},{3,1},{4,6},{5,7},{6,4},{7,5},{8,10},{9,11},{10,... | collective-permute-start | bytes 1081352 | tf_op jit(solution)/shard_map/ppermute | solution.py:31
  55.8 8.9 %collective-permute-done.4.came_p = bf16[128,1408]{1,0:T(8,128)(2,1)S(1)} collective-permute-done((bf16[128,1408]{1,0:T(8,128)(2,1)}, bf16[128,1408]{1,0:T(8,128)(2,1)S(1)}, u32[]{:S(2)}, u32[]{:S(2)}) %collective-permute-start.4) | collective-permute-done | bytes 360480 | tf_op jit(solution)/shard_map/ppermute | solution.py:31
  64.7 1.6 %all-to-all-done.came_q = bf16[4,64,768]{2,1,0:T(8,128)(2,1)S(1)} async-done(((bf16[4,64,768]{2,1,0:T(8,128)(2,1)}), bf16[4,64,768]{2,1,0:T(8,128)(2,1)S(1)}, u32[]{:S(2)}, u32[]{:S(2)}) %all-to-all-start) | async-done | bytes 393248 | tf_op jit(solution)/shard_map/all_to_all | solution.py:451
  66.3 1.4 %shard_map.115 = (bf16[32,768]{1,0:T(8,128)(2,1)S(1)}, f32[32,768]{1,0:T(8,128)S(1)}, bf16[4,32,1408]{2,1,0:T(8,128)(2,1)}) custom-call(s32[3]{0:T(128)S(1)} %pad_add_fusion.place, f32[128,1408]{1,0:T(8,128)S(1)} %get-tuple-element.58.kept_p, bf16[128,1408]{1,0:T(8,128)(2,1)S(1)} %collective-permute-done.4.came_p, bf16[4,64,768]{2,1,0:T(8,128)(2,1)S(1)} %all-to-all-done.came_q), custom_call_target="tpu_custom_call" | custom-call | flops 100000000 | bytes 1982476 | tf_op jit(solution)/shard_map/pallas_call | solution.py:47
  67.7 3.5 %all-to-all-start.1 = ((bf16[4,32,1408]{2,1,0:T(8,128)(2,1)}), bf16[4,32,1408]{2,1,0:T(8,128)(2,1)S(1)}, u32[]{:S(2)}, u32[]{:S(2)}) async-start(bf16[4,32,1408]{2,1,0:T(8,128)(2,1)} %get-tuple-element.65), calls=%async_computation.1 | async-start | bytes 720896 | tf_op jit(solution)/shard_map/all_to_all | solution.py:451
  71.1 1.6 %collective-permute-start.5 = (bf16[32,768]{1,0:T(8,128)(2,1)S(1)}, bf16[32,768]{1,0:T(8,128)(2,1)S(1)}, u32[]{:S(2)}, u32[]{:S(2)}) collective-permute-start(bf16[32,768]{1,0:T(8,128)(2,1)S(1)} %get-tuple-element.64), channel_id=1, source_target_pairs={{0,2},{1,3},{2,0},{3,1},{4,6},{5,7},{6,4},{7,5},{8,10},{9,11},{10,... | collective-permute-start | bytes 147464 | tf_op jit(solution)/shard_map/ppermute | solution.py:31
  72.7 2.6 %collective-permute-done.5.came_q = bf16[32,768]{1,0:T(8,128)(2,1)S(1)} collective-permute-done((bf16[32,768]{1,0:T(8,128)(2,1)S(1)}, bf16[32,768]{1,0:T(8,128)(2,1)S(1)}, u32[]{:S(2)}, u32[]{:S(2)}) %collective-permute-start.5) | collective-permute-done | bytes 49184 | tf_op jit(solution)/shard_map/ppermute | solution.py:31
  75.3 6.4 %all-to-all-done.1.came_p = bf16[4,32,1408]{2,1,0:T(8,128)(2,1)S(1)} async-done(((bf16[4,32,1408]{2,1,0:T(8,128)(2,1)}), bf16[4,32,1408]{2,1,0:T(8,128)(2,1)S(1)}, u32[]{:S(2)}, u32[]{:S(2)}) %all-to-all-start.1) | async-done | bytes 360480 | tf_op jit(solution)/shard_map/all_to_all | solution.py:451
  81.7 0.8 shard_map.117
  82.5 3.5 %all-to-all-start.2 = ((bf16[4,32,1280]{2,1,0:T(8,128)(2,1)}), bf16[4,32,1280]{2,1,0:T(8,128)(2,1)S(1)}, u32[]{:S(2)}, u32[]{:S(2)}) async-start(bf16[4,32,1280]{2,1,0:T(8,128)(2,1)} %get-tuple-element.67), calls=%async_computation.2 | async-start | bytes 655360 | tf_op jit(solution)/shard_map/all_to_all | solution.py:451
  85.9 1.6 %collective-permute-start.6 = (bf16[32,768]{1,0:T(8,128)(2,1)S(1)}, bf16[32,768]{1,0:T(8,128)(2,1)S(1)}, u32[]{:S(2)}, u32[]{:S(2)}) collective-permute-start(bf16[32,768]{1,0:T(8,128)(2,1)S(1)} %get-tuple-element.68.piece_q), channel_id=1, source_target_pairs={{0,2},{1,3},{2,0},{3,1},{4,6},{5,7},{6,4},{7,5},{8,10},{9,11},{10,... | collective-permute-start | bytes 147464 | tf_op jit(solution)/shard_map/ppermute | solution.py:31
  87.5 2.6 %collective-permute-done.6.other_q = bf16[32,768]{1,0:T(8,128)(2,1)S(1)} collective-permute-done((bf16[32,768]{1,0:T(8,128)(2,1)S(1)}, bf16[32,768]{1,0:T(8,128)(2,1)S(1)}, u32[]{:S(2)}, u32[]{:S(2)}) %collective-permute-start.6) | collective-permute-done | bytes 49184 | tf_op jit(solution)/shard_map/ppermute | solution.py:31
  90.1 4.3 %all-to-all-done.2.pieces_p = bf16[4,32,1280]{2,1,0:T(8,128)(2,1)S(1)} async-done(((bf16[4,32,1280]{2,1,0:T(8,128)(2,1)}), bf16[4,32,1280]{2,1,0:T(8,128)(2,1)S(1)}, u32[]{:S(2)}, u32[]{:S(2)}) %all-to-all-start.2) | async-done | bytes 327712 | tf_op jit(solution)/shard_map/all_to_all | solution.py:451
  94.4 1.3 %shard_map.118 = (bf16[128,1280]{1,0:T(8,128)(2,1)S(1)}, bf16[4,64,768]{2,1,0:T(8,128)(2,1)}) custom-call(s32[3]{0:T(128)S(1)} %pad_add_fusion.place, bf16[4,32,1280]{2,1,0:T(8,128)(2,1)S(1)} %all-to-all-done.2.pieces_p, bf16[32,768]{1,0:T(8,128)(2,1)S(1)} %get-tuple-element.68.piece_q, bf16[32,768]{1,0:T(8,128)(2,1)S(1)} %collective-permute-done.6.other_q), custom_call_target="tpu_custom_call" | custom-call | flops 100000000 | bytes 1146892 | tf_op jit(solution)/shard_map/pallas_call | solution.py:47
  95.8 3.5 %all-to-all-start.3 = ((bf16[4,64,768]{2,1,0:T(8,128)(2,1)}), bf16[4,64,768]{2,1,0:T(8,128)(2,1)S(1)}, u32[]{:S(2)}, u32[]{:S(2)}) async-start(bf16[4,64,768]{2,1,0:T(8,128)(2,1)} %get-tuple-element.70), calls=%async_computation.3 | async-start | bytes 786432 | tf_op jit(solution)/shard_map/all_to_all | solution.py:451
  99.2 1.6 %collective-permute-start.7 = (bf16[128,1280]{1,0:T(8,128)(2,1)S(1)}, bf16[128,1280]{1,0:T(8,128)(2,1)S(1)}, u32[]{:S(2)}, u32[]{:S(2)}) collective-permute-start(bf16[128,1280]{1,0:T(8,128)(2,1)S(1)} %get-tuple-element.69.block_p), channel_id=1, source_target_pairs={{0,2},{1,3},{2,0},{3,1},{4,6},{5,7},{6,4},{7,5},{8,10},{9,11},{10,... | collective-permute-start | bytes 983048 | tf_op jit(solution)/shard_map/ppermute | solution.py:31
  100.8 5.6 %collective-permute-done.7.other_p = bf16[128,1280]{1,0:T(8,128)(2,1)S(1)} collective-permute-done((bf16[128,1280]{1,0:T(8,128)(2,1)S(1)}, bf16[128,1280]{1,0:T(8,128)(2,1)S(1)}, u32[]{:S(2)}, u32[]{:S(2)}) %collective-permute-start.7) | collective-permute-done | bytes 327712 | tf_op jit(solution)/shard_map/ppermute | solution.py:31
  106.4 2.3 %all-to-all-done.3.blocks_q = bf16[4,64,768]{2,1,0:T(8,128)(2,1)S(1)} async-done(((bf16[4,64,768]{2,1,0:T(8,128)(2,1)}), bf16[4,64,768]{2,1,0:T(8,128)(2,1)S(1)}, u32[]{:S(2)}, u32[]{:S(2)}) %all-to-all-start.3) | async-done | bytes 393248 | tf_op jit(solution)/shard_map/all_to_all | solution.py:451
  108.6 1.0 shard_map.119
  109.6 0.0 collective-permute-start.8
  109.6 0.1 collective-permute-start.2
  109.7 0.1 collective-permute-start.11
  109.8 2.0 %collective-permute-start.10 = (f32[8,384]{1,0:T(8,128)S(1)}, f32[8,384]{1,0:T(8,128)S(1)}, u32[]{:S(2)}, u32[]{:S(2)}) collective-permute-start(f32[8,384]{1,0:T(8,128)S(1)} %get-tuple-element.72.row), channel_id=1, source_target_pairs={{0,16},{16,0},{1,17},{17,1},{2,18},{18,2},{3,19},{19,3},{4,20},{20... | collective-permute-start | bytes 36872 | tf_op jit(solution)/shard_map/ppermute | solution.py:31
  111.8 0.0 collective-permute-start.9
  111.8 4.3 %collective-permute-done.2.back = bf16[72,512]{1,0:T(8,128)(2,1)S(1)} collective-permute-done((bf16[72,512]{1,0:T(8,128)(2,1)S(1)}, bf16[72,512]{1,0:T(8,128)(2,1)S(1)}, u32[]{:S(2)}, u32[]{:S(2)}) %collective-permute-start.2) | collective-permute-done | bytes 73760 | tf_op jit(solution)/shard_map/ppermute | solution.py:20
  116.1 0.2 shard_map.116
  116.4 0.9 copy.14
  117.3 0.0 collective-permute-done.11.row_both
  117.3 0.0 collective-permute-done.10.row_section
  117.3 0.0 collective-permute-done.9.row_core
  117.3 0.0 collective-permute-done.8.other
  117.4 2.8 %shard_map.120 = (f32[512,1536]{1,0:T(8,128)}, f32[512,512]{1,0:T(8,128)}, f32[1,512]{1,0:T(1,128)}, f32[1,16]{1,0:T(1,128)}) custom-call(s32[3]{0:T(128)S(1)} %pad_add_fusion.place, bf16[256,2048]{1,0:T(8,128)(2,1)S(1)} %get-tuple-element.71.half, bf16[256,2048]{1,0:T(8,128)(2,1)S(1)} %collective-permute-done.8.other, f32[8,384]{1,0:T(8,128)S(1)} %get-tuple-element.72.row, ...), custom_call_target="tpu_custom_call" | custom-call | flops 100000000 | bytes 6346828 | tf_op jit(solution)/shard_map/pallas_call | solution.py:47
  (11 shorter events, 0.0 us)
Async XLA Ops:
  1.6 33.6 %copy-start.5 = (bf16[1,512,512]{2,1,0:T(8,128)(2,1)S(1)}, bf16[1,512,512]{2,1,0:T(8,128)(2,1)}, u32[]{:S(2)}) copy-start(bf16[1,512,512]{2,1,0:T(8,128)(2,1)} %param.12) | copy-start | bytes 1572868
  2.6 0.7 copy-start.10
  3.9 8.6 %collective-permute-start = (bf16[160,512]{1,0:T(8,128)(2,1)S(1)}, bf16[160,512]{1,0:T(8,128)(2,1)S(1)}, u32[]{:S(2)}, u32[]{:S(2)}) collective-permute-start(bf16[160,512]{1,0:T(8,128)(2,1)S(1)} %get-tuple-element.42), channel_id=1, source_target_pairs={{0,12},{4,0},{8,4},{12,8},{1,13},{5,1},{9,5},{13,9},{2,14},{6,2},{... | collective-permute-start | bytes 491528 | tf_op jit(solution)/shard_map/ppermute | solution.py:20
  12.5 1.4 %copy-start = (bf16[1,512,1536]{2,1,0:T(8,128)(2,1)S(1)}, bf16[1,512,1536]{2,1,0:T(8,128)(2,1)}, u32[]{:S(2)}) copy-start(bf16[1,512,1536]{2,1,0:T(8,128)(2,1)} %param.11) | copy-start | bytes 4718596
  13.9 1.0 copy-start.4
  14.9 0.7 copy-start.8
  15.6 0.7 copy-start.11
  16.3 0.7 copy-start.13
  16.9 26.7 %copy-start.9 = (f32[1,512]{1,0:T(1,128)S(1)}, f32[1,512]{1,0:T(1,128)}, u32[]{:S(2)}) copy-start(f32[1,512]{1,0:T(1,128)} %gain.5) | copy-start | bytes 6148
  25.6 1.4 %copy-start.2 = (f32[2304,144]{1,0:T(8,128)}, f32[2304,144]{1,0:T(8,128)S(1)}, u32[]{:S(2)}) copy-start(f32[2304,144]{1,0:T(8,128)S(1)} %get-tuple-element.46.probs_in) | copy-start | bytes 3981316
  27.0 0.7 copy-start.6
  27.7 15.9 %copy-start.1 = (bf16[1,512,1536]{2,1,0:T(8,128)(2,1)S(1)}, bf16[1,512,1536]{2,1,0:T(8,128)(2,1)}, u32[]{:S(2)}) copy-start(bf16[1,512,1536]{2,1,0:T(8,128)(2,1)} %param.11) | copy-start | bytes 4718596
  27.7 7.5 %collective-permute-start.1 = (bf16[144,512]{1,0:T(8,128)(2,1)}, bf16[144,512]{1,0:T(8,128)(2,1)}, u32[]{:S(2)}, u32[]{:S(2)}) collective-permute-start(bf16[144,512]{1,0:T(8,128)(2,1)} %get-tuple-element.43), channel_id=1, source_target_pairs={{16,0},{17,1},{18,2},{19,3},{20,4},{21,5},{22,6},{23,7},{24,8},{25... | collective-permute-start | bytes 442376 | tf_op jit(solution)/shard_map/ppermute | solution.py:26
  35.2 1.7 %copy-start.3 = (f32[2304,144]{1,0:T(8,128)S(1)}, f32[2304,144]{1,0:T(8,128)}, u32[]{:S(2)}) copy-start(f32[2304,144]{1,0:T(8,128)} %copy-done.2) | copy-start | bytes 3981316
  36.8 0.9 copy-start.7
  43.5 2.8 %collective-permute-start.3 = (bf16[256,2176]{1,0:T(8,128)(2,1)S(1)}, bf16[256,2176]{1,0:T(8,128)(2,1)S(1)}, u32[]{:S(2)}, u32[]{:S(2)}) collective-permute-start(bf16[256,2176]{1,0:T(8,128)(2,1)S(1)} %get-tuple-element.57), channel_id=1, source_target_pairs={{0,1},{1,0},{2,3},{3,2},{4,5},{5,4},{6,7},{7,6},{8,9},{9,8},{10,11... | collective-permute-start | bytes 3342344 | tf_op jit(solution)/shard_map/ppermute | solution.py:31
  48.0 0.7 copy-start.12
  48.7 17.5 %all-to-all-start = ((bf16[4,64,768]{2,1,0:T(8,128)(2,1)}), bf16[4,64,768]{2,1,0:T(8,128)(2,1)S(1)}, u32[]{:S(2)}, u32[]{:S(2)}) async-start(bf16[4,64,768]{2,1,0:T(8,128)(2,1)} %get-tuple-element.60), calls=%async_computation | async-start | bytes 786432 | tf_op jit(solution)/shard_map/all_to_all | solution.py:451
  54.3 10.4 %collective-permute-start.4 = (bf16[128,1408]{1,0:T(8,128)(2,1)}, bf16[128,1408]{1,0:T(8,128)(2,1)S(1)}, u32[]{:S(2)}, u32[]{:S(2)}) collective-permute-start(bf16[128,1408]{1,0:T(8,128)(2,1)} %copy-done.12), channel_id=1, source_target_pairs={{0,2},{1,3},{2,0},{3,1},{4,6},{5,7},{6,4},{7,5},{8,10},{9,11},{10,... | collective-permute-start | bytes 1081352 | tf_op jit(solution)/shard_map/ppermute | solution.py:31
  67.7 14.0 %all-to-all-start.1 = ((bf16[4,32,1408]{2,1,0:T(8,128)(2,1)}), bf16[4,32,1408]{2,1,0:T(8,128)(2,1)S(1)}, u32[]{:S(2)}, u32[]{:S(2)}) async-start(bf16[4,32,1408]{2,1,0:T(8,128)(2,1)} %get-tuple-element.65), calls=%async_computation.1 | async-start | bytes 720896 | tf_op jit(solution)/shard_map/all_to_all | solution.py:451
  71.1 4.2 %collective-permute-start.5 = (bf16[32,768]{1,0:T(8,128)(2,1)S(1)}, bf16[32,768]{1,0:T(8,128)(2,1)S(1)}, u32[]{:S(2)}, u32[]{:S(2)}) collective-permute-start(bf16[32,768]{1,0:T(8,128)(2,1)S(1)} %get-tuple-element.64), channel_id=1, source_target_pairs={{0,2},{1,3},{2,0},{3,1},{4,6},{5,7},{6,4},{7,5},{8,10},{9,11},{10,... | collective-permute-start | bytes 147464 | tf_op jit(solution)/shard_map/ppermute | solution.py:31
  82.5 12.0 %all-to-all-start.2 = ((bf16[4,32,1280]{2,1,0:T(8,128)(2,1)}), bf16[4,32,1280]{2,1,0:T(8,128)(2,1)S(1)}, u32[]{:S(2)}, u32[]{:S(2)}) async-start(bf16[4,32,1280]{2,1,0:T(8,128)(2,1)} %get-tuple-element.67), calls=%async_computation.2 | async-start | bytes 655360 | tf_op jit(solution)/shard_map/all_to_all | solution.py:451
  85.9 4.2 %collective-permute-start.6 = (bf16[32,768]{1,0:T(8,128)(2,1)S(1)}, bf16[32,768]{1,0:T(8,128)(2,1)S(1)}, u32[]{:S(2)}, u32[]{:S(2)}) collective-permute-start(bf16[32,768]{1,0:T(8,128)(2,1)S(1)} %get-tuple-element.68.piece_q), channel_id=1, source_target_pairs={{0,2},{1,3},{2,0},{3,1},{4,6},{5,7},{6,4},{7,5},{8,10},{9,11},{10,... | collective-permute-start | bytes 147464 | tf_op jit(solution)/shard_map/ppermute | solution.py:31
  95.8 12.9 %all-to-all-start.3 = ((bf16[4,64,768]{2,1,0:T(8,128)(2,1)}), bf16[4,64,768]{2,1,0:T(8,128)(2,1)S(1)}, u32[]{:S(2)}, u32[]{:S(2)}) async-start(bf16[4,64,768]{2,1,0:T(8,128)(2,1)} %get-tuple-element.70), calls=%async_computation.3 | async-start | bytes 786432 | tf_op jit(solution)/shard_map/all_to_all | solution.py:451
  99.2 7.1 %collective-permute-start.7 = (bf16[128,1280]{1,0:T(8,128)(2,1)S(1)}, bf16[128,1280]{1,0:T(8,128)(2,1)S(1)}, u32[]{:S(2)}, u32[]{:S(2)}) collective-permute-start(bf16[128,1280]{1,0:T(8,128)(2,1)S(1)} %get-tuple-element.69.block_p), channel_id=1, source_target_pairs={{0,2},{1,3},{2,0},{3,1},{4,6},{5,7},{6,4},{7,5},{8,10},{9,11},{10,... | collective-permute-start | bytes 983048 | tf_op jit(solution)/shard_map/ppermute | solution.py:31
  109.6 7.7 %collective-permute-start.8 = (bf16[256,2048]{1,0:T(8,128)(2,1)S(1)}, bf16[256,2048]{1,0:T(8,128)(2,1)S(1)}, u32[]{:S(2)}, u32[]{:S(2)}) collective-permute-start(bf16[256,2048]{1,0:T(8,128)(2,1)S(1)} %get-tuple-element.71.half), channel_id=1, source_target_pairs={{0,1},{1,0},{2,3},{3,2},{4,5},{5,4},{6,7},{7,6},{8,9},{9,8},{10,11... | collective-permute-start | bytes 3145736 | tf_op jit(solution)/shard_map/ppermute | solution.py:31
  109.6 6.5 %collective-permute-start.2 = (bf16[72,512]{1,0:T(8,128)(2,1)S(1)}, bf16[72,512]{1,0:T(8,128)(2,1)S(1)}, u32[]{:S(2)}, u32[]{:S(2)}) collective-permute-start(bf16[72,512]{1,0:T(8,128)(2,1)S(1)} %get-tuple-element.55), channel_id=1, source_target_pairs={{0,4},{4,8},{8,12},{12,0},{1,5},{5,9},{9,13},{13,1},{2,6},{6,10},{... | collective-permute-start | bytes 221192 | tf_op jit(solution)/shard_map/ppermute | solution.py:20
  109.7 7.6 %collective-permute-start.11 = (f32[8,384]{1,0:T(8,128)S(1)}, f32[8,384]{1,0:T(8,128)S(1)}, u32[]{:S(2)}, u32[]{:S(2)}) collective-permute-start(f32[8,384]{1,0:T(8,128)S(1)} %get-tuple-element.72.row), channel_id=1, source_target_pairs={{0,17},{1,16},{2,19},{3,18},{16,1},{17,0},{18,3},{19,2},{4,21},{5,... | collective-permute-start | bytes 36872 | tf_op jit(solution)/shard_map/ppermute | solution.py:644
  109.8 7.5 %collective-permute-start.10 = (f32[8,384]{1,0:T(8,128)S(1)}, f32[8,384]{1,0:T(8,128)S(1)}, u32[]{:S(2)}, u32[]{:S(2)}) collective-permute-start(f32[8,384]{1,0:T(8,128)S(1)} %get-tuple-element.72.row), channel_id=1, source_target_pairs={{0,16},{16,0},{1,17},{17,1},{2,18},{18,2},{3,19},{19,3},{4,20},{20... | collective-permute-start | bytes 36872 | tf_op jit(solution)/shard_map/ppermute | solution.py:31
  111.8 5.5 %collective-permute-start.9 = (f32[8,384]{1,0:T(8,128)S(1)}, f32[8,384]{1,0:T(8,128)S(1)}, u32[]{:S(2)}, u32[]{:S(2)}) collective-permute-start(f32[8,384]{1,0:T(8,128)S(1)} %get-tuple-element.72.row), channel_id=1, source_target_pairs={{0,1},{1,0},{2,3},{3,2},{4,5},{5,4},{6,7},{7,6},{8,9},{9,8},{10,11... | collective-permute-start | bytes 36872 | tf_op jit(solution)/shard_map/ppermute | solution.py:31

commit v5 on v4

--- a/solution.py
+++ b/solution.py
@@ -9,7 +9,7 @@
 
 SHIFT = 6
 GROUP = 128
-CUT = 1280
+CUT = 1152
 EPSILON = 1e-05
 F32 = jnp.float32
 BF16 = jnp.bfloat16
@@ -39,8 +39,8 @@
     return lax.dot_general(left, right, (((1,), (1,)), ((), ())), preferred_element_type=F32)
 
 
-def call(kernel, outs, scratch=(), places="", out_places="", operands=(), flops=10**8, limit=12):
-    spaces = {"v": pltpu.VMEM, "s": pltpu.SMEM, "a": pl.ANY}
+def call(kernel, outs, scratch=(), places="", out_places="", operands=(), flops=10**8, limit=8):
+    spaces = {"v": pltpu.VMEM, "s": pltpu.SMEM, "a": pl.ANY, "h": pltpu.HBM}
     places = places or "v" * len(operands)
     out_places = out_places or "v" * len(outs)
     moved = sum(o.size * o.dtype.itemsize for o in list(outs) + list(operands))
@@ -72,43 +72,45 @@
 def pack_kernel(tokens, cot, land, own, rim, tokens_v, cot_v, land_v, own32, rim32, sems):
     arrays = ((tokens, tokens_v), (cot, cot_v), (land, land_v))
     copies = [started(source, target, sems, i) for i, (source, target) in enumerate(arrays)]
-    levels, lats, cols, width = tokens.shape[1:]
+    lats, cols, levels, width = tokens.shape[1:]
     half = levels * lats * SHIFT
     rim32[2 * half :, :] = jnp.zeros((rim32.shape[0] - 2 * half, width), F32)
     for which, ref in enumerate((tokens_v, cot_v)):
         copies[which].wait()
-        for level in range(levels):
-            for lat in range(lats):
-                base = which * half + (level * lats + lat) * SHIFT
-                line = ref[0, level, lat].astype(F32)
-                rim32[base : base + SHIFT, :] = line[:SHIFT]
-                own32[base : base + SHIFT, :] = line[SHIFT:]
+        for lat in range(lats):
+            for col in range(cols):
+                row = which * half + (lat * SHIFT + col % SHIFT) * levels
+                part = rim32 if col < SHIFT else own32
+                part[row : row + levels, :] = ref[0, lat, col].astype(F32)
     copies[2].wait()
     rim32[2 * half : 2 * half + lats, :cols] = land_v[...].astype(F32)
     own[...] = own32[...].astype(BF16)
     rim[...] = rim32[...].astype(BF16)
 
 
-def unpack_kernel(own, back, grid, grid_v, sems):
-    levels, lats, cols, width = grid.shape[1:]
+def unpack_kernel(own, back, after, grid, grid_v, sems):
+    lats, cols, levels, width = grid.shape[1:]
     came = back[...].astype(F32)
-    for level in range(levels):
-        for lat in range(lats):
-            base = (level * lats + lat) * SHIFT
-            grid_v[0, level, lat, :SHIFT, :] = came[base : base + SHIFT]
-            grid_v[0, level, lat, SHIFT:, :] = own[base : base + SHIFT, :]
+    for lat in range(lats):
+        for col in range(cols):
+            row = (lat * SHIFT + col % SHIFT) * levels
+            if col < SHIFT:
+                grid_v[0, lat, col] = came[row : row + levels]
+            else:
+                grid_v[0, lat, col] = own[row : row + levels, :]
     started(grid_v, grid, sems, 0).wait()
 
 
 def land_column(land, rows, first):
     lats, cols = land.shape
     row = lax.broadcasted_iota(jnp.int32, (rows, lats), 0)
-    lat = lax.rem(lax.div(row, SHIFT), lats)
+    lat = lax.div(row, rows // lats)
     pick = (lat == lax.broadcasted_iota(jnp.int32, (rows, lats), 1)).astype(F32)
     lines = dot(pick.astype(BF16), land.astype(BF16))
     row = lax.broadcasted_iota(jnp.int32, (rows, cols), 0)
     column = lax.broadcasted_iota(jnp.int32, (rows, cols), 1)
-    here = column == lax.rem(row, SHIFT) + first
+    levels = rows // (lats * SHIFT)
+    here = column == lax.rem(lax.div(row, levels), SHIFT) + first
     return jnp.sum(jnp.where(here, lines, 0.0), axis=1, keepdims=True)
 
 
@@ -128,7 +130,7 @@
     return sum(block[i * rows : (i + 1) * rows] * mask for i, mask in enumerate(masks))
 
 
-def back_through(grad_out, probs, qkv, keys_t, weight_out, grad_proj, size, land, ready=None):
+def back_through(grad_out, probs, qkv, keys_t, weight_out, grad_proj, size, land):
     count, width = grad_out.shape
     per = GROUP // size
     scale = size ** (-0.5)
@@ -140,8 +142,6 @@
     bias_row = jnp.zeros((1, GROUP), F32)
     for group in range(width // GROUP):
         at = group * GROUP
-        if ready is not None:
-            ready[group].wait()
         values = qkv[:, 2 * width + at : 2 * width + at + GROUP]
         grad_probs = dot(stacked(values, masks_b), att_t[at : at + GROUP, :])
         scores_b, probs_b, queries_t = [], [], []
@@ -179,10 +179,9 @@
 
 def forward_kernel(
     bias, own, rim, land_own, gain, weight_qkv, weight_out,
-    skip, cot, normed_out, normed_t_out, qkv_out, probs_out, attended_t_out, extra_out,
+    skip, cot, normed_t, qkv, probs, attended_t, land_out, normed_out, inverse_out,
     bias_v, land_v, gain_v, qkv_v, out_v,
-    normed_v, normed_t, qkv, probs, attended_t, extra, queries_t, keys_t, values_t, grad_proj,
-    sems_in, sems_out,
+    normed_v, inverse_v, queries_t, keys_t, values_t, grad_proj, sems_in, sems_out,
 ):
     width = gain.shape[1]
     heads = bias.shape[1]
@@ -220,7 +219,6 @@
         copy.wait()
     normed_b = (normed * gain_v[...]).astype(BF16)
     normed_t[...] = normed_b.T
-    sent.append(started(normed_t, normed_t_out, sems_out, 1))
     land = jnp.concatenate(
         [
             land_column(land_v[...].astype(F32), half, SHIFT),
@@ -228,15 +226,14 @@
         ],
         axis=0,
     )
-    extra[:, :GROUP] = jnp.broadcast_to(land, (count, GROUP))
-    extra[:, GROUP:] = jnp.broadcast_to(inverse, (count, GROUP))
-    sent.append(started(extra, extra_out, sems_out, 2))
+    land_out[...] = jnp.broadcast_to(land, (count, GROUP))
+    inverse_v[...] = jnp.broadcast_to(inverse, (count, GROUP))
+    sent.append(started(inverse_v, inverse_out, sems_out, 1))
     for part, turned in enumerate((queries_t, keys_t, values_t)):
         got[3 + part].wait()
         columns = slice(part * width, (part + 1) * width)
         qkv[:, columns] = dot(normed_b, qkv_v[:, columns]).astype(BF16)
         turned[...] = qkv[:, columns].T
-    sent.append(started(qkv, qkv_out, sems_out, 3))
     for group in range(width // GROUP):
         at = group * GROUP
         keys = qkv[:, width + at : width + at + GROUP]
@@ -250,9 +247,6 @@
             probs[head * count : (head + 1) * count, :] = weights
             out = dot(values_t[head * size : (head + 1) * size, :], weights.astype(BF16))
             attended_t[head * size : (head + 1) * size, :] = out.astype(BF16)
-        rows = pl.ds(group * per * count, per * count)
-        sent.append(started(probs.at[rows, :], probs_out.at[rows, :], sems_out, 4 + group))
-    sent.append(started(attended_t, attended_t_out, sems_out, 4 + width // GROUP))
     grad_out = jnp.concatenate([mine[half:], came[half : 2 * half]], axis=0)
     cot[...] = grad_out.astype(BF16)
     got[6].wait()
@@ -265,41 +259,21 @@
 
 
 def backward_kernel(
-    place, skip, cot, qkv_in, probs_in, weight_out, extra_in, normed_t_in, attended_t_in,
+    place, skip, cot, qkv, probs, land, normed_t, attended_t, weight_out,
     total_out, grad_proj, bias_out, give,
-    qkv, probs, out_v, extra, normed_t, attended_t, keys_t, sems,
+    out_v, keys_t, sems,
     *, heads,
 ):
     count, width = cot.shape
-    per = probs.shape[0] * GROUP // width
-    got = [
-        started(source, target, sems, i)
-        for i, (source, target) in enumerate(
-            [
-                (weight_out, out_v),
-                (qkv_in, qkv),
-                (extra_in, extra),
-                (normed_t_in, normed_t),
-                (attended_t_in, attended_t),
-            ]
-        )
-    ]
-    groups = []
-    for group in range(width // GROUP):
-        rows = pl.ds(group * per, per)
-        groups.append(started(probs_in.at[rows, :], probs.at[rows, :], sems, len(got) + group))
+    got = started(weight_out, out_v, sems, 0)
     total_out[...] = (cot[...].astype(F32) + skip[...].astype(F32)).astype(BF16)
-    got[1].wait()
     keys_t[...] = qkv[:, width : 2 * width].T
-    got[2].wait()
-    got[0].wait()
+    got.wait()
     bias_row = back_through(
-        total_out[...], probs, qkv, keys_t, out_v, grad_proj, width // heads, extra[:, :1], groups
+        total_out[...], probs, qkv, keys_t, out_v, grad_proj, width // heads, land[:, :1]
     )
     bias_out[...] = jnp.broadcast_to(bias_row, bias_out.shape)
     half = width // 2
-    got[3].wait()
-    got[4].wait()
     rows = aligned((1 - place[0]) * half, half)
     weight_rows(rows, normed_t, attended_t, grad_proj, total_out, bias_row, give)
 
@@ -314,10 +288,10 @@
 
 
 def finish_kernel(
-    place, total, grad_proj, bias_row, normed_t_in, attended_t_in, normed_in, extra_in,
+    place, total, grad_proj, bias_row, normed_t, attended_t, normed_in, inverse_in,
     weight_qkv, gain,
     keep, own, back,
-    normed_t, attended_t, normed, extra, qkv_v, gain_v, sems,
+    normed, inverse, qkv_v, gain_v, sems,
 ):
     count, width = total.shape
     half = width // 2
@@ -325,85 +299,119 @@
         started(source, target, sems, i)
         for i, (source, target) in enumerate(
             [
-                (normed_t_in, normed_t),
-                (attended_t_in, attended_t),
                 (weight_qkv.at[:half, :], qkv_v.at[:half, :]),
                 (weight_qkv.at[half:, :], qkv_v.at[half:, :]),
                 (normed_in, normed),
-                (extra_in, extra),
+                (inverse_in, inverse),
                 (gain, gain_v),
             ]
         )
     ]
-    got[0].wait()
-    got[1].wait()
     rows = aligned(place[0] * half, half)
     bias_b = bias_row[:1, :].astype(BF16).astype(F32)
     weight_rows(rows, normed_t, attended_t, grad_proj, total, bias_b, keep)
-    for copy in got[2:]:
+    for copy in got:
         copy.wait()
-    final = through_norm(grad_proj[...], qkv_v, gain_v, normed[...], extra[:, GROUP : GROUP + 1])
+    final = through_norm(grad_proj[...], qkv_v, gain_v, normed[...], inverse[:, :1])
     final = final + total[...].astype(F32)
     own[...] = final[: count // 2]
     back[...] = final[count // 2 :].astype(BF16)
 
 
-def first_kernel(place, keep, came, give_p, kept_p, give_q, total):
-    wide_p = give_p.shape[1]
-    half = keep.shape[0] // 2
-    total[...] = keep[...] + came[...].astype(F32)
-    give_p[...] = total[aligned((1 - place[1]) * half, half), :wide_p].astype(BF16)
+def first_p_kernel(place, keep, came, give, kept, total):
+    wide = give.shape[1]
+    half = give.shape[0]
+    total[...] = keep[:, :wide] + came[:, :wide].astype(F32)
+    give[...] = total[aligned((1 - place[1]) * half, half), :].astype(BF16)
     mine = aligned(place[1] * half, half)
-    kept_p[:, :CUT] = total[mine, :CUT]
-    kept_p[:, CUT:] = total[mine, CUT:wide_p].astype(BF16).astype(F32)
-    give_q[...] = total[:, wide_p:].astype(BF16).reshape(give_q.shape)
-
-
-def added(pieces):
-    total = pieces[0].astype(F32)
-    for other in range(1, pieces.shape[0]):
-        total = total + pieces[other].astype(F32)
-    return total
-
-
-def second_kernel(place, kept_p, came_p, came_q, give_q, left_q, give_p, total_q):
-    give_p[...] = (kept_p[...] + came_p[...].astype(F32)).astype(BF16).reshape(give_p.shape)
-    total_q[...] = added(came_q)
-    half = give_q.shape[0]
-    give_q[...] = total_q[aligned((1 - place[1]) * half, half), :].astype(BF16)
-    left_q[...] = total_q[aligned(place[1] * half, half), :]
-
-
-def third_kernel(left_q, came_q, came_p, pieces_p, piece_q, bias):
-    total = added(came_p)
-    piece = total[:, :CUT].astype(BF16)
-    for other in range(pieces_p.shape[0]):
-        pieces_p[other] = piece
-    piece_q[...] = (left_q[...] + came_q[...].astype(F32)).astype(BF16)
-    bias[...] = total[:8, CUT:]
-
-
-def fourth_kernel(place, pieces_p, piece_q, other_q, block_p, blocks_q):
-    block_p[...] = pieces_p[...].reshape(block_p.shape)
-    piece = piece_q.shape[0]
-    for other in range(blocks_q.shape[0]):
-        blocks_q[other, aligned(place[1] * piece, piece), :] = piece_q[...]
-        blocks_q[other, aligned((1 - place[1]) * piece, piece), :] = other_q[...]
-
-
-def fifth_kernel(place, weight_qkv, gain, bias, block_p, other_p, blocks_q, half, row):
-    rows, width = half.shape[0], weight_qkv.shape[0]
+    kept[:, :CUT] = total[mine, :CUT]
+    kept[:, CUT:] = total[mine, CUT:].astype(BF16).astype(F32)
+
+
+def first_q_kernel(place, keep, came, after, kept, *rest):
+    *give, total = rest
+    piece, wide = kept.shape
+    total[...] = keep[:, -wide:] + came[:, -wide:].astype(F32)
+    kept[...] = total[aligned(place[2] * piece, piece), :]
+    for other, ref in enumerate(give, 1):
+        ref[...] = total[aligned((place[2] ^ other) * piece, piece), :].astype(BF16)
+
+
+def second_p_kernel(place, kept, came, left, *rest):
+    *give, total = rest
+    piece = left.shape[0]
+    total[...] = kept[...] + came[...].astype(F32)
+    mine = aligned(place[2] * piece, piece)
+    left[:, :CUT] = total[mine, :CUT]
+    left[:, CUT:] = total[mine, CUT:].astype(BF16).astype(F32)
+    for other, ref in enumerate(give, 1):
+        ref[...] = total[aligned((place[2] ^ other) * piece, piece), :].astype(BF16)
+
+
+def second_q_kernel(place, after, kept, *rest):
+    *came, give, left, sums = rest
+    total = kept[...]
+    for ref in came:
+        total = total + ref[...].astype(F32)
+    sums[...] = total
+    half = give.shape[0]
+    give[...] = sums[aligned((1 - place[1]) * half, half), :].astype(BF16)
+    left[...] = sums[aligned(place[1] * half, half), :]
+
+
+def third_q_kernel(left, came, piece):
+    piece[...] = (left[...] + came[...].astype(F32)).astype(BF16)
+
+
+def third_p_kernel(place, after, left, *rest):
+    *came, piece, bias = rest
+    total = left[:, :CUT]
+    for ref in came:
+        total = total + ref[:, :CUT].astype(F32)
+    piece[...] = total.astype(BF16)
+    terms = [left[:8, CUT:]] + [ref[...].astype(F32)[:8, CUT:] for ref in came]
+    total = jnp.zeros_like(terms[0])
+    for source in range(len(terms)):
+        for other, term in enumerate(terms):
+            total = total + jnp.where((place[2] ^ other) == source, term, 0.0)
+    bias[...] = total
+
+
+def fourth_q_kernel(place, after, own, came, block):
+    piece = own.shape[0]
+    block[aligned(place[1] * piece, piece), :] = own[...]
+    block[aligned((1 - place[1]) * piece, piece), :] = came[...]
+
+
+def fourth_p_kernel(place, after, *rest):
+    *parts, block = rest
+    piece = parts[0].shape[0]
+    for other, part in enumerate(parts):
+        block[aligned((place[2] ^ other) * piece, piece), :] = part[...]
+
+
+def fifth_kernel(place, weight_qkv, gain, bias, block_p, other_p, *rest):
+    *parts_q, half, row, weight_v, gain_v, sems = rest
+    rows = half.shape[0]
+    mine = aligned(place[0] * rows, rows)
+    got = [
+        started(weight_qkv.at[mine, :], weight_v, sems, 0),
+        started(gain, gain_v, sems, 1),
+    ]
     piece = block_p.shape[0]
     half[aligned(place[1] * piece, piece), :CUT] = block_p[...]
     half[aligned((1 - place[1]) * piece, piece), :CUT] = other_p[...]
-    half[:, CUT:] = blocks_q[...].reshape(rows, half.shape[1] - CUT)
-    three = weight_qkv.shape[1]
+    piece = parts_q[0].shape[0]
+    for other, part in enumerate(parts_q):
+        half[aligned((place[2] ^ other) * piece, piece), CUT:] = part[...]
+    three = weight_v.shape[1]
     wide = half[:, :three].astype(F32)
-    mine = aligned(place[0] * rows, rows)
-    gain_half = jnp.sum(wide * weight_qkv[mine, :].astype(F32), axis=1, keepdims=True)
+    for copy in got:
+        copy.wait()
+    gain_half = jnp.sum(wide * weight_v[...].astype(F32), axis=1, keepdims=True)
     gain_half = jnp.broadcast_to(gain_half, (rows, GROUP)).T[:8]
     core = place[0].astype(F32)
-    own_gain = gain[:, :rows] * (1.0 - core) + gain[:, rows:] * core
+    own_gain = gain_v[:, :rows] * (1.0 - core) + gain_v[:, rows:] * core
     gain_half = gain_half / own_gain
     out = half[:, three:].astype(F32)
     square = jnp.sum(jnp.sum(wide * wide, axis=0, keepdims=True), axis=1, keepdims=True)
@@ -447,8 +455,8 @@
         copy.wait()
 
 
-def exchanged(pieces, axis):
-    return lax.all_to_all(pieces, axis, 0, 0, tiled=True)
+def sent_round(pieces, axis):
+    return [swapped(piece, axis, other) for other, piece in enumerate(pieces, 1)]
 
 
 def vmem(dims, dtype):
@@ -470,52 +478,57 @@
     lat, lon = lax.axis_index("lat"), lax.axis_index("lon")
     place = jnp.stack([lat % 2, lat // 2, lon]).astype(jnp.int32)
 
+    tokens = inputs.transpose(0, 2, 3, 1, 4)
+    own_cot = cotangent.transpose(0, 2, 3, 1, 4)
+
     own, rim = call(
         pack_kernel,
         [shape((2 * half, width), BF16), shape((packed, width), BF16)],
         scratch=[
-            vmem(inputs.shape, BF16),
-            vmem(inputs.shape, BF16),
+            vmem(tokens.shape, BF16),
+            vmem(tokens.shape, BF16),
             vmem(land_sea.shape, jnp.int32),
             vmem((2 * half, width), F32),
             vmem((packed, width), F32),
             copies(3),
         ],
-        places="aaa",
-        operands=(inputs, cotangent, land_sea),
+        places="hhh",
+        operands=(tokens, own_cot, land_sea),
     )
     rim = from_behind(rim, "lon", -1)
-    groups = width // GROUP
-    state = [
-        shape((count, width), F32),
-        shape((width, count), BF16),
-        shape((count, 3 * width), BF16),
-        shape((heads * count, count), F32),
-        shape((width, count), BF16),
-        shape((count, 2 * GROUP), F32),
-    ]
-    skip, cot, normed, normed_t, qkv, probs, attended_t, extra = call(
+    skip, cot, normed_t, qkv, probs, attended_t, land, normed, inverse = call(
         forward_kernel,
-        [shape((count, width), BF16), shape((count, width), BF16), *state],
+        [
+            shape((count, width), BF16),
+            shape((count, width), BF16),
+            shape((width, count), BF16),
+            shape((count, 3 * width), BF16),
+            shape((heads * count, count), F32),
+            shape((width, count), BF16),
+            shape((count, GROUP), F32),
+            shape((count, width), F32),
+            shape((count, GROUP), F32),
+        ],
         scratch=[
             vmem(land_bias.shape, F32),
             vmem(land_sea.shape, jnp.int32),
             vmem(gains.shape, F32),
             vmem(weight_qkv.shape, BF16),
             vmem(weight_out.shape, BF16),
-            *(vmem(kept.shape, kept.dtype) for kept in state),
+            vmem((count, width), F32),
+            vmem((count, GROUP), F32),
             vmem((width, count), BF16),
             vmem((width, count), BF16),
             vmem((width, count), BF16),
             vmem((count, 3 * width), BF16),
             copies(7),
-            copies(5 + groups),
-        ],
-        places="avvaaaa",
-        out_places="vvaaaaaa",
+            copies(2),
+        ],
+        places="hvvhhhh",
+        out_places="vvvvvvvhh",
         operands=(land_bias, own, rim, land_sea, gains, weight_qkv, weight_out),
         flops=10**9,
-        limit=20,
+        limit=16,
     )
     skip = passed_along(skip, "section", -1)
     rows, wide = width // 2, 4 * width + GROUP
@@ -527,20 +540,10 @@
             shape((8, GROUP), F32),
             shape((rows, wide), BF16),
         ],
-        scratch=[
-            vmem(qkv.shape, BF16),
-            vmem(probs.shape, F32),
-            vmem(weight_out.shape, BF16),
-            vmem(extra.shape, F32),
-            vmem(normed_t.shape, BF16),
-            vmem(attended_t.shape, BF16),
-            vmem((width, count), BF16),
-            copies(5 + groups),
-        ],
-        places="svvaaaaaa",
-        operands=(place, skip, cot, qkv, probs, weight_out, extra, normed_t, attended_t),
+        scratch=[vmem(weight_out.shape, BF16), vmem((width, count), BF16), copies(1)],
+        places="svvvvvvvh",
+        operands=(place, skip, cot, qkv, probs, land, normed_t, attended_t, weight_out),
         flops=10**9,
-        limit=20,
     )
     came = swapped(give, "lat", 1)
     keep, own_grad, back = call(
@@ -551,35 +554,34 @@
             shape((half, width), BF16),
         ],
         scratch=[
-            vmem(normed_t.shape, BF16),
-            vmem(attended_t.shape, BF16),
             vmem(normed.shape, F32),
-            vmem(extra.shape, F32),
+            vmem(inverse.shape, F32),
             vmem(weight_qkv.shape, BF16),
             vmem(gains.shape, F32),
-            copies(7),
-        ],
-        places="svvvaaaaaa",
+            copies(5),
+        ],
+        places="svvvvvhhhh",
         operands=(
-            place, total, grad_proj, bias_row, normed_t, attended_t, normed, extra,
+            place, total, grad_proj, bias_row, normed_t, attended_t, normed, inverse,
             weight_qkv, gains,
         ),
         flops=5 * 10**8,
     )
     back = from_behind(back, "lon", 1)
     entries = 2 * (4 * width * width + width + heads)
-    if rows // 2 // lons % 16 == 0:
+    if rows // 2 // lons % 16 == 0 and lons & (lons - 1) == 0:
         grads, mark = staged(place, keep, came, weight_qkv, gains, lons, heads, entries)
     else:
         grads, mark = plain(keep, came, weight_qkv, gains, heads, entries)
-    own_grad, back, _ = lax.optimization_barrier((own_grad, back, mark))
     (final_grad,) = call(
         unpack_kernel,
-        [shape(inputs.shape, F32)],
-        scratch=[vmem(inputs.shape, F32), copies(1)],
-        out_places="a",
-        operands=(own_grad, back),
-    )
+        [shape(tokens.shape, F32)],
+        scratch=[vmem(tokens.shape, F32), copies(1)],
+        places="vva",
+        out_places="h",
+        operands=(own_grad, back, mark),
+    )
+    final_grad = final_grad.transpose(0, 3, 1, 2, 4)
     return (final_grad, *(grad[None] for grad in grads))
 
 
@@ -588,57 +590,72 @@
     width = 2 * rows
     wide_p = CUT + GROUP
     wide_q = wide - wide_p
-    give_p, kept_p, give_q = call(
-        first_kernel,
-        [
-            shape((rows // 2, wide_p), BF16),
-            shape((rows // 2, wide_p), F32),
-            shape((lons, rows // lons, wide_q), BF16),
-        ],
-        scratch=[vmem((rows, wide), F32)],
+    some = range(lons - 1)
+    piece = rows // 2 // lons
+    give_p, kept_p = call(
+        first_p_kernel,
+        [shape((rows // 2, wide_p), BF16), shape((rows // 2, wide_p), F32)],
+        scratch=[vmem((rows, wide_p), F32)],
         places="svv",
         operands=(place, keep, came),
     )
     came_p = swapped(give_p, "lat", 2)
-    came_q = exchanged(give_q, "lon")
-    piece = rows // 2 // lons
-    give_q, left_q, give_p = call(
-        second_kernel,
+    kept_q, *give_q = call(
+        first_q_kernel,
         [
-            shape((piece, wide_q), BF16),
-            shape((piece, wide_q), F32),
-            shape((lons, piece, wide_p), BF16),
-        ],
+            shape((rows // lons, wide_q), F32),
+            *(shape((rows // lons, wide_q), BF16) for _ in some),
+        ],
+        scratch=[vmem((rows, wide_q), F32)],
+        places="svva",
+        operands=(place, keep, came, kept_p),
+    )
+    came_q = sent_round(give_q, "lon")
+    left_p, *give_p = call(
+        second_p_kernel,
+        [shape((piece, wide_p), F32), *(shape((piece, wide_p), BF16) for _ in some)],
+        scratch=[vmem((rows // 2, wide_p), F32)],
+        places="svv",
+        operands=(place, kept_p, came_p),
+    )
+    came_p = sent_round(give_p, "lon")
+    give_q, left_q = call(
+        second_q_kernel,
+        [shape((piece, wide_q), BF16), shape((piece, wide_q), F32)],
         scratch=[vmem((rows // lons, wide_q), F32)],
-        places="svvv",
-        operands=(place, kept_p, came_p, came_q),
+        places="sav" + "v" * len(some),
+        operands=(place, left_p, kept_q, *came_q),
     )
     came_q = swapped(give_q, "lat", 2)
-    came_p = exchanged(give_p, "lon")
-    pieces_p, piece_q, bias = call(
-        third_kernel,
-        [
-            shape((lons, piece, CUT), BF16),
-            shape((piece, wide_q), BF16),
-            shape((8, GROUP), F32),
-        ],
-        operands=(left_q, came_q, came_p),
-    )
+    (piece_q,) = call(third_q_kernel, [shape((piece, wide_q), BF16)], operands=(left_q, came_q))
     other_q = swapped(piece_q, "lat", 2)
-    pieces_p = exchanged(pieces_p, "lon")
-    block_p, blocks_q = call(
-        fourth_kernel,
-        [shape((rows // 2, CUT), BF16), shape((lons, rows // lons, wide_q), BF16)],
-        places="svvv",
-        operands=(place, pieces_p, piece_q, other_q),
+    piece_p, bias = call(
+        third_p_kernel,
+        [shape((piece, CUT), BF16), shape((8, GROUP), F32)],
+        places="sav" + "v" * len(some),
+        operands=(place, piece_q, left_p, *came_p),
+    )
+    others_p = sent_round([piece_p for _ in some], "lon")
+    (block_q,) = call(
+        fourth_q_kernel,
+        [shape((rows // lons, wide_q), BF16)],
+        places="savv",
+        operands=(place, piece_p, piece_q, other_q),
+    )
+    others_q = sent_round([block_q for _ in some], "lon")
+    (block_p,) = call(
+        fourth_p_kernel,
+        [shape((rows // 2, CUT), BF16)],
+        places="sav" + "v" * len(some),
+        operands=(place, block_q, piece_p, *others_p),
     )
     other_p = swapped(block_p, "lat", 2)
-    blocks_q = exchanged(blocks_q, "lon")
     half, row = call(
         fifth_kernel,
         [shape((rows, 4 * width), BF16), shape((8, rows + GROUP), F32)],
-        places="svvvvvv",
-        operands=(place, weight_qkv, gains, bias, block_p, other_p, blocks_q),
+        scratch=[vmem((rows, 3 * width), BF16), vmem((1, width), F32), copies(2)],
+        places="shhvvvv" + "v" * len(some),
+        operands=(place, weight_qkv, gains, bias, block_p, other_p, block_q, *others_q),
     )
     row_section = swapped(row, "section", 1)
     row_both = lax.ppermute(row, ("section", "lat"), across())
@@ -660,7 +677,7 @@
             copies(4 * rows // 64 + 2),
         ],
         places="svvvvvvv",
-        out_places="aaaa",
+        out_places="hhhh",
         operands=(place, half, other, row, row_core, row_section, row_both, bias),
     )
     return (grads[0], grads[1], grads[2][0], grads[3][0]), left_q

time: 121 us -> 102 us (0.84)
  waiting for transfers between devices: 48.4 us -> 34 us
  Pallas kernels: 26.5 us -> 23.1 us
    ppermute x8 -> x20, starting transfers between devices: 8.37 us -> 24.6 us  [swapped(): return lax.ppermute(value, axis, [(i, i ^ bit) for i in range(count)])]
    all_to_all x4 -> x0, starting transfers between devices: 15.9 us -> none  [exchanged(): return lax.all_to_all(pieces, axis, 0, 0, tiled=True)]
    all_to_all x4 -> x0, waiting for transfers between devices: 14.6 us -> none  [exchanged(): return lax.all_to_all(pieces, axis, 0, 0, tiled=True)]
    pallas_call x11 -> x15, Pallas kernels: 26.5 us -> 23.1 us  [call(): pl.pallas_call(kernel, out_shape=list(outs), in_specs=[pl.BlockSpec(memor...]
    unnamed x31 -> x34, local copies, waits for them, and re-layouts: 13.4 us -> 12.2 us
    ppermute x8 -> x20, waiting for transfers between devices: 20.1 us -> 20.2 us  [swapped(): return lax.ppermute(value, axis, [(i, i ^ bit) for i in range(count)])]
  transfers between devices with their start and end apart: 16 -> 24, of which waited for: 12 -> 11; matrix products, arithmetic and copies ran while one was open for 1% -> 0% of each run, Pallas kernels for 2% -> 5%
where the time goes in v5:
time: 102 us; the launch traced here: 101 us
  waiting for transfers between devices  34 us (33%)
  starting transfers between devices  31.2 us (31%)
  Pallas kernels  23.1 us (23%)
  local copies, waits for them, and re-layouts  12.2 us (12%)
    ppermute x20, starting transfers between devices, swapped(): return lax.ppermute(value, axis, [(i, i ^ bit) for i in range(count)])  24.6 us
    pallas_call x15, Pallas kernels, call(): pl.pallas_call(kernel, out_shape=list(outs), in_specs=[pl.BlockSpec(memor...  23.1 us
    ppermute x20, waiting for transfers between devices, swapped(): return lax.ppermute(value, axis, [(i, i ^ bit) for i in range(count)])  20.2 us
    unnamed x34, local copies, waits for them, and re-layouts  12.2 us
    ppermute x2, waiting for transfers between devices, from_behind(): lax.ppermute(value, axis, [(i, (i + by) % count) for i in range(count)])  7.79 us
    ppermute x1, waiting for transfers between devices, passed_along(): return lax.ppermute(block, axis, route)  5.96 us
    ppermute x2, starting transfers between devices, from_behind(): lax.ppermute(value, axis, [(i, (i + by) % count) for i in range(count)])  5.27 us
  transfers between devices with their start and end apart: 24, of which 11 were waited for; matrix products, arithmetic and copies ran while one was open for 0% of the time, Pallas kernels for 5%

profile of v5, /device:TPU:0, one launch (start us, length us, event | category | flops | bytes accessed | tf_op | source)
XLA Modules:
  0.0 101.5 jit_solution(14849838042254564317)
XLA Ops:
  0.6 0.9 copy-done.12
  1.5 0.9 copy-done.13
  2.5 0.7 copy-done.14
  3.1 0.6 shard_map.110
  3.7 5.1 %collective-permute-start = (bf16[160,512]{1,0:T(8,128)(2,1)S(1)}, bf16[160,512]{1,0:T(8,128)(2,1)S(1)}, u32[]{:S(2)}, u32[]{:S(2)}) collective-permute-start(bf16[160,512]{1,0:T(8,128)(2,1)S(1)} %get-tuple-element.44), channel_id=1, source_target_pairs={{0,12},{4,0},{8,4},{12,8},{1,13},{5,1},{9,5},{13,9},{2,14},{6,2},{... | collective-permute-start | bytes 491528 | tf_op jit(solution)/shard_map/ppermute | solution.py:20
  8.8 3.5 %collective-permute-done.rim = bf16[160,512]{1,0:T(8,128)(2,1)S(1)} collective-permute-done((bf16[160,512]{1,0:T(8,128)(2,1)S(1)}, bf16[160,512]{1,0:T(8,128)(2,1)S(1)}, u32[]{:S(2)}, u32[]{:S(2)}) %collective-permute-start) | collective-permute-done | bytes 163872 | tf_op jit(solution)/shard_map/ppermute | solution.py:20
  12.3 1.4 %copy-done = bf16[1,512,1536]{2,1,0:T(8,128)(2,1)S(1)} copy-done((bf16[1,512,1536]{2,1,0:T(8,128)(2,1)S(1)}, bf16[1,512,1536]{2,1,0:T(8,128)(2,1)}, u32[]{:S(2)}) %copy-start) | copy-done | bytes 1572888
  13.7 1.0 %copy-done.4 = bf16[1,512,512]{2,1,0:T(8,128)(2,1)S(1)} copy-done((bf16[1,512,512]{2,1,0:T(8,128)(2,1)S(1)}, bf16[1,512,512]{2,1,0:T(8,128)(2,1)}, u32[]{:S(2)}) %copy-start.4) | copy-done | bytes 524312
  14.7 0.7 copy-done.10
  15.4 0.7 copy-done.15
  16.1 0.7 copy-done.16
  16.8 7.1 %shard_map.111 = (bf16[144,512]{1,0:T(8,128)(2,1)}, bf16[144,512]{1,0:T(8,128)(2,1)S(1)}, bf16[512,144]{1,0:T(8,128)(2,1)S(1)}, bf16[144,1536]{1,0:T(8,128)(2,1)...) custom-call(f32[1,16]{1,0:T(1,128)S(1)} %copy-done.16, ...), custom_call_target="tpu_custom_call" | custom-call | flops 1000000000 | bytes 5212512 | tf_op jit(solution)/shard_map/pallas_call | solution.py:47
  23.9 0.0 copy-start.2
  23.9 1.4 %copy-done.2 = f32[2304,144]{1,0:T(8,128)} copy-done((f32[2304,144]{1,0:T(8,128)}, f32[2304,144]{1,0:T(8,128)S(1)}, u32[]{:S(2)}) %copy-start.2) | copy-done | bytes 1327128
  25.3 0.6 copy-done.6
  26.0 0.6 copy-done.8
  26.6 1.4 %collective-permute-start.1 = (bf16[144,512]{1,0:T(8,128)(2,1)}, bf16[144,512]{1,0:T(8,128)(2,1)}, u32[]{:S(2)}, u32[]{:S(2)}) collective-permute-start(bf16[144,512]{1,0:T(8,128)(2,1)} %get-tuple-element.45), channel_id=1, source_target_pairs={{16,0},{17,1},{18,2},{19,3},{20,4},{21,5},{22,6},{23,7},{24,8},{25... | collective-permute-start | bytes 442376 | tf_op jit(solution)/shard_map/ppermute | solution.py:26
  28.0 0.1 pad_add_fusion.place
  28.1 6.0 %collective-permute-done.1.skip = bf16[144,512]{1,0:T(8,128)(2,1)} collective-permute-done((bf16[144,512]{1,0:T(8,128)(2,1)}, bf16[144,512]{1,0:T(8,128)(2,1)}, u32[]{:S(2)}, u32[]{:S(2)}) %collective-permute-start.1) | collective-permute-done | bytes 147488 | tf_op jit(solution)/shard_map/ppermute | solution.py:26
  34.1 1.7 %copy-done.3 = f32[2304,144]{1,0:T(8,128)S(1)} copy-done((f32[2304,144]{1,0:T(8,128)S(1)}, f32[2304,144]{1,0:T(8,128)}, u32[]{:S(2)}) %copy-start.3) | copy-done | bytes 1327128
  35.7 0.9 copy-done.9
  36.6 4.1 %shard_map.112 = (bf16[144,512]{1,0:T(8,128)(2,1)S(1)}, bf16[144,1536]{1,0:T(8,128)(2,1)S(1)}, f32[8,128]{1,0:T(8,128)S(1)}, bf16[256,2176]{1,0:T(8,128)(2,1)S(1)}) custom-call(s32[3]{0:T(128)S(1)} %pad_add_fusion.place, bf16[144,512]{1,0:T(8,128)(2,1)} %collective-permute-done.1.skip, bf16[144,512]{1,0:T(8,128)(2,1)S(1)} %get-tuple-element.46.cot, ...), custom_call_target="tpu_custom_call" | custom-call | flops 1000000000 | bytes 4665356 | tf_op jit(solution)/shard_map/pallas_call | solution.py:47
  40.7 0.1 collective-permute-start.3
  40.8 2.1 %shard_map.113 = (f32[256,2176]{1,0:T(8,128)S(1)}, f32[72,512]{1,0:T(8,128)S(1)}, bf16[72,512]{1,0:T(8,128)(2,1)S(1)}) custom-call(s32[3]{0:T(128)S(1)} %pad_add_fusion.place, bf16[144,512]{1,0:T(8,128)(2,1)S(1)} %get-tuple-element.52.total, bf16[144,1536]{1,0:T(8,128)(2,1)S(1)} %get-tuple-element.53.grad_proj, f32[8,128]{1,0:T(8,128)S(1)} %get-tuple-element.54.bias_row, ...), custom_call_target="tpu_custom_call" | custom-call | flops 500000000 | bytes 5281804 | tf_op jit(solution)/shard_map/pallas_call | solution.py:47
  42.9 0.6 collective-permute-done.3.came
  43.5 0.8 shard_map.114
  44.3 1.6 %collective-permute-start.4 = (bf16[128,1280]{1,0:T(8,128)(2,1)S(1)}, bf16[128,1280]{1,0:T(8,128)(2,1)S(1)}, u32[]{:S(2)}, u32[]{:S(2)}) collective-permute-start(bf16[128,1280]{1,0:T(8,128)(2,1)S(1)} %get-tuple-element.62), channel_id=1, source_target_pairs={{0,2},{1,3},{2,0},{3,1},{4,6},{5,7},{6,4},{7,5},{8,10},{9,11},{10,... | collective-permute-start | bytes 983048 | tf_op jit(solution)/shard_map/ppermute | solution.py:31
  45.9 0.7 shard_map.116
  46.6 0.5 collective-permute-start.5
  47.1 4.4 %collective-permute-start.6 = (bf16[64,896]{1,0:T(8,128)(2,1)S(1)}, bf16[64,896]{1,0:T(8,128)(2,1)S(1)}, u32[]{:S(2)}, u32[]{:S(2)}) collective-permute-start(bf16[64,896]{1,0:T(8,128)(2,1)S(1)} %get-tuple-element.66), channel_id=1, source_target_pairs={{0,8},{4,12},{8,0},{12,4},{1,9},{5,13},{9,1},{13,5},{2,10},{6,14},... | collective-permute-start | bytes 344072 | tf_op jit(solution)/shard_map/ppermute | solution.py:31
  51.5 2.6 %collective-permute-done.4.came = bf16[128,1280]{1,0:T(8,128)(2,1)S(1)} collective-permute-done((bf16[128,1280]{1,0:T(8,128)(2,1)S(1)}, bf16[128,1280]{1,0:T(8,128)(2,1)S(1)}, u32[]{:S(2)}, u32[]{:S(2)}) %collective-permute-start.4) | collective-permute-done | bytes 327712 | tf_op jit(solution)/shard_map/ppermute | solution.py:31
  54.1 0.7 shard_map.115
  54.8 0.5 collective-permute-start.9
  55.3 4.4 %collective-permute-start.10 = (bf16[32,1280]{1,0:T(8,128)(2,1)S(1)}, bf16[32,1280]{1,0:T(8,128)(2,1)S(1)}, u32[]{:S(2)}, u32[]{:S(2)}) collective-permute-start(bf16[32,1280]{1,0:T(8,128)(2,1)S(1)} %get-tuple-element.71), channel_id=1, source_target_pairs={{0,8},{4,12},{8,0},{12,4},{1,9},{5,13},{9,1},{13,5},{2,10},{6,14},... | collective-permute-start | bytes 245768 | tf_op jit(solution)/shard_map/ppermute | solution.py:31
  59.7 0.0 collective-permute-done.5.rest_0_
  59.7 0.0 collective-permute-start.11
  59.7 1.6 %collective-permute-done.6.rest_1_ = bf16[64,896]{1,0:T(8,128)(2,1)S(1)} collective-permute-done((bf16[64,896]{1,0:T(8,128)(2,1)S(1)}, bf16[64,896]{1,0:T(8,128)(2,1)S(1)}, u32[]{:S(2)}, u32[]{:S(2)}) %collective-permute-start.6) | collective-permute-done | bytes 114720 | tf_op jit(solution)/shard_map/ppermute | solution.py:31
  61.3 0.0 collective-permute-done.7.rest_2_
  61.3 0.6 shard_map.117
  61.9 0.1 collective-permute-start.8
  62.0 4.2 %collective-permute-done.8.came = bf16[32,896]{1,0:T(8,128)(2,1)S(1)} collective-permute-done((bf16[32,896]{1,0:T(8,128)(2,1)S(1)}, bf16[32,896]{1,0:T(8,128)(2,1)S(1)}, u32[]{:S(2)}, u32[]{:S(2)}) %collective-permute-start.8) | collective-permute-done | bytes 57376 | tf_op jit(solution)/shard_map/ppermute | solution.py:31
  66.2 0.0 collective-permute-done.9.rest_0_
  66.2 1.7 %collective-permute-done.10.rest_1_ = bf16[32,1280]{1,0:T(8,128)(2,1)S(1)} collective-permute-done((bf16[32,1280]{1,0:T(8,128)(2,1)S(1)}, bf16[32,1280]{1,0:T(8,128)(2,1)S(1)}, u32[]{:S(2)}, u32[]{:S(2)}) %collective-permute-start.10) | collective-permute-done | bytes 81952 | tf_op jit(solution)/shard_map/ppermute | solution.py:31
  67.9 0.6 shard_map.120
  68.5 2.5 %collective-permute-start.15 = (bf16[32,1152]{1,0:T(8,128)(2,1)S(1)}, bf16[32,1152]{1,0:T(8,128)(2,1)S(1)}, u32[]{:S(2)}, u32[]{:S(2)}) collective-permute-start(bf16[32,1152]{1,0:T(8,128)(2,1)S(1)} %get-tuple-element.74.after.rest_0_), channel_id=1, source_target_pairs={{0,12},{4,8},{8,4},{12,0},{1,13},{5,9},{9,5},{13,1},{2,14},{6,10},... | collective-permute-start | bytes 221192 | tf_op jit(solution)/shard_map/ppermute | solution.py:31
  71.0 3.0 %collective-permute-start.14 = (bf16[32,1152]{1,0:T(8,128)(2,1)S(1)}, bf16[32,1152]{1,0:T(8,128)(2,1)S(1)}, u32[]{:S(2)}, u32[]{:S(2)}) collective-permute-start(bf16[32,1152]{1,0:T(8,128)(2,1)S(1)} %get-tuple-element.74.after.rest_0_), channel_id=1, source_target_pairs={{0,8},{4,12},{8,0},{12,4},{1,9},{5,13},{9,1},{13,5},{2,10},{6,14},... | collective-permute-start | bytes 221192 | tf_op jit(solution)/shard_map/ppermute | solution.py:31
  74.0 0.0 collective-permute-start.13
  74.1 0.5 collective-permute-start.12
  74.6 4.3 %collective-permute-done.12.came = bf16[32,896]{1,0:T(8,128)(2,1)S(1)} collective-permute-done((bf16[32,896]{1,0:T(8,128)(2,1)S(1)}, bf16[32,896]{1,0:T(8,128)(2,1)S(1)}, u32[]{:S(2)}, u32[]{:S(2)}) %collective-permute-start.12) | collective-permute-done | bytes 57376 | tf_op jit(solution)/shard_map/ppermute | solution.py:31
  78.8 0.6 shard_map.121.after.rest_0_
  79.4 0.6 shard_map.122.block_p
  80.0 0.6 collective-permute-start.16
  80.6 2.4 %collective-permute-start.19 = (bf16[64,896]{1,0:T(8,128)(2,1)S(1)}, bf16[64,896]{1,0:T(8,128)(2,1)S(1)}, u32[]{:S(2)}, u32[]{:S(2)}) collective-permute-start(bf16[64,896]{1,0:T(8,128)(2,1)S(1)} %shard_map.121.after.rest_0_), channel_id=1, source_target_pairs={{0,12},{4,8},{8,4},{12,0},{1,13},{5,9},{9,5},{13,1},{2,14},{6,10},... | collective-permute-start | bytes 344072 | tf_op jit(solution)/shard_map/ppermute | solution.py:31
  82.9 0.7 collective-permute-start.18
  83.7 1.3 %collective-permute-start.17 = (bf16[64,896]{1,0:T(8,128)(2,1)S(1)}, bf16[64,896]{1,0:T(8,128)(2,1)S(1)}, u32[]{:S(2)}, u32[]{:S(2)}) collective-permute-start(bf16[64,896]{1,0:T(8,128)(2,1)S(1)} %shard_map.121.after.rest_0_), channel_id=1, source_target_pairs={{0,4},{4,0},{8,12},{12,8},{1,5},{5,1},{9,13},{13,9},{2,6},{6,2},{1... | collective-permute-start | bytes 344072 | tf_op jit(solution)/shard_map/ppermute | solution.py:31
  84.9 2.3 %collective-permute-done.19.rest_3_ = bf16[64,896]{1,0:T(8,128)(2,1)S(1)} collective-permute-done((bf16[64,896]{1,0:T(8,128)(2,1)S(1)}, bf16[64,896]{1,0:T(8,128)(2,1)S(1)}, u32[]{:S(2)}, u32[]{:S(2)}) %collective-permute-start.19) | collective-permute-done | bytes 114720 | tf_op jit(solution)/shard_map/ppermute | solution.py:31
  87.3 2.9 %collective-permute-done.18.rest_2_ = bf16[64,896]{1,0:T(8,128)(2,1)S(1)} collective-permute-done((bf16[64,896]{1,0:T(8,128)(2,1)S(1)}, bf16[64,896]{1,0:T(8,128)(2,1)S(1)}, u32[]{:S(2)}, u32[]{:S(2)}) %collective-permute-start.18) | collective-permute-done | bytes 114720 | tf_op jit(solution)/shard_map/ppermute | solution.py:31
  90.1 1.2 %shard_map.123 = (bf16[256,2048]{1,0:T(8,128)(2,1)S(1)}, f32[8,384]{1,0:T(8,128)S(1)}) custom-call(s32[3]{0:T(128)S(1)} %pad_add_fusion.place, bf16[512,1536]{1,0:T(8,128)(2,1)S(1)} %bitcast.12, f32[1,512]{1,0:T(1,128)S(1)} %copy-done.11, f32[8,128]{1,0:T(8,128)S(1)} %get-tuple-element.73.bias, bf16[128,1152]{1,0:T(8,128)(2,1)S(1)} %shard_map.122.block_p, ...), custom_call_target="tpu_custom_call" | custom-call | flops 100000000 | bytes 3688460 | tf_op jit(solution)/shard_map/pallas_call | solution.py:47
  91.3 0.1 collective-permute-start.20
  91.4 0.2 collective-permute-start.2
  91.6 2.0 %collective-permute-start.22 = (f32[8,384]{1,0:T(8,128)S(1)}, f32[8,384]{1,0:T(8,128)S(1)}, u32[]{:S(2)}, u32[]{:S(2)}) collective-permute-start(f32[8,384]{1,0:T(8,128)S(1)} %get-tuple-element.76.row), channel_id=1, source_target_pairs={{0,16},{16,0},{1,17},{17,1},{2,18},{18,2},{3,19},{19,3},{4,20},{20... | collective-permute-start | bytes 36872 | tf_op jit(solution)/shard_map/ppermute | solution.py:31
  93.5 4.3 %collective-permute-done.2.back = bf16[72,512]{1,0:T(8,128)(2,1)S(1)} collective-permute-done((bf16[72,512]{1,0:T(8,128)(2,1)S(1)}, bf16[72,512]{1,0:T(8,128)(2,1)S(1)}, u32[]{:S(2)}, u32[]{:S(2)}) %collective-permute-start.2) | collective-permute-done | bytes 73760 | tf_op jit(solution)/shard_map/ppermute | solution.py:20
  97.9 0.8 shard_map.118
  98.7 2.8 %shard_map.124 = (f32[512,1536]{1,0:T(8,128)}, f32[512,512]{1,0:T(8,128)}, f32[1,512]{1,0:T(1,128)}, f32[1,16]{1,0:T(1,128)}) custom-call(s32[3]{0:T(128)S(1)} %pad_add_fusion.place, bf16[256,2048]{1,0:T(8,128)(2,1)S(1)} %get-tuple-element.75.half, bf16[256,2048]{1,0:T(8,128)(2,1)S(1)} %collective-permute-done.20.other, f32[8,384]{1,0:T(8,128)S(1)} %get-tuple-element.76.row, ...), custom_call_target="tpu_custom_call" | custom-call | flops 100000000 | bytes 6346828 | tf_op jit(solution)/shard_map/pallas_call | solution.py:47
  (34 shorter events, 0.1 us)
Async XLA Ops:
  0.6 0.9 copy-start.12
  1.5 0.9 copy-start.13
  2.5 0.7 copy-start.14
  3.7 8.6 %collective-permute-start = (bf16[160,512]{1,0:T(8,128)(2,1)S(1)}, bf16[160,512]{1,0:T(8,128)(2,1)S(1)}, u32[]{:S(2)}, u32[]{:S(2)}) collective-permute-start(bf16[160,512]{1,0:T(8,128)(2,1)S(1)} %get-tuple-element.44), channel_id=1, source_target_pairs={{0,12},{4,0},{8,4},{12,8},{1,13},{5,1},{9,5},{13,9},{2,14},{6,2},{... | collective-permute-start | bytes 491528 | tf_op jit(solution)/shard_map/ppermute | solution.py:20
  12.3 1.4 %copy-start = (bf16[1,512,1536]{2,1,0:T(8,128)(2,1)S(1)}, bf16[1,512,1536]{2,1,0:T(8,128)(2,1)}, u32[]{:S(2)}) copy-start(bf16[1,512,1536]{2,1,0:T(8,128)(2,1)} %param.11) | copy-start | bytes 4718596
  13.7 1.0 %copy-start.4 = (bf16[1,512,512]{2,1,0:T(8,128)(2,1)S(1)}, bf16[1,512,512]{2,1,0:T(8,128)(2,1)}, u32[]{:S(2)}) copy-start(bf16[1,512,512]{2,1,0:T(8,128)(2,1)} %param.12) | copy-start | bytes 1572868
  14.7 0.7 copy-start.10
  15.4 0.7 copy-start.15
  16.1 0.7 copy-start.16
  16.8 17.3 %copy-start.5 = (bf16[1,512,512]{2,1,0:T(8,128)(2,1)S(1)}, bf16[1,512,512]{2,1,0:T(8,128)(2,1)}, u32[]{:S(2)}) copy-start(bf16[1,512,512]{2,1,0:T(8,128)(2,1)} %param.12) | copy-start | bytes 1572868
  16.8 24.0 %copy-start.11 = (f32[1,512]{1,0:T(1,128)S(1)}, f32[1,512]{1,0:T(1,128)}, u32[]{:S(2)}) copy-start(f32[1,512]{1,0:T(1,128)} %gain.5) | copy-start | bytes 6148
  23.9 1.4 %copy-start.2 = (f32[2304,144]{1,0:T(8,128)}, f32[2304,144]{1,0:T(8,128)S(1)}, u32[]{:S(2)}) copy-start(f32[2304,144]{1,0:T(8,128)S(1)} %get-tuple-element.48.probs) | copy-start | bytes 3981316
  25.3 0.6 copy-start.6
  25.9 0.6 copy-start.8
  26.6 14.2 %copy-start.1 = (bf16[1,512,1536]{2,1,0:T(8,128)(2,1)S(1)}, bf16[1,512,1536]{2,1,0:T(8,128)(2,1)}, u32[]{:S(2)}) copy-start(bf16[1,512,1536]{2,1,0:T(8,128)(2,1)} %param.11) | copy-start | bytes 4718596
  26.6 7.5 %collective-permute-start.1 = (bf16[144,512]{1,0:T(8,128)(2,1)}, bf16[144,512]{1,0:T(8,128)(2,1)}, u32[]{:S(2)}, u32[]{:S(2)}) collective-permute-start(bf16[144,512]{1,0:T(8,128)(2,1)} %get-tuple-element.45), channel_id=1, source_target_pairs={{16,0},{17,1},{18,2},{19,3},{20,4},{21,5},{22,6},{23,7},{24,8},{25... | collective-permute-start | bytes 442376 | tf_op jit(solution)/shard_map/ppermute | solution.py:26
  34.1 1.7 %copy-start.3 = (f32[2304,144]{1,0:T(8,128)S(1)}, f32[2304,144]{1,0:T(8,128)}, u32[]{:S(2)}) copy-start(f32[2304,144]{1,0:T(8,128)} %copy-done.2) | copy-start | bytes 3981316
  35.7 0.9 copy-start.9
  36.6 4.2 %copy-start.7 = (f32[144,128]{1,0:T(8,128)S(1)}, f32[144,128]{1,0:T(8,128)}, u32[]{:S(2)}) copy-start(f32[144,128]{1,0:T(8,128)} %copy-done.6) | copy-start | bytes 221188
  40.7 2.8 %collective-permute-start.3 = (bf16[256,2176]{1,0:T(8,128)(2,1)S(1)}, bf16[256,2176]{1,0:T(8,128)(2,1)S(1)}, u32[]{:S(2)}, u32[]{:S(2)}) collective-permute-start(bf16[256,2176]{1,0:T(8,128)(2,1)S(1)} %get-tuple-element.60), channel_id=1, source_target_pairs={{0,1},{1,0},{2,3},{3,2},{4,5},{5,4},{6,7},{7,6},{8,9},{9,8},{10,11... | collective-permute-start | bytes 3342344 | tf_op jit(solution)/shard_map/ppermute | solution.py:31
  44.3 9.8 %collective-permute-start.4 = (bf16[128,1280]{1,0:T(8,128)(2,1)S(1)}, bf16[128,1280]{1,0:T(8,128)(2,1)S(1)}, u32[]{:S(2)}, u32[]{:S(2)}) collective-permute-start(bf16[128,1280]{1,0:T(8,128)(2,1)S(1)} %get-tuple-element.62), channel_id=1, source_target_pairs={{0,2},{1,3},{2,0},{3,1},{4,6},{5,7},{6,4},{7,5},{8,10},{9,11},{10,... | collective-permute-start | bytes 983048 | tf_op jit(solution)/shard_map/ppermute | solution.py:31
  46.6 13.1 %collective-permute-start.5 = (bf16[64,896]{1,0:T(8,128)(2,1)S(1)}, bf16[64,896]{1,0:T(8,128)(2,1)S(1)}, u32[]{:S(2)}, u32[]{:S(2)}) collective-permute-start(bf16[64,896]{1,0:T(8,128)(2,1)S(1)} %get-tuple-element.65), channel_id=1, source_target_pairs={{0,4},{4,0},{8,12},{12,8},{1,5},{5,1},{9,13},{13,9},{2,6},{6,2},{1... | collective-permute-start | bytes 344072 | tf_op jit(solution)/shard_map/ppermute | solution.py:31
  47.1 14.2 %collective-permute-start.6 = (bf16[64,896]{1,0:T(8,128)(2,1)S(1)}, bf16[64,896]{1,0:T(8,128)(2,1)S(1)}, u32[]{:S(2)}, u32[]{:S(2)}) collective-permute-start(bf16[64,896]{1,0:T(8,128)(2,1)S(1)} %get-tuple-element.66), channel_id=1, source_target_pairs={{0,8},{4,12},{8,0},{12,4},{1,9},{5,13},{9,1},{13,5},{2,10},{6,14},... | collective-permute-start | bytes 344072 | tf_op jit(solution)/shard_map/ppermute | solution.py:31
  51.5 9.8 %collective-permute-start.7 = (bf16[64,896]{1,0:T(8,128)(2,1)S(1)}, bf16[64,896]{1,0:T(8,128)(2,1)S(1)}, u32[]{:S(2)}, u32[]{:S(2)}) collective-permute-start(bf16[64,896]{1,0:T(8,128)(2,1)S(1)} %get-tuple-element.67), channel_id=1, source_target_pairs={{0,12},{4,8},{8,4},{12,0},{1,13},{5,9},{9,5},{13,1},{2,14},{6,10},... | collective-permute-start | bytes 344072 | tf_op jit(solution)/shard_map/ppermute | solution.py:31
  54.8 11.4 %collective-permute-start.9 = (bf16[32,1280]{1,0:T(8,128)(2,1)S(1)}, bf16[32,1280]{1,0:T(8,128)(2,1)S(1)}, u32[]{:S(2)}, u32[]{:S(2)}) collective-permute-start(bf16[32,1280]{1,0:T(8,128)(2,1)S(1)} %get-tuple-element.70), channel_id=1, source_target_pairs={{0,4},{4,0},{8,12},{12,8},{1,5},{5,1},{9,13},{13,9},{2,6},{6,2},{1... | collective-permute-start | bytes 245768 | tf_op jit(solution)/shard_map/ppermute | solution.py:31
  55.3 12.6 %collective-permute-start.10 = (bf16[32,1280]{1,0:T(8,128)(2,1)S(1)}, bf16[32,1280]{1,0:T(8,128)(2,1)S(1)}, u32[]{:S(2)}, u32[]{:S(2)}) collective-permute-start(bf16[32,1280]{1,0:T(8,128)(2,1)S(1)} %get-tuple-element.71), channel_id=1, source_target_pairs={{0,8},{4,12},{8,0},{12,4},{1,9},{5,13},{9,1},{13,5},{2,10},{6,14},... | collective-permute-start | bytes 245768 | tf_op jit(solution)/shard_map/ppermute | solution.py:31
  59.7 8.3 %collective-permute-start.11 = (bf16[32,1280]{1,0:T(8,128)(2,1)S(1)}, bf16[32,1280]{1,0:T(8,128)(2,1)S(1)}, u32[]{:S(2)}, u32[]{:S(2)}) collective-permute-start(bf16[32,1280]{1,0:T(8,128)(2,1)S(1)} %get-tuple-element.72), channel_id=1, source_target_pairs={{0,12},{4,8},{8,4},{12,0},{1,13},{5,9},{9,5},{13,1},{2,14},{6,10},... | collective-permute-start | bytes 245768 | tf_op jit(solution)/shard_map/ppermute | solution.py:31
  61.9 4.2 %collective-permute-start.8 = (bf16[32,896]{1,0:T(8,128)(2,1)S(1)}, bf16[32,896]{1,0:T(8,128)(2,1)S(1)}, u32[]{:S(2)}, u32[]{:S(2)}) collective-permute-start(bf16[32,896]{1,0:T(8,128)(2,1)S(1)} %get-tuple-element.69), channel_id=1, source_target_pairs={{0,2},{1,3},{2,0},{3,1},{4,6},{5,7},{6,4},{7,5},{8,10},{9,11},{10,... | collective-permute-start | bytes 172040 | tf_op jit(solution)/shard_map/ppermute | solution.py:31
  68.5 10.9 %collective-permute-start.15 = (bf16[32,1152]{1,0:T(8,128)(2,1)S(1)}, bf16[32,1152]{1,0:T(8,128)(2,1)S(1)}, u32[]{:S(2)}, u32[]{:S(2)}) collective-permute-start(bf16[32,1152]{1,0:T(8,128)(2,1)S(1)} %get-tuple-element.74.after.rest_0_), channel_id=1, source_target_pairs={{0,12},{4,8},{8,4},{12,0},{1,13},{5,9},{9,5},{13,1},{2,14},{6,10},... | collective-permute-start | bytes 221192 | tf_op jit(solution)/shard_map/ppermute | solution.py:31
  71.0 8.4 %collective-permute-start.14 = (bf16[32,1152]{1,0:T(8,128)(2,1)S(1)}, bf16[32,1152]{1,0:T(8,128)(2,1)S(1)}, u32[]{:S(2)}, u32[]{:S(2)}) collective-permute-start(bf16[32,1152]{1,0:T(8,128)(2,1)S(1)} %get-tuple-element.74.after.rest_0_), channel_id=1, source_target_pairs={{0,8},{4,12},{8,0},{12,4},{1,9},{5,13},{9,1},{13,5},{2,10},{6,14},... | collective-permute-start | bytes 221192 | tf_op jit(solution)/shard_map/ppermute | solution.py:31
  74.0 5.4 %collective-permute-start.13 = (bf16[32,1152]{1,0:T(8,128)(2,1)S(1)}, bf16[32,1152]{1,0:T(8,128)(2,1)S(1)}, u32[]{:S(2)}, u32[]{:S(2)}) collective-permute-start(bf16[32,1152]{1,0:T(8,128)(2,1)S(1)} %get-tuple-element.74.after.rest_0_), channel_id=1, source_target_pairs={{0,4},{4,0},{8,12},{12,8},{1,5},{5,1},{9,13},{13,9},{2,6},{6,2},{1... | collective-permute-start | bytes 221192 | tf_op jit(solution)/shard_map/ppermute | solution.py:31
  74.1 4.8 %collective-permute-start.12 = (bf16[32,896]{1,0:T(8,128)(2,1)S(1)}, bf16[32,896]{1,0:T(8,128)(2,1)S(1)}, u32[]{:S(2)}, u32[]{:S(2)}) collective-permute-start(bf16[32,896]{1,0:T(8,128)(2,1)S(1)} %shard_map.119.after.own), channel_id=1, source_target_pairs={{0,2},{1,3},{2,0},{3,1},{4,6},{5,7},{6,4},{7,5},{8,10},{9,11},{10,... | collective-permute-start | bytes 172040 | tf_op jit(solution)/shard_map/ppermute | solution.py:31
  80.0 10.1 %collective-permute-start.16 = (bf16[128,1152]{1,0:T(8,128)(2,1)S(1)}, bf16[128,1152]{1,0:T(8,128)(2,1)S(1)}, u32[]{:S(2)}, u32[]{:S(2)}) collective-permute-start(bf16[128,1152]{1,0:T(8,128)(2,1)S(1)} %shard_map.122.block_p), channel_id=1, source_target_pairs={{0,2},{1,3},{2,0},{3,1},{4,6},{5,7},{6,4},{7,5},{8,10},{9,11},{10,... | collective-permute-start | bytes 884744 | tf_op jit(solution)/shard_map/ppermute | solution.py:31
  80.6 6.7 %collective-permute-start.19 = (bf16[64,896]{1,0:T(8,128)(2,1)S(1)}, bf16[64,896]{1,0:T(8,128)(2,1)S(1)}, u32[]{:S(2)}, u32[]{:S(2)}) collective-permute-start(bf16[64,896]{1,0:T(8,128)(2,1)S(1)} %shard_map.121.after.rest_0_), channel_id=1, source_target_pairs={{0,12},{4,8},{8,4},{12,0},{1,13},{5,9},{9,5},{13,1},{2,14},{6,10},... | collective-permute-start | bytes 344072 | tf_op jit(solution)/shard_map/ppermute | solution.py:31
  82.9 7.2 %collective-permute-start.18 = (bf16[64,896]{1,0:T(8,128)(2,1)S(1)}, bf16[64,896]{1,0:T(8,128)(2,1)S(1)}, u32[]{:S(2)}, u32[]{:S(2)}) collective-permute-start(bf16[64,896]{1,0:T(8,128)(2,1)S(1)} %shard_map.121.after.rest_0_), channel_id=1, source_target_pairs={{0,8},{4,12},{8,0},{12,4},{1,9},{5,13},{9,1},{13,5},{2,10},{6,14},... | collective-permute-start | bytes 344072 | tf_op jit(solution)/shard_map/ppermute | solution.py:31
  83.7 6.5 %collective-permute-start.17 = (bf16[64,896]{1,0:T(8,128)(2,1)S(1)}, bf16[64,896]{1,0:T(8,128)(2,1)S(1)}, u32[]{:S(2)}, u32[]{:S(2)}) collective-permute-start(bf16[64,896]{1,0:T(8,128)(2,1)S(1)} %shard_map.121.after.rest_0_), channel_id=1, source_target_pairs={{0,4},{4,0},{8,12},{12,8},{1,5},{5,1},{9,13},{13,9},{2,6},{6,2},{1... | collective-permute-start | bytes 344072 | tf_op jit(solution)/shard_map/ppermute | solution.py:31
  91.3 7.3 %collective-permute-start.20 = (bf16[256,2048]{1,0:T(8,128)(2,1)S(1)}, bf16[256,2048]{1,0:T(8,128)(2,1)S(1)}, u32[]{:S(2)}, u32[]{:S(2)}) collective-permute-start(bf16[256,2048]{1,0:T(8,128)(2,1)S(1)} %get-tuple-element.75.half), channel_id=1, source_target_pairs={{0,1},{1,0},{2,3},{3,2},{4,5},{5,4},{6,7},{7,6},{8,9},{9,8},{10,11... | collective-permute-start | bytes 3145736 | tf_op jit(solution)/shard_map/ppermute | solution.py:31
  91.4 6.5 %collective-permute-start.2 = (bf16[72,512]{1,0:T(8,128)(2,1)S(1)}, bf16[72,512]{1,0:T(8,128)(2,1)S(1)}, u32[]{:S(2)}, u32[]{:S(2)}) collective-permute-start(bf16[72,512]{1,0:T(8,128)(2,1)S(1)} %get-tuple-element.58), channel_id=1, source_target_pairs={{0,4},{4,8},{8,12},{12,0},{1,5},{5,9},{9,13},{13,1},{2,6},{6,10},{... | collective-permute-start | bytes 221192 | tf_op jit(solution)/shard_map/ppermute | solution.py:20
  91.6 7.1 %collective-permute-start.23 = (f32[8,384]{1,0:T(8,128)S(1)}, f32[8,384]{1,0:T(8,128)S(1)}, u32[]{:S(2)}, u32[]{:S(2)}) collective-permute-start(f32[8,384]{1,0:T(8,128)S(1)} %get-tuple-element.76.row), channel_id=1, source_target_pairs={{0,17},{1,16},{2,19},{3,18},{16,1},{17,0},{18,3},{19,2},{4,21},{5,... | collective-permute-start | bytes 36872 | tf_op jit(solution)/shard_map/ppermute | solution.py:661
  91.6 7.1 %collective-permute-start.22 = (f32[8,384]{1,0:T(8,128)S(1)}, f32[8,384]{1,0:T(8,128)S(1)}, u32[]{:S(2)}, u32[]{:S(2)}) collective-permute-start(f32[8,384]{1,0:T(8,128)S(1)} %get-tuple-element.76.row), channel_id=1, source_target_pairs={{0,16},{16,0},{1,17},{17,1},{2,18},{18,2},{3,19},{19,3},{4,20},{20... | collective-permute-start | bytes 36872 | tf_op jit(solution)/shard_map/ppermute | solution.py:31
  93.5 5.1 %collective-permute-start.21 = (f32[8,384]{1,0:T(8,128)S(1)}, f32[8,384]{1,0:T(8,128)S(1)}, u32[]{:S(2)}, u32[]{:S(2)}) collective-permute-start(f32[8,384]{1,0:T(8,128)S(1)} %get-tuple-element.76.row), channel_id=1, source_target_pairs={{0,1},{1,0},{2,3},{3,2},{4,5},{5,4},{6,7},{7,6},{8,9},{9,8},{10,11... | collective-permute-start | bytes 36872 | tf_op jit(solution)/shard_map/ppermute | solution.py:31

commit v6 on v5

v6 whole, which is shorter than its diff:
```python
import functools

import jax
import jax.numpy as jnp
from jax import lax
from jax.experimental import pallas as pl
from jax.experimental.pallas import tpu as pltpu
from jax.sharding import PartitionSpec as P

SHIFT = 6
GROUP = 128
CUT = 1280
EPSILON = 1e-05
F32 = jnp.float32
BF16 = jnp.bfloat16


def from_behind(value, axis, by):
    count = lax.axis_size(axis)
    return lax.ppermute(value, axis, [(i, (i + by) % count) for i in range(count)])


def passed_along(block, axis, distance):
    devices = range(lax.axis_size(axis))
    route = [(i - distance, i) for i in devices if i - distance in devices]
    return lax.ppermute(block, axis, route)


def swapped(value, axis, bit):
    count = lax.axis_size(axis)
    return lax.ppermute(value, axis, [(i, i ^ bit) for i in range(count)])


def dot(left, right):
    return jnp.dot(left, right, preferred_element_type=F32)


def dot_last(left, right):
    return lax.dot_general(left, right, (((1,), (1,)), ((), ())), preferred_element_type=F32)


def call(kernel, outs, scratch=(), places="", out_places="", operands=(), flops=10**8, limit=8):
    spaces = {"v": pltpu.VMEM, "s": pltpu.SMEM, "a": pl.ANY, "h": pltpu.HBM}
    places = places or "v" * len(operands)
    out_places = out_places or "v" * len(outs)
    moved = sum(o.size * o.dtype.itemsize for o in list(outs) + list(operands))
    return pl.pallas_call(
        kernel,
        out_shape=list(outs),
        in_specs=[pl.BlockSpec(memory_space=spaces[letter]) for letter in places],
        out_specs=[pl.BlockSpec(memory_space=spaces[letter]) for letter in out_places],
        scratch_shapes=list(scratch),
        compiler_params=pltpu.CompilerParams(vmem_limit_bytes=limit * 2**20),
        cost_estimate=pl.CostEstimate(flops=flops, bytes_accessed=moved, transcendentals=0),
    )(*operands)


def started(source, target, semaphores, index):
    copy = pltpu.make_async_copy(source, target, semaphores.at[index])
    copy.start()
    return copy


def shape(dims, dtype):
    return jax.ShapeDtypeStruct(dims, dtype)


def aligned(start, size):
    return pl.ds(pl.multiple_of(start, size), size)


def position():
    lat, lon = lax.axis_index("lat"), lax.axis_index("lon")
    return lax.rem(lat, 2), lax.div(lat, 2), lon


def pack_kernel(tokens, cot, land, own, rim, tokens_v, cot_v, land_v, own32, rim32, sems):
    arrays = ((tokens, tokens_v), (cot, cot_v), (land, land_v))
    copies = [started(source, target, sems, i) for i, (source, target) in enumerate(arrays)]
    lats, cols, levels, width = tokens.shape[1:]
    half = levels * lats * SHIFT
    rim32[2 * half :, :] = jnp.zeros((rim32.shape[0] - 2 * half, width), F32)
    for which, ref in enumerate((tokens_v, cot_v)):
        copies[which].wait()
        for lat in range(lats):
            for col in range(cols):
                row = which * half + (lat * SHIFT + col % SHIFT) * levels
                part = rim32 if col < SHIFT else own32
                part[row : row + levels, :] = ref[0, lat, col].astype(F32)
    copies[2].wait()
    rim32[2 * half : 2 * half + lats, :cols] = land_v[...].astype(F32)
    own[...] = own32[...].astype(BF16)
    rim[...] = rim32[...].astype(BF16)


def unpack_kernel(own, back, grid, grid_v, sems):
    lats, cols, levels, width = grid.shape[1:]
    came = back[...].astype(F32)
    for lat in range(lats):
        for col in range(cols):
            row = (lat * SHIFT + col % SHIFT) * levels
            if col < SHIFT:
                grid_v[0, lat, col] = came[row : row + levels]
            else:
                grid_v[0, lat, col] = own[row : row + levels, :]
    started(grid_v, grid, sems, 0).wait()


def land_column(land, rows, first):
    lats, cols = land.shape
    row = lax.broadcasted_iota(jnp.int32, (rows, lats), 0)
    lat = lax.div(row, rows // lats)
    pick = (lat == lax.broadcasted_iota(jnp.int32, (rows, lats), 1)).astype(F32)
    lines = dot(pick.astype(BF16), land.astype(BF16))
    row = lax.broadcasted_iota(jnp.int32, (rows, cols), 0)
    column = lax.broadcasted_iota(jnp.int32, (rows, cols), 1)
    levels = rows // (lats * SHIFT)
    here = column == lax.rem(lax.div(row, levels), SHIFT) + first
    return jnp.sum(jnp.where(here, lines, 0.0), axis=1, keepdims=True)


def head_masks(dtype, size):
    lane = lax.broadcasted_iota(jnp.int32, (1, GROUP), 1)
    return [
        (lax.div(lane, size) == part).astype(F32).astype(dtype) for part in range(GROUP // size)
    ]


def stacked(block, masks):
    return jnp.concatenate([block * mask for mask in masks], axis=0)


def folded(block, masks):
    rows = block.shape[0] // len(masks)
    return sum(block[i * rows : (i + 1) * rows] * mask for i, mask in enumerate(masks))


def back_through(grad_out, probs, probs_b, qkv, keys_t, weight_out, grad_proj, size, land):
    count, width = grad_out.shape
    per = GROUP // size
    scale = size ** (-0.5)
    masks_b, masks = head_masks(BF16, size), head_masks(F32, size)
    att_t = dot_last(weight_out[...], grad_out)
    grad_att = att_t.T.astype(BF16)
    att_t = att_t.astype(BF16)
    lane = lax.broadcasted_iota(jnp.int32, (1, GROUP), 1)
    bias_row = jnp.zeros((1, GROUP), F32)
    for group in range(width // GROUP):
        at = group * GROUP
        values = qkv[:, 2 * width + at : 2 * width + at + GROUP]
        grad_probs = dot(stacked(values, masks_b), att_t[at : at + GROUP, :])
        scores_b, queries_t = [], []
        for part in range(per):
            head = group * per + part
            weights = probs[head * count : (head + 1) * count, :].astype(F32)
            grad_weights = grad_probs[part * count : (part + 1) * count]
            inner = jnp.sum(weights * grad_weights, axis=0, keepdims=True)
            grad_scores = weights * (grad_weights - inner)
            if land is not None:
                on_land = jnp.sum(grad_scores * land, axis=0, keepdims=True)
                on_land = jnp.sum(on_land, axis=1, keepdims=True)
                bias_row = bias_row + jnp.where(lane == head, on_land, 0.0)
            scaled_b = (grad_scores * scale).astype(BF16)
            scores_b.append(scaled_b)
            queries_t.append(dot(keys_t[head * size : (head + 1) * size, :], scaled_b))
        queries = qkv[:, at : at + GROUP]
        grad_keys = dot(jnp.concatenate(scores_b, axis=0), queries)
        mixed = probs_b[group * per * count : (group + 1) * per * count, :]
        grad_values = dot(mixed, grad_att[:, at : at + GROUP])
        grad_proj[:, at : at + GROUP] = jnp.concatenate(queries_t, axis=0).T.astype(BF16)
        grad_proj[:, width + at : width + at + GROUP] = folded(grad_keys, masks).astype(BF16)
        grad_proj[:, 2 * width + at : 2 * width + at + GROUP] = folded(grad_values, masks).astype(
            BF16
        )
    return bias_row


def through_norm(grad_proj, weight_t, gain, normed, inverse):
    scaled = dot(grad_proj, weight_t[...]) * gain
    mean = jnp.mean(scaled, axis=-1, keepdims=True)
    along = jnp.mean(scaled * normed, axis=-1, keepdims=True)
    return inverse * (scaled - mean - normed * along)


def ready_kernel(
    own_in, weight_qkv, weight_out, gain, land, bias,
    own, qkv_v, qkv_t, out_v, params,
    gain_v, land_v, bias_v, sems,
):
    arrays = (
        (weight_qkv, qkv_v), (weight_out, out_v), (gain, gain_v), (land, land_v), (bias, bias_v),
        (own_in, own),
    )
    copies = [started(source, target, sems, i) for i, (source, target) in enumerate(arrays)]
    for copy in copies[1:]:
        copy.wait()
    lats, cols = land.shape
    params[...] = jnp.zeros(params.shape, F32)
    params[0:1, :] = gain_v[...]
    params[1:2, : bias.shape[1]] = bias_v[...]
    params[8 : 8 + lats, :cols] = land_v[...].astype(F32)
    copies[0].wait()
    width = weight_qkv.shape[0]
    for part in range(weight_qkv.shape[1] // width):
        rows = slice(part * width, (part + 1) * width)
        qkv_t[rows, :] = qkv_v[:, rows].T


def forward_kernel(
    own, rim, weight_qkv, weight_t, weight_out, params,
    skip, cot, normed_t, qkv, probs_b, attended_t, extra, normed_out,
    probs, queries_t, keys_t, values_t, grad_proj,
    *, heads, lats, cols,
):
    width = params.shape[1]
    size = width // heads
    half = own.shape[0] // 2
    count = 2 * half
    per = GROUP // size
    scale = size ** (-0.5)
    masks_b = head_masks(BF16, size)
    mine = own[...].astype(F32)
    came = rim[...].astype(F32)
    gain = params[0:1, :]
    values = jnp.concatenate([mine[:half], came[:half]], axis=0)
    centred = values - jnp.mean(values, axis=-1, keepdims=True)
    inverse = lax.rsqrt(jnp.mean(centred * centred, axis=-1, keepdims=True) + EPSILON)
    normed = centred * inverse
    normed_out[...] = normed
    normed_b = (normed * gain).astype(BF16)
    normed_t[...] = normed_b.T
    land = jnp.concatenate(
        [
            land_column(params[8 : 8 + lats, :cols], half, SHIFT),
            land_column(came[2 * half : 2 * half + lats, :cols], half, 0),
        ],
        axis=0,
    )
    extra[:, :GROUP] = jnp.broadcast_to(land, (count, GROUP))
    extra[:, GROUP:] = jnp.broadcast_to(inverse, (count, GROUP))
    for part, turned in enumerate((queries_t, keys_t, values_t)):
        columns = slice(part * width, (part + 1) * width)
        qkv[:, columns] = dot(normed_b, weight_qkv[:, columns]).astype(BF16)
        turned[...] = qkv[:, columns].T
    for group in range(width // GROUP):
        at = group * GROUP
        keys = qkv[:, width + at : width + at + GROUP]
        scores = dot(stacked(keys, masks_b), queries_t[at : at + GROUP, :])
        for part in range(per):
            head = group * per + part
            block = scores[part * count : (part + 1) * count] * scale
            block = block + params[1:2, head : head + 1] * land
            block = jnp.exp(block - jnp.max(block, axis=0, keepdims=True))
            weights = block * (1.0 / jnp.sum(block, axis=0, keepdims=True))
            probs[head * count : (head + 1) * count, :] = weights
            weights_b = weights.astype(BF16)
            probs_b[head * count : (head + 1) * count, :] = weights_b
            out = dot(values_t[head * size : (head + 1) * size, :], weights_b)
            attended_t[head * size : (head + 1) * size, :] = out.astype(BF16)
    grad_out = jnp.concatenate([mine[half:], came[half : 2 * half]], axis=0)
    cot[...] = grad_out.astype(BF16)
    back_through(cot[...], probs, probs_b, qkv, keys_t, weight_out, grad_proj, size, None)
    skip[...] = (
        through_norm(grad_proj[...], weight_t, gain, normed, inverse) + grad_out
    ).astype(BF16)


def backward_kernel(
    skip, cot, qkv, probs, weight_out, extra, normed_t, attended_t,
    total_out, grad_proj, bias_out, give,
    keys_t,
    *, heads,
):
    count, width = cot.shape
    core, _, _ = position()
    total_out[...] = (cot[...].astype(F32) + skip[...].astype(F32)).astype(BF16)
    keys_t[...] = qkv[:, width : 2 * width].T
    bias_row = back_through(
        total_out[...], probs, probs, qkv, keys_t, weight_out, grad_proj, width // heads,
        extra[:, :1],
    )
    bias_out[...] = jnp.broadcast_to(bias_row, bias_out.shape)
    half = width // 2
    rows = aligned((1 - core) * half, half)
    weight_rows(rows, normed_t, attended_t, grad_proj, total_out, bias_row, give)


def weight_rows(rows, normed_t, attended_t, grad_proj, total, bias_row, out):
    tokens = normed_t[rows, :]
    three = grad_proj.shape[1]
    out[:, :CUT] = dot(tokens, grad_proj[:, :CUT]).astype(out.dtype)
    out[:, CUT : CUT + GROUP] = jnp.broadcast_to(bias_row, (out.shape[0], GROUP)).astype(out.dtype)
    out[:, CUT + GROUP : three + GROUP] = dot(tokens, grad_proj[:, CUT:]).astype(out.dtype)
    out[:, three + GROUP :] = dot(attended_t[rows, :], total[...]).astype(out.dtype)


def finish_kernel(
    total, grad_proj, bias_row, normed_t, attended_t, normed, extra, weight_t, params,
    keep, own, back,
):
    count, width = total.shape
    half = width // 2
    core, _, _ = position()
    rows = aligned(core * half, half)
    bias_b = bias_row[:1, :].astype(BF16).astype(F32)
    weight_rows(rows, normed_t, attended_t, grad_proj, total, bias_b, keep)
    inverse = extra[:, GROUP : GROUP + 1]
    final = through_norm(grad_proj[...], weight_t, params[0:1, :], normed[...], inverse)
    final = final + total[...].astype(F32)
    own[...] = final[: count // 2]
    back[...] = final[count // 2 :].astype(BF16)


def first_kernel(keep, came, give_p, kept_p, kept_q, *rest):
    _, y, z = position()
    *give_q, total = rest
    wide_p = give_p.shape[1]
    half = keep.shape[0] // 2
    total[...] = keep[...] + came[...].astype(F32)
    give_p[...] = total[aligned((1 - y) * half, half), :wide_p].astype(BF16)
    mine = aligned(y * half, half)
    kept_p[:, :CUT] = total[mine, :CUT]
    kept_p[:, CUT:] = total[mine, CUT:wide_p].astype(BF16).astype(F32)
    piece = kept_q.shape[0]
    kept_q[...] = total[aligned(z * piece, piece), wide_p:]
    for other, ref in enumerate(give_q, 1):
        ref[...] = total[aligned((z ^ other) * piece, piece), wide_p:].astype(BF16)


def second_kernel(after, kept_p, came_p, kept_q, *rest):
    _, y, z = position()
    count = (len(rest) - 5) // 2
    came_q, (give_q, left_q, left_p) = rest[:count], rest[count : count + 3]
    *give_p, total_p, total_q = rest[count + 3 :]
    total_p[...] = kept_p[...] + came_p[...].astype(F32)
    piece = left_p.shape[0]
    mine = aligned(z * piece, piece)
    left_p[:, :CUT] = total_p[mine, :CUT]
    left_p[:, CUT:] = total_p[mine, CUT:].astype(BF16).astype(F32)
    for other, ref in enumerate(give_p, 1):
        ref[...] = total_p[aligned((z ^ other) * piece, piece), :].astype(BF16)
    total = kept_q[...]
    for ref in came_q:
        total = total + ref[...].astype(F32)
    total_q[...] = total
    half = give_q.shape[0]
    give_q[...] = total_q[aligned((1 - y) * half, half), :].astype(BF16)
    left_q[...] = total_q[aligned(y * half, half), :]


def third_kernel(left_p, left_q, came_q, *rest):
    _, _, z = position()
    *came_p, piece_p, piece_q, bias = rest
    total = left_p[:, :CUT]
    for ref in came_p:
        total = total + ref[:, :CUT].astype(F32)
    piece_p[...] = total.astype(BF16)
    piece_q[...] = (left_q[...] + came_q[...].astype(F32)).astype(BF16)
    terms = [left_p[:8, CUT:]] + [ref[...].astype(F32)[:8, CUT:] for ref in came_p]
    total = jnp.zeros_like(terms[0])
    for source in range(len(terms)):
        for other, term in enumerate(terms):
            total = total + jnp.where((z ^ other) == source, term, 0.0)
    bias[...] = total


def fourth_kernel(piece_q, other_q, *rest):
    _, y, z = position()
    *parts_p, block_p, block_q = rest
    piece = parts_p[0].shape[0]
    for other, part in enumerate(parts_p):
        block_p[aligned((z ^ other) * piece, piece), :] = part[...]
    piece = piece_q.shape[0]
    block_q[aligned(y * piece, piece), :] = piece_q[...]
    block_q[aligned((1 - y) * piece, piece), :] = other_q[...]


def fifth_kernel(weight_qkv, params, bias, block_p, other_p, *rest):
    *parts_q, half, row = rest
    core, y, z = position()
    rows = half.shape[0]
    mine = aligned(core * rows, rows)
    piece = block_p.shape[0]
    half[aligned(y * piece, piece), :CUT] = block_p[...]
    half[aligned((1 - y) * piece, piece), :CUT] = other_p[...]
    piece = parts_q[0].shape[0]
    for other, part in enumerate(parts_q):
        half[aligned((z ^ other) * piece, piece), CUT:] = part[...]
    three = weight_qkv.shape[1]
    wide = half[:, :three].astype(F32)
    gain_half = jnp.sum(wide * weight_qkv[mine, :].astype(F32), axis=1, keepdims=True)
    gain_half = jnp.broadcast_to(gain_half, (rows, GROUP)).T[:8]
    own_gain = jnp.where(core == 0, params[0:1, :rows], params[0:1, rows:])
    gain_half = gain_half / own_gain
    out = half[:, three:].astype(F32)
    square = jnp.sum(jnp.sum(wide * wide, axis=0, keepdims=True), axis=1, keepdims=True)
    square = square + jnp.sum(jnp.sum(out * out, axis=0, keepdims=True), axis=1, keepdims=True)
    square = square + jnp.sum(gain_half[:1] * gain_half[:1], axis=1, keepdims=True)
    square = square + 0.5 * jnp.sum(bias[:1, :] * bias[:1, :], axis=1, keepdims=True)
    row[:, :rows] = gain_half
    row[:, rows:] = jnp.broadcast_to(square, (8, GROUP))


def last_kernel(
    half, other, row, row_core, row_section, row_both, bias,
    grad_qkv, grad_out, grad_gain, grad_bias,
    qkv_v, out_v, gain_v, bias_v, sems,
    *, entries,
):
    core, _, _ = position()
    rows, three = half.shape[0], grad_qkv.shape[1]
    square = row[:1, rows : rows + 1] + row_core[:1, rows : rows + 1]
    square = square + (row_section[:1, rows : rows + 1] + row_both[:1, rows : rows + 1])
    factor = jnp.minimum(1.0, lax.rsqrt(square / entries + 1e-06))
    sent = []
    piece = 64
    for which, ref in enumerate((half, other)):
        base = core * rows if which == 0 else (1 - core) * rows
        for part in range(rows // piece):
            here = slice(part * piece, (part + 1) * piece)
            at = aligned(base + part * piece, piece)
            slot = slice(which * rows + part * piece, which * rows + (part + 1) * piece)
            qkv_v[slot, :] = ref[here, :three].astype(F32) * factor
            sent.append(started(qkv_v.at[slot, :], grad_qkv.at[at, :], sems, len(sent)))
            out_v[slot, :] = ref[here, three:].astype(F32) * factor
            sent.append(started(out_v.at[slot, :], grad_out.at[at, :], sems, len(sent)))
    mine, its = row[:1, :rows] * factor, row_core[:1, :rows] * factor
    gain_v[:, :rows] = jnp.where(core == 0, mine, its)
    gain_v[:, rows:] = jnp.where(core == 0, its, mine)
    bias_v[...] = bias[:1, : bias_v.shape[1]] * factor
    sent.append(started(gain_v, grad_gain, sems, len(sent)))
    sent.append(started(bias_v, grad_bias, sems, len(sent)))
    for copy in sent:
        copy.wait()


def sent_round(pieces, axis):
    return [swapped(piece, axis, other) for other, piece in enumerate(pieces, 1)]


def vmem(dims, dtype):
    return pltpu.VMEM(dims, dtype)


def copies(number):
    return pltpu.SemaphoreType.DMA((number,))


def body(inputs, cotangent, land_sea, gains, qkv_weight, out_weight, land_bias):
    weight_qkv, weight_out = qkv_weight[0], out_weight[0]
    levels, lats, cols, width = inputs.shape[1:]
    heads = land_bias.shape[1]
    half = levels * lats * SHIFT
    count = 2 * half
    packed = half * 2 + 16
    lons = lax.axis_size("lon")

    tokens = inputs.transpose(0, 2, 3, 1, 4)
    own_cot = cotangent.transpose(0, 2, 3, 1, 4)

    own, rim = call(
        pack_kernel,
        [shape((2 * half, width), BF16), shape((packed, width), BF16)],
        scratch=[
            vmem(tokens.shape, BF16),
            vmem(tokens.shape, BF16),
            vmem(land_sea.shape, jnp.int32),
            vmem((2 * half, width), F32),
            vmem((packed, width), F32),
            copies(3),
        ],
        places="hhh",
        operands=(tokens, own_cot, land_sea),
        limit=60,
    )
    rim = from_behind(rim, "lon", -1)
    own, qkv_v, qkv_t, out_v, params = call(
        ready_kernel,
        [
            shape(own.shape, BF16),
            shape(weight_qkv.shape, BF16),
            shape(weight_qkv.shape[::-1], BF16),
            shape(weight_out.shape, BF16),
            shape((16, width), F32),
        ],
        scratch=[
            vmem(gains.shape, F32),
            vmem(land_sea.shape, jnp.int32),
            vmem(land_bias.shape, F32),
            copies(6),
        ],
        places="hhhhhh",
        operands=(own, weight_qkv, weight_out, gains, land_sea, land_bias),
        limit=48,
    )
    skip, cot, normed_t, qkv, probs, attended_t, extra, normed = call(
        functools.partial(forward_kernel, heads=heads, lats=lats, cols=cols),
        [
            shape((count, width), BF16),
            shape((count, width), BF16),
            shape((width, count), BF16),
            shape((count, 3 * width), BF16),
            shape((heads * count, count), BF16),
            shape((width, count), BF16),
            shape((count, 2 * GROUP), F32),
            shape((count, width), F32),
        ],
        scratch=[
            vmem((heads * count, count), F32),
            vmem((width, count), BF16),
            vmem((width, count), BF16),
            vmem((width, count), BF16),
            vmem((count, 3 * width), BF16),
        ],
        operands=(own, rim, qkv_v, qkv_t, out_v, params),
        flops=10**9,
        limit=16,
    )
    skip = passed_along(skip, "section", -1)
    rows, wide = width // 2, 4 * width + GROUP
    total, grad_proj, bias_row, give = call(
        functools.partial(backward_kernel, heads=heads),
        [
            shape((count, width), BF16),
            shape((count, 3 * width), BF16),
            shape((8, GROUP), F32),
            shape((rows, wide), BF16),
        ],
        scratch=[vmem((width, count), BF16)],
        operands=(skip, cot, qkv, probs, out_v, extra, normed_t, attended_t),
        flops=10**9,
    )
    came = swapped(give, "lat", 1)
    keep, own_grad, back = call(
        finish_kernel,
        [
            shape((rows, wide), F32),
            shape((half, width), F32),
            shape((half, width), BF16),
        ],
        operands=(
            total, grad_proj, bias_row, normed_t, attended_t, normed, extra, qkv_t, params,
        ),
        flops=5 * 10**8,
    )
    back = from_behind(back, "lon", 1)
    entries = 2 * (4 * width * width + width + heads)
    if rows // 2 // lons % 16 == 0 and lons & (lons - 1) == 0:
        grads = staged(keep, came, back, qkv_v, params, lons, heads, entries)
    else:
        grads = plain(keep, came, weight_qkv, gains, heads, entries)
    (final_grad,) = call(
        unpack_kernel,
        [shape(tokens.shape, F32)],
        scratch=[vmem(tokens.shape, F32), copies(1)],
        out_places="h",
        operands=(own_grad, back),
    )
    final_grad = final_grad.transpose(0, 3, 1, 2, 4)
    return (final_grad, *(grad[None] for grad in grads))


def staged(keep, came, after, weight_qkv, params, lons, heads, entries):
    rows, wide = keep.shape
    width = 2 * rows
    wide_p = CUT + GROUP
    wide_q = wide - wide_p
    some = range(lons - 1)
    several = "v" * len(some)
    give_p, kept_p, kept_q, *give_q = call(
        first_kernel,
        [
            shape((rows // 2, wide_p), BF16),
            shape((rows // 2, wide_p), F32),
            shape((rows // lons, wide_q), F32),
            *(shape((rows // lons, wide_q), BF16) for _ in some),
        ],
        scratch=[vmem((rows, wide), F32)],
        operands=(keep, came),
    )
    came_p = swapped(give_p, "lat", 2)
    came_q = sent_round(give_q, "lon")
    piece = rows // 2 // lons
    give_q, left_q, left_p, *give_p = call(
        second_kernel,
        [
            shape((piece, wide_q), BF16),
            shape((piece, wide_q), F32),
            shape((piece, wide_p), F32),
            *(shape((piece, wide_p), BF16) for _ in some),
        ],
        scratch=[vmem((rows // 2, wide_p), F32), vmem((rows // lons, wide_q), F32)],
        places="avvv" + several,
        operands=(after, kept_p, came_p, kept_q, *came_q),
    )
    came_p = sent_round(give_p, "lon")
    came_q = swapped(give_q, "lat", 2)
    piece_p, piece_q, bias = call(
        third_kernel,
        [
            shape((piece, CUT), BF16),
            shape((piece, wide_q), BF16),
            shape((8, GROUP), F32),
        ],
        operands=(left_p, left_q, came_q, *came_p),
    )
    others_p = sent_round([piece_p for _ in some], "lon")
    other_q = swapped(piece_q, "lat", 2)
    block_p, block_q = call(
        fourth_kernel,
        [shape((rows // 2, CUT), BF16), shape((rows // lons, wide_q), BF16)],
        operands=(piece_q, other_q, piece_p, *others_p),
    )
    other_p = swapped(block_p, "lat", 2)
    others_q = sent_round([block_q for _ in some], "lon")
    half, row = call(
        fifth_kernel,
        [shape((rows, 4 * width), BF16), shape((8, rows + GROUP), F32)],
        operands=(weight_qkv, params, bias, block_p, other_p, block_q, *others_q),
    )
    row_section = swapped(row, "section", 1)
    row_both = lax.ppermute(row, ("section", "lat"), across())
    row_core = swapped(row, "lat", 1)
    other = swapped(half, "lat", 1)
    grads = call(
        functools.partial(last_kernel, entries=entries),
        [
            shape((width, 3 * width), F32),
            shape((width, width), F32),
            shape((1, width), F32),
            shape((1, heads), F32),
        ],
        scratch=[
            vmem((width, 3 * width), F32),
            vmem((width, width), F32),
            vmem((1, width), F32),
            vmem((1, heads), F32),
            copies(4 * rows // 64 + 2),
        ],
        out_places="hhhh",
        operands=(half, other, row, row_core, row_section, row_both, bias),
    )
    return grads[0], grads[1], grads[2][0], grads[3][0]


def across():
    sections, lats = lax.axis_size("section"), lax.axis_size("lat")
    return [
        (s * lats + i, (sections - 1 - s) * lats + (i ^ 1))
        for s in range(sections)
        for i in range(lats)
    ]


def split_two(block, axis, bit):
    mine = (lax.axis_index(axis) // bit) % 2
    pair = block.reshape(2, block.shape[0] // 2, -1)
    give = lax.dynamic_index_in_dim(pair, 1 - mine, 0, keepdims=False).astype(BF16)
    return give, lax.dynamic_index_in_dim(pair, mine, 0, keepdims=False)


def doubled(block, axis, bit):
    mine = (lax.axis_index(axis) // bit) % 2
    other = swapped(block, axis, bit)
    low = jnp.where(mine == 0, block, other)
    high = jnp.where(mine == 0, other, block)
    return jnp.concatenate([low, high], axis=0)


def scattered(block, axis):
    count = lax.axis_size(axis)
    mine = lax.axis_index(axis)
    pieces = block.reshape(count, block.shape[0] // count, -1)
    total = lax.dynamic_index_in_dim(pieces, mine, 0, keepdims=False)
    others = []
    for by in range(1, count):
        give = lax.dynamic_index_in_dim(pieces, (mine + by) % count, 0, keepdims=False)
        others.append(from_behind(give.astype(BF16), axis, by))
    for other in others:
        total = total + other.astype(F32)
    return total, others


def gathered(block, axis):
    count = lax.axis_size(axis)
    mine = lax.axis_index(axis)
    whole = jnp.zeros((count,) + block.shape, block.dtype)
    whole = lax.dynamic_update_index_in_dim(whole, block, mine, 0)
    for by in range(1, count):
        whole = lax.dynamic_update_index_in_dim(
            whole, from_behind(block, axis, by), (mine - by) % count, 0
        )
    return whole.reshape(count * block.shape[0], -1)


def sum_squares(block):
    wide = block.astype(F32)
    return jnp.sum(wide * wide)


def plain(keep, came, weight_qkv, gains, heads, entries):
    width = gains.shape[1]
    lat, lon = lax.axis_index("lat"), lax.axis_index("lon")
    part = keep + came.astype(F32)
    give, keep = split_two(part, "lat", 2)
    came = swapped(give, "lat", 2).astype(F32)
    column = lax.broadcasted_iota(jnp.int32, keep.shape, 1)
    is_bias = (column >= CUT) & (column < CUT + GROUP)
    part = jnp.where(is_bias, lax.reduce_precision(keep, 8, 7), keep) + came
    bias_part = lax.reduce_precision(part[:1, CUT : CUT + GROUP], 8, 7)
    part, others = scattered(part, "lon")
    terms = [bias_part] + [other[:1, CUT : CUT + GROUP].astype(F32) for other in others]
    terms = jnp.concatenate(terms[:1] + terms[:0:-1], axis=0)
    bias = jnp.sum(jnp.roll(terms, lon, axis=0), axis=0)[:heads]
    part = jnp.concatenate([part[:, :CUT], part[:, CUT + GROUP :]], axis=1).astype(BF16)
    half = doubled(gathered(part, "lon"), "lat", 2)
    mine = lat % 2
    weight_half = lax.dynamic_slice_in_dim(weight_qkv, mine * (width // 2), width // 2, 0)
    gain_half = lax.dynamic_slice_in_dim(gains[0], mine * (width // 2), width // 2, 0)
    weighed = half[:, : 3 * width].astype(F32) * weight_half.astype(F32)
    gain_half = jnp.sum(weighed, axis=1) / gain_half
    square = sum_squares(half) + sum_squares(gain_half) + 0.5 * sum_squares(bias)
    square = square.reshape(1)
    square = square + swapped(square, "lat", 1)
    square = square + swapped(square, "section", 1)
    factor = jnp.minimum(1.0, lax.rsqrt(square[0] / entries + 1e-06))
    grads = doubled(half, "lat", 1).astype(F32) * factor
    gain = doubled(gain_half.reshape(-1, 1), "lat", 1)[:, 0] * factor
    return grads[:, : 3 * width], grads[:, 3 * width :], gain, bias * factor


def solution(mesh):
    placed = (
        P("section", None, "lat", "lon", None),
        P("section", None, "lat", "lon", None),
        P("lat", "lon"),
        P("section", None),
        P("section", None, None),
        P("section", None, None),
        P("section", None),
    )
    return jax.shard_map(
        body,
        mesh=mesh,
        in_specs=placed,
        out_specs=(
            P("section", None, "lat", "lon", None),
            P("section", None, None),
            P("section", None, None),
            P("section", None),
            P("section", None),
        ),
        check_vma=False,
    )
```

time: 102 us -> 81.9 us (0.80)
  Pallas kernels: 23.1 us -> 15.4 us
  local copies, waits for them, and re-layouts: 12.2 us -> 5.38 us
  waiting for transfers between devices: 34 us -> 30.6 us
  starting transfers between devices: 31.2 us -> 29.5 us
    pallas_call x15 -> x12, Pallas kernels: 23.1 us -> 15.4 us  [call(): pl.pallas_call(kernel, out_shape=list(outs), in_specs=[pl.BlockSpec(memor...]
    unnamed x34 -> x12, local copies, waits for them, and re-layouts: 12.2 us -> 5.38 us
    ppermute x20, waiting for transfers between devices: 20.2 us -> 18.3 us  [swapped(): return lax.ppermute(value, axis, [(i, i ^ bit) for i in range(count)])]
    ppermute x2, waiting for transfers between devices: 7.79 us -> 6.15 us  [from_behind(): lax.ppermute(value, axis, [(i, (i + by) % count) for i in range(count)])]
    ppermute x20, starting transfers between devices: 24.6 us -> 23 us  [swapped(): return lax.ppermute(value, axis, [(i, i ^ bit) for i in range(count)])]
  transfers between devices with their start and end apart: 24 -> 24, of which waited for: 11 -> 11; matrix products, arithmetic and copies ran while one was open for 0% -> 0% of each run, Pallas kernels for 5% -> 3%
where the time goes in v6:
time: 81.9 us; the launch traced here: 81.6 us
  waiting for transfers between devices  30.6 us (37%)
  starting transfers between devices  29.5 us (36%)
  Pallas kernels  15.4 us (19%)
  local copies, waits for them, and re-layouts  5.38 us (7%)
    ppermute x20, starting transfers between devices, swapped(): return lax.ppermute(value, axis, [(i, i ^ bit) for i in range(count)])  23 us
    ppermute x20, waiting for transfers between devices, swapped(): return lax.ppermute(value, axis, [(i, i ^ bit) for i in range(count)])  18.3 us
    pallas_call x12, Pallas kernels, call(): pl.pallas_call(kernel, out_shape=list(outs), in_specs=[pl.BlockSpec(memor...  15.4 us
    ppermute x2, waiting for transfers between devices, from_behind(): lax.ppermute(value, axis, [(i, (i + by) % count) for i in range(count)])  6.15 us
    ppermute x1, waiting for transfers between devices, passed_along(): return lax.ppermute(block, axis, route)  5.9 us
    unnamed x12, local copies, waits for them, and re-layouts  5.38 us
    ppermute x2, starting transfers between devices, from_behind(): lax.ppermute(value, axis, [(i, (i + by) % count) for i in range(count)])  5.1 us
  transfers between devices with their start and end apart: 24, of which 11 were waited for; matrix products, arithmetic and copies ran while one was open for 0% of the time, Pallas kernels for 3%

profile of v6, /device:TPU:0, one launch (start us, length us, event | category | flops | bytes accessed | tf_op | source)
XLA Modules:
  0.0 81.6 jit_solution(4176683257059360738)
XLA Ops:
  0.6 1.8 %shard_map.110 = (bf16[144,512]{1,0:T(8,128)(2,1)}, bf16[160,512]{1,0:T(8,128)(2,1)}) custom-call(bf16[1,6,12,2,512]{4,3,2,1,0:T(2,128)(2,1)} %bitcast.12, bf16[1,6,12,2,512]{4,3,2,1,0:T(2,128)(2,1)} %bitcast.13, s32[6,12]{1,0:T(8,128)} %land.3), custom_call_target="tpu_custom_call" | custom-call | flops 100000000 | bytes 606496 | tf_op jit(solution)/shard_map/pallas_call | solution.py:47
  2.5 5.1 %collective-permute-start = (bf16[160,512]{1,0:T(8,128)(2,1)}, bf16[160,512]{1,0:T(8,128)(2,1)S(1)}, u32[]{:S(2)}, u32[]{:S(2)}) collective-permute-start(bf16[160,512]{1,0:T(8,128)(2,1)} %get-tuple-element.52), channel_id=1, source_target_pairs={{0,12},{4,0},{8,4},{12,8},{1,13},{5,1},{9,5},{13,9},{2,14},{6,2},{... | collective-permute-start | bytes 491528 | tf_op jit(solution)/shard_map/ppermute | solution.py:20
  7.6 1.4 %copy-done = bf16[1,512,1536]{2,1,0:T(8,128)(2,1)S(1)} copy-done((bf16[1,512,1536]{2,1,0:T(8,128)(2,1)S(1)}, bf16[1,512,1536]{2,1,0:T(8,128)(2,1)}, u32[]{:S(2)}) %copy-start) | copy-done | bytes 1572888
  9.0 1.0 %copy-done.1 = bf16[1,512,512]{2,1,0:T(8,128)(2,1)S(1)} copy-done((bf16[1,512,512]{2,1,0:T(8,128)(2,1)S(1)}, bf16[1,512,512]{2,1,0:T(8,128)(2,1)}, u32[]{:S(2)}) %copy-start.1) | copy-done | bytes 524312
  10.0 0.9 %copy-done.2 = bf16[144,512]{1,0:T(8,128)(2,1)S(1)} copy-done((bf16[144,512]{1,0:T(8,128)(2,1)S(1)}, bf16[144,512]{1,0:T(8,128)(2,1)}, u32[]{:S(2)}) %copy-start.2) | copy-done | bytes 147480
  10.9 0.7 copy-done.3
  11.6 0.7 copy-done.4
  12.3 0.7 copy-done.5
  13.0 0.9 %shard_map.111 = (bf16[144,512]{1,0:T(8,128)(2,1)S(1)}, bf16[512,1536]{1,0:T(8,128)(2,1)S(1)}, bf16[1536,512]{1,0:T(8,128)(2,1)S(1)}, bf16[512,512]{1,0:T(8,128)(2,1)S(1)}, f32[16,512]{1,0:T(8,128)S(1)}) custom-call(bf16[144,512]{1,0:T(8,128)(2,1)S(1)} %copy-done.2, bf16[512,1536]{1,0:T(8,128)(2,1)S(1)} %bitcast.7, bf16[512,512]{1,0:T(8,128)(2,1)S(1)} %bitcast.8, ...), custom_call_target="tpu_custom_call" | custom-call | flops 100000000 | bytes 6097248 | tf_op jit(solution)/shard_map/pallas_call | solution.py:47
  13.8 0.0 collective-permute-done.rim
  13.8 4.8 %shard_map.112 = (bf16[144,512]{1,0:T(8,128)(2,1)S(1)}, bf16[144,512]{1,0:T(8,128)(2,1)S(1)}, bf16[512,144]{1,0:T(8,128)(2,1)S(1)}, bf16[144,1536]{1,0:T(8,128)(...) custom-call(bf16[144,512]{1,0:T(8,128)(2,1)S(1)} %get-tuple-element., ...), custom_call_target="tpu_custom_call" | custom-call | flops 1000000000 | bytes 6152192 | tf_op jit(solution)/shard_map/pallas_call | solution.py:47
  18.6 1.3 %collective-permute-start.1 = (bf16[144,512]{1,0:T(8,128)(2,1)S(1)}, bf16[144,512]{1,0:T(8,128)(2,1)S(1)}, u32[]{:S(2)}, u32[]{:S(2)}) collective-permute-start(bf16[144,512]{1,0:T(8,128)(2,1)S(1)} %get-tuple-element.57), channel_id=1, source_target_pairs={{16,0},{17,1},{18,2},{19,3},{20,4},{21,5},{22,6},{23,7},{24,8},{25... | collective-permute-start | bytes 442376 | tf_op jit(solution)/shard_map/ppermute | solution.py:26
  19.9 5.9 %collective-permute-done.1.skip = bf16[144,512]{1,0:T(8,128)(2,1)S(1)} collective-permute-done((bf16[144,512]{1,0:T(8,128)(2,1)S(1)}, bf16[144,512]{1,0:T(8,128)(2,1)S(1)}, u32[]{:S(2)}, u32[]{:S(2)}) %collective-permute-start.1) | collective-permute-done | bytes 147488 | tf_op jit(solution)/shard_map/ppermute | solution.py:26
  25.8 2.9 %shard_map.113 = (bf16[144,512]{1,0:T(8,128)(2,1)S(1)}, bf16[144,1536]{1,0:T(8,128)(2,1)S(1)}, f32[8,128]{1,0:T(8,128)S(1)}, bf16[256,2176]{1,0:T(8,128)(2,1)S(1)}) custom-call(bf16[144,512]{1,0:T(8,128)(2,1)S(1)} %collective-permute-done.1.skip, bf16[144,512]{1,0:T(8,128)(2,1)S(1)} %get-tuple-element.58.cot, bf16[144,1536]{1,0:T(8,128)(2,1)S(1)} %get-tuple-element.59.qkv, ...), custom_call_target="tpu_custom_call" | custom-call | flops 1000000000 | bytes 4075520 | tf_op jit(solution)/shard_map/pallas_call | solution.py:47
  28.7 0.1 collective-permute-start.3
  28.8 0.8 shard_map.114
  29.6 2.0 %collective-permute-done.3.came = bf16[256,2176]{1,0:T(8,128)(2,1)S(1)} collective-permute-done((bf16[256,2176]{1,0:T(8,128)(2,1)S(1)}, bf16[256,2176]{1,0:T(8,128)(2,1)S(1)}, u32[]{:S(2)}, u32[]{:S(2)}) %collective-permute-start.3) | collective-permute-done | bytes 1114144 | tf_op jit(solution)/shard_map/ppermute | solution.py:31
  31.6 0.4 shard_map.116
  32.0 1.6 %collective-permute-start.4 = (bf16[128,1408]{1,0:T(8,128)(2,1)S(1)}, bf16[128,1408]{1,0:T(8,128)(2,1)S(1)}, u32[]{:S(2)}, u32[]{:S(2)}) collective-permute-start(bf16[128,1408]{1,0:T(8,128)(2,1)S(1)} %get-tuple-element.73), channel_id=1, source_target_pairs={{0,2},{1,3},{2,0},{3,1},{4,6},{5,7},{6,4},{7,5},{8,10},{9,11},{10,... | collective-permute-start | bytes 1081352 | tf_op jit(solution)/shard_map/ppermute | solution.py:31
  33.5 0.0 collective-permute-start.5
  33.5 2.1 %collective-permute-start.6 = (bf16[64,768]{1,0:T(8,128)(2,1)S(1)}, bf16[64,768]{1,0:T(8,128)(2,1)S(1)}, u32[]{:S(2)}, u32[]{:S(2)}) collective-permute-start(bf16[64,768]{1,0:T(8,128)(2,1)S(1)} %get-tuple-element.76), channel_id=1, source_target_pairs={{0,8},{4,12},{8,0},{12,4},{1,9},{5,13},{9,1},{13,5},{2,10},{6,14},... | collective-permute-start | bytes 294920 | tf_op jit(solution)/shard_map/ppermute | solution.py:31
  35.6 2.3 %collective-permute-start.7 = (bf16[64,768]{1,0:T(8,128)(2,1)S(1)}, bf16[64,768]{1,0:T(8,128)(2,1)S(1)}, u32[]{:S(2)}, u32[]{:S(2)}) collective-permute-start(bf16[64,768]{1,0:T(8,128)(2,1)S(1)} %get-tuple-element.77), channel_id=1, source_target_pairs={{0,12},{4,8},{8,4},{12,0},{1,13},{5,9},{9,5},{13,1},{2,14},{6,10},... | collective-permute-start | bytes 294920 | tf_op jit(solution)/shard_map/ppermute | solution.py:31
  37.9 0.0 collective-permute-start.2
  37.9 6.1 %collective-permute-done.2.back.after = bf16[72,512]{1,0:T(8,128)(2,1)S(1)} collective-permute-done((bf16[72,512]{1,0:T(8,128)(2,1)S(1)}, bf16[72,512]{1,0:T(8,128)(2,1)S(1)}, u32[]{:S(2)}, u32[]{:S(2)}) %collective-permute-start.2) | collective-permute-done | bytes 73760 | tf_op jit(solution)/shard_map/ppermute | solution.py:20
  44.1 0.0 collective-permute-done.5.rest_0_
  44.1 1.8 %collective-permute-done.6.rest_1_ = bf16[64,768]{1,0:T(8,128)(2,1)S(1)} collective-permute-done((bf16[64,768]{1,0:T(8,128)(2,1)S(1)}, bf16[64,768]{1,0:T(8,128)(2,1)S(1)}, u32[]{:S(2)}, u32[]{:S(2)}) %collective-permute-start.6) | collective-permute-done | bytes 98336 | tf_op jit(solution)/shard_map/ppermute | solution.py:31
  45.9 0.0 collective-permute-done.7.rest_2_
  45.9 0.0 collective-permute-done.4.came_p
  45.9 0.2 shard_map.117
  46.1 1.7 %collective-permute-start.9 = (bf16[32,1408]{1,0:T(8,128)(2,1)S(1)}, bf16[32,1408]{1,0:T(8,128)(2,1)S(1)}, u32[]{:S(2)}, u32[]{:S(2)}) collective-permute-start(bf16[32,1408]{1,0:T(8,128)(2,1)S(1)} %get-tuple-element.81), channel_id=1, source_target_pairs={{0,4},{4,0},{8,12},{12,8},{1,5},{5,1},{9,13},{13,9},{2,6},{6,2},{1... | collective-permute-start | bytes 270344 | tf_op jit(solution)/shard_map/ppermute | solution.py:31
  47.8 0.2 collective-permute-start.10
  47.9 2.6 %collective-permute-start.11 = (bf16[32,1408]{1,0:T(8,128)(2,1)S(1)}, bf16[32,1408]{1,0:T(8,128)(2,1)S(1)}, u32[]{:S(2)}, u32[]{:S(2)}) collective-permute-start(bf16[32,1408]{1,0:T(8,128)(2,1)S(1)} %get-tuple-element.83), channel_id=1, source_target_pairs={{0,12},{4,8},{8,4},{12,0},{1,13},{5,9},{9,5},{13,1},{2,14},{6,10},... | collective-permute-start | bytes 270344 | tf_op jit(solution)/shard_map/ppermute | solution.py:31
  50.5 0.5 collective-permute-start.8
  51.0 3.6 %collective-permute-done.8.came_q = bf16[32,768]{1,0:T(8,128)(2,1)S(1)} collective-permute-done((bf16[32,768]{1,0:T(8,128)(2,1)S(1)}, bf16[32,768]{1,0:T(8,128)(2,1)S(1)}, u32[]{:S(2)}, u32[]{:S(2)}) %collective-permute-start.8) | collective-permute-done | bytes 49184 | tf_op jit(solution)/shard_map/ppermute | solution.py:31
  54.6 0.0 collective-permute-done.9.rest_0_
  54.6 1.8 %collective-permute-done.10.rest_1_ = bf16[32,1408]{1,0:T(8,128)(2,1)S(1)} collective-permute-done((bf16[32,1408]{1,0:T(8,128)(2,1)S(1)}, bf16[32,1408]{1,0:T(8,128)(2,1)S(1)}, u32[]{:S(2)}, u32[]{:S(2)}) %collective-permute-start.10) | collective-permute-done | bytes 90144 | tf_op jit(solution)/shard_map/ppermute | solution.py:31
  56.5 0.0 collective-permute-done.11.rest_2_
  56.5 0.1 shard_map.118
  56.5 1.9 %collective-permute-start.15 = (bf16[32,1280]{1,0:T(8,128)(2,1)S(1)}, bf16[32,1280]{1,0:T(8,128)(2,1)S(1)}, u32[]{:S(2)}, u32[]{:S(2)}) collective-permute-start(bf16[32,1280]{1,0:T(8,128)(2,1)S(1)} %get-tuple-element.86.rest_0_), channel_id=1, source_target_pairs={{0,12},{4,8},{8,4},{12,0},{1,13},{5,9},{9,5},{13,1},{2,14},{6,10},... | collective-permute-start | bytes 245768 | tf_op jit(solution)/shard_map/ppermute | solution.py:31
  58.4 1.2 %collective-permute-start.14 = (bf16[32,1280]{1,0:T(8,128)(2,1)S(1)}, bf16[32,1280]{1,0:T(8,128)(2,1)S(1)}, u32[]{:S(2)}, u32[]{:S(2)}) collective-permute-start(bf16[32,1280]{1,0:T(8,128)(2,1)S(1)} %get-tuple-element.86.rest_0_), channel_id=1, source_target_pairs={{0,8},{4,12},{8,0},{12,4},{1,9},{5,13},{9,1},{13,5},{2,10},{6,14},... | collective-permute-start | bytes 245768 | tf_op jit(solution)/shard_map/ppermute | solution.py:31
  59.6 1.4 %collective-permute-start.13 = (bf16[32,1280]{1,0:T(8,128)(2,1)S(1)}, bf16[32,1280]{1,0:T(8,128)(2,1)S(1)}, u32[]{:S(2)}, u32[]{:S(2)}) collective-permute-start(bf16[32,1280]{1,0:T(8,128)(2,1)S(1)} %get-tuple-element.86.rest_0_), channel_id=1, source_target_pairs={{0,4},{4,0},{8,12},{12,8},{1,5},{5,1},{9,13},{13,9},{2,6},{6,2},{1... | collective-permute-start | bytes 245768 | tf_op jit(solution)/shard_map/ppermute | solution.py:31
  61.0 0.5 collective-permute-start.12
  61.5 4.0 %collective-permute-done.12.other_q = bf16[32,768]{1,0:T(8,128)(2,1)S(1)} collective-permute-done((bf16[32,768]{1,0:T(8,128)(2,1)S(1)}, bf16[32,768]{1,0:T(8,128)(2,1)S(1)}, u32[]{:S(2)}, u32[]{:S(2)}) %collective-permute-start.12) | collective-permute-done | bytes 49184 | tf_op jit(solution)/shard_map/ppermute | solution.py:31
  65.5 0.0 collective-permute-done.15.rest_3_
  65.5 0.0 collective-permute-done.14.rest_2_
  65.5 0.0 collective-permute-done.13.rest_1_
  65.6 0.6 collective-permute-start.16
  66.2 1.9 %collective-permute-start.19 = (bf16[64,768]{1,0:T(8,128)(2,1)S(1)}, bf16[64,768]{1,0:T(8,128)(2,1)S(1)}, u32[]{:S(2)}, u32[]{:S(2)}) collective-permute-start(bf16[64,768]{1,0:T(8,128)(2,1)S(1)} %get-tuple-element.88.rest_0_), channel_id=1, source_target_pairs={{0,12},{4,8},{8,4},{12,0},{1,13},{5,9},{9,5},{13,1},{2,14},{6,10},... | collective-permute-start | bytes 294920 | tf_op jit(solution)/shard_map/ppermute | solution.py:31
  68.1 0.0 collective-permute-start.18
  68.1 2.5 %collective-permute-start.17 = (bf16[64,768]{1,0:T(8,128)(2,1)S(1)}, bf16[64,768]{1,0:T(8,128)(2,1)S(1)}, u32[]{:S(2)}, u32[]{:S(2)}) collective-permute-start(bf16[64,768]{1,0:T(8,128)(2,1)S(1)} %get-tuple-element.88.rest_0_), channel_id=1, source_target_pairs={{0,4},{4,0},{8,12},{12,8},{1,5},{5,1},{9,13},{13,9},{2,6},{6,2},{1... | collective-permute-start | bytes 294920 | tf_op jit(solution)/shard_map/ppermute | solution.py:31
  70.6 2.3 %collective-permute-done.19.rest_3_ = bf16[64,768]{1,0:T(8,128)(2,1)S(1)} collective-permute-done((bf16[64,768]{1,0:T(8,128)(2,1)S(1)}, bf16[64,768]{1,0:T(8,128)(2,1)S(1)}, u32[]{:S(2)}, u32[]{:S(2)}) %collective-permute-start.19) | collective-permute-done | bytes 98336 | tf_op jit(solution)/shard_map/ppermute | solution.py:31
  72.8 2.0 %collective-permute-done.18.rest_2_ = bf16[64,768]{1,0:T(8,128)(2,1)S(1)} collective-permute-done((bf16[64,768]{1,0:T(8,128)(2,1)S(1)}, bf16[64,768]{1,0:T(8,128)(2,1)S(1)}, u32[]{:S(2)}, u32[]{:S(2)}) %collective-permute-start.18) | collective-permute-done | bytes 98336 | tf_op jit(solution)/shard_map/ppermute | solution.py:31
  74.9 0.0 collective-permute-done.17.rest_1_
  74.9 0.0 collective-permute-done.16.other_p
  74.9 0.5 shard_map.120
  75.4 0.0 collective-permute-start.20
  75.4 0.1 collective-permute-start.23
  75.5 2.1 %collective-permute-start.22 = (f32[8,384]{1,0:T(8,128)S(1)}, f32[8,384]{1,0:T(8,128)S(1)}, u32[]{:S(2)}, u32[]{:S(2)}) collective-permute-start(f32[8,384]{1,0:T(8,128)S(1)} %get-tuple-element.90.row), channel_id=1, source_target_pairs={{0,16},{16,0},{1,17},{17,1},{2,18},{18,2},{3,19},{19,3},{4,20},{20... | collective-permute-start | bytes 36872 | tf_op jit(solution)/shard_map/ppermute | solution.py:31
  77.5 0.0 collective-permute-start.21
  77.5 0.8 shard_map.115
  78.3 0.3 collective-permute-done.23.row_both
  78.6 0.8 collective-permute-done.22.row_section
  79.3 0.0 collective-permute-done.21.row_core
  79.3 2.3 %shard_map.121 = (f32[512,1536]{1,0:T(8,128)}, f32[512,512]{1,0:T(8,128)}, f32[1,512]{1,0:T(1,128)}, f32[1,16]{1,0:T(1,128)}) custom-call(bf16[256,2048]{1,0:T(8,128)(2,1)S(1)} %get-tuple-element.89.half, bf16[256,2048]{1,0:T(8,128)(2,1)S(1)} %collective-permute-done.20.other, f32[8,384]{1,0:T(8,128)S(1)} %get-tuple-element.90.row, ...), custom_call_target="tpu_custom_call" | custom-call | flops 100000000 | bytes 6346816 | tf_op jit(solution)/shard_map/pallas_call | solution.py:47
  (8 shorter events, 0.1 us)
Async XLA Ops:
  2.5 11.4 %collective-permute-start = (bf16[160,512]{1,0:T(8,128)(2,1)}, bf16[160,512]{1,0:T(8,128)(2,1)S(1)}, u32[]{:S(2)}, u32[]{:S(2)}) collective-permute-start(bf16[160,512]{1,0:T(8,128)(2,1)} %get-tuple-element.52), channel_id=1, source_target_pairs={{0,12},{4,0},{8,4},{12,8},{1,13},{5,1},{9,5},{13,9},{2,14},{6,2},{... | collective-permute-start | bytes 491528 | tf_op jit(solution)/shard_map/ppermute | solution.py:20
  7.6 1.4 %copy-start = (bf16[1,512,1536]{2,1,0:T(8,128)(2,1)S(1)}, bf16[1,512,1536]{2,1,0:T(8,128)(2,1)}, u32[]{:S(2)}) copy-start(bf16[1,512,1536]{2,1,0:T(8,128)(2,1)} %param.11) | copy-start | bytes 4718596
  9.0 1.0 %copy-start.1 = (bf16[1,512,512]{2,1,0:T(8,128)(2,1)S(1)}, bf16[1,512,512]{2,1,0:T(8,128)(2,1)}, u32[]{:S(2)}) copy-start(bf16[1,512,512]{2,1,0:T(8,128)(2,1)} %param.12) | copy-start | bytes 1572868
  10.0 0.9 %copy-start.2 = (bf16[144,512]{1,0:T(8,128)(2,1)S(1)}, bf16[144,512]{1,0:T(8,128)(2,1)}, u32[]{:S(2)}) copy-start(bf16[144,512]{1,0:T(8,128)(2,1)} %get-tuple-element.50.own_in) | copy-start | bytes 442372
  10.9 0.7 copy-start.3
  11.6 0.7 copy-start.4
  12.3 0.7 copy-start.5
  18.6 7.2 %collective-permute-start.1 = (bf16[144,512]{1,0:T(8,128)(2,1)S(1)}, bf16[144,512]{1,0:T(8,128)(2,1)S(1)}, u32[]{:S(2)}, u32[]{:S(2)}) collective-permute-start(bf16[144,512]{1,0:T(8,128)(2,1)S(1)} %get-tuple-element.57), channel_id=1, source_target_pairs={{16,0},{17,1},{18,2},{19,3},{20,4},{21,5},{22,6},{23,7},{24,8},{25... | collective-permute-start | bytes 442376 | tf_op jit(solution)/shard_map/ppermute | solution.py:26
  28.7 2.8 %collective-permute-start.3 = (bf16[256,2176]{1,0:T(8,128)(2,1)S(1)}, bf16[256,2176]{1,0:T(8,128)(2,1)S(1)}, u32[]{:S(2)}, u32[]{:S(2)}) collective-permute-start(bf16[256,2176]{1,0:T(8,128)(2,1)S(1)} %get-tuple-element.71), channel_id=1, source_target_pairs={{0,1},{1,0},{2,3},{3,2},{4,5},{5,4},{6,7},{7,6},{8,9},{9,8},{10,11... | collective-permute-start | bytes 3342344 | tf_op jit(solution)/shard_map/ppermute | solution.py:31
  32.0 13.9 %collective-permute-start.4 = (bf16[128,1408]{1,0:T(8,128)(2,1)S(1)}, bf16[128,1408]{1,0:T(8,128)(2,1)S(1)}, u32[]{:S(2)}, u32[]{:S(2)}) collective-permute-start(bf16[128,1408]{1,0:T(8,128)(2,1)S(1)} %get-tuple-element.73), channel_id=1, source_target_pairs={{0,2},{1,3},{2,0},{3,1},{4,6},{5,7},{6,4},{7,5},{8,10},{9,11},{10,... | collective-permute-start | bytes 1081352 | tf_op jit(solution)/shard_map/ppermute | solution.py:31
  33.5 10.5 %collective-permute-start.5 = (bf16[64,768]{1,0:T(8,128)(2,1)S(1)}, bf16[64,768]{1,0:T(8,128)(2,1)S(1)}, u32[]{:S(2)}, u32[]{:S(2)}) collective-permute-start(bf16[64,768]{1,0:T(8,128)(2,1)S(1)} %get-tuple-element.75), channel_id=1, source_target_pairs={{0,4},{4,0},{8,12},{12,8},{1,5},{5,1},{9,13},{13,9},{2,6},{6,2},{1... | collective-permute-start | bytes 294920 | tf_op jit(solution)/shard_map/ppermute | solution.py:31
  33.5 12.3 %collective-permute-start.6 = (bf16[64,768]{1,0:T(8,128)(2,1)S(1)}, bf16[64,768]{1,0:T(8,128)(2,1)S(1)}, u32[]{:S(2)}, u32[]{:S(2)}) collective-permute-start(bf16[64,768]{1,0:T(8,128)(2,1)S(1)} %get-tuple-element.76), channel_id=1, source_target_pairs={{0,8},{4,12},{8,0},{12,4},{1,9},{5,13},{9,1},{13,5},{2,10},{6,14},... | collective-permute-start | bytes 294920 | tf_op jit(solution)/shard_map/ppermute | solution.py:31
  35.6 10.3 %collective-permute-start.7 = (bf16[64,768]{1,0:T(8,128)(2,1)S(1)}, bf16[64,768]{1,0:T(8,128)(2,1)S(1)}, u32[]{:S(2)}, u32[]{:S(2)}) collective-permute-start(bf16[64,768]{1,0:T(8,128)(2,1)S(1)} %get-tuple-element.77), channel_id=1, source_target_pairs={{0,12},{4,8},{8,4},{12,0},{1,13},{5,9},{9,5},{13,1},{2,14},{6,10},... | collective-permute-start | bytes 294920 | tf_op jit(solution)/shard_map/ppermute | solution.py:31
  37.9 6.2 %collective-permute-start.2 = (bf16[72,512]{1,0:T(8,128)(2,1)S(1)}, bf16[72,512]{1,0:T(8,128)(2,1)S(1)}, u32[]{:S(2)}, u32[]{:S(2)}) collective-permute-start(bf16[72,512]{1,0:T(8,128)(2,1)S(1)} %get-tuple-element.69), channel_id=1, source_target_pairs={{0,4},{4,8},{8,12},{12,0},{1,5},{5,9},{9,13},{13,1},{2,6},{6,10},{... | collective-permute-start | bytes 221192 | tf_op jit(solution)/shard_map/ppermute | solution.py:20
  46.1 8.5 %collective-permute-start.9 = (bf16[32,1408]{1,0:T(8,128)(2,1)S(1)}, bf16[32,1408]{1,0:T(8,128)(2,1)S(1)}, u32[]{:S(2)}, u32[]{:S(2)}) collective-permute-start(bf16[32,1408]{1,0:T(8,128)(2,1)S(1)} %get-tuple-element.81), channel_id=1, source_target_pairs={{0,4},{4,0},{8,12},{12,8},{1,5},{5,1},{9,13},{13,9},{2,6},{6,2},{1... | collective-permute-start | bytes 270344 | tf_op jit(solution)/shard_map/ppermute | solution.py:31
  47.8 8.7 %collective-permute-start.10 = (bf16[32,1408]{1,0:T(8,128)(2,1)S(1)}, bf16[32,1408]{1,0:T(8,128)(2,1)S(1)}, u32[]{:S(2)}, u32[]{:S(2)}) collective-permute-start(bf16[32,1408]{1,0:T(8,128)(2,1)S(1)} %get-tuple-element.82), channel_id=1, source_target_pairs={{0,8},{4,12},{8,0},{12,4},{1,9},{5,13},{9,1},{13,5},{2,10},{6,14},... | collective-permute-start | bytes 270344 | tf_op jit(solution)/shard_map/ppermute | solution.py:31
  47.9 8.5 %collective-permute-start.11 = (bf16[32,1408]{1,0:T(8,128)(2,1)S(1)}, bf16[32,1408]{1,0:T(8,128)(2,1)S(1)}, u32[]{:S(2)}, u32[]{:S(2)}) collective-permute-start(bf16[32,1408]{1,0:T(8,128)(2,1)S(1)} %get-tuple-element.83), channel_id=1, source_target_pairs={{0,12},{4,8},{8,4},{12,0},{1,13},{5,9},{9,5},{13,1},{2,14},{6,10},... | collective-permute-start | bytes 270344 | tf_op jit(solution)/shard_map/ppermute | solution.py:31
  50.5 4.1 %collective-permute-start.8 = (bf16[32,768]{1,0:T(8,128)(2,1)S(1)}, bf16[32,768]{1,0:T(8,128)(2,1)S(1)}, u32[]{:S(2)}, u32[]{:S(2)}) collective-permute-start(bf16[32,768]{1,0:T(8,128)(2,1)S(1)} %get-tuple-element.80), channel_id=1, source_target_pairs={{0,2},{1,3},{2,0},{3,1},{4,6},{5,7},{6,4},{7,5},{8,10},{9,11},{10,... | collective-permute-start | bytes 147464 | tf_op jit(solution)/shard_map/ppermute | solution.py:31
  56.5 9.0 %collective-permute-start.15 = (bf16[32,1280]{1,0:T(8,128)(2,1)S(1)}, bf16[32,1280]{1,0:T(8,128)(2,1)S(1)}, u32[]{:S(2)}, u32[]{:S(2)}) collective-permute-start(bf16[32,1280]{1,0:T(8,128)(2,1)S(1)} %get-tuple-element.86.rest_0_), channel_id=1, source_target_pairs={{0,12},{4,8},{8,4},{12,0},{1,13},{5,9},{9,5},{13,1},{2,14},{6,10},... | collective-permute-start | bytes 245768 | tf_op jit(solution)/shard_map/ppermute | solution.py:31
  58.4 7.1 %collective-permute-start.14 = (bf16[32,1280]{1,0:T(8,128)(2,1)S(1)}, bf16[32,1280]{1,0:T(8,128)(2,1)S(1)}, u32[]{:S(2)}, u32[]{:S(2)}) collective-permute-start(bf16[32,1280]{1,0:T(8,128)(2,1)S(1)} %get-tuple-element.86.rest_0_), channel_id=1, source_target_pairs={{0,8},{4,12},{8,0},{12,4},{1,9},{5,13},{9,1},{13,5},{2,10},{6,14},... | collective-permute-start | bytes 245768 | tf_op jit(solution)/shard_map/ppermute | solution.py:31
  59.6 5.9 %collective-permute-start.13 = (bf16[32,1280]{1,0:T(8,128)(2,1)S(1)}, bf16[32,1280]{1,0:T(8,128)(2,1)S(1)}, u32[]{:S(2)}, u32[]{:S(2)}) collective-permute-start(bf16[32,1280]{1,0:T(8,128)(2,1)S(1)} %get-tuple-element.86.rest_0_), channel_id=1, source_target_pairs={{0,4},{4,0},{8,12},{12,8},{1,5},{5,1},{9,13},{13,9},{2,6},{6,2},{1... | collective-permute-start | bytes 245768 | tf_op jit(solution)/shard_map/ppermute | solution.py:31
  61.0 4.5 %collective-permute-start.12 = (bf16[32,768]{1,0:T(8,128)(2,1)S(1)}, bf16[32,768]{1,0:T(8,128)(2,1)S(1)}, u32[]{:S(2)}, u32[]{:S(2)}) collective-permute-start(bf16[32,768]{1,0:T(8,128)(2,1)S(1)} %get-tuple-element.85.piece_q), channel_id=1, source_target_pairs={{0,2},{1,3},{2,0},{3,1},{4,6},{5,7},{6,4},{7,5},{8,10},{9,11},{10,... | collective-permute-start | bytes 147464 | tf_op jit(solution)/shard_map/ppermute | solution.py:31
  65.6 9.3 %collective-permute-start.16 = (bf16[128,1280]{1,0:T(8,128)(2,1)S(1)}, bf16[128,1280]{1,0:T(8,128)(2,1)S(1)}, u32[]{:S(2)}, u32[]{:S(2)}) collective-permute-start(bf16[128,1280]{1,0:T(8,128)(2,1)S(1)} %get-tuple-element.87.block_p), channel_id=1, source_target_pairs={{0,2},{1,3},{2,0},{3,1},{4,6},{5,7},{6,4},{7,5},{8,10},{9,11},{10,... | collective-permute-start | bytes 983048 | tf_op jit(solution)/shard_map/ppermute | solution.py:31
  66.2 6.7 %collective-permute-start.19 = (bf16[64,768]{1,0:T(8,128)(2,1)S(1)}, bf16[64,768]{1,0:T(8,128)(2,1)S(1)}, u32[]{:S(2)}, u32[]{:S(2)}) collective-permute-start(bf16[64,768]{1,0:T(8,128)(2,1)S(1)} %get-tuple-element.88.rest_0_), channel_id=1, source_target_pairs={{0,12},{4,8},{8,4},{12,0},{1,13},{5,9},{9,5},{13,1},{2,14},{6,10},... | collective-permute-start | bytes 294920 | tf_op jit(solution)/shard_map/ppermute | solution.py:31
  68.1 6.8 %collective-permute-start.18 = (bf16[64,768]{1,0:T(8,128)(2,1)S(1)}, bf16[64,768]{1,0:T(8,128)(2,1)S(1)}, u32[]{:S(2)}, u32[]{:S(2)}) collective-permute-start(bf16[64,768]{1,0:T(8,128)(2,1)S(1)} %get-tuple-element.88.rest_0_), channel_id=1, source_target_pairs={{0,8},{4,12},{8,0},{12,4},{1,9},{5,13},{9,1},{13,5},{2,10},{6,14},... | collective-permute-start | bytes 294920 | tf_op jit(solution)/shard_map/ppermute | solution.py:31
  68.1 6.8 %collective-permute-start.17 = (bf16[64,768]{1,0:T(8,128)(2,1)S(1)}, bf16[64,768]{1,0:T(8,128)(2,1)S(1)}, u32[]{:S(2)}, u32[]{:S(2)}) collective-permute-start(bf16[64,768]{1,0:T(8,128)(2,1)S(1)} %get-tuple-element.88.rest_0_), channel_id=1, source_target_pairs={{0,4},{4,0},{8,12},{12,8},{1,5},{5,1},{9,13},{13,9},{2,6},{6,2},{1... | collective-permute-start | bytes 294920 | tf_op jit(solution)/shard_map/ppermute | solution.py:31
  75.4 4.0 %collective-permute-start.20 = (bf16[256,2048]{1,0:T(8,128)(2,1)S(1)}, bf16[256,2048]{1,0:T(8,128)(2,1)S(1)}, u32[]{:S(2)}, u32[]{:S(2)}) collective-permute-start(bf16[256,2048]{1,0:T(8,128)(2,1)S(1)} %get-tuple-element.89.half), channel_id=1, source_target_pairs={{0,1},{1,0},{2,3},{3,2},{4,5},{5,4},{6,7},{7,6},{8,9},{9,8},{10,11... | collective-permute-start | bytes 3145736 | tf_op jit(solution)/shard_map/ppermute | solution.py:31
  75.4 3.2 %collective-permute-start.23 = (f32[8,384]{1,0:T(8,128)S(1)}, f32[8,384]{1,0:T(8,128)S(1)}, u32[]{:S(2)}, u32[]{:S(2)}) collective-permute-start(f32[8,384]{1,0:T(8,128)S(1)} %get-tuple-element.90.row), channel_id=1, source_target_pairs={{0,17},{1,16},{2,19},{3,18},{16,1},{17,0},{18,3},{19,2},{4,21},{5,... | collective-permute-start | bytes 36872 | tf_op jit(solution)/shard_map/ppermute | solution.py:622
  75.5 3.9 %collective-permute-start.22 = (f32[8,384]{1,0:T(8,128)S(1)}, f32[8,384]{1,0:T(8,128)S(1)}, u32[]{:S(2)}, u32[]{:S(2)}) collective-permute-start(f32[8,384]{1,0:T(8,128)S(1)} %get-tuple-element.90.row), channel_id=1, source_target_pairs={{0,16},{16,0},{1,17},{17,1},{2,18},{18,2},{3,19},{19,3},{4,20},{20... | collective-permute-start | bytes 36872 | tf_op jit(solution)/shard_map/ppermute | solution.py:31
  77.5 1.8 %collective-permute-start.21 = (f32[8,384]{1,0:T(8,128)S(1)}, f32[8,384]{1,0:T(8,128)S(1)}, u32[]{:S(2)}, u32[]{:S(2)}) collective-permute-start(f32[8,384]{1,0:T(8,128)S(1)} %get-tuple-element.90.row), channel_id=1, source_target_pairs={{0,1},{1,0},{2,3},{3,2},{4,5},{5,4},{6,7},{7,6},{8,9},{9,8},{10,11... | collective-permute-start | bytes 36872 | tf_op jit(solution)/shard_map/ppermute | solution.py:31

commit v7 on v6

--- a/solution.py
+++ b/solution.py
@@ -9,7 +9,7 @@
 
 SHIFT = 6
 GROUP = 128
-CUT = 1280
+CUT = 1408
 EPSILON = 1e-05
 F32 = jnp.float32
 BF16 = jnp.bfloat16
@@ -74,22 +74,29 @@
     return lax.rem(lat, 2), lax.div(lat, 2), lon
 
 
-def pack_kernel(tokens, cot, land, own, rim, tokens_v, cot_v, land_v, own32, rim32, sems):
-    arrays = ((tokens, tokens_v), (cot, cot_v), (land, land_v))
+def pack_kernel(
+    tokens, cot, land, gain, bias, own, rim,
+    tokens_v, cot_v, land_v, gain_v, bias_v, rim32, sems,
+):
+    arrays = ((tokens, tokens_v), (cot, cot_v), (land, land_v), (gain, gain_v), (bias, bias_v))
     copies = [started(source, target, sems, i) for i, (source, target) in enumerate(arrays)]
     lats, cols, levels, width = tokens.shape[1:]
     half = levels * lats * SHIFT
     rim32[2 * half :, :] = jnp.zeros((rim32.shape[0] - 2 * half, width), F32)
+    own[2 * half :, :] = jnp.zeros((own.shape[0] - 2 * half, width), F32)
     for which, ref in enumerate((tokens_v, cot_v)):
         copies[which].wait()
         for lat in range(lats):
             for col in range(cols):
                 row = which * half + (lat * SHIFT + col % SHIFT) * levels
-                part = rim32 if col < SHIFT else own32
+                part = rim32 if col < SHIFT else own
                 part[row : row + levels, :] = ref[0, lat, col].astype(F32)
-    copies[2].wait()
+    for copy in copies[2:]:
+        copy.wait()
     rim32[2 * half : 2 * half + lats, :cols] = land_v[...].astype(F32)
-    own[...] = own32[...].astype(BF16)
+    own[2 * half : 2 * half + 1, :] = gain_v[...]
+    own[2 * half + 1 : 2 * half + 2, : bias.shape[1]] = bias_v[...]
+    own[2 * half + 8 : 2 * half + 8 + lats, :cols] = land_v[...].astype(F32)
     rim[...] = rim32[...].astype(BF16)
 
 
@@ -182,44 +189,34 @@
     return inverse * (scaled - mean - normed * along)
 
 
-def ready_kernel(
-    own_in, weight_qkv, weight_out, gain, land, bias,
-    own, qkv_v, qkv_t, out_v, params,
-    gain_v, land_v, bias_v, sems,
-):
-    arrays = (
-        (weight_qkv, qkv_v), (weight_out, out_v), (gain, gain_v), (land, land_v), (bias, bias_v),
-        (own_in, own),
-    )
-    copies = [started(source, target, sems, i) for i, (source, target) in enumerate(arrays)]
-    for copy in copies[1:]:
-        copy.wait()
-    lats, cols = land.shape
-    params[...] = jnp.zeros(params.shape, F32)
-    params[0:1, :] = gain_v[...]
-    params[1:2, : bias.shape[1]] = bias_v[...]
-    params[8 : 8 + lats, :cols] = land_v[...].astype(F32)
+def ready_kernel(after, weight_qkv, weight_out, qkv_v, qkv_t, out_v, sems):
+    copies = [
+        started(weight_qkv, qkv_v, sems, 0),
+        started(weight_out, out_v, sems, 1),
+    ]
     copies[0].wait()
     width = weight_qkv.shape[0]
     for part in range(weight_qkv.shape[1] // width):
         rows = slice(part * width, (part + 1) * width)
         qkv_t[rows, :] = qkv_v[:, rows].T
+    copies[1].wait()
 
 
 def forward_kernel(
-    own, rim, weight_qkv, weight_t, weight_out, params,
+    own, rim, weight_qkv, weight_t, weight_out,
     skip, cot, normed_t, qkv, probs_b, attended_t, extra, normed_out,
     probs, queries_t, keys_t, values_t, grad_proj,
     *, heads, lats, cols,
 ):
-    width = params.shape[1]
+    width = own.shape[1]
     size = width // heads
-    half = own.shape[0] // 2
+    half = cot.shape[0] // 2
     count = 2 * half
     per = GROUP // size
     scale = size ** (-0.5)
     masks_b = head_masks(BF16, size)
-    mine = own[...].astype(F32)
+    mine = own[: 2 * half, :]
+    params = own[2 * half :, :]
     came = rim[...].astype(F32)
     gain = params[0:1, :]
     values = jnp.concatenate([mine[:half], came[:half]], axis=0)
@@ -305,7 +302,7 @@
     bias_b = bias_row[:1, :].astype(BF16).astype(F32)
     weight_rows(rows, normed_t, attended_t, grad_proj, total, bias_b, keep)
     inverse = extra[:, GROUP : GROUP + 1]
-    final = through_norm(grad_proj[...], weight_t, params[0:1, :], normed[...], inverse)
+    final = through_norm(grad_proj[...], weight_t, params[count : count + 1, :], normed[...], inverse)
     final = final + total[...].astype(F32)
     own[...] = final[: count // 2]
     back[...] = final[count // 2 :].astype(BF16)
@@ -323,7 +320,7 @@
     kept_p[:, CUT:] = total[mine, CUT:wide_p].astype(BF16).astype(F32)
     piece = kept_q.shape[0]
     kept_q[...] = total[aligned(z * piece, piece), wide_p:]
-    for other, ref in enumerate(give_q, 1):
+    for other, ref in zip(range(len(give_q), 0, -1), give_q):
         ref[...] = total[aligned((z ^ other) * piece, piece), wide_p:].astype(BF16)
 
 
@@ -337,7 +334,7 @@
     mine = aligned(z * piece, piece)
     left_p[:, :CUT] = total_p[mine, :CUT]
     left_p[:, CUT:] = total_p[mine, CUT:].astype(BF16).astype(F32)
-    for other, ref in enumerate(give_p, 1):
+    for other, ref in zip(range(len(give_p), 0, -1), give_p):
         ref[...] = total_p[aligned((z ^ other) * piece, piece), :].astype(BF16)
     total = kept_q[...]
     for ref in came_q:
@@ -356,7 +353,7 @@
         total = total + ref[:, :CUT].astype(F32)
     piece_p[...] = total.astype(BF16)
     piece_q[...] = (left_q[...] + came_q[...].astype(F32)).astype(BF16)
-    terms = [left_p[:8, CUT:]] + [ref[...].astype(F32)[:8, CUT:] for ref in came_p]
+    terms = [left_p[:8, CUT:]] + [ref[...].astype(F32)[:8, CUT:] for ref in came_p[::-1]]
     total = jnp.zeros_like(terms[0])
     for source in range(len(terms)):
         for other, term in enumerate(terms):
@@ -375,7 +372,7 @@
     block_q[aligned((1 - y) * piece, piece), :] = other_q[...]
 
 
-def fifth_kernel(weight_qkv, params, bias, block_p, other_p, *rest):
+def fifth_kernel(weight_qkv, gain, bias, block_p, other_p, *rest):
     *parts_q, half, row = rest
     core, y, z = position()
     rows = half.shape[0]
@@ -390,7 +387,7 @@
     wide = half[:, :three].astype(F32)
     gain_half = jnp.sum(wide * weight_qkv[mine, :].astype(F32), axis=1, keepdims=True)
     gain_half = jnp.broadcast_to(gain_half, (rows, GROUP)).T[:8]
-    own_gain = jnp.where(core == 0, params[0:1, :rows], params[0:1, rows:])
+    own_gain = jnp.where(core == 0, gain[:, :rows], gain[:, rows:])
     gain_half = gain_half / own_gain
     out = half[:, three:].astype(F32)
     square = jnp.sum(jnp.sum(wide * wide, axis=0, keepdims=True), axis=1, keepdims=True)
@@ -434,8 +431,13 @@
         copy.wait()
 
 
-def sent_round(pieces, axis):
-    return [swapped(piece, axis, other) for other, piece in enumerate(pieces, 1)]
+def far_first(pieces, axis):
+    others = range(len(pieces), 0, -1)
+    return [swapped(piece, axis, other) for other, piece in zip(others, pieces)]
+
+
+def to_all(piece, axis):
+    return [swapped(piece, axis, other) for other in range(1, lax.axis_size(axis))]
 
 
 def vmem(dims, dtype):
@@ -460,37 +462,31 @@
 
     own, rim = call(
         pack_kernel,
-        [shape((2 * half, width), BF16), shape((packed, width), BF16)],
+        [shape((packed, width), F32), shape((packed, width), BF16)],
         scratch=[
             vmem(tokens.shape, BF16),
             vmem(tokens.shape, BF16),
             vmem(land_sea.shape, jnp.int32),
-            vmem((2 * half, width), F32),
+            vmem(gains.shape, F32),
+            vmem(land_bias.shape, F32),
             vmem((packed, width), F32),
-            copies(3),
-        ],
-        places="hhh",
-        operands=(tokens, own_cot, land_sea),
+            copies(5),
+        ],
+        places="hhhhh",
+        operands=(tokens, own_cot, land_sea, gains, land_bias),
         limit=60,
     )
     rim = from_behind(rim, "lon", -1)
-    own, qkv_v, qkv_t, out_v, params = call(
+    qkv_v, qkv_t, out_v = call(
         ready_kernel,
         [
-            shape(own.shape, BF16),
             shape(weight_qkv.shape, BF16),
             shape(weight_qkv.shape[::-1], BF16),
             shape(weight_out.shape, BF16),
-            shape((16, width), F32),
-        ],
-        scratch=[
-            vmem(gains.shape, F32),
-            vmem(land_sea.shape, jnp.int32),
-            vmem(land_bias.shape, F32),
-            copies(6),
-        ],
-        places="hhhhhh",
-        operands=(own, weight_qkv, weight_out, gains, land_sea, land_bias),
+        ],
+        scratch=[copies(2)],
+        places="ahh",
+        operands=(own, weight_qkv, weight_out),
         limit=48,
     )
     skip, cot, normed_t, qkv, probs, attended_t, extra, normed = call(
@@ -512,7 +508,7 @@
             vmem((width, count), BF16),
             vmem((count, 3 * width), BF16),
         ],
-        operands=(own, rim, qkv_v, qkv_t, out_v, params),
+        operands=(own, rim, qkv_v, qkv_t, out_v),
         flops=10**9,
         limit=16,
     )
@@ -539,14 +535,14 @@
             shape((half, width), BF16),
         ],
         operands=(
-            total, grad_proj, bias_row, normed_t, attended_t, normed, extra, qkv_t, params,
+            total, grad_proj, bias_row, normed_t, attended_t, normed, extra, qkv_t, own,
         ),
         flops=5 * 10**8,
     )
     back = from_behind(back, "lon", 1)
     entries = 2 * (4 * width * width + width + heads)
     if rows // 2 // lons % 16 == 0 and lons & (lons - 1) == 0:
-        grads = staged(keep, came, back, qkv_v, params, lons, heads, entries)
+        grads = staged(keep, came, back, qkv_v, gains, lons, heads, entries)
     else:
         grads = plain(keep, came, weight_qkv, gains, heads, entries)
     (final_grad,) = call(
@@ -560,7 +556,7 @@
     return (final_grad, *(grad[None] for grad in grads))
 
 
-def staged(keep, came, after, weight_qkv, params, lons, heads, entries):
+def staged(keep, came, after, weight_qkv, gains, lons, heads, entries):
     rows, wide = keep.shape
     width = 2 * rows
     wide_p = CUT + GROUP
@@ -579,7 +575,7 @@
         operands=(keep, came),
     )
     came_p = swapped(give_p, "lat", 2)
-    came_q = sent_round(give_q, "lon")
+    came_q = far_first(give_q, "lon")
     piece = rows // 2 // lons
     give_q, left_q, left_p, *give_p = call(
         second_kernel,
@@ -593,7 +589,7 @@
         places="avvv" + several,
         operands=(after, kept_p, came_p, kept_q, *came_q),
     )
-    came_p = sent_round(give_p, "lon")
+    came_p = far_first(give_p, "lon")
     came_q = swapped(give_q, "lat", 2)
     piece_p, piece_q, bias = call(
         third_kernel,
@@ -604,7 +600,7 @@
         ],
         operands=(left_p, left_q, came_q, *came_p),
     )
-    others_p = sent_round([piece_p for _ in some], "lon")
+    others_p = to_all(piece_p, "lon")
     other_q = swapped(piece_q, "lat", 2)
     block_p, block_q = call(
         fourth_kernel,
@@ -612,11 +608,11 @@
         operands=(piece_q, other_q, piece_p, *others_p),
     )
     other_p = swapped(block_p, "lat", 2)
-    others_q = sent_round([block_q for _ in some], "lon")
+    others_q = to_all(block_q, "lon")
     half, row = call(
         fifth_kernel,
         [shape((rows, 4 * width), BF16), shape((8, rows + GROUP), F32)],
-        operands=(weight_qkv, params, bias, block_p, other_p, block_q, *others_q),
+        operands=(weight_qkv, gains, bias, block_p, other_p, block_q, *others_q),
     )
     row_section = swapped(row, "section", 1)
     row_both = lax.ppermute(row, ("section", "lat"), across())

time: 81.9 us -> 81.5 us (level)
  local copies, waits for them, and re-layouts: 5.38 us -> 3.43 us
  starting transfers between devices: 29.5 us -> 30.9 us
    unnamed x12 -> x8, local copies, waits for them, and re-layouts: 5.38 us -> 3.43 us
    ppermute x2, starting transfers between devices: 5.1 us -> 6.45 us  [from_behind(): lax.ppermute(value, axis, [(i, (i + by) % count) for i in range(count)])]
  transfers between devices with their start and end apart: 24 -> 24, of which waited for: 11 -> 13; matrix products, arithmetic and copies ran while one was open for 0% -> 0% of each run, Pallas kernels for 3% -> 3%
where the time goes in v7:
time: 81.5 us; the launch traced here: 81.3 us
  starting transfers between devices  30.9 us (38%)
  waiting for transfers between devices  30.8 us (38%)
  Pallas kernels  15.3 us (19%)
  local copies, waits for them, and re-layouts  3.43 us (4%)
    ppermute x20, starting transfers between devices, swapped(): return lax.ppermute(value, axis, [(i, i ^ bit) for i in range(count)])  23.1 us
    ppermute x20, waiting for transfers between devices, swapped(): return lax.ppermute(value, axis, [(i, i ^ bit) for i in range(count)])  19 us
    pallas_call x12, Pallas kernels, call(): pl.pallas_call(kernel, out_shape=list(outs), in_specs=[pl.BlockSpec(memor...  15.3 us
    ppermute x2, starting transfers between devices, from_behind(): lax.ppermute(value, axis, [(i, (i + by) % count) for i in range(count)])  6.45 us
    ppermute x1, waiting for transfers between devices, passed_along(): return lax.ppermute(block, axis, route)  5.93 us
    ppermute x2, waiting for transfers between devices, from_behind(): lax.ppermute(value, axis, [(i, (i + by) % count) for i in range(count)])  5.62 us
    unnamed x8, local copies, waits for them, and re-layouts  3.43 us
  transfers between devices with their start and end apart: 24, of which 13 were waited for; matrix products, arithmetic and copies ran while one was open for 0% of the time, Pallas kernels for 3%

profile of v7, /device:TPU:0, one launch (start us, length us, event | category | flops | bytes accessed | tf_op | source)
XLA Modules:
  0.0 81.3 jit_solution(17765462565921561544)
XLA Ops:
  0.6 1.9 %shard_map.110 = (f32[160,512]{1,0:T(8,128)}, bf16[160,512]{1,0:T(8,128)(2,1)}) custom-call(bf16[1,6,12,2,512]{4,3,2,1,0:T(2,128)(2,1)} %bitcast.12, bf16[1,6,12,2,512]{4,3,2,1,0:T(2,128)(2,1)} %bitcast.13, s32[6,12]{1,0:T(8,128)} %land.1, f32[1,512]{1,0:T(1,128)} %gain.3, f32[1,16]{1,0:T(1,128)} %bias.1), custom_call_target="tpu_custom_call" | custom-call | flops 100000000 | bytes 788832 | tf_op jit(solution)/shard_map/pallas_call | solution.py:47
  2.5 5.1 %collective-permute-start = (bf16[160,512]{1,0:T(8,128)(2,1)}, bf16[160,512]{1,0:T(8,128)(2,1)S(1)}, u32[]{:S(2)}, u32[]{:S(2)}) collective-permute-start(bf16[160,512]{1,0:T(8,128)(2,1)} %get-tuple-element.49), channel_id=1, source_target_pairs={{0,12},{4,0},{8,4},{12,8},{1,13},{5,1},{9,5},{13,9},{2,14},{6,2},{... | collective-permute-start | bytes 491528 | tf_op jit(solution)/shard_map/ppermute | solution.py:20
  7.6 1.0 %copy-done = f32[160,512]{1,0:T(8,128)S(1)} copy-done((f32[160,512]{1,0:T(8,128)S(1)}, f32[160,512]{1,0:T(8,128)}, u32[]{:S(2)}) %copy-start) | copy-done | bytes 327704
  8.6 1.4 %copy-done.1 = bf16[1,512,1536]{2,1,0:T(8,128)(2,1)S(1)} copy-done((bf16[1,512,1536]{2,1,0:T(8,128)(2,1)S(1)}, bf16[1,512,1536]{2,1,0:T(8,128)(2,1)}, u32[]{:S(2)}) %copy-start.1) | copy-done | bytes 1572888
  10.0 1.0 %copy-done.2 = bf16[1,512,512]{2,1,0:T(8,128)(2,1)S(1)} copy-done((bf16[1,512,512]{2,1,0:T(8,128)(2,1)S(1)}, bf16[1,512,512]{2,1,0:T(8,128)(2,1)}, u32[]{:S(2)}) %copy-start.2) | copy-done | bytes 524312
  11.1 0.6 shard_map.111
  11.7 0.0 collective-permute-done.rim
  11.7 4.7 %shard_map.112 = (bf16[144,512]{1,0:T(8,128)(2,1)S(1)}, bf16[144,512]{1,0:T(8,128)(2,1)S(1)}, bf16[512,144]{1,0:T(8,128)(2,1)S(1)}, bf16[144,1536]{1,0:T(8,128)(...) custom-call(f32[160,512]{1,0:T(8,128)S(1)} %copy-done, ...), custom_call_target="tpu_custom_call" | custom-call | flops 1000000000 | bytes 6299648 | tf_op jit(solution)/shard_map/pallas_call | solution.py:47
  16.5 1.3 %collective-permute-start.1 = (bf16[144,512]{1,0:T(8,128)(2,1)S(1)}, bf16[144,512]{1,0:T(8,128)(2,1)S(1)}, u32[]{:S(2)}, u32[]{:S(2)}) collective-permute-start(bf16[144,512]{1,0:T(8,128)(2,1)S(1)} %get-tuple-element.53), channel_id=1, source_target_pairs={{16,0},{17,1},{18,2},{19,3},{20,4},{21,5},{22,6},{23,7},{24,8},{25... | collective-permute-start | bytes 442376 | tf_op jit(solution)/shard_map/ppermute | solution.py:26
  17.8 5.9 %collective-permute-done.1.skip = bf16[144,512]{1,0:T(8,128)(2,1)S(1)} collective-permute-done((bf16[144,512]{1,0:T(8,128)(2,1)S(1)}, bf16[144,512]{1,0:T(8,128)(2,1)S(1)}, u32[]{:S(2)}, u32[]{:S(2)}) %collective-permute-start.1) | collective-permute-done | bytes 147488 | tf_op jit(solution)/shard_map/ppermute | solution.py:26
  23.7 3.0 %shard_map.113 = (bf16[144,512]{1,0:T(8,128)(2,1)S(1)}, bf16[144,1536]{1,0:T(8,128)(2,1)S(1)}, f32[8,128]{1,0:T(8,128)S(1)}, bf16[256,2176]{1,0:T(8,128)(2,1)S(1)}) custom-call(bf16[144,512]{1,0:T(8,128)(2,1)S(1)} %collective-permute-done.1.skip, bf16[144,512]{1,0:T(8,128)(2,1)S(1)} %get-tuple-element.54.cot, bf16[144,1536]{1,0:T(8,128)(2,1)S(1)} %get-tuple-element.55.qkv, ...), custom_call_target="tpu_custom_call" | custom-call | flops 1000000000 | bytes 4075520 | tf_op jit(solution)/shard_map/pallas_call | solution.py:47
  26.7 0.1 collective-permute-start.3
  26.8 0.8 shard_map.114
  27.6 1.9 %collective-permute-done.3.came = bf16[256,2176]{1,0:T(8,128)(2,1)S(1)} collective-permute-done((bf16[256,2176]{1,0:T(8,128)(2,1)S(1)}, bf16[256,2176]{1,0:T(8,128)(2,1)S(1)}, u32[]{:S(2)}, u32[]{:S(2)}) %collective-permute-start.3) | collective-permute-done | bytes 1114144 | tf_op jit(solution)/shard_map/ppermute | solution.py:31
  29.5 0.4 shard_map.116
  29.9 0.0 copy-start.3
  30.0 1.6 %collective-permute-start.4 = (bf16[128,1536]{1,0:T(8,128)(2,1)S(1)}, bf16[128,1536]{1,0:T(8,128)(2,1)S(1)}, u32[]{:S(2)}, u32[]{:S(2)}) collective-permute-start(bf16[128,1536]{1,0:T(8,128)(2,1)S(1)} %get-tuple-element.69), channel_id=1, source_target_pairs={{0,2},{1,3},{2,0},{3,1},{4,6},{5,7},{6,4},{7,5},{8,10},{9,11},{10,... | collective-permute-start | bytes 1179656 | tf_op jit(solution)/shard_map/ppermute | solution.py:31
  31.5 3.7 %collective-permute-start.5 = (bf16[64,640]{1,0:T(8,128)(2,1)S(1)}, bf16[64,640]{1,0:T(8,128)(2,1)S(1)}, u32[]{:S(2)}, u32[]{:S(2)}) collective-permute-start(bf16[64,640]{1,0:T(8,128)(2,1)S(1)} %get-tuple-element.71), channel_id=1, source_target_pairs={{0,12},{4,8},{8,4},{12,0},{1,13},{5,9},{9,5},{13,1},{2,14},{6,10},... | collective-permute-start | bytes 245768 | tf_op jit(solution)/shard_map/ppermute | solution.py:31
  35.2 0.0 collective-permute-start.6
  35.2 0.7 collective-permute-start.7
  35.9 1.3 %collective-permute-start.2 = (bf16[72,512]{1,0:T(8,128)(2,1)S(1)}, bf16[72,512]{1,0:T(8,128)(2,1)S(1)}, u32[]{:S(2)}, u32[]{:S(2)}) collective-permute-start(bf16[72,512]{1,0:T(8,128)(2,1)S(1)} %get-tuple-element.65), channel_id=1, source_target_pairs={{0,4},{4,8},{8,12},{12,0},{1,5},{5,9},{9,13},{13,1},{2,6},{6,10},{... | collective-permute-start | bytes 221192 | tf_op jit(solution)/shard_map/ppermute | solution.py:20
  37.3 5.6 %collective-permute-done.2.back.after = bf16[72,512]{1,0:T(8,128)(2,1)S(1)} collective-permute-done((bf16[72,512]{1,0:T(8,128)(2,1)S(1)}, bf16[72,512]{1,0:T(8,128)(2,1)S(1)}, u32[]{:S(2)}, u32[]{:S(2)}) %collective-permute-start.2) | collective-permute-done | bytes 73760 | tf_op jit(solution)/shard_map/ppermute | solution.py:20
  42.9 0.0 collective-permute-done.5.rest_0_
  42.9 0.0 collective-permute-done.6.rest_1_
  42.9 0.2 collective-permute-done.7.rest_2_
  43.1 0.0 collective-permute-done.4.came_p
  43.1 0.2 shard_map.117
  43.3 2.4 %collective-permute-start.9 = (bf16[32,1536]{1,0:T(8,128)(2,1)S(1)}, bf16[32,1536]{1,0:T(8,128)(2,1)S(1)}, u32[]{:S(2)}, u32[]{:S(2)}) collective-permute-start(bf16[32,1536]{1,0:T(8,128)(2,1)S(1)} %get-tuple-element.77), channel_id=1, source_target_pairs={{0,12},{4,8},{8,4},{12,0},{1,13},{5,9},{9,5},{13,1},{2,14},{6,10},... | collective-permute-start | bytes 294920 | tf_op jit(solution)/shard_map/ppermute | solution.py:31
  45.7 0.6 collective-permute-start.10
  46.3 1.4 %collective-permute-start.11 = (bf16[32,1536]{1,0:T(8,128)(2,1)S(1)}, bf16[32,1536]{1,0:T(8,128)(2,1)S(1)}, u32[]{:S(2)}, u32[]{:S(2)}) collective-permute-start(bf16[32,1536]{1,0:T(8,128)(2,1)S(1)} %get-tuple-element.79), channel_id=1, source_target_pairs={{0,4},{4,0},{8,12},{12,8},{1,5},{5,1},{9,13},{13,9},{2,6},{6,2},{1... | collective-permute-start | bytes 294920 | tf_op jit(solution)/shard_map/ppermute | solution.py:31
  47.7 0.5 collective-permute-start.8
  48.3 3.5 %collective-permute-done.8.came_q = bf16[32,640]{1,0:T(8,128)(2,1)S(1)} collective-permute-done((bf16[32,640]{1,0:T(8,128)(2,1)S(1)}, bf16[32,640]{1,0:T(8,128)(2,1)S(1)}, u32[]{:S(2)}, u32[]{:S(2)}) %collective-permute-start.8) | collective-permute-done | bytes 40992 | tf_op jit(solution)/shard_map/ppermute | solution.py:31
  51.8 0.0 collective-permute-done.9.rest_0_
  51.8 2.5 %collective-permute-done.10.rest_1_ = bf16[32,1536]{1,0:T(8,128)(2,1)S(1)} collective-permute-done((bf16[32,1536]{1,0:T(8,128)(2,1)S(1)}, bf16[32,1536]{1,0:T(8,128)(2,1)S(1)}, u32[]{:S(2)}, u32[]{:S(2)}) %collective-permute-start.10) | collective-permute-done | bytes 98336 | tf_op jit(solution)/shard_map/ppermute | solution.py:31
  54.3 0.0 collective-permute-done.11.rest_2_
  54.3 0.1 shard_map.118
  54.4 2.3 %collective-permute-start.15 = (bf16[32,1408]{1,0:T(8,128)(2,1)S(1)}, bf16[32,1408]{1,0:T(8,128)(2,1)S(1)}, u32[]{:S(2)}, u32[]{:S(2)}) collective-permute-start(bf16[32,1408]{1,0:T(8,128)(2,1)S(1)} %get-tuple-element.82.rest_0_), channel_id=1, source_target_pairs={{0,12},{4,8},{8,4},{12,0},{1,13},{5,9},{9,5},{13,1},{2,14},{6,10},... | collective-permute-start | bytes 270344 | tf_op jit(solution)/shard_map/ppermute | solution.py:31
  56.7 0.0 collective-permute-start.14
  56.7 2.1 %collective-permute-start.13 = (bf16[32,1408]{1,0:T(8,128)(2,1)S(1)}, bf16[32,1408]{1,0:T(8,128)(2,1)S(1)}, u32[]{:S(2)}, u32[]{:S(2)}) collective-permute-start(bf16[32,1408]{1,0:T(8,128)(2,1)S(1)} %get-tuple-element.82.rest_0_), channel_id=1, source_target_pairs={{0,4},{4,0},{8,12},{12,8},{1,5},{5,1},{9,13},{13,9},{2,6},{6,2},{1... | collective-permute-start | bytes 270344 | tf_op jit(solution)/shard_map/ppermute | solution.py:31
  58.8 0.5 collective-permute-start.12
  59.3 3.5 %collective-permute-done.12.other_q = bf16[32,640]{1,0:T(8,128)(2,1)S(1)} collective-permute-done((bf16[32,640]{1,0:T(8,128)(2,1)S(1)}, bf16[32,640]{1,0:T(8,128)(2,1)S(1)}, u32[]{:S(2)}, u32[]{:S(2)}) %collective-permute-start.12) | collective-permute-done | bytes 40992 | tf_op jit(solution)/shard_map/ppermute | solution.py:31
  62.8 0.0 collective-permute-done.15.rest_3_
  62.8 1.3 %collective-permute-done.14.rest_2_ = bf16[32,1408]{1,0:T(8,128)(2,1)S(1)} collective-permute-done((bf16[32,1408]{1,0:T(8,128)(2,1)S(1)}, bf16[32,1408]{1,0:T(8,128)(2,1)S(1)}, u32[]{:S(2)}, u32[]{:S(2)}) %collective-permute-start.14) | collective-permute-done | bytes 90144 | tf_op jit(solution)/shard_map/ppermute | solution.py:31
  64.2 0.0 collective-permute-done.13.rest_1_
  64.2 0.7 collective-permute-start.16
  64.9 1.6 %collective-permute-start.19 = (bf16[64,640]{1,0:T(8,128)(2,1)S(1)}, bf16[64,640]{1,0:T(8,128)(2,1)S(1)}, u32[]{:S(2)}, u32[]{:S(2)}) collective-permute-start(bf16[64,640]{1,0:T(8,128)(2,1)S(1)} %get-tuple-element.84.rest_0_), channel_id=1, source_target_pairs={{0,12},{4,8},{8,4},{12,0},{1,13},{5,9},{9,5},{13,1},{2,14},{6,10},... | collective-permute-start | bytes 245768 | tf_op jit(solution)/shard_map/ppermute | solution.py:31
  66.6 0.0 collective-permute-start.18
  66.6 2.7 %collective-permute-start.17 = (bf16[64,640]{1,0:T(8,128)(2,1)S(1)}, bf16[64,640]{1,0:T(8,128)(2,1)S(1)}, u32[]{:S(2)}, u32[]{:S(2)}) collective-permute-start(bf16[64,640]{1,0:T(8,128)(2,1)S(1)} %get-tuple-element.84.rest_0_), channel_id=1, source_target_pairs={{0,4},{4,0},{8,12},{12,8},{1,5},{5,1},{9,13},{13,9},{2,6},{6,2},{1... | collective-permute-start | bytes 245768 | tf_op jit(solution)/shard_map/ppermute | solution.py:31
  69.3 2.8 %collective-permute-done.19.rest_3_ = bf16[64,640]{1,0:T(8,128)(2,1)S(1)} collective-permute-done((bf16[64,640]{1,0:T(8,128)(2,1)S(1)}, bf16[64,640]{1,0:T(8,128)(2,1)S(1)}, u32[]{:S(2)}, u32[]{:S(2)}) %collective-permute-start.19) | collective-permute-done | bytes 81952 | tf_op jit(solution)/shard_map/ppermute | solution.py:31
  72.1 2.0 %collective-permute-done.18.rest_2_ = bf16[64,640]{1,0:T(8,128)(2,1)S(1)} collective-permute-done((bf16[64,640]{1,0:T(8,128)(2,1)S(1)}, bf16[64,640]{1,0:T(8,128)(2,1)S(1)}, u32[]{:S(2)}, u32[]{:S(2)}) %collective-permute-start.18) | collective-permute-done | bytes 81952 | tf_op jit(solution)/shard_map/ppermute | solution.py:31
  74.1 0.0 collective-permute-done.17.rest_1_
  74.1 0.4 collective-permute-done.16.other_p
  74.5 0.0 copy-done.3
  74.5 0.5 shard_map.120
  75.0 0.0 collective-permute-start.20
  75.0 0.1 collective-permute-start.23
  75.1 2.1 %collective-permute-start.22 = (f32[8,384]{1,0:T(8,128)S(1)}, f32[8,384]{1,0:T(8,128)S(1)}, u32[]{:S(2)}, u32[]{:S(2)}) collective-permute-start(f32[8,384]{1,0:T(8,128)S(1)} %get-tuple-element.86.row), channel_id=1, source_target_pairs={{0,16},{16,0},{1,17},{17,1},{2,18},{18,2},{3,19},{19,3},{4,20},{20... | collective-permute-start | bytes 36872 | tf_op jit(solution)/shard_map/ppermute | solution.py:31
  77.2 0.0 collective-permute-start.21
  77.2 0.8 shard_map.115
  78.0 0.3 collective-permute-done.23.row_both
  78.2 0.8 collective-permute-done.22.row_section
  79.0 0.0 collective-permute-done.21.row_core
  79.0 0.0 collective-permute-done.20.other
  79.0 2.3 %shard_map.121 = (f32[512,1536]{1,0:T(8,128)}, f32[512,512]{1,0:T(8,128)}, f32[1,512]{1,0:T(1,128)}, f32[1,16]{1,0:T(1,128)}) custom-call(bf16[256,2048]{1,0:T(8,128)(2,1)S(1)} %get-tuple-element.85.half, bf16[256,2048]{1,0:T(8,128)(2,1)S(1)} %collective-permute-done.20.other, f32[8,384]{1,0:T(8,128)S(1)} %get-tuple-element.86.row, ...), custom_call_target="tpu_custom_call" | custom-call | flops 100000000 | bytes 6346816 | tf_op jit(solution)/shard_map/pallas_call | solution.py:47
  (4 shorter events, 0.1 us)
Async XLA Ops:
  2.5 9.2 %collective-permute-start = (bf16[160,512]{1,0:T(8,128)(2,1)}, bf16[160,512]{1,0:T(8,128)(2,1)S(1)}, u32[]{:S(2)}, u32[]{:S(2)}) collective-permute-start(bf16[160,512]{1,0:T(8,128)(2,1)} %get-tuple-element.49), channel_id=1, source_target_pairs={{0,12},{4,0},{8,4},{12,8},{1,13},{5,1},{9,5},{13,9},{2,14},{6,2},{... | collective-permute-start | bytes 491528 | tf_op jit(solution)/shard_map/ppermute | solution.py:20
  7.6 1.0 %copy-start = (f32[160,512]{1,0:T(8,128)S(1)}, f32[160,512]{1,0:T(8,128)}, u32[]{:S(2)}) copy-start(f32[160,512]{1,0:T(8,128)} %get-tuple-element.48.after.own.params) | copy-start | bytes 983044
  8.6 1.4 %copy-start.1 = (bf16[1,512,1536]{2,1,0:T(8,128)(2,1)S(1)}, bf16[1,512,1536]{2,1,0:T(8,128)(2,1)}, u32[]{:S(2)}) copy-start(bf16[1,512,1536]{2,1,0:T(8,128)(2,1)} %param.11) | copy-start | bytes 4718596
  10.0 1.0 %copy-start.2 = (bf16[1,512,512]{2,1,0:T(8,128)(2,1)S(1)}, bf16[1,512,512]{2,1,0:T(8,128)(2,1)}, u32[]{:S(2)}) copy-start(bf16[1,512,512]{2,1,0:T(8,128)(2,1)} %param.12) | copy-start | bytes 1572868
  16.5 7.2 %collective-permute-start.1 = (bf16[144,512]{1,0:T(8,128)(2,1)S(1)}, bf16[144,512]{1,0:T(8,128)(2,1)S(1)}, u32[]{:S(2)}, u32[]{:S(2)}) collective-permute-start(bf16[144,512]{1,0:T(8,128)(2,1)S(1)} %get-tuple-element.53), channel_id=1, source_target_pairs={{16,0},{17,1},{18,2},{19,3},{20,4},{21,5},{22,6},{23,7},{24,8},{25... | collective-permute-start | bytes 442376 | tf_op jit(solution)/shard_map/ppermute | solution.py:26
  26.7 2.8 %collective-permute-start.3 = (bf16[256,2176]{1,0:T(8,128)(2,1)S(1)}, bf16[256,2176]{1,0:T(8,128)(2,1)S(1)}, u32[]{:S(2)}, u32[]{:S(2)}) collective-permute-start(bf16[256,2176]{1,0:T(8,128)(2,1)S(1)} %get-tuple-element.67), channel_id=1, source_target_pairs={{0,1},{1,0},{2,3},{3,2},{4,5},{5,4},{6,7},{7,6},{8,9},{9,8},{10,11... | collective-permute-start | bytes 3342344 | tf_op jit(solution)/shard_map/ppermute | solution.py:31
  29.9 44.6 %copy-start.3 = (f32[1,512]{1,0:T(1,128)S(1)}, f32[1,512]{1,0:T(1,128)}, u32[]{:S(2)}) copy-start(f32[1,512]{1,0:T(1,128)} %gain.3) | copy-start | bytes 6148
  30.0 13.2 %collective-permute-start.4 = (bf16[128,1536]{1,0:T(8,128)(2,1)S(1)}, bf16[128,1536]{1,0:T(8,128)(2,1)S(1)}, u32[]{:S(2)}, u32[]{:S(2)}) collective-permute-start(bf16[128,1536]{1,0:T(8,128)(2,1)S(1)} %get-tuple-element.69), channel_id=1, source_target_pairs={{0,2},{1,3},{2,0},{3,1},{4,6},{5,7},{6,4},{7,5},{8,10},{9,11},{10,... | collective-permute-start | bytes 1179656 | tf_op jit(solution)/shard_map/ppermute | solution.py:31
  31.5 11.4 %collective-permute-start.5 = (bf16[64,640]{1,0:T(8,128)(2,1)S(1)}, bf16[64,640]{1,0:T(8,128)(2,1)S(1)}, u32[]{:S(2)}, u32[]{:S(2)}) collective-permute-start(bf16[64,640]{1,0:T(8,128)(2,1)S(1)} %get-tuple-element.71), channel_id=1, source_target_pairs={{0,12},{4,8},{8,4},{12,0},{1,13},{5,9},{9,5},{13,1},{2,14},{6,10},... | collective-permute-start | bytes 245768 | tf_op jit(solution)/shard_map/ppermute | solution.py:31
  35.2 7.7 %collective-permute-start.6 = (bf16[64,640]{1,0:T(8,128)(2,1)S(1)}, bf16[64,640]{1,0:T(8,128)(2,1)S(1)}, u32[]{:S(2)}, u32[]{:S(2)}) collective-permute-start(bf16[64,640]{1,0:T(8,128)(2,1)S(1)} %get-tuple-element.72), channel_id=1, source_target_pairs={{0,8},{4,12},{8,0},{12,4},{1,9},{5,13},{9,1},{13,5},{2,10},{6,14},... | collective-permute-start | bytes 245768 | tf_op jit(solution)/shard_map/ppermute | solution.py:31
  35.2 7.9 %collective-permute-start.7 = (bf16[64,640]{1,0:T(8,128)(2,1)S(1)}, bf16[64,640]{1,0:T(8,128)(2,1)S(1)}, u32[]{:S(2)}, u32[]{:S(2)}) collective-permute-start(bf16[64,640]{1,0:T(8,128)(2,1)S(1)} %get-tuple-element.73), channel_id=1, source_target_pairs={{0,4},{4,0},{8,12},{12,8},{1,5},{5,1},{9,13},{13,9},{2,6},{6,2},{1... | collective-permute-start | bytes 245768 | tf_op jit(solution)/shard_map/ppermute | solution.py:31
  35.9 7.0 %collective-permute-start.2 = (bf16[72,512]{1,0:T(8,128)(2,1)S(1)}, bf16[72,512]{1,0:T(8,128)(2,1)S(1)}, u32[]{:S(2)}, u32[]{:S(2)}) collective-permute-start(bf16[72,512]{1,0:T(8,128)(2,1)S(1)} %get-tuple-element.65), channel_id=1, source_target_pairs={{0,4},{4,8},{8,12},{12,0},{1,5},{5,9},{9,13},{13,1},{2,6},{6,10},{... | collective-permute-start | bytes 221192 | tf_op jit(solution)/shard_map/ppermute | solution.py:20
  43.3 8.5 %collective-permute-start.9 = (bf16[32,1536]{1,0:T(8,128)(2,1)S(1)}, bf16[32,1536]{1,0:T(8,128)(2,1)S(1)}, u32[]{:S(2)}, u32[]{:S(2)}) collective-permute-start(bf16[32,1536]{1,0:T(8,128)(2,1)S(1)} %get-tuple-element.77), channel_id=1, source_target_pairs={{0,12},{4,8},{8,4},{12,0},{1,13},{5,9},{9,5},{13,1},{2,14},{6,10},... | collective-permute-start | bytes 294920 | tf_op jit(solution)/shard_map/ppermute | solution.py:31
  45.7 8.6 %collective-permute-start.10 = (bf16[32,1536]{1,0:T(8,128)(2,1)S(1)}, bf16[32,1536]{1,0:T(8,128)(2,1)S(1)}, u32[]{:S(2)}, u32[]{:S(2)}) collective-permute-start(bf16[32,1536]{1,0:T(8,128)(2,1)S(1)} %get-tuple-element.78), channel_id=1, source_target_pairs={{0,8},{4,12},{8,0},{12,4},{1,9},{5,13},{9,1},{13,5},{2,10},{6,14},... | collective-permute-start | bytes 294920 | tf_op jit(solution)/shard_map/ppermute | solution.py:31
  46.3 8.0 %collective-permute-start.11 = (bf16[32,1536]{1,0:T(8,128)(2,1)S(1)}, bf16[32,1536]{1,0:T(8,128)(2,1)S(1)}, u32[]{:S(2)}, u32[]{:S(2)}) collective-permute-start(bf16[32,1536]{1,0:T(8,128)(2,1)S(1)} %get-tuple-element.79), channel_id=1, source_target_pairs={{0,4},{4,0},{8,12},{12,8},{1,5},{5,1},{9,13},{13,9},{2,6},{6,2},{1... | collective-permute-start | bytes 294920 | tf_op jit(solution)/shard_map/ppermute | solution.py:31
  47.7 4.0 %collective-permute-start.8 = (bf16[32,640]{1,0:T(8,128)(2,1)S(1)}, bf16[32,640]{1,0:T(8,128)(2,1)S(1)}, u32[]{:S(2)}, u32[]{:S(2)}) collective-permute-start(bf16[32,640]{1,0:T(8,128)(2,1)S(1)} %get-tuple-element.76), channel_id=1, source_target_pairs={{0,2},{1,3},{2,0},{3,1},{4,6},{5,7},{6,4},{7,5},{8,10},{9,11},{10,... | collective-permute-start | bytes 122888 | tf_op jit(solution)/shard_map/ppermute | solution.py:31
  54.4 8.5 %collective-permute-start.15 = (bf16[32,1408]{1,0:T(8,128)(2,1)S(1)}, bf16[32,1408]{1,0:T(8,128)(2,1)S(1)}, u32[]{:S(2)}, u32[]{:S(2)}) collective-permute-start(bf16[32,1408]{1,0:T(8,128)(2,1)S(1)} %get-tuple-element.82.rest_0_), channel_id=1, source_target_pairs={{0,12},{4,8},{8,4},{12,0},{1,13},{5,9},{9,5},{13,1},{2,14},{6,10},... | collective-permute-start | bytes 270344 | tf_op jit(solution)/shard_map/ppermute | solution.py:31
  56.7 7.5 %collective-permute-start.14 = (bf16[32,1408]{1,0:T(8,128)(2,1)S(1)}, bf16[32,1408]{1,0:T(8,128)(2,1)S(1)}, u32[]{:S(2)}, u32[]{:S(2)}) collective-permute-start(bf16[32,1408]{1,0:T(8,128)(2,1)S(1)} %get-tuple-element.82.rest_0_), channel_id=1, source_target_pairs={{0,8},{4,12},{8,0},{12,4},{1,9},{5,13},{9,1},{13,5},{2,10},{6,14},... | collective-permute-start | bytes 270344 | tf_op jit(solution)/shard_map/ppermute | solution.py:31
  56.7 7.5 %collective-permute-start.13 = (bf16[32,1408]{1,0:T(8,128)(2,1)S(1)}, bf16[32,1408]{1,0:T(8,128)(2,1)S(1)}, u32[]{:S(2)}, u32[]{:S(2)}) collective-permute-start(bf16[32,1408]{1,0:T(8,128)(2,1)S(1)} %get-tuple-element.82.rest_0_), channel_id=1, source_target_pairs={{0,4},{4,0},{8,12},{12,8},{1,5},{5,1},{9,13},{13,9},{2,6},{6,2},{1... | collective-permute-start | bytes 270344 | tf_op jit(solution)/shard_map/ppermute | solution.py:31
  58.8 4.0 %collective-permute-start.12 = (bf16[32,640]{1,0:T(8,128)(2,1)S(1)}, bf16[32,640]{1,0:T(8,128)(2,1)S(1)}, u32[]{:S(2)}, u32[]{:S(2)}) collective-permute-start(bf16[32,640]{1,0:T(8,128)(2,1)S(1)} %get-tuple-element.81.piece_q), channel_id=1, source_target_pairs={{0,2},{1,3},{2,0},{3,1},{4,6},{5,7},{6,4},{7,5},{8,10},{9,11},{10,... | collective-permute-start | bytes 122888 | tf_op jit(solution)/shard_map/ppermute | solution.py:31
  64.2 10.3 %collective-permute-start.16 = (bf16[128,1408]{1,0:T(8,128)(2,1)S(1)}, bf16[128,1408]{1,0:T(8,128)(2,1)S(1)}, u32[]{:S(2)}, u32[]{:S(2)}) collective-permute-start(bf16[128,1408]{1,0:T(8,128)(2,1)S(1)} %get-tuple-element.83.block_p), channel_id=1, source_target_pairs={{0,2},{1,3},{2,0},{3,1},{4,6},{5,7},{6,4},{7,5},{8,10},{9,11},{10,... | collective-permute-start | bytes 1081352 | tf_op jit(solution)/shard_map/ppermute | solution.py:31
  64.9 7.2 %collective-permute-start.19 = (bf16[64,640]{1,0:T(8,128)(2,1)S(1)}, bf16[64,640]{1,0:T(8,128)(2,1)S(1)}, u32[]{:S(2)}, u32[]{:S(2)}) collective-permute-start(bf16[64,640]{1,0:T(8,128)(2,1)S(1)} %get-tuple-element.84.rest_0_), channel_id=1, source_target_pairs={{0,12},{4,8},{8,4},{12,0},{1,13},{5,9},{9,5},{13,1},{2,14},{6,10},... | collective-permute-start | bytes 245768 | tf_op jit(solution)/shard_map/ppermute | solution.py:31
  66.6 7.6 %collective-permute-start.18 = (bf16[64,640]{1,0:T(8,128)(2,1)S(1)}, bf16[64,640]{1,0:T(8,128)(2,1)S(1)}, u32[]{:S(2)}, u32[]{:S(2)}) collective-permute-start(bf16[64,640]{1,0:T(8,128)(2,1)S(1)} %get-tuple-element.84.rest_0_), channel_id=1, source_target_pairs={{0,8},{4,12},{8,0},{12,4},{1,9},{5,13},{9,1},{13,5},{2,10},{6,14},... | collective-permute-start | bytes 245768 | tf_op jit(solution)/shard_map/ppermute | solution.py:31
  66.6 7.6 %collective-permute-start.17 = (bf16[64,640]{1,0:T(8,128)(2,1)S(1)}, bf16[64,640]{1,0:T(8,128)(2,1)S(1)}, u32[]{:S(2)}, u32[]{:S(2)}) collective-permute-start(bf16[64,640]{1,0:T(8,128)(2,1)S(1)} %get-tuple-element.84.rest_0_), channel_id=1, source_target_pairs={{0,4},{4,0},{8,12},{12,8},{1,5},{5,1},{9,13},{13,9},{2,6},{6,2},{1... | collective-permute-start | bytes 245768 | tf_op jit(solution)/shard_map/ppermute | solution.py:31
  75.0 4.0 %collective-permute-start.20 = (bf16[256,2048]{1,0:T(8,128)(2,1)S(1)}, bf16[256,2048]{1,0:T(8,128)(2,1)S(1)}, u32[]{:S(2)}, u32[]{:S(2)}) collective-permute-start(bf16[256,2048]{1,0:T(8,128)(2,1)S(1)} %get-tuple-element.85.half), channel_id=1, source_target_pairs={{0,1},{1,0},{2,3},{3,2},{4,5},{5,4},{6,7},{7,6},{8,9},{9,8},{10,11... | collective-permute-start | bytes 3145736 | tf_op jit(solution)/shard_map/ppermute | solution.py:31
  75.0 3.2 %collective-permute-start.23 = (f32[8,384]{1,0:T(8,128)S(1)}, f32[8,384]{1,0:T(8,128)S(1)}, u32[]{:S(2)}, u32[]{:S(2)}) collective-permute-start(f32[8,384]{1,0:T(8,128)S(1)} %get-tuple-element.86.row), channel_id=1, source_target_pairs={{0,17},{1,16},{2,19},{3,18},{16,1},{17,0},{18,3},{19,2},{4,21},{5,... | collective-permute-start | bytes 36872 | tf_op jit(solution)/shard_map/ppermute | solution.py:618
  75.1 3.9 %collective-permute-start.22 = (f32[8,384]{1,0:T(8,128)S(1)}, f32[8,384]{1,0:T(8,128)S(1)}, u32[]{:S(2)}, u32[]{:S(2)}) collective-permute-start(f32[8,384]{1,0:T(8,128)S(1)} %get-tuple-element.86.row), channel_id=1, source_target_pairs={{0,16},{16,0},{1,17},{17,1},{2,18},{18,2},{3,19},{19,3},{4,20},{20... | collective-permute-start | bytes 36872 | tf_op jit(solution)/shard_map/ppermute | solution.py:31
  77.2 1.8 %collective-permute-start.21 = (f32[8,384]{1,0:T(8,128)S(1)}, f32[8,384]{1,0:T(8,128)S(1)}, u32[]{:S(2)}, u32[]{:S(2)}) collective-permute-start(f32[8,384]{1,0:T(8,128)S(1)} %get-tuple-element.86.row), channel_id=1, source_target_pairs={{0,1},{1,0},{2,3},{3,2},{4,5},{5,4},{6,7},{7,6},{8,9},{9,8},{10,11... | collective-permute-start | bytes 36872 | tf_op jit(solution)/shard_map/ppermute | solution.py:31

commit v8 on v7

--- a/solution.py
+++ b/solution.py
@@ -9,7 +9,7 @@
 
 SHIFT = 6
 GROUP = 128
-CUT = 1408
+CUT = 1280
 EPSILON = 1e-05
 F32 = jnp.float32
 BF16 = jnp.bfloat16
@@ -74,26 +74,41 @@
     return lax.rem(lat, 2), lax.div(lat, 2), lon
 
 
+def pack_rim_kernel(tokens, land, rim, tokens_v, land_v, rim32, sems):
+    copies = [started(tokens, tokens_v, sems, 0), started(land, land_v, sems, 1)]
+    lats, cols, levels, width = tokens.shape[1:]
+    half = levels * lats * SHIFT
+    rim32[half:, :] = jnp.zeros((rim32.shape[0] - half, width), F32)
+    copies[0].wait()
+    for lat in range(lats):
+        for col in range(SHIFT):
+            row = (lat * SHIFT + col) * levels
+            rim32[row : row + levels, :] = tokens_v[0, lat, col].astype(F32)
+    copies[1].wait()
+    rim32[half : half + lats, :cols] = land_v[...].astype(F32)
+    rim[...] = rim32[...].astype(BF16)
+
+
 def pack_kernel(
-    tokens, cot, land, gain, bias, own, rim,
+    after, tokens, cot, land, gain, bias, own, rim,
     tokens_v, cot_v, land_v, gain_v, bias_v, rim32, sems,
 ):
-    arrays = ((tokens, tokens_v), (cot, cot_v), (land, land_v), (gain, gain_v), (bias, bias_v))
+    arrays = ((cot, cot_v), (tokens, tokens_v), (land, land_v), (gain, gain_v), (bias, bias_v))
     copies = [started(source, target, sems, i) for i, (source, target) in enumerate(arrays)]
     lats, cols, levels, width = tokens.shape[1:]
     half = levels * lats * SHIFT
-    rim32[2 * half :, :] = jnp.zeros((rim32.shape[0] - 2 * half, width), F32)
+    rim32[half:, :] = jnp.zeros((rim32.shape[0] - half, width), F32)
     own[2 * half :, :] = jnp.zeros((own.shape[0] - 2 * half, width), F32)
-    for which, ref in enumerate((tokens_v, cot_v)):
-        copies[which].wait()
-        for lat in range(lats):
-            for col in range(cols):
-                row = which * half + (lat * SHIFT + col % SHIFT) * levels
-                part = rim32 if col < SHIFT else own
-                part[row : row + levels, :] = ref[0, lat, col].astype(F32)
+    copies[0].wait()
+    copies[1].wait()
+    for lat in range(lats):
+        for col in range(SHIFT):
+            row = (lat * SHIFT + col) * levels
+            rim32[row : row + levels, :] = cot_v[0, lat, col].astype(F32)
+            own[row : row + levels, :] = tokens_v[0, lat, SHIFT + col].astype(F32)
+            own[half + row : half + row + levels, :] = cot_v[0, lat, SHIFT + col].astype(F32)
     for copy in copies[2:]:
         copy.wait()
-    rim32[2 * half : 2 * half + lats, :cols] = land_v[...].astype(F32)
     own[2 * half : 2 * half + 1, :] = gain_v[...]
     own[2 * half + 1 : 2 * half + 2, : bias.shape[1]] = bias_v[...]
     own[2 * half + 8 : 2 * half + 8 + lats, :cols] = land_v[...].astype(F32)
@@ -142,7 +157,7 @@
     return sum(block[i * rows : (i + 1) * rows] * mask for i, mask in enumerate(masks))
 
 
-def back_through(grad_out, probs, probs_b, qkv, keys_t, weight_out, grad_proj, size, land):
+def back_through(grad_out, probs, qkv, keys_t, weight_out, grad_proj, size, land):
     count, width = grad_out.shape
     per = GROUP // size
     scale = size ** (-0.5)
@@ -172,7 +187,7 @@
             queries_t.append(dot(keys_t[head * size : (head + 1) * size, :], scaled_b))
         queries = qkv[:, at : at + GROUP]
         grad_keys = dot(jnp.concatenate(scores_b, axis=0), queries)
-        mixed = probs_b[group * per * count : (group + 1) * per * count, :]
+        mixed = probs[group * per * count : (group + 1) * per * count, :]
         grad_values = dot(mixed, grad_att[:, at : at + GROUP])
         grad_proj[:, at : at + GROUP] = jnp.concatenate(queries_t, axis=0).T.astype(BF16)
         grad_proj[:, width + at : width + at + GROUP] = folded(grad_keys, masks).astype(BF16)
@@ -203,23 +218,22 @@
 
 
 def forward_kernel(
-    own, rim, weight_qkv, weight_t, weight_out,
-    skip, cot, normed_t, qkv, probs_b, attended_t, extra, normed_out,
-    probs, queries_t, keys_t, values_t, grad_proj,
+    own, rim, weight_qkv,
+    normed_t, qkv, probs, attended_t, extra, normed_out,
+    queries_t, values_t,
     *, heads, lats, cols,
 ):
     width = own.shape[1]
     size = width // heads
-    half = cot.shape[0] // 2
-    count = 2 * half
+    count = qkv.shape[0]
+    half = count // 2
     per = GROUP // size
     scale = size ** (-0.5)
     masks_b = head_masks(BF16, size)
-    mine = own[: 2 * half, :]
-    params = own[2 * half :, :]
+    params = own[count:, :]
     came = rim[...].astype(F32)
     gain = params[0:1, :]
-    values = jnp.concatenate([mine[:half], came[:half]], axis=0)
+    values = jnp.concatenate([own[:half, :], came[:half]], axis=0)
     centred = values - jnp.mean(values, axis=-1, keepdims=True)
     inverse = lax.rsqrt(jnp.mean(centred * centred, axis=-1, keepdims=True) + EPSILON)
     normed = centred * inverse
@@ -229,16 +243,17 @@
     land = jnp.concatenate(
         [
             land_column(params[8 : 8 + lats, :cols], half, SHIFT),
-            land_column(came[2 * half : 2 * half + lats, :cols], half, 0),
+            land_column(came[half : half + lats, :cols], half, 0),
         ],
         axis=0,
     )
     extra[:, :GROUP] = jnp.broadcast_to(land, (count, GROUP))
     extra[:, GROUP:] = jnp.broadcast_to(inverse, (count, GROUP))
-    for part, turned in enumerate((queries_t, keys_t, values_t)):
+    for part, turned in enumerate((queries_t, None, values_t)):
         columns = slice(part * width, (part + 1) * width)
         qkv[:, columns] = dot(normed_b, weight_qkv[:, columns]).astype(BF16)
-        turned[...] = qkv[:, columns].T
+        if turned is not None:
+            turned[...] = qkv[:, columns].T
     for group in range(width // GROUP):
         at = group * GROUP
         keys = qkv[:, width + at : width + at + GROUP]
@@ -249,16 +264,28 @@
             block = block + params[1:2, head : head + 1] * land
             block = jnp.exp(block - jnp.max(block, axis=0, keepdims=True))
             weights = block * (1.0 / jnp.sum(block, axis=0, keepdims=True))
-            probs[head * count : (head + 1) * count, :] = weights
             weights_b = weights.astype(BF16)
-            probs_b[head * count : (head + 1) * count, :] = weights_b
+            probs[head * count : (head + 1) * count, :] = weights_b
             out = dot(values_t[head * size : (head + 1) * size, :], weights_b)
             attended_t[head * size : (head + 1) * size, :] = out.astype(BF16)
-    grad_out = jnp.concatenate([mine[half:], came[half : 2 * half]], axis=0)
+
+
+def first_backward_kernel(
+    own, rim, qkv, probs, weight_out, weight_t, extra, normed,
+    skip, cot,
+    keys_t, grad_proj,
+    *, heads,
+):
+    count, width = cot.shape
+    half = count // 2
+    came = rim[...].astype(F32)
+    grad_out = jnp.concatenate([own[half:count, :], came[:half]], axis=0)
     cot[...] = grad_out.astype(BF16)
-    back_through(cot[...], probs, probs_b, qkv, keys_t, weight_out, grad_proj, size, None)
+    keys_t[...] = qkv[:, width : 2 * width].T
+    back_through(cot[...], probs, qkv, keys_t, weight_out, grad_proj, width // heads, None)
+    gain, inverse = own[count : count + 1, :], extra[:, GROUP : GROUP + 1]
     skip[...] = (
-        through_norm(grad_proj[...], weight_t, gain, normed, inverse) + grad_out
+        through_norm(grad_proj[...], weight_t, gain, normed[...], inverse) + grad_out
     ).astype(BF16)
 
 
@@ -273,7 +300,7 @@
     total_out[...] = (cot[...].astype(F32) + skip[...].astype(F32)).astype(BF16)
     keys_t[...] = qkv[:, width : 2 * width].T
     bias_row = back_through(
-        total_out[...], probs, probs, qkv, keys_t, weight_out, grad_proj, width // heads,
+        total_out[...], probs, qkv, keys_t, weight_out, grad_proj, width // heads,
         extra[:, :1],
     )
     bias_out[...] = jnp.broadcast_to(bias_row, bias_out.shape)
@@ -324,7 +351,7 @@
         ref[...] = total[aligned((z ^ other) * piece, piece), wide_p:].astype(BF16)
 
 
-def second_kernel(after, kept_p, came_p, kept_q, *rest):
+def second_kernel(kept_p, came_p, kept_q, *rest):
     _, y, z = position()
     count = (len(rest) - 5) // 2
     came_q, (give_q, left_q, left_p) = rest[:count], rest[count : count + 3]
@@ -345,7 +372,7 @@
     left_q[...] = total_q[aligned(y * half, half), :]
 
 
-def third_kernel(left_p, left_q, came_q, *rest):
+def third_kernel(after, left_p, left_q, came_q, *rest):
     _, _, z = position()
     *came_p, piece_p, piece_q, bias = rest
     total = left_p[:, :CUT]
@@ -460,23 +487,37 @@
     tokens = inputs.transpose(0, 2, 3, 1, 4)
     own_cot = cotangent.transpose(0, 2, 3, 1, 4)
 
-    own, rim = call(
+    (rim,) = call(
+        pack_rim_kernel,
+        [shape((half + 8, width), BF16)],
+        scratch=[
+            vmem(tokens.shape, BF16),
+            vmem(land_sea.shape, jnp.int32),
+            vmem((half + 8, width), F32),
+            copies(2),
+        ],
+        places="hh",
+        operands=(tokens, land_sea),
+        limit=60,
+    )
+    own, rim_cot = call(
         pack_kernel,
-        [shape((packed, width), F32), shape((packed, width), BF16)],
+        [shape((packed, width), F32), shape((half + 8, width), BF16)],
         scratch=[
             vmem(tokens.shape, BF16),
             vmem(tokens.shape, BF16),
             vmem(land_sea.shape, jnp.int32),
             vmem(gains.shape, F32),
             vmem(land_bias.shape, F32),
-            vmem((packed, width), F32),
+            vmem((half + 8, width), F32),
             copies(5),
         ],
-        places="hhhhh",
-        operands=(tokens, own_cot, land_sea, gains, land_bias),
+        places="ahhhhh",
+        operands=(rim, tokens, own_cot, land_sea, gains, land_bias),
         limit=60,
     )
     rim = from_behind(rim, "lon", -1)
+    rim_cot = from_behind(rim_cot, "lon", -1)
     qkv_v, qkv_t, out_v = call(
         ready_kernel,
         [
@@ -489,11 +530,9 @@
         operands=(own, weight_qkv, weight_out),
         limit=48,
     )
-    skip, cot, normed_t, qkv, probs, attended_t, extra, normed = call(
+    normed_t, qkv, probs, attended_t, extra, normed = call(
         functools.partial(forward_kernel, heads=heads, lats=lats, cols=cols),
         [
-            shape((count, width), BF16),
-            shape((count, width), BF16),
             shape((width, count), BF16),
             shape((count, 3 * width), BF16),
             shape((heads * count, count), BF16),
@@ -501,16 +540,16 @@
             shape((count, 2 * GROUP), F32),
             shape((count, width), F32),
         ],
-        scratch=[
-            vmem((heads * count, count), F32),
-            vmem((width, count), BF16),
-            vmem((width, count), BF16),
-            vmem((width, count), BF16),
-            vmem((count, 3 * width), BF16),
-        ],
-        operands=(own, rim, qkv_v, qkv_t, out_v),
+        scratch=[vmem((width, count), BF16), vmem((width, count), BF16)],
+        operands=(own, rim, qkv_v),
         flops=10**9,
-        limit=16,
+    )
+    skip, cot = call(
+        functools.partial(first_backward_kernel, heads=heads),
+        [shape((count, width), BF16), shape((count, width), BF16)],
+        scratch=[vmem((width, count), BF16), vmem((count, 3 * width), BF16)],
+        operands=(own, rim_cot, qkv, probs, out_v, qkv_t, extra, normed),
+        flops=10**9,
     )
     skip = passed_along(skip, "section", -1)
     rows, wide = width // 2, 4 * width + GROUP
@@ -586,8 +625,7 @@
             *(shape((piece, wide_p), BF16) for _ in some),
         ],
         scratch=[vmem((rows // 2, wide_p), F32), vmem((rows // lons, wide_q), F32)],
-        places="avvv" + several,
-        operands=(after, kept_p, came_p, kept_q, *came_q),
+        operands=(kept_p, came_p, kept_q, *came_q),
     )
     came_p = far_first(give_p, "lon")
     came_q = swapped(give_q, "lat", 2)
@@ -598,7 +636,8 @@
             shape((piece, wide_q), BF16),
             shape((8, GROUP), F32),
         ],
-        operands=(left_p, left_q, came_q, *came_p),
+        places="avvv" + several,
+        operands=(after, left_p, left_q, came_q, *came_p),
     )
     others_p = to_all(piece_p, "lon")
     other_q = swapped(piece_q, "lat", 2)

time: 81.5 us -> 84.6 us (1.038)
  Pallas kernels: 15.3 us -> 17.3 us
  waiting for transfers between devices: 30.8 us -> 32.8 us
  starting transfers between devices: 30.9 us -> 30 us
    pallas_call x12 -> x14, Pallas kernels: 15.3 us -> 17.3 us  [call(): pl.pallas_call(kernel, out_shape=list(outs), in_specs=[pl.BlockSpec(memor...]
    ppermute x20, waiting for transfers between devices: 19 us -> 20.8 us  [swapped(): return lax.ppermute(value, axis, [(i, i ^ bit) for i in range(count)])]
    ppermute x2 -> x3, starting transfers between devices: 6.45 us -> 5.64 us  [from_behind(): lax.ppermute(value, axis, [(i, (i + by) % count) for i in range(count)])]
    ppermute x2 -> x3, waiting for transfers between devices: 5.62 us -> 6.06 us  [from_behind(): lax.ppermute(value, axis, [(i, (i + by) % count) for i in range(count)])]
  transfers between devices with their start and end apart: 24 -> 25, of which waited for: 13 -> 11; matrix products, arithmetic and copies ran while one was open for 0% -> 0% of each run, Pallas kernels for 3% -> 8%
where the time goes in v8:
time: 84.6 us; the launch traced here: 84.4 us
  waiting for transfers between devices  32.8 us (39%)
  starting transfers between devices  30 us (35%)
  Pallas kernels  17.3 us (20%)
  local copies, waits for them, and re-layouts  3.43 us (4%)
    ppermute x20, starting transfers between devices, swapped(): return lax.ppermute(value, axis, [(i, i ^ bit) for i in range(count)])  23 us
    ppermute x20, waiting for transfers between devices, swapped(): return lax.ppermute(value, axis, [(i, i ^ bit) for i in range(count)])  20.8 us
    pallas_call x14, Pallas kernels, call(): pl.pallas_call(kernel, out_shape=list(outs), in_specs=[pl.BlockSpec(memor...  17.3 us
    ppermute x3, waiting for transfers between devices, from_behind(): lax.ppermute(value, axis, [(i, (i + by) % count) for i in range(count)])  6.06 us
    ppermute x1, waiting for transfers between devices, passed_along(): return lax.ppermute(block, axis, route)  5.74 us
    ppermute x3, starting transfers between devices, from_behind(): lax.ppermute(value, axis, [(i, (i + by) % count) for i in range(count)])  5.64 us
    unnamed x8, local copies, waits for them, and re-layouts  3.43 us
  transfers between devices with their start and end apart: 25, of which 11 were waited for; matrix products, arithmetic and copies ran while one was open for 0% of the time, Pallas kernels for 8%

profile of v8, /device:TPU:0, one launch (start us, length us, event | category | flops | bytes accessed | tf_op | source)
XLA Modules:
  0.0 84.4 jit_solution(671386944633094399)
XLA Ops:
  0.6 1.6 %shard_map.110.after = bf16[80,512]{1,0:T(8,128)(2,1)} custom-call(bf16[1,6,12,2,512]{4,3,2,1,0:T(2,128)(2,1)} %bitcast.10, s32[6,12]{1,0:T(8,128)} %land.3), custom_call_target="tpu_custom_call" | custom-call | flops 100000000 | bytes 229664 | tf_op jit(solution)/shard_map/pallas_call | solution.py:47
  2.3 5.1 %collective-permute-start.1 = (bf16[80,512]{1,0:T(8,128)(2,1)}, bf16[80,512]{1,0:T(8,128)(2,1)S(1)}, u32[]{:S(2)}, u32[]{:S(2)}) collective-permute-start(bf16[80,512]{1,0:T(8,128)(2,1)} %shard_map.110.after), channel_id=1, source_target_pairs={{0,12},{4,0},{8,4},{12,8},{1,13},{5,1},{9,5},{13,9},{2,14},{6,2},{... | collective-permute-start | bytes 245768 | tf_op jit(solution)/shard_map/ppermute | solution.py:20
  7.4 1.9 %shard_map.111 = (f32[160,512]{1,0:T(8,128)}, bf16[80,512]{1,0:T(8,128)(2,1)}) custom-call(bf16[80,512]{1,0:T(8,128)(2,1)} %shard_map.110.after, bf16[1,6,12,2,512]{4,3,2,1,0:T(2,128)(2,1)} %bitcast.11, bf16[1,6,12,2,512]{4,3,2,1,0:T(2,128)(2,1)} %bitcast.12, s32[6,12]{1,0:T(8,128)} %land.3, f32[1,512]{1,0:T(1,128)} %gain.3, f32[1,16]{1,0:T(1,128)} %bias.1), custom_call_target="tpu_custom_call" | custom-call | flops 100000000 | bytes 788832 | tf_op jit(solution)/shard_map/pallas_call | solution.py:47
  9.3 0.5 collective-permute-start
  9.8 1.0 %copy-done = f32[160,512]{1,0:T(8,128)S(1)} copy-done((f32[160,512]{1,0:T(8,128)S(1)}, f32[160,512]{1,0:T(8,128)}, u32[]{:S(2)}) %copy-start) | copy-done | bytes 327704
  10.7 1.4 %copy-done.1 = bf16[1,512,1536]{2,1,0:T(8,128)(2,1)S(1)} copy-done((bf16[1,512,1536]{2,1,0:T(8,128)(2,1)S(1)}, bf16[1,512,1536]{2,1,0:T(8,128)(2,1)}, u32[]{:S(2)}) %copy-start.1) | copy-done | bytes 1572888
  12.1 1.0 %copy-done.2 = bf16[1,512,512]{2,1,0:T(8,128)(2,1)S(1)} copy-done((bf16[1,512,512]{2,1,0:T(8,128)(2,1)S(1)}, bf16[1,512,512]{2,1,0:T(8,128)(2,1)}, u32[]{:S(2)}) %copy-start.2) | copy-done | bytes 524312
  13.2 0.6 shard_map.112
  13.8 0.0 collective-permute-done.1.rim
  13.8 2.4 %shard_map.113 = (bf16[512,144]{1,0:T(8,128)(2,1)S(1)}, bf16[144,1536]{1,0:T(8,128)(2,1)S(1)}, bf16[2304,144]{1,0:T(8,128)(2,1)S(1)}, bf16[512,144]{1,0:T(8,128)...) custom-call(f32[160,512]{1,0:T(8,128)S(1)} %copy-done, bf16[80,512]{1,0:T(8,128)(2,1)S(1)} %collective-permute-done.1.rim, ...), custom_call_target="tpu_custom_call" | custom-call | flops 1000000000 | bytes 3825664 | tf_op jit(solution)/shard_map/pallas_call | solution.py:47
  16.2 0.0 collective-permute-done.rim
  16.2 2.9 %shard_map.114 = (bf16[144,512]{1,0:T(8,128)(2,1)S(1)}, bf16[144,512]{1,0:T(8,128)(2,1)S(1)}) custom-call(f32[160,512]{1,0:T(8,128)S(1)} %copy-done, bf16[80,512]{1,0:T(8,128)(2,1)S(1)} %collective-permute-done.rim, bf16[144,1536]{1,0:T(8,128)(2,1)S(1)} %get-tuple-element.51.qkv, bf16[2304,144]{1,0:T(8,128)(2,1)S(1)} %get-tuple-element.52.probs, ...), custom_call_target="tpu_custom_call" | custom-call | flops 1000000000 | bytes 4349952 | tf_op jit(solution)/shard_map/pallas_call | solution.py:47
  19.1 1.3 %collective-permute-start.2 = (bf16[144,512]{1,0:T(8,128)(2,1)S(1)}, bf16[144,512]{1,0:T(8,128)(2,1)S(1)}, u32[]{:S(2)}, u32[]{:S(2)}) collective-permute-start(bf16[144,512]{1,0:T(8,128)(2,1)S(1)} %get-tuple-element.57), channel_id=1, source_target_pairs={{16,0},{17,1},{18,2},{19,3},{20,4},{21,5},{22,6},{23,7},{24,8},{25... | collective-permute-start | bytes 442376 | tf_op jit(solution)/shard_map/ppermute | solution.py:26
  20.4 5.7 %collective-permute-done.2.skip = bf16[144,512]{1,0:T(8,128)(2,1)S(1)} collective-permute-done((bf16[144,512]{1,0:T(8,128)(2,1)S(1)}, bf16[144,512]{1,0:T(8,128)(2,1)S(1)}, u32[]{:S(2)}, u32[]{:S(2)}) %collective-permute-start.2) | collective-permute-done | bytes 147488 | tf_op jit(solution)/shard_map/ppermute | solution.py:26
  26.1 2.9 %shard_map.115 = (bf16[144,512]{1,0:T(8,128)(2,1)S(1)}, bf16[144,1536]{1,0:T(8,128)(2,1)S(1)}, f32[8,128]{1,0:T(8,128)S(1)}, bf16[256,2176]{1,0:T(8,128)(2,1)S(1)}) custom-call(bf16[144,512]{1,0:T(8,128)(2,1)S(1)} %collective-permute-done.2.skip, bf16[144,512]{1,0:T(8,128)(2,1)S(1)} %get-tuple-element.58.cot, bf16[144,1536]{1,0:T(8,128)(2,1)S(1)} %get-tuple-element.51.qkv, ...), custom_call_target="tpu_custom_call" | custom-call | flops 1000000000 | bytes 4075520 | tf_op jit(solution)/shard_map/pallas_call | solution.py:47
  29.1 0.1 collective-permute-start.4
  29.2 0.8 shard_map.116
  29.9 2.0 %collective-permute-done.4.came = bf16[256,2176]{1,0:T(8,128)(2,1)S(1)} collective-permute-done((bf16[256,2176]{1,0:T(8,128)(2,1)S(1)}, bf16[256,2176]{1,0:T(8,128)(2,1)S(1)}, u32[]{:S(2)}, u32[]{:S(2)}) %collective-permute-start.4) | collective-permute-done | bytes 1114144 | tf_op jit(solution)/shard_map/ppermute | solution.py:31
  31.9 0.4 shard_map.118
  32.3 0.0 copy-start.3
  32.3 1.6 %collective-permute-start.5 = (bf16[128,1408]{1,0:T(8,128)(2,1)S(1)}, bf16[128,1408]{1,0:T(8,128)(2,1)S(1)}, u32[]{:S(2)}, u32[]{:S(2)}) collective-permute-start(bf16[128,1408]{1,0:T(8,128)(2,1)S(1)} %get-tuple-element.69), channel_id=1, source_target_pairs={{0,2},{1,3},{2,0},{3,1},{4,6},{5,7},{6,4},{7,5},{8,10},{9,11},{10,... | collective-permute-start | bytes 1081352 | tf_op jit(solution)/shard_map/ppermute | solution.py:31
  33.9 0.5 collective-permute-start.6
  34.4 2.6 %collective-permute-start.7 = (bf16[64,768]{1,0:T(8,128)(2,1)S(1)}, bf16[64,768]{1,0:T(8,128)(2,1)S(1)}, u32[]{:S(2)}, u32[]{:S(2)}) collective-permute-start(bf16[64,768]{1,0:T(8,128)(2,1)S(1)} %get-tuple-element.72), channel_id=1, source_target_pairs={{0,8},{4,12},{8,0},{12,4},{1,9},{5,13},{9,1},{13,5},{2,10},{6,14},... | collective-permute-start | bytes 294920 | tf_op jit(solution)/shard_map/ppermute | solution.py:31
  36.9 1.3 %collective-permute-start.8 = (bf16[64,768]{1,0:T(8,128)(2,1)S(1)}, bf16[64,768]{1,0:T(8,128)(2,1)S(1)}, u32[]{:S(2)}, u32[]{:S(2)}) collective-permute-start(bf16[64,768]{1,0:T(8,128)(2,1)S(1)} %get-tuple-element.73), channel_id=1, source_target_pairs={{0,4},{4,0},{8,12},{12,8},{1,5},{5,1},{9,13},{13,9},{2,6},{6,2},{1... | collective-permute-start | bytes 294920 | tf_op jit(solution)/shard_map/ppermute | solution.py:31
  38.3 3.1 %collective-permute-done.6.rest_0_ = bf16[64,768]{1,0:T(8,128)(2,1)S(1)} collective-permute-done((bf16[64,768]{1,0:T(8,128)(2,1)S(1)}, bf16[64,768]{1,0:T(8,128)(2,1)S(1)}, u32[]{:S(2)}, u32[]{:S(2)}) %collective-permute-start.6) | collective-permute-done | bytes 98336 | tf_op jit(solution)/shard_map/ppermute | solution.py:31
  41.4 4.4 %collective-permute-done.7.rest_1_ = bf16[64,768]{1,0:T(8,128)(2,1)S(1)} collective-permute-done((bf16[64,768]{1,0:T(8,128)(2,1)S(1)}, bf16[64,768]{1,0:T(8,128)(2,1)S(1)}, u32[]{:S(2)}, u32[]{:S(2)}) %collective-permute-start.7) | collective-permute-done | bytes 98336 | tf_op jit(solution)/shard_map/ppermute | solution.py:31
  45.8 0.0 collective-permute-done.8.rest_2_
  45.8 0.0 collective-permute-done.5.came_p
  45.8 0.2 shard_map.119
  46.0 1.2 %collective-permute-start.10 = (bf16[32,1408]{1,0:T(8,128)(2,1)S(1)}, bf16[32,1408]{1,0:T(8,128)(2,1)S(1)}, u32[]{:S(2)}, u32[]{:S(2)}) collective-permute-start(bf16[32,1408]{1,0:T(8,128)(2,1)S(1)} %get-tuple-element.77), channel_id=1, source_target_pairs={{0,12},{4,8},{8,4},{12,0},{1,13},{5,9},{9,5},{13,1},{2,14},{6,10},... | collective-permute-start | bytes 270344 | tf_op jit(solution)/shard_map/ppermute | solution.py:31
  47.2 0.0 collective-permute-start.11
  47.2 3.2 %collective-permute-start.12 = (bf16[32,1408]{1,0:T(8,128)(2,1)S(1)}, bf16[32,1408]{1,0:T(8,128)(2,1)S(1)}, u32[]{:S(2)}, u32[]{:S(2)}) collective-permute-start(bf16[32,1408]{1,0:T(8,128)(2,1)S(1)} %get-tuple-element.79), channel_id=1, source_target_pairs={{0,4},{4,0},{8,12},{12,8},{1,5},{5,1},{9,13},{13,9},{2,6},{6,2},{1... | collective-permute-start | bytes 270344 | tf_op jit(solution)/shard_map/ppermute | solution.py:31
  50.4 0.0 collective-permute-start.3
  50.5 0.5 collective-permute-start.9
  51.0 6.1 %collective-permute-done.3.back.after = bf16[72,512]{1,0:T(8,128)(2,1)S(1)} collective-permute-done((bf16[72,512]{1,0:T(8,128)(2,1)S(1)}, bf16[72,512]{1,0:T(8,128)(2,1)S(1)}, u32[]{:S(2)}, u32[]{:S(2)}) %collective-permute-start.3) | collective-permute-done | bytes 73760 | tf_op jit(solution)/shard_map/ppermute | solution.py:20
  57.0 0.0 collective-permute-done.9.came_q
  57.0 0.0 collective-permute-done.10.rest_0_
  57.0 0.0 collective-permute-done.11.rest_1_
  57.0 0.0 collective-permute-done.12.rest_2_
  57.1 0.1 shard_map.120
  57.1 2.0 %collective-permute-start.16 = (bf16[32,1280]{1,0:T(8,128)(2,1)S(1)}, bf16[32,1280]{1,0:T(8,128)(2,1)S(1)}, u32[]{:S(2)}, u32[]{:S(2)}) collective-permute-start(bf16[32,1280]{1,0:T(8,128)(2,1)S(1)} %get-tuple-element.82.rest_0_), channel_id=1, source_target_pairs={{0,12},{4,8},{8,4},{12,0},{1,13},{5,9},{9,5},{13,1},{2,14},{6,10},... | collective-permute-start | bytes 245768 | tf_op jit(solution)/shard_map/ppermute | solution.py:31
  59.1 0.0 collective-permute-start.15
  59.1 2.5 %collective-permute-start.14 = (bf16[32,1280]{1,0:T(8,128)(2,1)S(1)}, bf16[32,1280]{1,0:T(8,128)(2,1)S(1)}, u32[]{:S(2)}, u32[]{:S(2)}) collective-permute-start(bf16[32,1280]{1,0:T(8,128)(2,1)S(1)} %get-tuple-element.82.rest_0_), channel_id=1, source_target_pairs={{0,4},{4,0},{8,12},{12,8},{1,5},{5,1},{9,13},{13,9},{2,6},{6,2},{1... | collective-permute-start | bytes 245768 | tf_op jit(solution)/shard_map/ppermute | solution.py:31
  61.6 0.5 collective-permute-start.13
  62.1 3.6 %collective-permute-done.13.other_q = bf16[32,768]{1,0:T(8,128)(2,1)S(1)} collective-permute-done((bf16[32,768]{1,0:T(8,128)(2,1)S(1)}, bf16[32,768]{1,0:T(8,128)(2,1)S(1)}, u32[]{:S(2)}, u32[]{:S(2)}) %collective-permute-start.13) | collective-permute-done | bytes 49184 | tf_op jit(solution)/shard_map/ppermute | solution.py:31
  65.7 0.8 collective-permute-done.15.rest_2_
  66.5 0.0 collective-permute-done.14.rest_1_
  66.5 0.6 collective-permute-start.17
  67.1 2.3 %collective-permute-start.20 = (bf16[64,768]{1,0:T(8,128)(2,1)S(1)}, bf16[64,768]{1,0:T(8,128)(2,1)S(1)}, u32[]{:S(2)}, u32[]{:S(2)}) collective-permute-start(bf16[64,768]{1,0:T(8,128)(2,1)S(1)} %get-tuple-element.84.rest_0_), channel_id=1, source_target_pairs={{0,12},{4,8},{8,4},{12,0},{1,13},{5,9},{9,5},{13,1},{2,14},{6,10},... | collective-permute-start | bytes 294920 | tf_op jit(solution)/shard_map/ppermute | solution.py:31
  69.4 0.0 collective-permute-start.19
  69.4 2.1 %collective-permute-start.18 = (bf16[64,768]{1,0:T(8,128)(2,1)S(1)}, bf16[64,768]{1,0:T(8,128)(2,1)S(1)}, u32[]{:S(2)}, u32[]{:S(2)}) collective-permute-start(bf16[64,768]{1,0:T(8,128)(2,1)S(1)} %get-tuple-element.84.rest_0_), channel_id=1, source_target_pairs={{0,4},{4,0},{8,12},{12,8},{1,5},{5,1},{9,13},{13,9},{2,6},{6,2},{1... | collective-permute-start | bytes 294920 | tf_op jit(solution)/shard_map/ppermute | solution.py:31
  71.5 3.1 %collective-permute-done.20.rest_3_ = bf16[64,768]{1,0:T(8,128)(2,1)S(1)} collective-permute-done((bf16[64,768]{1,0:T(8,128)(2,1)S(1)}, bf16[64,768]{1,0:T(8,128)(2,1)S(1)}, u32[]{:S(2)}, u32[]{:S(2)}) %collective-permute-start.20) | collective-permute-done | bytes 98336 | tf_op jit(solution)/shard_map/ppermute | solution.py:31
  74.7 3.0 %collective-permute-done.19.rest_2_ = bf16[64,768]{1,0:T(8,128)(2,1)S(1)} collective-permute-done((bf16[64,768]{1,0:T(8,128)(2,1)S(1)}, bf16[64,768]{1,0:T(8,128)(2,1)S(1)}, u32[]{:S(2)}, u32[]{:S(2)}) %collective-permute-start.19) | collective-permute-done | bytes 98336 | tf_op jit(solution)/shard_map/ppermute | solution.py:31
  77.6 0.0 collective-permute-done.18.rest_1_
  77.6 0.0 collective-permute-done.17.other_p
  77.6 0.5 shard_map.122
  78.1 0.1 collective-permute-start.21
  78.2 0.0 collective-permute-start.24
  78.2 2.1 %collective-permute-start.23 = (f32[8,384]{1,0:T(8,128)S(1)}, f32[8,384]{1,0:T(8,128)S(1)}, u32[]{:S(2)}, u32[]{:S(2)}) collective-permute-start(f32[8,384]{1,0:T(8,128)S(1)} %get-tuple-element.86.row), channel_id=1, source_target_pairs={{0,16},{16,0},{1,17},{17,1},{2,18},{18,2},{3,19},{19,3},{4,20},{20... | collective-permute-start | bytes 36872 | tf_op jit(solution)/shard_map/ppermute | solution.py:31
  80.3 0.0 collective-permute-start.22
  80.3 0.8 shard_map.117
  81.1 0.3 collective-permute-done.24.row_both
  81.3 0.8 collective-permute-done.23.row_section
  82.1 2.3 %shard_map.123 = (f32[512,1536]{1,0:T(8,128)}, f32[512,512]{1,0:T(8,128)}, f32[1,512]{1,0:T(1,128)}, f32[1,16]{1,0:T(1,128)}) custom-call(bf16[256,2048]{1,0:T(8,128)(2,1)S(1)} %get-tuple-element.85.half, bf16[256,2048]{1,0:T(8,128)(2,1)S(1)} %collective-permute-done.21.other, f32[8,384]{1,0:T(8,128)S(1)} %get-tuple-element.86.row, ...), custom_call_target="tpu_custom_call" | custom-call | flops 100000000 | bytes 6346816 | tf_op jit(solution)/shard_map/pallas_call | solution.py:47
  (8 shorter events, 0.1 us)
Async XLA Ops:
  2.3 11.6 %collective-permute-start.1 = (bf16[80,512]{1,0:T(8,128)(2,1)}, bf16[80,512]{1,0:T(8,128)(2,1)S(1)}, u32[]{:S(2)}, u32[]{:S(2)}) collective-permute-start(bf16[80,512]{1,0:T(8,128)(2,1)} %shard_map.110.after), channel_id=1, source_target_pairs={{0,12},{4,0},{8,4},{12,8},{1,13},{5,1},{9,5},{13,9},{2,14},{6,2},{... | collective-permute-start | bytes 245768 | tf_op jit(solution)/shard_map/ppermute | solution.py:20
  9.3 7.0 %collective-permute-start = (bf16[80,512]{1,0:T(8,128)(2,1)}, bf16[80,512]{1,0:T(8,128)(2,1)S(1)}, u32[]{:S(2)}, u32[]{:S(2)}) collective-permute-start(bf16[80,512]{1,0:T(8,128)(2,1)} %get-tuple-element.49), channel_id=1, source_target_pairs={{0,12},{4,0},{8,4},{12,8},{1,13},{5,1},{9,5},{13,9},{2,14},{6,2},{... | collective-permute-start | bytes 245768 | tf_op jit(solution)/shard_map/ppermute | solution.py:20
  9.8 1.0 %copy-start = (f32[160,512]{1,0:T(8,128)S(1)}, f32[160,512]{1,0:T(8,128)}, u32[]{:S(2)}) copy-start(f32[160,512]{1,0:T(8,128)} %get-tuple-element.48.after.own.params) | copy-start | bytes 983044
  10.7 1.4 %copy-start.1 = (bf16[1,512,1536]{2,1,0:T(8,128)(2,1)S(1)}, bf16[1,512,1536]{2,1,0:T(8,128)(2,1)}, u32[]{:S(2)}) copy-start(bf16[1,512,1536]{2,1,0:T(8,128)(2,1)} %param.11) | copy-start | bytes 4718596
  12.1 1.0 %copy-start.2 = (bf16[1,512,512]{2,1,0:T(8,128)(2,1)S(1)}, bf16[1,512,512]{2,1,0:T(8,128)(2,1)}, u32[]{:S(2)}) copy-start(bf16[1,512,512]{2,1,0:T(8,128)(2,1)} %param.12) | copy-start | bytes 1572868
  19.1 7.0 %collective-permute-start.2 = (bf16[144,512]{1,0:T(8,128)(2,1)S(1)}, bf16[144,512]{1,0:T(8,128)(2,1)S(1)}, u32[]{:S(2)}, u32[]{:S(2)}) collective-permute-start(bf16[144,512]{1,0:T(8,128)(2,1)S(1)} %get-tuple-element.57), channel_id=1, source_target_pairs={{16,0},{17,1},{18,2},{19,3},{20,4},{21,5},{22,6},{23,7},{24,8},{25... | collective-permute-start | bytes 442376 | tf_op jit(solution)/shard_map/ppermute | solution.py:26
  29.1 2.8 %collective-permute-start.4 = (bf16[256,2176]{1,0:T(8,128)(2,1)S(1)}, bf16[256,2176]{1,0:T(8,128)(2,1)S(1)}, u32[]{:S(2)}, u32[]{:S(2)}) collective-permute-start(bf16[256,2176]{1,0:T(8,128)(2,1)S(1)} %get-tuple-element.67), channel_id=1, source_target_pairs={{0,1},{1,0},{2,3},{3,2},{4,5},{5,4},{6,7},{7,6},{8,9},{9,8},{10,11... | collective-permute-start | bytes 3342344 | tf_op jit(solution)/shard_map/ppermute | solution.py:31
  32.3 45.3 %copy-start.3 = (f32[1,512]{1,0:T(1,128)S(1)}, f32[1,512]{1,0:T(1,128)}, u32[]{:S(2)}) copy-start(f32[1,512]{1,0:T(1,128)} %gain.3) | copy-start | bytes 6148
  32.3 13.5 %collective-permute-start.5 = (bf16[128,1408]{1,0:T(8,128)(2,1)S(1)}, bf16[128,1408]{1,0:T(8,128)(2,1)S(1)}, u32[]{:S(2)}, u32[]{:S(2)}) collective-permute-start(bf16[128,1408]{1,0:T(8,128)(2,1)S(1)} %get-tuple-element.69), channel_id=1, source_target_pairs={{0,2},{1,3},{2,0},{3,1},{4,6},{5,7},{6,4},{7,5},{8,10},{9,11},{10,... | collective-permute-start | bytes 1081352 | tf_op jit(solution)/shard_map/ppermute | solution.py:31
  33.9 7.5 %collective-permute-start.6 = (bf16[64,768]{1,0:T(8,128)(2,1)S(1)}, bf16[64,768]{1,0:T(8,128)(2,1)S(1)}, u32[]{:S(2)}, u32[]{:S(2)}) collective-permute-start(bf16[64,768]{1,0:T(8,128)(2,1)S(1)} %get-tuple-element.71), channel_id=1, source_target_pairs={{0,12},{4,8},{8,4},{12,0},{1,13},{5,9},{9,5},{13,1},{2,14},{6,10},... | collective-permute-start | bytes 294920 | tf_op jit(solution)/shard_map/ppermute | solution.py:31
  34.4 11.4 %collective-permute-start.7 = (bf16[64,768]{1,0:T(8,128)(2,1)S(1)}, bf16[64,768]{1,0:T(8,128)(2,1)S(1)}, u32[]{:S(2)}, u32[]{:S(2)}) collective-permute-start(bf16[64,768]{1,0:T(8,128)(2,1)S(1)} %get-tuple-element.72), channel_id=1, source_target_pairs={{0,8},{4,12},{8,0},{12,4},{1,9},{5,13},{9,1},{13,5},{2,10},{6,14},... | collective-permute-start | bytes 294920 | tf_op jit(solution)/shard_map/ppermute | solution.py:31
  36.9 8.9 %collective-permute-start.8 = (bf16[64,768]{1,0:T(8,128)(2,1)S(1)}, bf16[64,768]{1,0:T(8,128)(2,1)S(1)}, u32[]{:S(2)}, u32[]{:S(2)}) collective-permute-start(bf16[64,768]{1,0:T(8,128)(2,1)S(1)} %get-tuple-element.73), channel_id=1, source_target_pairs={{0,4},{4,0},{8,12},{12,8},{1,5},{5,1},{9,13},{13,9},{2,6},{6,2},{1... | collective-permute-start | bytes 294920 | tf_op jit(solution)/shard_map/ppermute | solution.py:31
  46.0 11.1 %collective-permute-start.10 = (bf16[32,1408]{1,0:T(8,128)(2,1)S(1)}, bf16[32,1408]{1,0:T(8,128)(2,1)S(1)}, u32[]{:S(2)}, u32[]{:S(2)}) collective-permute-start(bf16[32,1408]{1,0:T(8,128)(2,1)S(1)} %get-tuple-element.77), channel_id=1, source_target_pairs={{0,12},{4,8},{8,4},{12,0},{1,13},{5,9},{9,5},{13,1},{2,14},{6,10},... | collective-permute-start | bytes 270344 | tf_op jit(solution)/shard_map/ppermute | solution.py:31
  47.2 9.8 %collective-permute-start.11 = (bf16[32,1408]{1,0:T(8,128)(2,1)S(1)}, bf16[32,1408]{1,0:T(8,128)(2,1)S(1)}, u32[]{:S(2)}, u32[]{:S(2)}) collective-permute-start(bf16[32,1408]{1,0:T(8,128)(2,1)S(1)} %get-tuple-element.78), channel_id=1, source_target_pairs={{0,8},{4,12},{8,0},{12,4},{1,9},{5,13},{9,1},{13,5},{2,10},{6,14},... | collective-permute-start | bytes 270344 | tf_op jit(solution)/shard_map/ppermute | solution.py:31
  47.2 9.8 %collective-permute-start.12 = (bf16[32,1408]{1,0:T(8,128)(2,1)S(1)}, bf16[32,1408]{1,0:T(8,128)(2,1)S(1)}, u32[]{:S(2)}, u32[]{:S(2)}) collective-permute-start(bf16[32,1408]{1,0:T(8,128)(2,1)S(1)} %get-tuple-element.79), channel_id=1, source_target_pairs={{0,4},{4,0},{8,12},{12,8},{1,5},{5,1},{9,13},{13,9},{2,6},{6,2},{1... | collective-permute-start | bytes 270344 | tf_op jit(solution)/shard_map/ppermute | solution.py:31
  50.4 6.6 %collective-permute-start.3 = (bf16[72,512]{1,0:T(8,128)(2,1)S(1)}, bf16[72,512]{1,0:T(8,128)(2,1)S(1)}, u32[]{:S(2)}, u32[]{:S(2)}) collective-permute-start(bf16[72,512]{1,0:T(8,128)(2,1)S(1)} %get-tuple-element.65), channel_id=1, source_target_pairs={{0,4},{4,8},{8,12},{12,0},{1,5},{5,9},{9,13},{13,1},{2,6},{6,10},{... | collective-permute-start | bytes 221192 | tf_op jit(solution)/shard_map/ppermute | solution.py:20
  50.5 6.6 %collective-permute-start.9 = (bf16[32,768]{1,0:T(8,128)(2,1)S(1)}, bf16[32,768]{1,0:T(8,128)(2,1)S(1)}, u32[]{:S(2)}, u32[]{:S(2)}) collective-permute-start(bf16[32,768]{1,0:T(8,128)(2,1)S(1)} %get-tuple-element.76), channel_id=1, source_target_pairs={{0,2},{1,3},{2,0},{3,1},{4,6},{5,7},{6,4},{7,5},{8,10},{9,11},{10,... | collective-permute-start | bytes 147464 | tf_op jit(solution)/shard_map/ppermute | solution.py:31
  57.1 8.5 %collective-permute-start.16 = (bf16[32,1280]{1,0:T(8,128)(2,1)S(1)}, bf16[32,1280]{1,0:T(8,128)(2,1)S(1)}, u32[]{:S(2)}, u32[]{:S(2)}) collective-permute-start(bf16[32,1280]{1,0:T(8,128)(2,1)S(1)} %get-tuple-element.82.rest_0_), channel_id=1, source_target_pairs={{0,12},{4,8},{8,4},{12,0},{1,13},{5,9},{9,5},{13,1},{2,14},{6,10},... | collective-permute-start | bytes 245768 | tf_op jit(solution)/shard_map/ppermute | solution.py:31
  59.1 7.4 %collective-permute-start.15 = (bf16[32,1280]{1,0:T(8,128)(2,1)S(1)}, bf16[32,1280]{1,0:T(8,128)(2,1)S(1)}, u32[]{:S(2)}, u32[]{:S(2)}) collective-permute-start(bf16[32,1280]{1,0:T(8,128)(2,1)S(1)} %get-tuple-element.82.rest_0_), channel_id=1, source_target_pairs={{0,8},{4,12},{8,0},{12,4},{1,9},{5,13},{9,1},{13,5},{2,10},{6,14},... | collective-permute-start | bytes 245768 | tf_op jit(solution)/shard_map/ppermute | solution.py:31
  59.1 7.4 %collective-permute-start.14 = (bf16[32,1280]{1,0:T(8,128)(2,1)S(1)}, bf16[32,1280]{1,0:T(8,128)(2,1)S(1)}, u32[]{:S(2)}, u32[]{:S(2)}) collective-permute-start(bf16[32,1280]{1,0:T(8,128)(2,1)S(1)} %get-tuple-element.82.rest_0_), channel_id=1, source_target_pairs={{0,4},{4,0},{8,12},{12,8},{1,5},{5,1},{9,13},{13,9},{2,6},{6,2},{1... | collective-permute-start | bytes 245768 | tf_op jit(solution)/shard_map/ppermute | solution.py:31
  61.6 4.1 %collective-permute-start.13 = (bf16[32,768]{1,0:T(8,128)(2,1)S(1)}, bf16[32,768]{1,0:T(8,128)(2,1)S(1)}, u32[]{:S(2)}, u32[]{:S(2)}) collective-permute-start(bf16[32,768]{1,0:T(8,128)(2,1)S(1)} %get-tuple-element.81.piece_q), channel_id=1, source_target_pairs={{0,2},{1,3},{2,0},{3,1},{4,6},{5,7},{6,4},{7,5},{8,10},{9,11},{10,... | collective-permute-start | bytes 147464 | tf_op jit(solution)/shard_map/ppermute | solution.py:31
  66.5 11.1 %collective-permute-start.17 = (bf16[128,1280]{1,0:T(8,128)(2,1)S(1)}, bf16[128,1280]{1,0:T(8,128)(2,1)S(1)}, u32[]{:S(2)}, u32[]{:S(2)}) collective-permute-start(bf16[128,1280]{1,0:T(8,128)(2,1)S(1)} %get-tuple-element.83.block_p), channel_id=1, source_target_pairs={{0,2},{1,3},{2,0},{3,1},{4,6},{5,7},{6,4},{7,5},{8,10},{9,11},{10,... | collective-permute-start | bytes 983048 | tf_op jit(solution)/shard_map/ppermute | solution.py:31
  67.1 7.5 %collective-permute-start.20 = (bf16[64,768]{1,0:T(8,128)(2,1)S(1)}, bf16[64,768]{1,0:T(8,128)(2,1)S(1)}, u32[]{:S(2)}, u32[]{:S(2)}) collective-permute-start(bf16[64,768]{1,0:T(8,128)(2,1)S(1)} %get-tuple-element.84.rest_0_), channel_id=1, source_target_pairs={{0,12},{4,8},{8,4},{12,0},{1,13},{5,9},{9,5},{13,1},{2,14},{6,10},... | collective-permute-start | bytes 294920 | tf_op jit(solution)/shard_map/ppermute | solution.py:31
  69.4 8.2 %collective-permute-start.19 = (bf16[64,768]{1,0:T(8,128)(2,1)S(1)}, bf16[64,768]{1,0:T(8,128)(2,1)S(1)}, u32[]{:S(2)}, u32[]{:S(2)}) collective-permute-start(bf16[64,768]{1,0:T(8,128)(2,1)S(1)} %get-tuple-element.84.rest_0_), channel_id=1, source_target_pairs={{0,8},{4,12},{8,0},{12,4},{1,9},{5,13},{9,1},{13,5},{2,10},{6,14},... | collective-permute-start | bytes 294920 | tf_op jit(solution)/shard_map/ppermute | solution.py:31
  69.4 8.2 %collective-permute-start.18 = (bf16[64,768]{1,0:T(8,128)(2,1)S(1)}, bf16[64,768]{1,0:T(8,128)(2,1)S(1)}, u32[]{:S(2)}, u32[]{:S(2)}) collective-permute-start(bf16[64,768]{1,0:T(8,128)(2,1)S(1)} %get-tuple-element.84.rest_0_), channel_id=1, source_target_pairs={{0,4},{4,0},{8,12},{12,8},{1,5},{5,1},{9,13},{13,9},{2,6},{6,2},{1... | collective-permute-start | bytes 294920 | tf_op jit(solution)/shard_map/ppermute | solution.py:31
  78.1 4.0 %collective-permute-start.21 = (bf16[256,2048]{1,0:T(8,128)(2,1)S(1)}, bf16[256,2048]{1,0:T(8,128)(2,1)S(1)}, u32[]{:S(2)}, u32[]{:S(2)}) collective-permute-start(bf16[256,2048]{1,0:T(8,128)(2,1)S(1)} %get-tuple-element.85.half), channel_id=1, source_target_pairs={{0,1},{1,0},{2,3},{3,2},{4,5},{5,4},{6,7},{7,6},{8,9},{9,8},{10,11... | collective-permute-start | bytes 3145736 | tf_op jit(solution)/shard_map/ppermute | solution.py:31
  78.2 3.2 %collective-permute-start.24 = (f32[8,384]{1,0:T(8,128)S(1)}, f32[8,384]{1,0:T(8,128)S(1)}, u32[]{:S(2)}, u32[]{:S(2)}) collective-permute-start(f32[8,384]{1,0:T(8,128)S(1)} %get-tuple-element.86.row), channel_id=1, source_target_pairs={{0,17},{1,16},{2,19},{3,18},{16,1},{17,0},{18,3},{19,2},{4,21},{5,... | collective-permute-start | bytes 36872 | tf_op jit(solution)/shard_map/ppermute | solution.py:657
  78.2 3.9 %collective-permute-start.23 = (f32[8,384]{1,0:T(8,128)S(1)}, f32[8,384]{1,0:T(8,128)S(1)}, u32[]{:S(2)}, u32[]{:S(2)}) collective-permute-start(f32[8,384]{1,0:T(8,128)S(1)} %get-tuple-element.86.row), channel_id=1, source_target_pairs={{0,16},{16,0},{1,17},{17,1},{2,18},{18,2},{3,19},{19,3},{4,20},{20... | collective-permute-start | bytes 36872 | tf_op jit(solution)/shard_map/ppermute | solution.py:31
  80.3 1.8 %collective-permute-start.22 = (f32[8,384]{1,0:T(8,128)S(1)}, f32[8,384]{1,0:T(8,128)S(1)}, u32[]{:S(2)}, u32[]{:S(2)}) collective-permute-start(f32[8,384]{1,0:T(8,128)S(1)} %get-tuple-element.86.row), channel_id=1, source_target_pairs={{0,1},{1,0},{2,3},{3,2},{4,5},{5,4},{6,7},{7,6},{8,9},{9,8},{10,11... | collective-permute-start | bytes 36872 | tf_op jit(solution)/shard_map/ppermute | solution.py:31

commit v9 on v8

--- a/solution.py
+++ b/solution.py
@@ -74,45 +74,33 @@
     return lax.rem(lat, 2), lax.div(lat, 2), lon
 
 
-def pack_rim_kernel(tokens, land, rim, tokens_v, land_v, rim32, sems):
-    copies = [started(tokens, tokens_v, sems, 0), started(land, land_v, sems, 1)]
-    lats, cols, levels, width = tokens.shape[1:]
-    half = levels * lats * SHIFT
-    rim32[half:, :] = jnp.zeros((rim32.shape[0] - half, width), F32)
-    copies[0].wait()
-    for lat in range(lats):
-        for col in range(SHIFT):
-            row = (lat * SHIFT + col) * levels
-            rim32[row : row + levels, :] = tokens_v[0, lat, col].astype(F32)
-    copies[1].wait()
-    rim32[half : half + lats, :cols] = land_v[...].astype(F32)
-    rim[...] = rim32[...].astype(BF16)
-
-
 def pack_kernel(
-    after, tokens, cot, land, gain, bias, own, rim,
-    tokens_v, cot_v, land_v, gain_v, bias_v, rim32, sems,
+    tokens, cot, land, gain, bias, own, rim, rim_cot,
+    tokens_v, cot_v, land_v, gain_v, bias_v, rim32, rim_cot32, sems,
 ):
-    arrays = ((cot, cot_v), (tokens, tokens_v), (land, land_v), (gain, gain_v), (bias, bias_v))
+    arrays = ((tokens, tokens_v), (cot, cot_v), (land, land_v), (gain, gain_v), (bias, bias_v))
     copies = [started(source, target, sems, i) for i, (source, target) in enumerate(arrays)]
     lats, cols, levels, width = tokens.shape[1:]
     half = levels * lats * SHIFT
     rim32[half:, :] = jnp.zeros((rim32.shape[0] - half, width), F32)
+    rim_cot32[half:, :] = jnp.zeros((rim32.shape[0] - half, width), F32)
     own[2 * half :, :] = jnp.zeros((own.shape[0] - 2 * half, width), F32)
-    copies[0].wait()
-    copies[1].wait()
-    for lat in range(lats):
-        for col in range(SHIFT):
-            row = (lat * SHIFT + col) * levels
-            rim32[row : row + levels, :] = cot_v[0, lat, col].astype(F32)
-            own[row : row + levels, :] = tokens_v[0, lat, SHIFT + col].astype(F32)
-            own[half + row : half + row + levels, :] = cot_v[0, lat, SHIFT + col].astype(F32)
+    for which, (ref, part) in enumerate(((tokens_v, rim32), (cot_v, rim_cot32))):
+        copies[which].wait()
+        for lat in range(lats):
+            for col in range(SHIFT):
+                row = (lat * SHIFT + col) * levels
+                part[row : row + levels, :] = ref[0, lat, col].astype(F32)
+                row = row + which * half
+                own[row : row + levels, :] = ref[0, lat, SHIFT + col].astype(F32)
     for copy in copies[2:]:
         copy.wait()
+    rim32[half : half + lats, :cols] = land_v[...].astype(F32)
     own[2 * half : 2 * half + 1, :] = gain_v[...]
     own[2 * half + 1 : 2 * half + 2, : bias.shape[1]] = bias_v[...]
     own[2 * half + 8 : 2 * half + 8 + lats, :cols] = land_v[...].astype(F32)
     rim[...] = rim32[...].astype(BF16)
+    rim_cot[...] = rim_cot32[...].astype(BF16)
 
 
 def unpack_kernel(own, back, grid, grid_v, sems):
@@ -351,7 +339,7 @@
         ref[...] = total[aligned((z ^ other) * piece, piece), wide_p:].astype(BF16)
 
 
-def second_kernel(kept_p, came_p, kept_q, *rest):
+def second_kernel(after, kept_p, came_p, kept_q, *rest):
     _, y, z = position()
     count = (len(rest) - 5) // 2
     came_q, (give_q, left_q, left_p) = rest[:count], rest[count : count + 3]
@@ -372,7 +360,7 @@
     left_q[...] = total_q[aligned(y * half, half), :]
 
 
-def third_kernel(after, left_p, left_q, came_q, *rest):
+def third_kernel(left_p, left_q, came_q, *rest):
     _, _, z = position()
     *came_p, piece_p, piece_q, bias = rest
     total = left_p[:, :CUT]
@@ -487,22 +475,13 @@
     tokens = inputs.transpose(0, 2, 3, 1, 4)
     own_cot = cotangent.transpose(0, 2, 3, 1, 4)
 
-    (rim,) = call(
-        pack_rim_kernel,
-        [shape((half + 8, width), BF16)],
-        scratch=[
-            vmem(tokens.shape, BF16),
-            vmem(land_sea.shape, jnp.int32),
-            vmem((half + 8, width), F32),
-            copies(2),
-        ],
-        places="hh",
-        operands=(tokens, land_sea),
-        limit=60,
-    )
-    own, rim_cot = call(
+    own, rim, rim_cot = call(
         pack_kernel,
-        [shape((packed, width), F32), shape((half + 8, width), BF16)],
+        [
+            shape((packed, width), F32),
+            shape((half + 8, width), BF16),
+            shape((half + 8, width), BF16),
+        ],
         scratch=[
             vmem(tokens.shape, BF16),
             vmem(tokens.shape, BF16),
@@ -510,10 +489,11 @@
             vmem(gains.shape, F32),
             vmem(land_bias.shape, F32),
             vmem((half + 8, width), F32),
+            vmem((half + 8, width), F32),
             copies(5),
         ],
-        places="ahhhhh",
-        operands=(rim, tokens, own_cot, land_sea, gains, land_bias),
+        places="hhhhh",
+        operands=(tokens, own_cot, land_sea, gains, land_bias),
         limit=60,
     )
     rim = from_behind(rim, "lon", -1)
@@ -625,7 +605,8 @@
             *(shape((piece, wide_p), BF16) for _ in some),
         ],
         scratch=[vmem((rows // 2, wide_p), F32), vmem((rows // lons, wide_q), F32)],
-        operands=(kept_p, came_p, kept_q, *came_q),
+        places="avvv" + several,
+        operands=(after, kept_p, came_p, kept_q, *came_q),
     )
     came_p = far_first(give_p, "lon")
     came_q = swapped(give_q, "lat", 2)
@@ -636,8 +617,7 @@
             shape((piece, wide_q), BF16),
             shape((8, GROUP), F32),
         ],
-        places="avvv" + several,
-        operands=(after, left_p, left_q, came_q, *came_p),
+        operands=(left_p, left_q, came_q, *came_p),
     )
     others_p = to_all(piece_p, "lon")
     other_q = swapped(piece_q, "lat", 2)

time: 84.6 us -> 83.4 us (0.986)
  Pallas kernels: 17.3 us -> 15.6 us
    pallas_call x14 -> x13, Pallas kernels: 17.3 us -> 15.6 us  [call(): pl.pallas_call(kernel, out_shape=list(outs), in_specs=[pl.BlockSpec(memor...]
    ppermute x20, waiting for transfers between devices: 20.8 us -> 19.6 us  [swapped(): return lax.ppermute(value, axis, [(i, i ^ bit) for i in range(count)])]
    ppermute x3, waiting for transfers between devices: 6.06 us -> 7.13 us  [from_behind(): lax.ppermute(value, axis, [(i, (i + by) % count) for i in range(count)])]
  transfers between devices with their start and end apart: 25 -> 25, of which waited for: 11 -> 12; matrix products, arithmetic and copies ran while one was open for 0% -> 0% of each run, Pallas kernels for 8% -> 5%
where the time goes in v9:
time: 83.4 us; the launch traced here: 83.2 us
  waiting for transfers between devices  32.8 us (39%)
  starting transfers between devices  30.6 us (37%)
  Pallas kernels  15.6 us (19%)
  local copies, waits for them, and re-layouts  3.43 us (4%)
    ppermute x20, starting transfers between devices, swapped(): return lax.ppermute(value, axis, [(i, i ^ bit) for i in range(count)])  23 us
    ppermute x20, waiting for transfers between devices, swapped(): return lax.ppermute(value, axis, [(i, i ^ bit) for i in range(count)])  19.6 us
    pallas_call x13, Pallas kernels, call(): pl.pallas_call(kernel, out_shape=list(outs), in_specs=[pl.BlockSpec(memor...  15.6 us
    ppermute x3, waiting for transfers between devices, from_behind(): lax.ppermute(value, axis, [(i, (i + by) % count) for i in range(count)])  7.13 us
    ppermute x3, starting transfers between devices, from_behind(): lax.ppermute(value, axis, [(i, (i + by) % count) for i in range(count)])  6.23 us
    ppermute x1, waiting for transfers between devices, passed_along(): return lax.ppermute(block, axis, route)  5.74 us
    unnamed x8, local copies, waits for them, and re-layouts  3.43 us
  transfers between devices with their start and end apart: 25, of which 12 were waited for; matrix products, arithmetic and copies ran while one was open for 0% of the time, Pallas kernels for 5%

profile of v9, /device:TPU:0, one launch (start us, length us, event | category | flops | bytes accessed | tf_op | source)
XLA Modules:
  0.0 83.2 jit_solution(1966518518300025787)
XLA Ops:
  0.6 1.9 %shard_map.110 = (f32[160,512]{1,0:T(8,128)}, bf16[80,512]{1,0:T(8,128)(2,1)}, bf16[80,512]{1,0:T(8,128)(2,1)}) custom-call(bf16[1,6,12,2,512]{4,3,2,1,0:T(2,128)(2,1)} %bitcast.12, bf16[1,6,12,2,512]{4,3,2,1,0:T(2,128)(2,1)} %bitcast.13, s32[6,12]{1,0:T(8,128)} %land.1, f32[1,512]{1,0:T(1,128)} %gain.3, f32[1,16]{1,0:T(1,128)} %bias.1), custom_call_target="tpu_custom_call" | custom-call | flops 100000000 | bytes 788832 | tf_op jit(solution)/shard_map/pallas_call | solution.py:47
  2.5 5.1 %collective-permute-start.1 = (bf16[80,512]{1,0:T(8,128)(2,1)}, bf16[80,512]{1,0:T(8,128)(2,1)S(1)}, u32[]{:S(2)}, u32[]{:S(2)}) collective-permute-start(bf16[80,512]{1,0:T(8,128)(2,1)} %get-tuple-element.51), channel_id=1, source_target_pairs={{0,12},{4,0},{8,4},{12,8},{1,13},{5,1},{9,5},{13,9},{2,14},{6,2},{... | collective-permute-start | bytes 245768 | tf_op jit(solution)/shard_map/ppermute | solution.py:20
  7.6 0.4 collective-permute-start
  8.1 1.0 %copy-done = f32[160,512]{1,0:T(8,128)S(1)} copy-done((f32[160,512]{1,0:T(8,128)S(1)}, f32[160,512]{1,0:T(8,128)}, u32[]{:S(2)}) %copy-start) | copy-done | bytes 327704
  9.1 1.4 %copy-done.1 = bf16[1,512,1536]{2,1,0:T(8,128)(2,1)S(1)} copy-done((bf16[1,512,1536]{2,1,0:T(8,128)(2,1)S(1)}, bf16[1,512,1536]{2,1,0:T(8,128)(2,1)}, u32[]{:S(2)}) %copy-start.1) | copy-done | bytes 1572888
  10.5 1.0 %copy-done.2 = bf16[1,512,512]{2,1,0:T(8,128)(2,1)S(1)} copy-done((bf16[1,512,512]{2,1,0:T(8,128)(2,1)S(1)}, bf16[1,512,512]{2,1,0:T(8,128)(2,1)}, u32[]{:S(2)}) %copy-start.2) | copy-done | bytes 524312
  11.5 0.6 shard_map.111
  12.1 0.0 collective-permute-done.1.rim
  12.2 2.4 %shard_map.112 = (bf16[512,144]{1,0:T(8,128)(2,1)S(1)}, bf16[144,1536]{1,0:T(8,128)(2,1)S(1)}, bf16[2304,144]{1,0:T(8,128)(2,1)S(1)}, bf16[512,144]{1,0:T(8,128)...) custom-call(f32[160,512]{1,0:T(8,128)S(1)} %copy-done, bf16[80,512]{1,0:T(8,128)(2,1)S(1)} %collective-permute-done.1.rim, ...), custom_call_target="tpu_custom_call" | custom-call | flops 1000000000 | bytes 3825664 | tf_op jit(solution)/shard_map/pallas_call | solution.py:47
  14.6 0.0 collective-permute-done.rim
  14.6 2.8 %shard_map.113 = (bf16[144,512]{1,0:T(8,128)(2,1)S(1)}, bf16[144,512]{1,0:T(8,128)(2,1)S(1)}) custom-call(f32[160,512]{1,0:T(8,128)S(1)} %copy-done, bf16[80,512]{1,0:T(8,128)(2,1)S(1)} %collective-permute-done.rim, bf16[144,1536]{1,0:T(8,128)(2,1)S(1)} %get-tuple-element.53.qkv, bf16[2304,144]{1,0:T(8,128)(2,1)S(1)} %get-tuple-element.54.probs, ...), custom_call_target="tpu_custom_call" | custom-call | flops 1000000000 | bytes 4349952 | tf_op jit(solution)/shard_map/pallas_call | solution.py:47
  17.4 1.3 %collective-permute-start.2 = (bf16[144,512]{1,0:T(8,128)(2,1)S(1)}, bf16[144,512]{1,0:T(8,128)(2,1)S(1)}, u32[]{:S(2)}, u32[]{:S(2)}) collective-permute-start(bf16[144,512]{1,0:T(8,128)(2,1)S(1)} %get-tuple-element.59), channel_id=1, source_target_pairs={{16,0},{17,1},{18,2},{19,3},{20,4},{21,5},{22,6},{23,7},{24,8},{25... | collective-permute-start | bytes 442376 | tf_op jit(solution)/shard_map/ppermute | solution.py:26
  18.7 5.7 %collective-permute-done.2.skip = bf16[144,512]{1,0:T(8,128)(2,1)S(1)} collective-permute-done((bf16[144,512]{1,0:T(8,128)(2,1)S(1)}, bf16[144,512]{1,0:T(8,128)(2,1)S(1)}, u32[]{:S(2)}, u32[]{:S(2)}) %collective-permute-start.2) | collective-permute-done | bytes 147488 | tf_op jit(solution)/shard_map/ppermute | solution.py:26
  24.4 2.9 %shard_map.114 = (bf16[144,512]{1,0:T(8,128)(2,1)S(1)}, bf16[144,1536]{1,0:T(8,128)(2,1)S(1)}, f32[8,128]{1,0:T(8,128)S(1)}, bf16[256,2176]{1,0:T(8,128)(2,1)S(1)}) custom-call(bf16[144,512]{1,0:T(8,128)(2,1)S(1)} %collective-permute-done.2.skip, bf16[144,512]{1,0:T(8,128)(2,1)S(1)} %get-tuple-element.60.cot, bf16[144,1536]{1,0:T(8,128)(2,1)S(1)} %get-tuple-element.53.qkv, ...), custom_call_target="tpu_custom_call" | custom-call | flops 1000000000 | bytes 4075520 | tf_op jit(solution)/shard_map/pallas_call | solution.py:47
  27.3 0.1 collective-permute-start.4
  27.4 0.8 shard_map.115
  28.2 2.0 %collective-permute-done.4.came = bf16[256,2176]{1,0:T(8,128)(2,1)S(1)} collective-permute-done((bf16[256,2176]{1,0:T(8,128)(2,1)S(1)}, bf16[256,2176]{1,0:T(8,128)(2,1)S(1)}, u32[]{:S(2)}, u32[]{:S(2)}) %collective-permute-start.4) | collective-permute-done | bytes 1114144 | tf_op jit(solution)/shard_map/ppermute | solution.py:31
  30.2 0.4 shard_map.117
  30.5 0.0 copy-start.3
  30.5 1.6 %collective-permute-start.5 = (bf16[128,1408]{1,0:T(8,128)(2,1)S(1)}, bf16[128,1408]{1,0:T(8,128)(2,1)S(1)}, u32[]{:S(2)}, u32[]{:S(2)}) collective-permute-start(bf16[128,1408]{1,0:T(8,128)(2,1)S(1)} %get-tuple-element.71), channel_id=1, source_target_pairs={{0,2},{1,3},{2,0},{3,1},{4,6},{5,7},{6,4},{7,5},{8,10},{9,11},{10,... | collective-permute-start | bytes 1081352 | tf_op jit(solution)/shard_map/ppermute | solution.py:31
  32.1 2.6 %collective-permute-start.6 = (bf16[64,768]{1,0:T(8,128)(2,1)S(1)}, bf16[64,768]{1,0:T(8,128)(2,1)S(1)}, u32[]{:S(2)}, u32[]{:S(2)}) collective-permute-start(bf16[64,768]{1,0:T(8,128)(2,1)S(1)} %get-tuple-element.73), channel_id=1, source_target_pairs={{0,12},{4,8},{8,4},{12,0},{1,13},{5,9},{9,5},{13,1},{2,14},{6,10},... | collective-permute-start | bytes 294920 | tf_op jit(solution)/shard_map/ppermute | solution.py:31
  34.7 0.5 collective-permute-start.7
  35.2 1.3 %collective-permute-start.8 = (bf16[64,768]{1,0:T(8,128)(2,1)S(1)}, bf16[64,768]{1,0:T(8,128)(2,1)S(1)}, u32[]{:S(2)}, u32[]{:S(2)}) collective-permute-start(bf16[64,768]{1,0:T(8,128)(2,1)S(1)} %get-tuple-element.75), channel_id=1, source_target_pairs={{0,4},{4,0},{8,12},{12,8},{1,5},{5,1},{9,13},{13,9},{2,6},{6,2},{1... | collective-permute-start | bytes 294920 | tf_op jit(solution)/shard_map/ppermute | solution.py:31
  36.5 0.7 collective-permute-start.3
  37.2 7.1 %collective-permute-done.3.back.after = bf16[72,512]{1,0:T(8,128)(2,1)S(1)} collective-permute-done((bf16[72,512]{1,0:T(8,128)(2,1)S(1)}, bf16[72,512]{1,0:T(8,128)(2,1)S(1)}, u32[]{:S(2)}, u32[]{:S(2)}) %collective-permute-start.3) | collective-permute-done | bytes 73760 | tf_op jit(solution)/shard_map/ppermute | solution.py:20
  44.3 0.0 collective-permute-done.6.rest_0_
  44.3 1.3 %collective-permute-done.7.rest_1_ = bf16[64,768]{1,0:T(8,128)(2,1)S(1)} collective-permute-done((bf16[64,768]{1,0:T(8,128)(2,1)S(1)}, bf16[64,768]{1,0:T(8,128)(2,1)S(1)}, u32[]{:S(2)}, u32[]{:S(2)}) %collective-permute-start.7) | collective-permute-done | bytes 98336 | tf_op jit(solution)/shard_map/ppermute | solution.py:31
  45.6 0.0 collective-permute-done.8.rest_2_
  45.6 0.0 collective-permute-done.5.came_p
  45.6 0.2 shard_map.118
  45.8 1.3 %collective-permute-start.10 = (bf16[32,1408]{1,0:T(8,128)(2,1)S(1)}, bf16[32,1408]{1,0:T(8,128)(2,1)S(1)}, u32[]{:S(2)}, u32[]{:S(2)}) collective-permute-start(bf16[32,1408]{1,0:T(8,128)(2,1)S(1)} %get-tuple-element.79), channel_id=1, source_target_pairs={{0,12},{4,8},{8,4},{12,0},{1,13},{5,9},{9,5},{13,1},{2,14},{6,10},... | collective-permute-start | bytes 270344 | tf_op jit(solution)/shard_map/ppermute | solution.py:31
  47.1 0.0 collective-permute-start.11
  47.1 3.1 %collective-permute-start.12 = (bf16[32,1408]{1,0:T(8,128)(2,1)S(1)}, bf16[32,1408]{1,0:T(8,128)(2,1)S(1)}, u32[]{:S(2)}, u32[]{:S(2)}) collective-permute-start(bf16[32,1408]{1,0:T(8,128)(2,1)S(1)} %get-tuple-element.81), channel_id=1, source_target_pairs={{0,4},{4,0},{8,12},{12,8},{1,5},{5,1},{9,13},{13,9},{2,6},{6,2},{1... | collective-permute-start | bytes 270344 | tf_op jit(solution)/shard_map/ppermute | solution.py:31
  50.3 0.5 collective-permute-start.9
  50.8 3.6 %collective-permute-done.9.came_q = bf16[32,768]{1,0:T(8,128)(2,1)S(1)} collective-permute-done((bf16[32,768]{1,0:T(8,128)(2,1)S(1)}, bf16[32,768]{1,0:T(8,128)(2,1)S(1)}, u32[]{:S(2)}, u32[]{:S(2)}) %collective-permute-start.9) | collective-permute-done | bytes 49184 | tf_op jit(solution)/shard_map/ppermute | solution.py:31
  54.3 0.0 collective-permute-done.10.rest_0_
  54.4 0.9 %collective-permute-done.11.rest_1_ = bf16[32,1408]{1,0:T(8,128)(2,1)S(1)} collective-permute-done((bf16[32,1408]{1,0:T(8,128)(2,1)S(1)}, bf16[32,1408]{1,0:T(8,128)(2,1)S(1)}, u32[]{:S(2)}, u32[]{:S(2)}) %collective-permute-start.11) | collective-permute-done | bytes 90144 | tf_op jit(solution)/shard_map/ppermute | solution.py:31
  55.3 0.0 collective-permute-done.12.rest_2_
  55.3 0.1 shard_map.119
  55.3 2.2 %collective-permute-start.16 = (bf16[32,1280]{1,0:T(8,128)(2,1)S(1)}, bf16[32,1280]{1,0:T(8,128)(2,1)S(1)}, u32[]{:S(2)}, u32[]{:S(2)}) collective-permute-start(bf16[32,1280]{1,0:T(8,128)(2,1)S(1)} %get-tuple-element.84.rest_0_), channel_id=1, source_target_pairs={{0,12},{4,8},{8,4},{12,0},{1,13},{5,9},{9,5},{13,1},{2,14},{6,10},... | collective-permute-start | bytes 245768 | tf_op jit(solution)/shard_map/ppermute | solution.py:31
  57.6 2.2 %collective-permute-start.14 = (bf16[32,1280]{1,0:T(8,128)(2,1)S(1)}, bf16[32,1280]{1,0:T(8,128)(2,1)S(1)}, u32[]{:S(2)}, u32[]{:S(2)}) collective-permute-start(bf16[32,1280]{1,0:T(8,128)(2,1)S(1)} %get-tuple-element.84.rest_0_), channel_id=1, source_target_pairs={{0,4},{4,0},{8,12},{12,8},{1,5},{5,1},{9,13},{13,9},{2,6},{6,2},{1... | collective-permute-start | bytes 245768 | tf_op jit(solution)/shard_map/ppermute | solution.py:31
  59.8 0.5 collective-permute-start.13
  60.3 3.6 %collective-permute-done.13.other_q = bf16[32,768]{1,0:T(8,128)(2,1)S(1)} collective-permute-done((bf16[32,768]{1,0:T(8,128)(2,1)S(1)}, bf16[32,768]{1,0:T(8,128)(2,1)S(1)}, u32[]{:S(2)}, u32[]{:S(2)}) %collective-permute-start.13) | collective-permute-done | bytes 49184 | tf_op jit(solution)/shard_map/ppermute | solution.py:31
  63.9 0.0 collective-permute-done.16.rest_3_
  63.9 1.2 %collective-permute-done.15.rest_2_ = bf16[32,1280]{1,0:T(8,128)(2,1)S(1)} collective-permute-done((bf16[32,1280]{1,0:T(8,128)(2,1)S(1)}, bf16[32,1280]{1,0:T(8,128)(2,1)S(1)}, u32[]{:S(2)}, u32[]{:S(2)}) %collective-permute-start.15) | collective-permute-done | bytes 81952 | tf_op jit(solution)/shard_map/ppermute | solution.py:31
  65.1 0.0 collective-permute-done.14.rest_1_
  65.1 0.6 collective-permute-start.17
  65.7 2.1 %collective-permute-start.20 = (bf16[64,768]{1,0:T(8,128)(2,1)S(1)}, bf16[64,768]{1,0:T(8,128)(2,1)S(1)}, u32[]{:S(2)}, u32[]{:S(2)}) collective-permute-start(bf16[64,768]{1,0:T(8,128)(2,1)S(1)} %get-tuple-element.86.rest_0_), channel_id=1, source_target_pairs={{0,12},{4,8},{8,4},{12,0},{1,13},{5,9},{9,5},{13,1},{2,14},{6,10},... | collective-permute-start | bytes 294920 | tf_op jit(solution)/shard_map/ppermute | solution.py:31
  67.8 2.3 %collective-permute-start.18 = (bf16[64,768]{1,0:T(8,128)(2,1)S(1)}, bf16[64,768]{1,0:T(8,128)(2,1)S(1)}, u32[]{:S(2)}, u32[]{:S(2)}) collective-permute-start(bf16[64,768]{1,0:T(8,128)(2,1)S(1)} %get-tuple-element.86.rest_0_), channel_id=1, source_target_pairs={{0,4},{4,0},{8,12},{12,8},{1,5},{5,1},{9,13},{13,9},{2,6},{6,2},{1... | collective-permute-start | bytes 294920 | tf_op jit(solution)/shard_map/ppermute | solution.py:31
  70.1 3.1 %collective-permute-done.20.rest_3_ = bf16[64,768]{1,0:T(8,128)(2,1)S(1)} collective-permute-done((bf16[64,768]{1,0:T(8,128)(2,1)S(1)}, bf16[64,768]{1,0:T(8,128)(2,1)S(1)}, u32[]{:S(2)}, u32[]{:S(2)}) %collective-permute-start.20) | collective-permute-done | bytes 98336 | tf_op jit(solution)/shard_map/ppermute | solution.py:31
  73.2 3.2 %collective-permute-done.19.rest_2_ = bf16[64,768]{1,0:T(8,128)(2,1)S(1)} collective-permute-done((bf16[64,768]{1,0:T(8,128)(2,1)S(1)}, bf16[64,768]{1,0:T(8,128)(2,1)S(1)}, u32[]{:S(2)}, u32[]{:S(2)}) %collective-permute-start.19) | collective-permute-done | bytes 98336 | tf_op jit(solution)/shard_map/ppermute | solution.py:31
  76.4 0.0 collective-permute-done.18.rest_1_
  76.4 0.0 collective-permute-done.17.other_p
  76.4 0.5 shard_map.121
  76.9 0.0 collective-permute-start.21
  77.0 0.1 collective-permute-start.24
  77.0 2.1 %collective-permute-start.23 = (f32[8,384]{1,0:T(8,128)S(1)}, f32[8,384]{1,0:T(8,128)S(1)}, u32[]{:S(2)}, u32[]{:S(2)}) collective-permute-start(f32[8,384]{1,0:T(8,128)S(1)} %get-tuple-element.88.row), channel_id=1, source_target_pairs={{0,16},{16,0},{1,17},{17,1},{2,18},{18,2},{3,19},{19,3},{4,20},{20... | collective-permute-start | bytes 36872 | tf_op jit(solution)/shard_map/ppermute | solution.py:31
  79.1 0.0 collective-permute-start.22
  79.1 0.8 shard_map.116
  79.9 0.3 collective-permute-done.24.row_both
  80.1 0.8 collective-permute-done.23.row_section
  80.9 0.0 collective-permute-done.22.row_core
  80.9 0.0 collective-permute-done.21.other
  80.9 2.3 %shard_map.122 = (f32[512,1536]{1,0:T(8,128)}, f32[512,512]{1,0:T(8,128)}, f32[1,512]{1,0:T(1,128)}, f32[1,16]{1,0:T(1,128)}) custom-call(bf16[256,2048]{1,0:T(8,128)(2,1)S(1)} %get-tuple-element.87.half, bf16[256,2048]{1,0:T(8,128)(2,1)S(1)} %collective-permute-done.21.other, f32[8,384]{1,0:T(8,128)S(1)} %get-tuple-element.88.row, ...), custom_call_target="tpu_custom_call" | custom-call | flops 100000000 | bytes 6346816 | tf_op jit(solution)/shard_map/pallas_call | solution.py:47
  (7 shorter events, 0.1 us)
Async XLA Ops:
  2.5 9.6 %collective-permute-start.1 = (bf16[80,512]{1,0:T(8,128)(2,1)}, bf16[80,512]{1,0:T(8,128)(2,1)S(1)}, u32[]{:S(2)}, u32[]{:S(2)}) collective-permute-start(bf16[80,512]{1,0:T(8,128)(2,1)} %get-tuple-element.51), channel_id=1, source_target_pairs={{0,12},{4,0},{8,4},{12,8},{1,13},{5,1},{9,5},{13,9},{2,14},{6,2},{... | collective-permute-start | bytes 245768 | tf_op jit(solution)/shard_map/ppermute | solution.py:20
  7.6 6.9 %collective-permute-start = (bf16[80,512]{1,0:T(8,128)(2,1)}, bf16[80,512]{1,0:T(8,128)(2,1)S(1)}, u32[]{:S(2)}, u32[]{:S(2)}) collective-permute-start(bf16[80,512]{1,0:T(8,128)(2,1)} %get-tuple-element.50), channel_id=1, source_target_pairs={{0,12},{4,0},{8,4},{12,8},{1,13},{5,1},{9,5},{13,9},{2,14},{6,2},{... | collective-permute-start | bytes 245768 | tf_op jit(solution)/shard_map/ppermute | solution.py:20
  8.1 1.0 %copy-start = (f32[160,512]{1,0:T(8,128)S(1)}, f32[160,512]{1,0:T(8,128)}, u32[]{:S(2)}) copy-start(f32[160,512]{1,0:T(8,128)} %get-tuple-element.49.after.own.params) | copy-start | bytes 983044
  9.1 1.4 %copy-start.1 = (bf16[1,512,1536]{2,1,0:T(8,128)(2,1)S(1)}, bf16[1,512,1536]{2,1,0:T(8,128)(2,1)}, u32[]{:S(2)}) copy-start(bf16[1,512,1536]{2,1,0:T(8,128)(2,1)} %param.11) | copy-start | bytes 4718596
  10.5 1.0 %copy-start.2 = (bf16[1,512,512]{2,1,0:T(8,128)(2,1)S(1)}, bf16[1,512,512]{2,1,0:T(8,128)(2,1)}, u32[]{:S(2)}) copy-start(bf16[1,512,512]{2,1,0:T(8,128)(2,1)} %param.12) | copy-start | bytes 1572868
  17.4 7.0 %collective-permute-start.2 = (bf16[144,512]{1,0:T(8,128)(2,1)S(1)}, bf16[144,512]{1,0:T(8,128)(2,1)S(1)}, u32[]{:S(2)}, u32[]{:S(2)}) collective-permute-start(bf16[144,512]{1,0:T(8,128)(2,1)S(1)} %get-tuple-element.59), channel_id=1, source_target_pairs={{16,0},{17,1},{18,2},{19,3},{20,4},{21,5},{22,6},{23,7},{24,8},{25... | collective-permute-start | bytes 442376 | tf_op jit(solution)/shard_map/ppermute | solution.py:26
  27.3 2.8 %collective-permute-start.4 = (bf16[256,2176]{1,0:T(8,128)(2,1)S(1)}, bf16[256,2176]{1,0:T(8,128)(2,1)S(1)}, u32[]{:S(2)}, u32[]{:S(2)}) collective-permute-start(bf16[256,2176]{1,0:T(8,128)(2,1)S(1)} %get-tuple-element.69), channel_id=1, source_target_pairs={{0,1},{1,0},{2,3},{3,2},{4,5},{5,4},{6,7},{7,6},{8,9},{9,8},{10,11... | collective-permute-start | bytes 3342344 | tf_op jit(solution)/shard_map/ppermute | solution.py:31
  30.5 45.9 %copy-start.3 = (f32[1,512]{1,0:T(1,128)S(1)}, f32[1,512]{1,0:T(1,128)}, u32[]{:S(2)}) copy-start(f32[1,512]{1,0:T(1,128)} %gain.3) | copy-start | bytes 6148
  30.5 15.1 %collective-permute-start.5 = (bf16[128,1408]{1,0:T(8,128)(2,1)S(1)}, bf16[128,1408]{1,0:T(8,128)(2,1)S(1)}, u32[]{:S(2)}, u32[]{:S(2)}) collective-permute-start(bf16[128,1408]{1,0:T(8,128)(2,1)S(1)} %get-tuple-element.71), channel_id=1, source_target_pairs={{0,2},{1,3},{2,0},{3,1},{4,6},{5,7},{6,4},{7,5},{8,10},{9,11},{10,... | collective-permute-start | bytes 1081352 | tf_op jit(solution)/shard_map/ppermute | solution.py:31
  32.1 12.2 %collective-permute-start.6 = (bf16[64,768]{1,0:T(8,128)(2,1)S(1)}, bf16[64,768]{1,0:T(8,128)(2,1)S(1)}, u32[]{:S(2)}, u32[]{:S(2)}) collective-permute-start(bf16[64,768]{1,0:T(8,128)(2,1)S(1)} %get-tuple-element.73), channel_id=1, source_target_pairs={{0,12},{4,8},{8,4},{12,0},{1,13},{5,9},{9,5},{13,1},{2,14},{6,10},... | collective-permute-start | bytes 294920 | tf_op jit(solution)/shard_map/ppermute | solution.py:31
  34.7 10.9 %collective-permute-start.7 = (bf16[64,768]{1,0:T(8,128)(2,1)S(1)}, bf16[64,768]{1,0:T(8,128)(2,1)S(1)}, u32[]{:S(2)}, u32[]{:S(2)}) collective-permute-start(bf16[64,768]{1,0:T(8,128)(2,1)S(1)} %get-tuple-element.74), channel_id=1, source_target_pairs={{0,8},{4,12},{8,0},{12,4},{1,9},{5,13},{9,1},{13,5},{2,10},{6,14},... | collective-permute-start | bytes 294920 | tf_op jit(solution)/shard_map/ppermute | solution.py:31
  35.2 10.4 %collective-permute-start.8 = (bf16[64,768]{1,0:T(8,128)(2,1)S(1)}, bf16[64,768]{1,0:T(8,128)(2,1)S(1)}, u32[]{:S(2)}, u32[]{:S(2)}) collective-permute-start(bf16[64,768]{1,0:T(8,128)(2,1)S(1)} %get-tuple-element.75), channel_id=1, source_target_pairs={{0,4},{4,0},{8,12},{12,8},{1,5},{5,1},{9,13},{13,9},{2,6},{6,2},{1... | collective-permute-start | bytes 294920 | tf_op jit(solution)/shard_map/ppermute | solution.py:31
  36.5 7.8 %collective-permute-start.3 = (bf16[72,512]{1,0:T(8,128)(2,1)S(1)}, bf16[72,512]{1,0:T(8,128)(2,1)S(1)}, u32[]{:S(2)}, u32[]{:S(2)}) collective-permute-start(bf16[72,512]{1,0:T(8,128)(2,1)S(1)} %get-tuple-element.67), channel_id=1, source_target_pairs={{0,4},{4,8},{8,12},{12,0},{1,5},{5,9},{9,13},{13,1},{2,6},{6,10},{... | collective-permute-start | bytes 221192 | tf_op jit(solution)/shard_map/ppermute | solution.py:20
  45.8 8.5 %collective-permute-start.10 = (bf16[32,1408]{1,0:T(8,128)(2,1)S(1)}, bf16[32,1408]{1,0:T(8,128)(2,1)S(1)}, u32[]{:S(2)}, u32[]{:S(2)}) collective-permute-start(bf16[32,1408]{1,0:T(8,128)(2,1)S(1)} %get-tuple-element.79), channel_id=1, source_target_pairs={{0,12},{4,8},{8,4},{12,0},{1,13},{5,9},{9,5},{13,1},{2,14},{6,10},... | collective-permute-start | bytes 270344 | tf_op jit(solution)/shard_map/ppermute | solution.py:31
  47.1 8.2 %collective-permute-start.11 = (bf16[32,1408]{1,0:T(8,128)(2,1)S(1)}, bf16[32,1408]{1,0:T(8,128)(2,1)S(1)}, u32[]{:S(2)}, u32[]{:S(2)}) collective-permute-start(bf16[32,1408]{1,0:T(8,128)(2,1)S(1)} %get-tuple-element.80), channel_id=1, source_target_pairs={{0,8},{4,12},{8,0},{12,4},{1,9},{5,13},{9,1},{13,5},{2,10},{6,14},... | collective-permute-start | bytes 270344 | tf_op jit(solution)/shard_map/ppermute | solution.py:31
  47.1 8.2 %collective-permute-start.12 = (bf16[32,1408]{1,0:T(8,128)(2,1)S(1)}, bf16[32,1408]{1,0:T(8,128)(2,1)S(1)}, u32[]{:S(2)}, u32[]{:S(2)}) collective-permute-start(bf16[32,1408]{1,0:T(8,128)(2,1)S(1)} %get-tuple-element.81), channel_id=1, source_target_pairs={{0,4},{4,0},{8,12},{12,8},{1,5},{5,1},{9,13},{13,9},{2,6},{6,2},{1... | collective-permute-start | bytes 270344 | tf_op jit(solution)/shard_map/ppermute | solution.py:31
  50.3 4.1 %collective-permute-start.9 = (bf16[32,768]{1,0:T(8,128)(2,1)S(1)}, bf16[32,768]{1,0:T(8,128)(2,1)S(1)}, u32[]{:S(2)}, u32[]{:S(2)}) collective-permute-start(bf16[32,768]{1,0:T(8,128)(2,1)S(1)} %get-tuple-element.78), channel_id=1, source_target_pairs={{0,2},{1,3},{2,0},{3,1},{4,6},{5,7},{6,4},{7,5},{8,10},{9,11},{10,... | collective-permute-start | bytes 147464 | tf_op jit(solution)/shard_map/ppermute | solution.py:31
  55.3 8.5 %collective-permute-start.16 = (bf16[32,1280]{1,0:T(8,128)(2,1)S(1)}, bf16[32,1280]{1,0:T(8,128)(2,1)S(1)}, u32[]{:S(2)}, u32[]{:S(2)}) collective-permute-start(bf16[32,1280]{1,0:T(8,128)(2,1)S(1)} %get-tuple-element.84.rest_0_), channel_id=1, source_target_pairs={{0,12},{4,8},{8,4},{12,0},{1,13},{5,9},{9,5},{13,1},{2,14},{6,10},... | collective-permute-start | bytes 245768 | tf_op jit(solution)/shard_map/ppermute | solution.py:31
  57.6 7.5 %collective-permute-start.15 = (bf16[32,1280]{1,0:T(8,128)(2,1)S(1)}, bf16[32,1280]{1,0:T(8,128)(2,1)S(1)}, u32[]{:S(2)}, u32[]{:S(2)}) collective-permute-start(bf16[32,1280]{1,0:T(8,128)(2,1)S(1)} %get-tuple-element.84.rest_0_), channel_id=1, source_target_pairs={{0,8},{4,12},{8,0},{12,4},{1,9},{5,13},{9,1},{13,5},{2,10},{6,14},... | collective-permute-start | bytes 245768 | tf_op jit(solution)/shard_map/ppermute | solution.py:31
  57.6 7.5 %collective-permute-start.14 = (bf16[32,1280]{1,0:T(8,128)(2,1)S(1)}, bf16[32,1280]{1,0:T(8,128)(2,1)S(1)}, u32[]{:S(2)}, u32[]{:S(2)}) collective-permute-start(bf16[32,1280]{1,0:T(8,128)(2,1)S(1)} %get-tuple-element.84.rest_0_), channel_id=1, source_target_pairs={{0,4},{4,0},{8,12},{12,8},{1,5},{5,1},{9,13},{13,9},{2,6},{6,2},{1... | collective-permute-start | bytes 245768 | tf_op jit(solution)/shard_map/ppermute | solution.py:31
  59.8 4.1 %collective-permute-start.13 = (bf16[32,768]{1,0:T(8,128)(2,1)S(1)}, bf16[32,768]{1,0:T(8,128)(2,1)S(1)}, u32[]{:S(2)}, u32[]{:S(2)}) collective-permute-start(bf16[32,768]{1,0:T(8,128)(2,1)S(1)} %get-tuple-element.83.piece_q), channel_id=1, source_target_pairs={{0,2},{1,3},{2,0},{3,1},{4,6},{5,7},{6,4},{7,5},{8,10},{9,11},{10,... | collective-permute-start | bytes 147464 | tf_op jit(solution)/shard_map/ppermute | solution.py:31
  65.1 11.3 %collective-permute-start.17 = (bf16[128,1280]{1,0:T(8,128)(2,1)S(1)}, bf16[128,1280]{1,0:T(8,128)(2,1)S(1)}, u32[]{:S(2)}, u32[]{:S(2)}) collective-permute-start(bf16[128,1280]{1,0:T(8,128)(2,1)S(1)} %get-tuple-element.85.block_p), channel_id=1, source_target_pairs={{0,2},{1,3},{2,0},{3,1},{4,6},{5,7},{6,4},{7,5},{8,10},{9,11},{10,... | collective-permute-start | bytes 983048 | tf_op jit(solution)/shard_map/ppermute | solution.py:31
  65.7 7.5 %collective-permute-start.20 = (bf16[64,768]{1,0:T(8,128)(2,1)S(1)}, bf16[64,768]{1,0:T(8,128)(2,1)S(1)}, u32[]{:S(2)}, u32[]{:S(2)}) collective-permute-start(bf16[64,768]{1,0:T(8,128)(2,1)S(1)} %get-tuple-element.86.rest_0_), channel_id=1, source_target_pairs={{0,12},{4,8},{8,4},{12,0},{1,13},{5,9},{9,5},{13,1},{2,14},{6,10},... | collective-permute-start | bytes 294920 | tf_op jit(solution)/shard_map/ppermute | solution.py:31
  67.8 8.6 %collective-permute-start.19 = (bf16[64,768]{1,0:T(8,128)(2,1)S(1)}, bf16[64,768]{1,0:T(8,128)(2,1)S(1)}, u32[]{:S(2)}, u32[]{:S(2)}) collective-permute-start(bf16[64,768]{1,0:T(8,128)(2,1)S(1)} %get-tuple-element.86.rest_0_), channel_id=1, source_target_pairs={{0,8},{4,12},{8,0},{12,4},{1,9},{5,13},{9,1},{13,5},{2,10},{6,14},... | collective-permute-start | bytes 294920 | tf_op jit(solution)/shard_map/ppermute | solution.py:31
  67.8 8.6 %collective-permute-start.18 = (bf16[64,768]{1,0:T(8,128)(2,1)S(1)}, bf16[64,768]{1,0:T(8,128)(2,1)S(1)}, u32[]{:S(2)}, u32[]{:S(2)}) collective-permute-start(bf16[64,768]{1,0:T(8,128)(2,1)S(1)} %get-tuple-element.86.rest_0_), channel_id=1, source_target_pairs={{0,4},{4,0},{8,12},{12,8},{1,5},{5,1},{9,13},{13,9},{2,6},{6,2},{1... | collective-permute-start | bytes 294920 | tf_op jit(solution)/shard_map/ppermute | solution.py:31
  76.9 4.0 %collective-permute-start.21 = (bf16[256,2048]{1,0:T(8,128)(2,1)S(1)}, bf16[256,2048]{1,0:T(8,128)(2,1)S(1)}, u32[]{:S(2)}, u32[]{:S(2)}) collective-permute-start(bf16[256,2048]{1,0:T(8,128)(2,1)S(1)} %get-tuple-element.87.half), channel_id=1, source_target_pairs={{0,1},{1,0},{2,3},{3,2},{4,5},{5,4},{6,7},{7,6},{8,9},{9,8},{10,11... | collective-permute-start | bytes 3145736 | tf_op jit(solution)/shard_map/ppermute | solution.py:31
  77.0 3.2 %collective-permute-start.24 = (f32[8,384]{1,0:T(8,128)S(1)}, f32[8,384]{1,0:T(8,128)S(1)}, u32[]{:S(2)}, u32[]{:S(2)}) collective-permute-start(f32[8,384]{1,0:T(8,128)S(1)} %get-tuple-element.88.row), channel_id=1, source_target_pairs={{0,17},{1,16},{2,19},{3,18},{16,1},{17,0},{18,3},{19,2},{4,21},{5,... | collective-permute-start | bytes 36872 | tf_op jit(solution)/shard_map/ppermute | solution.py:637
  77.0 3.9 %collective-permute-start.23 = (f32[8,384]{1,0:T(8,128)S(1)}, f32[8,384]{1,0:T(8,128)S(1)}, u32[]{:S(2)}, u32[]{:S(2)}) collective-permute-start(f32[8,384]{1,0:T(8,128)S(1)} %get-tuple-element.88.row), channel_id=1, source_target_pairs={{0,16},{16,0},{1,17},{17,1},{2,18},{18,2},{3,19},{19,3},{4,20},{20... | collective-permute-start | bytes 36872 | tf_op jit(solution)/shard_map/ppermute | solution.py:31
  79.1 1.8 %collective-permute-start.22 = (f32[8,384]{1,0:T(8,128)S(1)}, f32[8,384]{1,0:T(8,128)S(1)}, u32[]{:S(2)}, u32[]{:S(2)}) collective-permute-start(f32[8,384]{1,0:T(8,128)S(1)} %get-tuple-element.88.row), channel_id=1, source_target_pairs={{0,1},{1,0},{2,3},{3,2},{4,5},{5,4},{6,7},{7,6},{8,9},{9,8},{10,11... | collective-permute-start | bytes 36872 | tf_op jit(solution)/shard_map/ppermute | solution.py:31

commit v10 on v7

--- a/solution.py
+++ b/solution.py
@@ -9,7 +9,7 @@
 
 SHIFT = 6
 GROUP = 128
-CUT = 1408
+CUT = 1280
 EPSILON = 1e-05
 F32 = jnp.float32
 BF16 = jnp.bfloat16
@@ -320,7 +320,7 @@
     kept_p[:, CUT:] = total[mine, CUT:wide_p].astype(BF16).astype(F32)
     piece = kept_q.shape[0]
     kept_q[...] = total[aligned(z * piece, piece), wide_p:]
-    for other, ref in zip(range(len(give_q), 0, -1), give_q):
+    for other, ref in enumerate(give_q, 1):
         ref[...] = total[aligned((z ^ other) * piece, piece), wide_p:].astype(BF16)
 
 
@@ -334,7 +334,7 @@
     mine = aligned(z * piece, piece)
     left_p[:, :CUT] = total_p[mine, :CUT]
     left_p[:, CUT:] = total_p[mine, CUT:].astype(BF16).astype(F32)
-    for other, ref in zip(range(len(give_p), 0, -1), give_p):
+    for other, ref in enumerate(give_p, 1):
         ref[...] = total_p[aligned((z ^ other) * piece, piece), :].astype(BF16)
     total = kept_q[...]
     for ref in came_q:
@@ -353,7 +353,7 @@
         total = total + ref[:, :CUT].astype(F32)
     piece_p[...] = total.astype(BF16)
     piece_q[...] = (left_q[...] + came_q[...].astype(F32)).astype(BF16)
-    terms = [left_p[:8, CUT:]] + [ref[...].astype(F32)[:8, CUT:] for ref in came_p[::-1]]
+    terms = [left_p[:8, CUT:]] + [ref[...].astype(F32)[:8, CUT:] for ref in came_p]
     total = jnp.zeros_like(terms[0])
     for source in range(len(terms)):
         for other, term in enumerate(terms):
@@ -373,7 +373,7 @@
 
 
 def fifth_kernel(weight_qkv, gain, bias, block_p, other_p, *rest):
-    *parts_q, half, row = rest
+    *parts_q, row, half = rest
     core, y, z = position()
     rows = half.shape[0]
     mine = aligned(core * rows, rows)
@@ -431,13 +431,8 @@
         copy.wait()
 
 
-def far_first(pieces, axis):
-    others = range(len(pieces), 0, -1)
-    return [swapped(piece, axis, other) for other, piece in zip(others, pieces)]
-
-
-def to_all(piece, axis):
-    return [swapped(piece, axis, other) for other in range(1, lax.axis_size(axis))]
+def sent_round(pieces, axis):
+    return [swapped(piece, axis, other) for other, piece in enumerate(pieces, 1)]
 
 
 def vmem(dims, dtype):
@@ -575,7 +570,7 @@
         operands=(keep, came),
     )
     came_p = swapped(give_p, "lat", 2)
-    came_q = far_first(give_q, "lon")
+    came_q = sent_round(give_q, "lon")
     piece = rows // 2 // lons
     give_q, left_q, left_p, *give_p = call(
         second_kernel,
@@ -589,7 +584,7 @@
         places="avvv" + several,
         operands=(after, kept_p, came_p, kept_q, *came_q),
     )
-    came_p = far_first(give_p, "lon")
+    came_p = sent_round(give_p, "lon")
     came_q = swapped(give_q, "lat", 2)
     piece_p, piece_q, bias = call(
         third_kernel,
@@ -600,7 +595,7 @@
         ],
         operands=(left_p, left_q, came_q, *came_p),
     )
-    others_p = to_all(piece_p, "lon")
+    others_p = sent_round([piece_p for _ in some], "lon")
     other_q = swapped(piece_q, "lat", 2)
     block_p, block_q = call(
         fourth_kernel,
@@ -608,10 +603,10 @@
         operands=(piece_q, other_q, piece_p, *others_p),
     )
     other_p = swapped(block_p, "lat", 2)
-    others_q = to_all(block_q, "lon")
-    half, row = call(
+    others_q = sent_round([block_q for _ in some], "lon")
+    row, half = call(
         fifth_kernel,
-        [shape((rows, 4 * width), BF16), shape((8, rows + GROUP), F32)],
+        [shape((8, rows + GROUP), F32), shape((rows, 4 * width), BF16)],
         operands=(weight_qkv, gains, bias, block_p, other_p, block_q, *others_q),
     )
     row_section = swapped(row, "section", 1)

time: 81.5 us -> 83.3 us (1.022)
  waiting for transfers between devices: 30.8 us -> 33.8 us
  starting transfers between devices: 30.9 us -> 29.9 us
    ppermute x2, waiting for transfers between devices: 5.62 us -> 7.58 us  [from_behind(): lax.ppermute(value, axis, [(i, (i + by) % count) for i in range(count)])]
    ppermute x20, waiting for transfers between devices: 19 us -> 20 us  [swapped(): return lax.ppermute(value, axis, [(i, i ^ bit) for i in range(count)])]
    ppermute x2, starting transfers between devices: 6.45 us -> 5.55 us  [from_behind(): lax.ppermute(value, axis, [(i, (i + by) % count) for i in range(count)])]
  transfers between devices with their start and end apart: 24 -> 24, of which waited for: 13 -> 12; matrix products, arithmetic and copies ran while one was open for 0% -> 0% of each run, Pallas kernels for 3% -> 3%
where the time goes in v10:
time: 83.3 us; the launch traced here: 83 us
  waiting for transfers between devices  33.8 us (41%)
  starting transfers between devices  29.9 us (36%)
  Pallas kernels  15.1 us (18%)
  local copies, waits for them, and re-layouts  3.43 us (4%)
    ppermute x20, starting transfers between devices, swapped(): return lax.ppermute(value, axis, [(i, i ^ bit) for i in range(count)])  23 us
    ppermute x20, waiting for transfers between devices, swapped(): return lax.ppermute(value, axis, [(i, i ^ bit) for i in range(count)])  20 us
    pallas_call x12, Pallas kernels, call(): pl.pallas_call(kernel, out_shape=list(outs), in_specs=[pl.BlockSpec(memor...  15.1 us
    ppermute x2, waiting for transfers between devices, from_behind(): lax.ppermute(value, axis, [(i, (i + by) % count) for i in range(count)])  7.58 us
    ppermute x1, waiting for transfers between devices, passed_along(): return lax.ppermute(block, axis, route)  5.93 us
    ppermute x2, starting transfers between devices, from_behind(): lax.ppermute(value, axis, [(i, (i + by) % count) for i in range(count)])  5.55 us
    unnamed x8, local copies, waits for them, and re-layouts  3.43 us
  transfers between devices with their start and end apart: 24, of which 12 were waited for; matrix products, arithmetic and copies ran while one was open for 0% of the time, Pallas kernels for 3%

profile of v10, /device:TPU:0, one launch (start us, length us, event | category | flops | bytes accessed | tf_op | source)
XLA Modules:
  0.0 83.0 jit_solution(10318390224609658411)
XLA Ops:
  0.6 1.9 %shard_map.110 = (f32[160,512]{1,0:T(8,128)}, bf16[160,512]{1,0:T(8,128)(2,1)}) custom-call(bf16[1,6,12,2,512]{4,3,2,1,0:T(2,128)(2,1)} %bitcast.12, bf16[1,6,12,2,512]{4,3,2,1,0:T(2,128)(2,1)} %bitcast.13, s32[6,12]{1,0:T(8,128)} %land.1, f32[1,512]{1,0:T(1,128)} %gain.3, f32[1,16]{1,0:T(1,128)} %bias.1), custom_call_target="tpu_custom_call" | custom-call | flops 100000000 | bytes 788832 | tf_op jit(solution)/shard_map/pallas_call | solution.py:47
  2.5 5.1 %collective-permute-start = (bf16[160,512]{1,0:T(8,128)(2,1)}, bf16[160,512]{1,0:T(8,128)(2,1)S(1)}, u32[]{:S(2)}, u32[]{:S(2)}) collective-permute-start(bf16[160,512]{1,0:T(8,128)(2,1)} %get-tuple-element.49), channel_id=1, source_target_pairs={{0,12},{4,0},{8,4},{12,8},{1,13},{5,1},{9,5},{13,9},{2,14},{6,2},{... | collective-permute-start | bytes 491528 | tf_op jit(solution)/shard_map/ppermute | solution.py:20
  7.6 1.0 %copy-done = f32[160,512]{1,0:T(8,128)S(1)} copy-done((f32[160,512]{1,0:T(8,128)S(1)}, f32[160,512]{1,0:T(8,128)}, u32[]{:S(2)}) %copy-start) | copy-done | bytes 327704
  8.6 1.4 %copy-done.1 = bf16[1,512,1536]{2,1,0:T(8,128)(2,1)S(1)} copy-done((bf16[1,512,1536]{2,1,0:T(8,128)(2,1)S(1)}, bf16[1,512,1536]{2,1,0:T(8,128)(2,1)}, u32[]{:S(2)}) %copy-start.1) | copy-done | bytes 1572888
  10.0 1.0 %copy-done.2 = bf16[1,512,512]{2,1,0:T(8,128)(2,1)S(1)} copy-done((bf16[1,512,512]{2,1,0:T(8,128)(2,1)S(1)}, bf16[1,512,512]{2,1,0:T(8,128)(2,1)}, u32[]{:S(2)}) %copy-start.2) | copy-done | bytes 524312
  11.1 0.6 shard_map.111
  11.7 0.0 collective-permute-done.rim
  11.7 4.7 %shard_map.112 = (bf16[144,512]{1,0:T(8,128)(2,1)S(1)}, bf16[144,512]{1,0:T(8,128)(2,1)S(1)}, bf16[512,144]{1,0:T(8,128)(2,1)S(1)}, bf16[144,1536]{1,0:T(8,128)(...) custom-call(f32[160,512]{1,0:T(8,128)S(1)} %copy-done, ...), custom_call_target="tpu_custom_call" | custom-call | flops 1000000000 | bytes 6299648 | tf_op jit(solution)/shard_map/pallas_call | solution.py:47
  16.5 1.3 %collective-permute-start.1 = (bf16[144,512]{1,0:T(8,128)(2,1)S(1)}, bf16[144,512]{1,0:T(8,128)(2,1)S(1)}, u32[]{:S(2)}, u32[]{:S(2)}) collective-permute-start(bf16[144,512]{1,0:T(8,128)(2,1)S(1)} %get-tuple-element.53), channel_id=1, source_target_pairs={{16,0},{17,1},{18,2},{19,3},{20,4},{21,5},{22,6},{23,7},{24,8},{25... | collective-permute-start | bytes 442376 | tf_op jit(solution)/shard_map/ppermute | solution.py:26
  17.8 5.9 %collective-permute-done.1.skip = bf16[144,512]{1,0:T(8,128)(2,1)S(1)} collective-permute-done((bf16[144,512]{1,0:T(8,128)(2,1)S(1)}, bf16[144,512]{1,0:T(8,128)(2,1)S(1)}, u32[]{:S(2)}, u32[]{:S(2)}) %collective-permute-start.1) | collective-permute-done | bytes 147488 | tf_op jit(solution)/shard_map/ppermute | solution.py:26
  23.7 2.9 %shard_map.113 = (bf16[144,512]{1,0:T(8,128)(2,1)S(1)}, bf16[144,1536]{1,0:T(8,128)(2,1)S(1)}, f32[8,128]{1,0:T(8,128)S(1)}, bf16[256,2176]{1,0:T(8,128)(2,1)S(1)}) custom-call(bf16[144,512]{1,0:T(8,128)(2,1)S(1)} %collective-permute-done.1.skip, bf16[144,512]{1,0:T(8,128)(2,1)S(1)} %get-tuple-element.54.cot, bf16[144,1536]{1,0:T(8,128)(2,1)S(1)} %get-tuple-element.55.qkv, ...), custom_call_target="tpu_custom_call" | custom-call | flops 1000000000 | bytes 4075520 | tf_op jit(solution)/shard_map/pallas_call | solution.py:47
  26.6 0.1 collective-permute-start.3
  26.7 0.8 shard_map.114
  27.4 2.0 %collective-permute-done.3.came = bf16[256,2176]{1,0:T(8,128)(2,1)S(1)} collective-permute-done((bf16[256,2176]{1,0:T(8,128)(2,1)S(1)}, bf16[256,2176]{1,0:T(8,128)(2,1)S(1)}, u32[]{:S(2)}, u32[]{:S(2)}) %collective-permute-start.3) | collective-permute-done | bytes 1114144 | tf_op jit(solution)/shard_map/ppermute | solution.py:31
  29.4 0.4 shard_map.116
  29.8 0.0 copy-start.3
  29.8 1.6 %collective-permute-start.4 = (bf16[128,1408]{1,0:T(8,128)(2,1)S(1)}, bf16[128,1408]{1,0:T(8,128)(2,1)S(1)}, u32[]{:S(2)}, u32[]{:S(2)}) collective-permute-start(bf16[128,1408]{1,0:T(8,128)(2,1)S(1)} %get-tuple-element.69), channel_id=1, source_target_pairs={{0,2},{1,3},{2,0},{3,1},{4,6},{5,7},{6,4},{7,5},{8,10},{9,11},{10,... | collective-permute-start | bytes 1081352 | tf_op jit(solution)/shard_map/ppermute | solution.py:31
  31.4 0.0 collective-permute-start.5
  31.4 4.3 %collective-permute-start.6 = (bf16[64,768]{1,0:T(8,128)(2,1)S(1)}, bf16[64,768]{1,0:T(8,128)(2,1)S(1)}, u32[]{:S(2)}, u32[]{:S(2)}) collective-permute-start(bf16[64,768]{1,0:T(8,128)(2,1)S(1)} %get-tuple-element.72), channel_id=1, source_target_pairs={{0,8},{4,12},{8,0},{12,4},{1,9},{5,13},{9,1},{13,5},{2,10},{6,14},... | collective-permute-start | bytes 294920 | tf_op jit(solution)/shard_map/ppermute | solution.py:31
  35.7 0.1 collective-permute-start.7
  35.8 0.4 collective-permute-start.2
  36.2 7.6 %collective-permute-done.2.back.after = bf16[72,512]{1,0:T(8,128)(2,1)S(1)} collective-permute-done((bf16[72,512]{1,0:T(8,128)(2,1)S(1)}, bf16[72,512]{1,0:T(8,128)(2,1)S(1)}, u32[]{:S(2)}, u32[]{:S(2)}) %collective-permute-start.2) | collective-permute-done | bytes 73760 | tf_op jit(solution)/shard_map/ppermute | solution.py:20
  43.8 0.0 collective-permute-done.5.rest_0_
  43.8 1.2 %collective-permute-done.6.rest_1_ = bf16[64,768]{1,0:T(8,128)(2,1)S(1)} collective-permute-done((bf16[64,768]{1,0:T(8,128)(2,1)S(1)}, bf16[64,768]{1,0:T(8,128)(2,1)S(1)}, u32[]{:S(2)}, u32[]{:S(2)}) %collective-permute-start.6) | collective-permute-done | bytes 98336 | tf_op jit(solution)/shard_map/ppermute | solution.py:31
  45.0 0.0 collective-permute-done.7.rest_2_
  45.0 0.0 collective-permute-done.4.came_p
  45.0 0.2 shard_map.117
  45.2 1.7 %collective-permute-start.9 = (bf16[32,1408]{1,0:T(8,128)(2,1)S(1)}, bf16[32,1408]{1,0:T(8,128)(2,1)S(1)}, u32[]{:S(2)}, u32[]{:S(2)}) collective-permute-start(bf16[32,1408]{1,0:T(8,128)(2,1)S(1)} %get-tuple-element.77), channel_id=1, source_target_pairs={{0,4},{4,0},{8,12},{12,8},{1,5},{5,1},{9,13},{13,9},{2,6},{6,2},{1... | collective-permute-start | bytes 270344 | tf_op jit(solution)/shard_map/ppermute | solution.py:31
  46.9 1.0 %collective-permute-start.10 = (bf16[32,1408]{1,0:T(8,128)(2,1)S(1)}, bf16[32,1408]{1,0:T(8,128)(2,1)S(1)}, u32[]{:S(2)}, u32[]{:S(2)}) collective-permute-start(bf16[32,1408]{1,0:T(8,128)(2,1)S(1)} %get-tuple-element.78), channel_id=1, source_target_pairs={{0,8},{4,12},{8,0},{12,4},{1,9},{5,13},{9,1},{13,5},{2,10},{6,14},... | collective-permute-start | bytes 270344 | tf_op jit(solution)/shard_map/ppermute | solution.py:31
  48.0 1.7 %collective-permute-start.11 = (bf16[32,1408]{1,0:T(8,128)(2,1)S(1)}, bf16[32,1408]{1,0:T(8,128)(2,1)S(1)}, u32[]{:S(2)}, u32[]{:S(2)}) collective-permute-start(bf16[32,1408]{1,0:T(8,128)(2,1)S(1)} %get-tuple-element.79), channel_id=1, source_target_pairs={{0,12},{4,8},{8,4},{12,0},{1,13},{5,9},{9,5},{13,1},{2,14},{6,10},... | collective-permute-start | bytes 270344 | tf_op jit(solution)/shard_map/ppermute | solution.py:31
  49.7 0.5 collective-permute-start.8
  50.2 3.6 %collective-permute-done.8.came_q = bf16[32,768]{1,0:T(8,128)(2,1)S(1)} collective-permute-done((bf16[32,768]{1,0:T(8,128)(2,1)S(1)}, bf16[32,768]{1,0:T(8,128)(2,1)S(1)}, u32[]{:S(2)}, u32[]{:S(2)}) %collective-permute-start.8) | collective-permute-done | bytes 49184 | tf_op jit(solution)/shard_map/ppermute | solution.py:31
  53.8 0.0 collective-permute-done.9.rest_0_
  53.8 2.2 %collective-permute-done.10.rest_1_ = bf16[32,1408]{1,0:T(8,128)(2,1)S(1)} collective-permute-done((bf16[32,1408]{1,0:T(8,128)(2,1)S(1)}, bf16[32,1408]{1,0:T(8,128)(2,1)S(1)}, u32[]{:S(2)}, u32[]{:S(2)}) %collective-permute-start.10) | collective-permute-done | bytes 90144 | tf_op jit(solution)/shard_map/ppermute | solution.py:31
  56.0 0.0 collective-permute-done.11.rest_2_
  56.0 0.1 shard_map.118
  56.1 2.2 %collective-permute-start.15 = (bf16[32,1280]{1,0:T(8,128)(2,1)S(1)}, bf16[32,1280]{1,0:T(8,128)(2,1)S(1)}, u32[]{:S(2)}, u32[]{:S(2)}) collective-permute-start(bf16[32,1280]{1,0:T(8,128)(2,1)S(1)} %get-tuple-element.82.rest_0_), channel_id=1, source_target_pairs={{0,12},{4,8},{8,4},{12,0},{1,13},{5,9},{9,5},{13,1},{2,14},{6,10},... | collective-permute-start | bytes 245768 | tf_op jit(solution)/shard_map/ppermute | solution.py:31
  58.2 0.9 %collective-permute-start.14 = (bf16[32,1280]{1,0:T(8,128)(2,1)S(1)}, bf16[32,1280]{1,0:T(8,128)(2,1)S(1)}, u32[]{:S(2)}, u32[]{:S(2)}) collective-permute-start(bf16[32,1280]{1,0:T(8,128)(2,1)S(1)} %get-tuple-element.82.rest_0_), channel_id=1, source_target_pairs={{0,8},{4,12},{8,0},{12,4},{1,9},{5,13},{9,1},{13,5},{2,10},{6,14},... | collective-permute-start | bytes 245768 | tf_op jit(solution)/shard_map/ppermute | solution.py:31
  59.1 1.4 %collective-permute-start.13 = (bf16[32,1280]{1,0:T(8,128)(2,1)S(1)}, bf16[32,1280]{1,0:T(8,128)(2,1)S(1)}, u32[]{:S(2)}, u32[]{:S(2)}) collective-permute-start(bf16[32,1280]{1,0:T(8,128)(2,1)S(1)} %get-tuple-element.82.rest_0_), channel_id=1, source_target_pairs={{0,4},{4,0},{8,12},{12,8},{1,5},{5,1},{9,13},{13,9},{2,6},{6,2},{1... | collective-permute-start | bytes 245768 | tf_op jit(solution)/shard_map/ppermute | solution.py:31
  60.5 0.5 collective-permute-start.12
  61.0 3.9 %collective-permute-done.12.other_q = bf16[32,768]{1,0:T(8,128)(2,1)S(1)} collective-permute-done((bf16[32,768]{1,0:T(8,128)(2,1)S(1)}, bf16[32,768]{1,0:T(8,128)(2,1)S(1)}, u32[]{:S(2)}, u32[]{:S(2)}) %collective-permute-start.12) | collective-permute-done | bytes 49184 | tf_op jit(solution)/shard_map/ppermute | solution.py:31
  64.9 0.0 collective-permute-done.15.rest_3_
  64.9 0.1 collective-permute-done.14.rest_2_
  65.1 0.0 collective-permute-done.13.rest_1_
  65.1 0.6 collective-permute-start.16
  65.7 2.9 %collective-permute-start.19 = (bf16[64,768]{1,0:T(8,128)(2,1)S(1)}, bf16[64,768]{1,0:T(8,128)(2,1)S(1)}, u32[]{:S(2)}, u32[]{:S(2)}) collective-permute-start(bf16[64,768]{1,0:T(8,128)(2,1)S(1)} %get-tuple-element.84.rest_0_), channel_id=1, source_target_pairs={{0,12},{4,8},{8,4},{12,0},{1,13},{5,9},{9,5},{13,1},{2,14},{6,10},... | collective-permute-start | bytes 294920 | tf_op jit(solution)/shard_map/ppermute | solution.py:31
  68.6 0.0 collective-permute-start.18
  68.6 1.5 %collective-permute-start.17 = (bf16[64,768]{1,0:T(8,128)(2,1)S(1)}, bf16[64,768]{1,0:T(8,128)(2,1)S(1)}, u32[]{:S(2)}, u32[]{:S(2)}) collective-permute-start(bf16[64,768]{1,0:T(8,128)(2,1)S(1)} %get-tuple-element.84.rest_0_), channel_id=1, source_target_pairs={{0,4},{4,0},{8,12},{12,8},{1,5},{5,1},{9,13},{13,9},{2,6},{6,2},{1... | collective-permute-start | bytes 294920 | tf_op jit(solution)/shard_map/ppermute | solution.py:31
  70.1 2.3 %collective-permute-done.19.rest_3_ = bf16[64,768]{1,0:T(8,128)(2,1)S(1)} collective-permute-done((bf16[64,768]{1,0:T(8,128)(2,1)S(1)}, bf16[64,768]{1,0:T(8,128)(2,1)S(1)}, u32[]{:S(2)}, u32[]{:S(2)}) %collective-permute-start.19) | collective-permute-done | bytes 98336 | tf_op jit(solution)/shard_map/ppermute | solution.py:31
  72.3 4.0 %collective-permute-done.18.rest_2_ = bf16[64,768]{1,0:T(8,128)(2,1)S(1)} collective-permute-done((bf16[64,768]{1,0:T(8,128)(2,1)S(1)}, bf16[64,768]{1,0:T(8,128)(2,1)S(1)}, u32[]{:S(2)}, u32[]{:S(2)}) %collective-permute-start.18) | collective-permute-done | bytes 98336 | tf_op jit(solution)/shard_map/ppermute | solution.py:31
  76.3 0.0 collective-permute-done.17.rest_1_
  76.3 0.0 collective-permute-done.16.other_p
  76.3 0.0 copy-done.3
  76.3 0.5 shard_map.120
  76.8 0.0 collective-permute-start.20
  76.8 0.1 collective-permute-start.23
  76.9 2.1 %collective-permute-start.22 = (f32[8,384]{1,0:T(8,128)S(1)}, f32[8,384]{1,0:T(8,128)S(1)}, u32[]{:S(2)}, u32[]{:S(2)}) collective-permute-start(f32[8,384]{1,0:T(8,128)S(1)} %get-tuple-element.86.row), channel_id=1, source_target_pairs={{0,16},{16,0},{1,17},{17,1},{2,18},{18,2},{3,19},{19,3},{4,20},{20... | collective-permute-start | bytes 36872 | tf_op jit(solution)/shard_map/ppermute | solution.py:31
  79.0 0.0 collective-permute-start.21
  79.0 0.8 shard_map.115
  79.7 0.3 collective-permute-done.23.row_both
  80.0 0.8 collective-permute-done.22.row_section
  80.8 0.0 collective-permute-done.21.row_core
  80.8 0.0 collective-permute-done.20.other
  80.8 2.3 %shard_map.121 = (f32[512,1536]{1,0:T(8,128)}, f32[512,512]{1,0:T(8,128)}, f32[1,512]{1,0:T(1,128)}, f32[1,16]{1,0:T(1,128)}) custom-call(bf16[256,2048]{1,0:T(8,128)(2,1)S(1)} %get-tuple-element.85.half, bf16[256,2048]{1,0:T(8,128)(2,1)S(1)} %collective-permute-done.20.other, f32[8,384]{1,0:T(8,128)S(1)} %get-tuple-element.86.row, ...), custom_call_target="tpu_custom_call" | custom-call | flops 100000000 | bytes 6346816 | tf_op jit(solution)/shard_map/pallas_call | solution.py:47
  (4 shorter events, 0.0 us)
Async XLA Ops:
  2.5 9.2 %collective-permute-start = (bf16[160,512]{1,0:T(8,128)(2,1)}, bf16[160,512]{1,0:T(8,128)(2,1)S(1)}, u32[]{:S(2)}, u32[]{:S(2)}) collective-permute-start(bf16[160,512]{1,0:T(8,128)(2,1)} %get-tuple-element.49), channel_id=1, source_target_pairs={{0,12},{4,0},{8,4},{12,8},{1,13},{5,1},{9,5},{13,9},{2,14},{6,2},{... | collective-permute-start | bytes 491528 | tf_op jit(solution)/shard_map/ppermute | solution.py:20
  7.6 1.0 %copy-start = (f32[160,512]{1,0:T(8,128)S(1)}, f32[160,512]{1,0:T(8,128)}, u32[]{:S(2)}) copy-start(f32[160,512]{1,0:T(8,128)} %get-tuple-element.48.after.own.params) | copy-start | bytes 983044
  8.6 1.4 %copy-start.1 = (bf16[1,512,1536]{2,1,0:T(8,128)(2,1)S(1)}, bf16[1,512,1536]{2,1,0:T(8,128)(2,1)}, u32[]{:S(2)}) copy-start(bf16[1,512,1536]{2,1,0:T(8,128)(2,1)} %param.11) | copy-start | bytes 4718596
  10.0 1.0 %copy-start.2 = (bf16[1,512,512]{2,1,0:T(8,128)(2,1)S(1)}, bf16[1,512,512]{2,1,0:T(8,128)(2,1)}, u32[]{:S(2)}) copy-start(bf16[1,512,512]{2,1,0:T(8,128)(2,1)} %param.12) | copy-start | bytes 1572868
  16.5 7.2 %collective-permute-start.1 = (bf16[144,512]{1,0:T(8,128)(2,1)S(1)}, bf16[144,512]{1,0:T(8,128)(2,1)S(1)}, u32[]{:S(2)}, u32[]{:S(2)}) collective-permute-start(bf16[144,512]{1,0:T(8,128)(2,1)S(1)} %get-tuple-element.53), channel_id=1, source_target_pairs={{16,0},{17,1},{18,2},{19,3},{20,4},{21,5},{22,6},{23,7},{24,8},{25... | collective-permute-start | bytes 442376 | tf_op jit(solution)/shard_map/ppermute | solution.py:26
  26.6 2.8 %collective-permute-start.3 = (bf16[256,2176]{1,0:T(8,128)(2,1)S(1)}, bf16[256,2176]{1,0:T(8,128)(2,1)S(1)}, u32[]{:S(2)}, u32[]{:S(2)}) collective-permute-start(bf16[256,2176]{1,0:T(8,128)(2,1)S(1)} %get-tuple-element.67), channel_id=1, source_target_pairs={{0,1},{1,0},{2,3},{3,2},{4,5},{5,4},{6,7},{7,6},{8,9},{9,8},{10,11... | collective-permute-start | bytes 3342344 | tf_op jit(solution)/shard_map/ppermute | solution.py:31
  29.8 46.5 %copy-start.3 = (f32[1,512]{1,0:T(1,128)S(1)}, f32[1,512]{1,0:T(1,128)}, u32[]{:S(2)}) copy-start(f32[1,512]{1,0:T(1,128)} %gain.3) | copy-start | bytes 6148
  29.8 15.2 %collective-permute-start.4 = (bf16[128,1408]{1,0:T(8,128)(2,1)S(1)}, bf16[128,1408]{1,0:T(8,128)(2,1)S(1)}, u32[]{:S(2)}, u32[]{:S(2)}) collective-permute-start(bf16[128,1408]{1,0:T(8,128)(2,1)S(1)} %get-tuple-element.69), channel_id=1, source_target_pairs={{0,2},{1,3},{2,0},{3,1},{4,6},{5,7},{6,4},{7,5},{8,10},{9,11},{10,... | collective-permute-start | bytes 1081352 | tf_op jit(solution)/shard_map/ppermute | solution.py:31
  31.4 12.4 %collective-permute-start.5 = (bf16[64,768]{1,0:T(8,128)(2,1)S(1)}, bf16[64,768]{1,0:T(8,128)(2,1)S(1)}, u32[]{:S(2)}, u32[]{:S(2)}) collective-permute-start(bf16[64,768]{1,0:T(8,128)(2,1)S(1)} %get-tuple-element.71), channel_id=1, source_target_pairs={{0,4},{4,0},{8,12},{12,8},{1,5},{5,1},{9,13},{13,9},{2,6},{6,2},{1... | collective-permute-start | bytes 294920 | tf_op jit(solution)/shard_map/ppermute | solution.py:31
  31.4 13.6 %collective-permute-start.6 = (bf16[64,768]{1,0:T(8,128)(2,1)S(1)}, bf16[64,768]{1,0:T(8,128)(2,1)S(1)}, u32[]{:S(2)}, u32[]{:S(2)}) collective-permute-start(bf16[64,768]{1,0:T(8,128)(2,1)S(1)} %get-tuple-element.72), channel_id=1, source_target_pairs={{0,8},{4,12},{8,0},{12,4},{1,9},{5,13},{9,1},{13,5},{2,10},{6,14},... | collective-permute-start | bytes 294920 | tf_op jit(solution)/shard_map/ppermute | solution.py:31
  35.7 9.4 %collective-permute-start.7 = (bf16[64,768]{1,0:T(8,128)(2,1)S(1)}, bf16[64,768]{1,0:T(8,128)(2,1)S(1)}, u32[]{:S(2)}, u32[]{:S(2)}) collective-permute-start(bf16[64,768]{1,0:T(8,128)(2,1)S(1)} %get-tuple-element.73), channel_id=1, source_target_pairs={{0,12},{4,8},{8,4},{12,0},{1,13},{5,9},{9,5},{13,1},{2,14},{6,10},... | collective-permute-start | bytes 294920 | tf_op jit(solution)/shard_map/ppermute | solution.py:31
  35.8 8.0 %collective-permute-start.2 = (bf16[72,512]{1,0:T(8,128)(2,1)S(1)}, bf16[72,512]{1,0:T(8,128)(2,1)S(1)}, u32[]{:S(2)}, u32[]{:S(2)}) collective-permute-start(bf16[72,512]{1,0:T(8,128)(2,1)S(1)} %get-tuple-element.65), channel_id=1, source_target_pairs={{0,4},{4,8},{8,12},{12,0},{1,5},{5,9},{9,13},{13,1},{2,6},{6,10},{... | collective-permute-start | bytes 221192 | tf_op jit(solution)/shard_map/ppermute | solution.py:20
  45.2 8.5 %collective-permute-start.9 = (bf16[32,1408]{1,0:T(8,128)(2,1)S(1)}, bf16[32,1408]{1,0:T(8,128)(2,1)S(1)}, u32[]{:S(2)}, u32[]{:S(2)}) collective-permute-start(bf16[32,1408]{1,0:T(8,128)(2,1)S(1)} %get-tuple-element.77), channel_id=1, source_target_pairs={{0,4},{4,0},{8,12},{12,8},{1,5},{5,1},{9,13},{13,9},{2,6},{6,2},{1... | collective-permute-start | bytes 270344 | tf_op jit(solution)/shard_map/ppermute | solution.py:31
  46.9 9.1 %collective-permute-start.10 = (bf16[32,1408]{1,0:T(8,128)(2,1)S(1)}, bf16[32,1408]{1,0:T(8,128)(2,1)S(1)}, u32[]{:S(2)}, u32[]{:S(2)}) collective-permute-start(bf16[32,1408]{1,0:T(8,128)(2,1)S(1)} %get-tuple-element.78), channel_id=1, source_target_pairs={{0,8},{4,12},{8,0},{12,4},{1,9},{5,13},{9,1},{13,5},{2,10},{6,14},... | collective-permute-start | bytes 270344 | tf_op jit(solution)/shard_map/ppermute | solution.py:31
  48.0 8.0 %collective-permute-start.11 = (bf16[32,1408]{1,0:T(8,128)(2,1)S(1)}, bf16[32,1408]{1,0:T(8,128)(2,1)S(1)}, u32[]{:S(2)}, u32[]{:S(2)}) collective-permute-start(bf16[32,1408]{1,0:T(8,128)(2,1)S(1)} %get-tuple-element.79), channel_id=1, source_target_pairs={{0,12},{4,8},{8,4},{12,0},{1,13},{5,9},{9,5},{13,1},{2,14},{6,10},... | collective-permute-start | bytes 270344 | tf_op jit(solution)/shard_map/ppermute | solution.py:31
  49.7 4.1 %collective-permute-start.8 = (bf16[32,768]{1,0:T(8,128)(2,1)S(1)}, bf16[32,768]{1,0:T(8,128)(2,1)S(1)}, u32[]{:S(2)}, u32[]{:S(2)}) collective-permute-start(bf16[32,768]{1,0:T(8,128)(2,1)S(1)} %get-tuple-element.76), channel_id=1, source_target_pairs={{0,2},{1,3},{2,0},{3,1},{4,6},{5,7},{6,4},{7,5},{8,10},{9,11},{10,... | collective-permute-start | bytes 147464 | tf_op jit(solution)/shard_map/ppermute | solution.py:31
  56.1 8.8 %collective-permute-start.15 = (bf16[32,1280]{1,0:T(8,128)(2,1)S(1)}, bf16[32,1280]{1,0:T(8,128)(2,1)S(1)}, u32[]{:S(2)}, u32[]{:S(2)}) collective-permute-start(bf16[32,1280]{1,0:T(8,128)(2,1)S(1)} %get-tuple-element.82.rest_0_), channel_id=1, source_target_pairs={{0,12},{4,8},{8,4},{12,0},{1,13},{5,9},{9,5},{13,1},{2,14},{6,10},... | collective-permute-start | bytes 245768 | tf_op jit(solution)/shard_map/ppermute | solution.py:31
  58.2 6.8 %collective-permute-start.14 = (bf16[32,1280]{1,0:T(8,128)(2,1)S(1)}, bf16[32,1280]{1,0:T(8,128)(2,1)S(1)}, u32[]{:S(2)}, u32[]{:S(2)}) collective-permute-start(bf16[32,1280]{1,0:T(8,128)(2,1)S(1)} %get-tuple-element.82.rest_0_), channel_id=1, source_target_pairs={{0,8},{4,12},{8,0},{12,4},{1,9},{5,13},{9,1},{13,5},{2,10},{6,14},... | collective-permute-start | bytes 245768 | tf_op jit(solution)/shard_map/ppermute | solution.py:31
  59.1 5.9 %collective-permute-start.13 = (bf16[32,1280]{1,0:T(8,128)(2,1)S(1)}, bf16[32,1280]{1,0:T(8,128)(2,1)S(1)}, u32[]{:S(2)}, u32[]{:S(2)}) collective-permute-start(bf16[32,1280]{1,0:T(8,128)(2,1)S(1)} %get-tuple-element.82.rest_0_), channel_id=1, source_target_pairs={{0,4},{4,0},{8,12},{12,8},{1,5},{5,1},{9,13},{13,9},{2,6},{6,2},{1... | collective-permute-start | bytes 245768 | tf_op jit(solution)/shard_map/ppermute | solution.py:31
  60.5 4.4 %collective-permute-start.12 = (bf16[32,768]{1,0:T(8,128)(2,1)S(1)}, bf16[32,768]{1,0:T(8,128)(2,1)S(1)}, u32[]{:S(2)}, u32[]{:S(2)}) collective-permute-start(bf16[32,768]{1,0:T(8,128)(2,1)S(1)} %get-tuple-element.81.piece_q), channel_id=1, source_target_pairs={{0,2},{1,3},{2,0},{3,1},{4,6},{5,7},{6,4},{7,5},{8,10},{9,11},{10,... | collective-permute-start | bytes 147464 | tf_op jit(solution)/shard_map/ppermute | solution.py:31
  65.1 11.2 %collective-permute-start.16 = (bf16[128,1280]{1,0:T(8,128)(2,1)S(1)}, bf16[128,1280]{1,0:T(8,128)(2,1)S(1)}, u32[]{:S(2)}, u32[]{:S(2)}) collective-permute-start(bf16[128,1280]{1,0:T(8,128)(2,1)S(1)} %get-tuple-element.83.block_p), channel_id=1, source_target_pairs={{0,2},{1,3},{2,0},{3,1},{4,6},{5,7},{6,4},{7,5},{8,10},{9,11},{10,... | collective-permute-start | bytes 983048 | tf_op jit(solution)/shard_map/ppermute | solution.py:31
  65.7 6.7 %collective-permute-start.19 = (bf16[64,768]{1,0:T(8,128)(2,1)S(1)}, bf16[64,768]{1,0:T(8,128)(2,1)S(1)}, u32[]{:S(2)}, u32[]{:S(2)}) collective-permute-start(bf16[64,768]{1,0:T(8,128)(2,1)S(1)} %get-tuple-element.84.rest_0_), channel_id=1, source_target_pairs={{0,12},{4,8},{8,4},{12,0},{1,13},{5,9},{9,5},{13,1},{2,14},{6,10},... | collective-permute-start | bytes 294920 | tf_op jit(solution)/shard_map/ppermute | solution.py:31
  68.6 7.7 %collective-permute-start.18 = (bf16[64,768]{1,0:T(8,128)(2,1)S(1)}, bf16[64,768]{1,0:T(8,128)(2,1)S(1)}, u32[]{:S(2)}, u32[]{:S(2)}) collective-permute-start(bf16[64,768]{1,0:T(8,128)(2,1)S(1)} %get-tuple-element.84.rest_0_), channel_id=1, source_target_pairs={{0,8},{4,12},{8,0},{12,4},{1,9},{5,13},{9,1},{13,5},{2,10},{6,14},... | collective-permute-start | bytes 294920 | tf_op jit(solution)/shard_map/ppermute | solution.py:31
  68.6 7.7 %collective-permute-start.17 = (bf16[64,768]{1,0:T(8,128)(2,1)S(1)}, bf16[64,768]{1,0:T(8,128)(2,1)S(1)}, u32[]{:S(2)}, u32[]{:S(2)}) collective-permute-start(bf16[64,768]{1,0:T(8,128)(2,1)S(1)} %get-tuple-element.84.rest_0_), channel_id=1, source_target_pairs={{0,4},{4,0},{8,12},{12,8},{1,5},{5,1},{9,13},{13,9},{2,6},{6,2},{1... | collective-permute-start | bytes 294920 | tf_op jit(solution)/shard_map/ppermute | solution.py:31
  76.8 4.0 %collective-permute-start.20 = (bf16[256,2048]{1,0:T(8,128)(2,1)S(1)}, bf16[256,2048]{1,0:T(8,128)(2,1)S(1)}, u32[]{:S(2)}, u32[]{:S(2)}) collective-permute-start(bf16[256,2048]{1,0:T(8,128)(2,1)S(1)} %get-tuple-element.85.half), channel_id=1, source_target_pairs={{0,1},{1,0},{2,3},{3,2},{4,5},{5,4},{6,7},{7,6},{8,9},{9,8},{10,11... | collective-permute-start | bytes 3145736 | tf_op jit(solution)/shard_map/ppermute | solution.py:31
  76.8 3.2 %collective-permute-start.23 = (f32[8,384]{1,0:T(8,128)S(1)}, f32[8,384]{1,0:T(8,128)S(1)}, u32[]{:S(2)}, u32[]{:S(2)}) collective-permute-start(f32[8,384]{1,0:T(8,128)S(1)} %get-tuple-element.86.row), channel_id=1, source_target_pairs={{0,17},{1,16},{2,19},{3,18},{16,1},{17,0},{18,3},{19,2},{4,21},{5,... | collective-permute-start | bytes 36872 | tf_op jit(solution)/shard_map/ppermute | solution.py:613
  76.9 3.9 %collective-permute-start.22 = (f32[8,384]{1,0:T(8,128)S(1)}, f32[8,384]{1,0:T(8,128)S(1)}, u32[]{:S(2)}, u32[]{:S(2)}) collective-permute-start(f32[8,384]{1,0:T(8,128)S(1)} %get-tuple-element.86.row), channel_id=1, source_target_pairs={{0,16},{16,0},{1,17},{17,1},{2,18},{18,2},{3,19},{19,3},{4,20},{20... | collective-permute-start | bytes 36872 | tf_op jit(solution)/shard_map/ppermute | solution.py:31
  79.0 1.8 %collective-permute-start.21 = (f32[8,384]{1,0:T(8,128)S(1)}, f32[8,384]{1,0:T(8,128)S(1)}, u32[]{:S(2)}, u32[]{:S(2)}) collective-permute-start(f32[8,384]{1,0:T(8,128)S(1)} %get-tuple-element.86.row), channel_id=1, source_target_pairs={{0,1},{1,0},{2,3},{3,2},{4,5},{5,4},{6,7},{7,6},{8,9},{9,8},{10,11... | collective-permute-start | bytes 36872 | tf_op jit(solution)/shard_map/ppermute | solution.py:31

commit v11 on v7

--- a/solution.py
+++ b/solution.py
@@ -9,7 +9,7 @@
 
 SHIFT = 6
 GROUP = 128
-CUT = 1408
+CUT = 1536
 EPSILON = 1e-05
 F32 = jnp.float32
 BF16 = jnp.bfloat16
@@ -287,7 +287,8 @@
     three = grad_proj.shape[1]
     out[:, :CUT] = dot(tokens, grad_proj[:, :CUT]).astype(out.dtype)
     out[:, CUT : CUT + GROUP] = jnp.broadcast_to(bias_row, (out.shape[0], GROUP)).astype(out.dtype)
-    out[:, CUT + GROUP : three + GROUP] = dot(tokens, grad_proj[:, CUT:]).astype(out.dtype)
+    if CUT < three:
+        out[:, CUT + GROUP : three + GROUP] = dot(tokens, grad_proj[:, CUT:]).astype(out.dtype)
     out[:, three + GROUP :] = dot(attended_t[rows, :], total[...]).astype(out.dtype)
 
 

time: 81.5 us -> 83.6 us (1.026)
  waiting for transfers between devices: 30.8 us -> 33.4 us
    ppermute x20, waiting for transfers between devices: 19 us -> 25.2 us  [swapped(): return lax.ppermute(value, axis, [(i, i ^ bit) for i in range(count)])]
    ppermute x2, waiting for transfers between devices: 5.62 us -> 2.02 us  [from_behind(): lax.ppermute(value, axis, [(i, (i + by) % count) for i in range(count)])]
    ppermute x2, starting transfers between devices: 6.45 us -> 5.1 us  [from_behind(): lax.ppermute(value, axis, [(i, (i + by) % count) for i in range(count)])]
    ppermute x20, starting transfers between devices: 23.1 us -> 24.1 us  [swapped(): return lax.ppermute(value, axis, [(i, i ^ bit) for i in range(count)])]
  transfers between devices with their start and end apart: 24 -> 24, of which waited for: 13 -> 14; matrix products, arithmetic and copies ran while one was open for 0% -> 0% of each run, Pallas kernels for 3% -> 3%
where the time goes in v11:
time: 83.6 us; the launch traced here: 83.3 us
  waiting for transfers between devices  33.4 us (40%)
  starting transfers between devices  30.5 us (36%)
  Pallas kernels  15.1 us (18%)
  local copies, waits for them, and re-layouts  3.43 us (4%)
    ppermute x20, waiting for transfers between devices, swapped(): return lax.ppermute(value, axis, [(i, i ^ bit) for i in range(count)])  25.2 us
    ppermute x20, starting transfers between devices, swapped(): return lax.ppermute(value, axis, [(i, i ^ bit) for i in range(count)])  24.1 us
    pallas_call x12, Pallas kernels, call(): pl.pallas_call(kernel, out_shape=list(outs), in_specs=[pl.BlockSpec(memor...  15.1 us
    ppermute x1, waiting for transfers between devices, passed_along(): return lax.ppermute(block, axis, route)  5.93 us
    ppermute x2, starting transfers between devices, from_behind(): lax.ppermute(value, axis, [(i, (i + by) % count) for i in range(count)])  5.1 us
    unnamed x8, local copies, waits for them, and re-layouts  3.43 us
    ppermute x2, waiting for transfers between devices, from_behind(): lax.ppermute(value, axis, [(i, (i + by) % count) for i in range(count)])  2.02 us
  transfers between devices with their start and end apart: 24, of which 14 were waited for; matrix products, arithmetic and copies ran while one was open for 0% of the time, Pallas kernels for 3%

profile of v11, /device:TPU:0, one launch (start us, length us, event | category | flops | bytes accessed | tf_op | source)
XLA Modules:
  0.0 83.3 jit_solution(17084170459142117155)
XLA Ops:
  0.6 1.9 %shard_map.110 = (f32[160,512]{1,0:T(8,128)}, bf16[160,512]{1,0:T(8,128)(2,1)}) custom-call(bf16[1,6,12,2,512]{4,3,2,1,0:T(2,128)(2,1)} %bitcast.12, bf16[1,6,12,2,512]{4,3,2,1,0:T(2,128)(2,1)} %bitcast.13, s32[6,12]{1,0:T(8,128)} %land.1, f32[1,512]{1,0:T(1,128)} %gain.3, f32[1,16]{1,0:T(1,128)} %bias.1), custom_call_target="tpu_custom_call" | custom-call | flops 100000000 | bytes 788832 | tf_op jit(solution)/shard_map/pallas_call | solution.py:47
  2.5 5.1 %collective-permute-start = (bf16[160,512]{1,0:T(8,128)(2,1)}, bf16[160,512]{1,0:T(8,128)(2,1)S(1)}, u32[]{:S(2)}, u32[]{:S(2)}) collective-permute-start(bf16[160,512]{1,0:T(8,128)(2,1)} %get-tuple-element.49), channel_id=1, source_target_pairs={{0,12},{4,0},{8,4},{12,8},{1,13},{5,1},{9,5},{13,9},{2,14},{6,2},{... | collective-permute-start | bytes 491528 | tf_op jit(solution)/shard_map/ppermute | solution.py:20
  7.6 1.0 %copy-done = f32[160,512]{1,0:T(8,128)S(1)} copy-done((f32[160,512]{1,0:T(8,128)S(1)}, f32[160,512]{1,0:T(8,128)}, u32[]{:S(2)}) %copy-start) | copy-done | bytes 327704
  8.6 1.4 %copy-done.1 = bf16[1,512,1536]{2,1,0:T(8,128)(2,1)S(1)} copy-done((bf16[1,512,1536]{2,1,0:T(8,128)(2,1)S(1)}, bf16[1,512,1536]{2,1,0:T(8,128)(2,1)}, u32[]{:S(2)}) %copy-start.1) | copy-done | bytes 1572888
  10.0 1.0 %copy-done.2 = bf16[1,512,512]{2,1,0:T(8,128)(2,1)S(1)} copy-done((bf16[1,512,512]{2,1,0:T(8,128)(2,1)S(1)}, bf16[1,512,512]{2,1,0:T(8,128)(2,1)}, u32[]{:S(2)}) %copy-start.2) | copy-done | bytes 524312
  11.1 0.6 shard_map.111
  11.7 0.0 collective-permute-done.rim
  11.7 4.7 %shard_map.112 = (bf16[144,512]{1,0:T(8,128)(2,1)S(1)}, bf16[144,512]{1,0:T(8,128)(2,1)S(1)}, bf16[512,144]{1,0:T(8,128)(2,1)S(1)}, bf16[144,1536]{1,0:T(8,128)(...) custom-call(f32[160,512]{1,0:T(8,128)S(1)} %copy-done, ...), custom_call_target="tpu_custom_call" | custom-call | flops 1000000000 | bytes 6299648 | tf_op jit(solution)/shard_map/pallas_call | solution.py:47
  16.5 1.3 %collective-permute-start.1 = (bf16[144,512]{1,0:T(8,128)(2,1)S(1)}, bf16[144,512]{1,0:T(8,128)(2,1)S(1)}, u32[]{:S(2)}, u32[]{:S(2)}) collective-permute-start(bf16[144,512]{1,0:T(8,128)(2,1)S(1)} %get-tuple-element.53), channel_id=1, source_target_pairs={{16,0},{17,1},{18,2},{19,3},{20,4},{21,5},{22,6},{23,7},{24,8},{25... | collective-permute-start | bytes 442376 | tf_op jit(solution)/shard_map/ppermute | solution.py:26
  17.8 5.9 %collective-permute-done.1.skip = bf16[144,512]{1,0:T(8,128)(2,1)S(1)} collective-permute-done((bf16[144,512]{1,0:T(8,128)(2,1)S(1)}, bf16[144,512]{1,0:T(8,128)(2,1)S(1)}, u32[]{:S(2)}, u32[]{:S(2)}) %collective-permute-start.1) | collective-permute-done | bytes 147488 | tf_op jit(solution)/shard_map/ppermute | solution.py:26
  23.7 2.9 %shard_map.113 = (bf16[144,512]{1,0:T(8,128)(2,1)S(1)}, bf16[144,1536]{1,0:T(8,128)(2,1)S(1)}, f32[8,128]{1,0:T(8,128)S(1)}, bf16[256,2176]{1,0:T(8,128)(2,1)S(1)}) custom-call(bf16[144,512]{1,0:T(8,128)(2,1)S(1)} %collective-permute-done.1.skip, bf16[144,512]{1,0:T(8,128)(2,1)S(1)} %get-tuple-element.54.cot, bf16[144,1536]{1,0:T(8,128)(2,1)S(1)} %get-tuple-element.55.qkv, ...), custom_call_target="tpu_custom_call" | custom-call | flops 1000000000 | bytes 4075520 | tf_op jit(solution)/shard_map/pallas_call | solution.py:47
  26.6 0.1 collective-permute-start.3
  26.7 0.8 shard_map.114
  27.4 2.0 %collective-permute-done.3.came = bf16[256,2176]{1,0:T(8,128)(2,1)S(1)} collective-permute-done((bf16[256,2176]{1,0:T(8,128)(2,1)S(1)}, bf16[256,2176]{1,0:T(8,128)(2,1)S(1)}, u32[]{:S(2)}, u32[]{:S(2)}) %collective-permute-start.3) | collective-permute-done | bytes 1114144 | tf_op jit(solution)/shard_map/ppermute | solution.py:31
  29.4 0.4 shard_map.116
  29.8 0.0 copy-start.3
  29.8 1.6 %collective-permute-start.4 = (bf16[128,1664]{1,0:T(8,128)(2,1)S(1)}, bf16[128,1664]{1,0:T(8,128)(2,1)S(1)}, u32[]{:S(2)}, u32[]{:S(2)}) collective-permute-start(bf16[128,1664]{1,0:T(8,128)(2,1)S(1)} %get-tuple-element.69), channel_id=1, source_target_pairs={{0,2},{1,3},{2,0},{3,1},{4,6},{5,7},{6,4},{7,5},{8,10},{9,11},{10,... | collective-permute-start | bytes 1277960 | tf_op jit(solution)/shard_map/ppermute | solution.py:31
  31.4 0.0 collective-permute-start.2
  31.4 3.8 %collective-permute-start.5 = (bf16[64,512]{1,0:T(8,128)(2,1)S(1)}, bf16[64,512]{1,0:T(8,128)(2,1)S(1)}, u32[]{:S(2)}, u32[]{:S(2)}) collective-permute-start(bf16[64,512]{1,0:T(8,128)(2,1)S(1)} %get-tuple-element.71), channel_id=1, source_target_pairs={{0,12},{4,8},{8,4},{12,0},{1,13},{5,9},{9,5},{13,1},{2,14},{6,10},... | collective-permute-start | bytes 196616 | tf_op jit(solution)/shard_map/ppermute | solution.py:31
  35.2 0.4 collective-permute-start.6
  35.7 0.6 collective-permute-start.7
  36.2 2.0 %collective-permute-done.2.back.after = bf16[72,512]{1,0:T(8,128)(2,1)S(1)} collective-permute-done((bf16[72,512]{1,0:T(8,128)(2,1)S(1)}, bf16[72,512]{1,0:T(8,128)(2,1)S(1)}, u32[]{:S(2)}, u32[]{:S(2)}) %collective-permute-start.2) | collective-permute-done | bytes 73760 | tf_op jit(solution)/shard_map/ppermute | solution.py:20
  38.3 0.9 %collective-permute-done.5.rest_0_ = bf16[64,512]{1,0:T(8,128)(2,1)S(1)} collective-permute-done((bf16[64,512]{1,0:T(8,128)(2,1)S(1)}, bf16[64,512]{1,0:T(8,128)(2,1)S(1)}, u32[]{:S(2)}, u32[]{:S(2)}) %collective-permute-start.5) | collective-permute-done | bytes 65568 | tf_op jit(solution)/shard_map/ppermute | solution.py:31
  39.2 3.8 %collective-permute-done.6.rest_1_ = bf16[64,512]{1,0:T(8,128)(2,1)S(1)} collective-permute-done((bf16[64,512]{1,0:T(8,128)(2,1)S(1)}, bf16[64,512]{1,0:T(8,128)(2,1)S(1)}, u32[]{:S(2)}, u32[]{:S(2)}) %collective-permute-start.6) | collective-permute-done | bytes 65568 | tf_op jit(solution)/shard_map/ppermute | solution.py:31
  43.0 0.0 collective-permute-done.7.rest_2_
  43.0 0.0 collective-permute-done.4.came_p
  43.0 0.2 shard_map.117
  43.2 2.5 %collective-permute-start.9 = (bf16[32,1664]{1,0:T(8,128)(2,1)S(1)}, bf16[32,1664]{1,0:T(8,128)(2,1)S(1)}, u32[]{:S(2)}, u32[]{:S(2)}) collective-permute-start(bf16[32,1664]{1,0:T(8,128)(2,1)S(1)} %get-tuple-element.77), channel_id=1, source_target_pairs={{0,12},{4,8},{8,4},{12,0},{1,13},{5,9},{9,5},{13,1},{2,14},{6,10},... | collective-permute-start | bytes 319496 | tf_op jit(solution)/shard_map/ppermute | solution.py:31
  45.7 0.0 collective-permute-start.10
  45.7 2.0 %collective-permute-start.11 = (bf16[32,1664]{1,0:T(8,128)(2,1)S(1)}, bf16[32,1664]{1,0:T(8,128)(2,1)S(1)}, u32[]{:S(2)}, u32[]{:S(2)}) collective-permute-start(bf16[32,1664]{1,0:T(8,128)(2,1)S(1)} %get-tuple-element.79), channel_id=1, source_target_pairs={{0,4},{4,0},{8,12},{12,8},{1,5},{5,1},{9,13},{13,9},{2,6},{6,2},{1... | collective-permute-start | bytes 319496 | tf_op jit(solution)/shard_map/ppermute | solution.py:31
  47.7 0.5 collective-permute-start.8
  48.2 3.4 %collective-permute-done.8.came_q = bf16[32,512]{1,0:T(8,128)(2,1)S(1)} collective-permute-done((bf16[32,512]{1,0:T(8,128)(2,1)S(1)}, bf16[32,512]{1,0:T(8,128)(2,1)S(1)}, u32[]{:S(2)}, u32[]{:S(2)}) %collective-permute-start.8) | collective-permute-done | bytes 32800 | tf_op jit(solution)/shard_map/ppermute | solution.py:31
  51.6 0.0 collective-permute-done.9.rest_0_
  51.6 2.9 %collective-permute-done.10.rest_1_ = bf16[32,1664]{1,0:T(8,128)(2,1)S(1)} collective-permute-done((bf16[32,1664]{1,0:T(8,128)(2,1)S(1)}, bf16[32,1664]{1,0:T(8,128)(2,1)S(1)}, u32[]{:S(2)}, u32[]{:S(2)}) %collective-permute-start.10) | collective-permute-done | bytes 106528 | tf_op jit(solution)/shard_map/ppermute | solution.py:31
  54.5 0.0 collective-permute-done.11.rest_2_
  54.5 0.1 shard_map.118
  54.6 1.8 %collective-permute-start.15 = (bf16[32,1536]{1,0:T(8,128)(2,1)S(1)}, bf16[32,1536]{1,0:T(8,128)(2,1)S(1)}, u32[]{:S(2)}, u32[]{:S(2)}) collective-permute-start(bf16[32,1536]{1,0:T(8,128)(2,1)S(1)} %get-tuple-element.82.rest_0_), channel_id=1, source_target_pairs={{0,12},{4,8},{8,4},{12,0},{1,13},{5,9},{9,5},{13,1},{2,14},{6,10},... | collective-permute-start | bytes 294920 | tf_op jit(solution)/shard_map/ppermute | solution.py:31
  56.4 0.0 collective-permute-start.14
  56.4 2.7 %collective-permute-start.13 = (bf16[32,1536]{1,0:T(8,128)(2,1)S(1)}, bf16[32,1536]{1,0:T(8,128)(2,1)S(1)}, u32[]{:S(2)}, u32[]{:S(2)}) collective-permute-start(bf16[32,1536]{1,0:T(8,128)(2,1)S(1)} %get-tuple-element.82.rest_0_), channel_id=1, source_target_pairs={{0,4},{4,0},{8,12},{12,8},{1,5},{5,1},{9,13},{13,9},{2,6},{6,2},{1... | collective-permute-start | bytes 294920 | tf_op jit(solution)/shard_map/ppermute | solution.py:31
  59.1 0.5 collective-permute-start.12
  59.6 3.4 %collective-permute-done.12.other_q = bf16[32,512]{1,0:T(8,128)(2,1)S(1)} collective-permute-done((bf16[32,512]{1,0:T(8,128)(2,1)S(1)}, bf16[32,512]{1,0:T(8,128)(2,1)S(1)}, u32[]{:S(2)}, u32[]{:S(2)}) %collective-permute-start.12) | collective-permute-done | bytes 32800 | tf_op jit(solution)/shard_map/ppermute | solution.py:31
  63.0 0.0 collective-permute-done.15.rest_3_
  63.0 2.4 %collective-permute-done.14.rest_2_ = bf16[32,1536]{1,0:T(8,128)(2,1)S(1)} collective-permute-done((bf16[32,1536]{1,0:T(8,128)(2,1)S(1)}, bf16[32,1536]{1,0:T(8,128)(2,1)S(1)}, u32[]{:S(2)}, u32[]{:S(2)}) %collective-permute-start.14) | collective-permute-done | bytes 98336 | tf_op jit(solution)/shard_map/ppermute | solution.py:31
  65.4 0.0 collective-permute-done.13.rest_1_
  65.4 1.2 %collective-permute-start.16 = (bf16[128,1536]{1,0:T(8,128)(2,1)S(1)}, bf16[128,1536]{1,0:T(8,128)(2,1)S(1)}, u32[]{:S(2)}, u32[]{:S(2)}) collective-permute-start(bf16[128,1536]{1,0:T(8,128)(2,1)S(1)} %get-tuple-element.83.block_p), channel_id=1, source_target_pairs={{0,2},{1,3},{2,0},{3,1},{4,6},{5,7},{6,4},{7,5},{8,10},{9,11},{10,... | collective-permute-start | bytes 1179656 | tf_op jit(solution)/shard_map/ppermute | solution.py:31
  66.6 1.9 %collective-permute-start.19 = (bf16[64,512]{1,0:T(8,128)(2,1)S(1)}, bf16[64,512]{1,0:T(8,128)(2,1)S(1)}, u32[]{:S(2)}, u32[]{:S(2)}) collective-permute-start(bf16[64,512]{1,0:T(8,128)(2,1)S(1)} %get-tuple-element.84.rest_0_), channel_id=1, source_target_pairs={{0,12},{4,8},{8,4},{12,0},{1,13},{5,9},{9,5},{13,1},{2,14},{6,10},... | collective-permute-start | bytes 196616 | tf_op jit(solution)/shard_map/ppermute | solution.py:31
  68.6 0.0 collective-permute-start.18
  68.6 2.5 %collective-permute-start.17 = (bf16[64,512]{1,0:T(8,128)(2,1)S(1)}, bf16[64,512]{1,0:T(8,128)(2,1)S(1)}, u32[]{:S(2)}, u32[]{:S(2)}) collective-permute-start(bf16[64,512]{1,0:T(8,128)(2,1)S(1)} %get-tuple-element.84.rest_0_), channel_id=1, source_target_pairs={{0,4},{4,0},{8,12},{12,8},{1,5},{5,1},{9,13},{13,9},{2,6},{6,2},{1... | collective-permute-start | bytes 196616 | tf_op jit(solution)/shard_map/ppermute | solution.py:31
  71.0 1.7 %collective-permute-done.19.rest_3_ = bf16[64,512]{1,0:T(8,128)(2,1)S(1)} collective-permute-done((bf16[64,512]{1,0:T(8,128)(2,1)S(1)}, bf16[64,512]{1,0:T(8,128)(2,1)S(1)}, u32[]{:S(2)}, u32[]{:S(2)}) %collective-permute-start.19) | collective-permute-done | bytes 65568 | tf_op jit(solution)/shard_map/ppermute | solution.py:31
  72.7 2.0 %collective-permute-done.18.rest_2_ = bf16[64,512]{1,0:T(8,128)(2,1)S(1)} collective-permute-done((bf16[64,512]{1,0:T(8,128)(2,1)S(1)}, bf16[64,512]{1,0:T(8,128)(2,1)S(1)}, u32[]{:S(2)}, u32[]{:S(2)}) %collective-permute-start.18) | collective-permute-done | bytes 65568 | tf_op jit(solution)/shard_map/ppermute | solution.py:31
  74.7 0.0 collective-permute-done.17.rest_1_
  74.7 1.8 %collective-permute-done.16.other_p = bf16[128,1536]{1,0:T(8,128)(2,1)S(1)} collective-permute-done((bf16[128,1536]{1,0:T(8,128)(2,1)S(1)}, bf16[128,1536]{1,0:T(8,128)(2,1)S(1)}, u32[]{:S(2)}, u32[]{:S(2)}) %collective-permute-start.16) | collective-permute-done | bytes 393248 | tf_op jit(solution)/shard_map/ppermute | solution.py:31
  76.6 0.0 copy-done.3
  76.6 0.5 shard_map.120
  77.0 0.0 collective-permute-start.20
  77.1 0.1 collective-permute-start.23
  77.2 2.1 %collective-permute-start.22 = (f32[8,384]{1,0:T(8,128)S(1)}, f32[8,384]{1,0:T(8,128)S(1)}, u32[]{:S(2)}, u32[]{:S(2)}) collective-permute-start(f32[8,384]{1,0:T(8,128)S(1)} %get-tuple-element.86.row), channel_id=1, source_target_pairs={{0,16},{16,0},{1,17},{17,1},{2,18},{18,2},{3,19},{19,3},{4,20},{20... | collective-permute-start | bytes 36872 | tf_op jit(solution)/shard_map/ppermute | solution.py:31
  79.2 0.0 collective-permute-start.21
  79.2 0.8 shard_map.115
  80.0 0.3 collective-permute-done.23.row_both
  80.3 0.8 collective-permute-done.22.row_section
  81.0 0.0 collective-permute-done.21.row_core
  81.0 0.0 collective-permute-done.20.other
  81.0 2.3 %shard_map.121 = (f32[512,1536]{1,0:T(8,128)}, f32[512,512]{1,0:T(8,128)}, f32[1,512]{1,0:T(1,128)}, f32[1,16]{1,0:T(1,128)}) custom-call(bf16[256,2048]{1,0:T(8,128)(2,1)S(1)} %get-tuple-element.85.half, bf16[256,2048]{1,0:T(8,128)(2,1)S(1)} %collective-permute-done.20.other, f32[8,384]{1,0:T(8,128)S(1)} %get-tuple-element.86.row, ...), custom_call_target="tpu_custom_call" | custom-call | flops 100000000 | bytes 6346816 | tf_op jit(solution)/shard_map/pallas_call | solution.py:47
  (4 shorter events, 0.0 us)
Async XLA Ops:
  2.5 9.2 %collective-permute-start = (bf16[160,512]{1,0:T(8,128)(2,1)}, bf16[160,512]{1,0:T(8,128)(2,1)S(1)}, u32[]{:S(2)}, u32[]{:S(2)}) collective-permute-start(bf16[160,512]{1,0:T(8,128)(2,1)} %get-tuple-element.49), channel_id=1, source_target_pairs={{0,12},{4,0},{8,4},{12,8},{1,13},{5,1},{9,5},{13,9},{2,14},{6,2},{... | collective-permute-start | bytes 491528 | tf_op jit(solution)/shard_map/ppermute | solution.py:20
  7.6 1.0 %copy-start = (f32[160,512]{1,0:T(8,128)S(1)}, f32[160,512]{1,0:T(8,128)}, u32[]{:S(2)}) copy-start(f32[160,512]{1,0:T(8,128)} %get-tuple-element.48.after.own.params) | copy-start | bytes 983044
  8.6 1.4 %copy-start.1 = (bf16[1,512,1536]{2,1,0:T(8,128)(2,1)S(1)}, bf16[1,512,1536]{2,1,0:T(8,128)(2,1)}, u32[]{:S(2)}) copy-start(bf16[1,512,1536]{2,1,0:T(8,128)(2,1)} %param.11) | copy-start | bytes 4718596
  10.0 1.0 %copy-start.2 = (bf16[1,512,512]{2,1,0:T(8,128)(2,1)S(1)}, bf16[1,512,512]{2,1,0:T(8,128)(2,1)}, u32[]{:S(2)}) copy-start(bf16[1,512,512]{2,1,0:T(8,128)(2,1)} %param.12) | copy-start | bytes 1572868
  16.5 7.2 %collective-permute-start.1 = (bf16[144,512]{1,0:T(8,128)(2,1)S(1)}, bf16[144,512]{1,0:T(8,128)(2,1)S(1)}, u32[]{:S(2)}, u32[]{:S(2)}) collective-permute-start(bf16[144,512]{1,0:T(8,128)(2,1)S(1)} %get-tuple-element.53), channel_id=1, source_target_pairs={{16,0},{17,1},{18,2},{19,3},{20,4},{21,5},{22,6},{23,7},{24,8},{25... | collective-permute-start | bytes 442376 | tf_op jit(solution)/shard_map/ppermute | solution.py:26
  26.6 2.8 %collective-permute-start.3 = (bf16[256,2176]{1,0:T(8,128)(2,1)S(1)}, bf16[256,2176]{1,0:T(8,128)(2,1)S(1)}, u32[]{:S(2)}, u32[]{:S(2)}) collective-permute-start(bf16[256,2176]{1,0:T(8,128)(2,1)S(1)} %get-tuple-element.67), channel_id=1, source_target_pairs={{0,1},{1,0},{2,3},{3,2},{4,5},{5,4},{6,7},{7,6},{8,9},{9,8},{10,11... | collective-permute-start | bytes 3342344 | tf_op jit(solution)/shard_map/ppermute | solution.py:31
  29.8 46.7 %copy-start.3 = (f32[1,512]{1,0:T(1,128)S(1)}, f32[1,512]{1,0:T(1,128)}, u32[]{:S(2)}) copy-start(f32[1,512]{1,0:T(1,128)} %gain.3) | copy-start | bytes 6148
  29.8 13.2 %collective-permute-start.4 = (bf16[128,1664]{1,0:T(8,128)(2,1)S(1)}, bf16[128,1664]{1,0:T(8,128)(2,1)S(1)}, u32[]{:S(2)}, u32[]{:S(2)}) collective-permute-start(bf16[128,1664]{1,0:T(8,128)(2,1)S(1)} %get-tuple-element.69), channel_id=1, source_target_pairs={{0,2},{1,3},{2,0},{3,1},{4,6},{5,7},{6,4},{7,5},{8,10},{9,11},{10,... | collective-permute-start | bytes 1277960 | tf_op jit(solution)/shard_map/ppermute | solution.py:31
  31.4 6.9 %collective-permute-start.2 = (bf16[72,512]{1,0:T(8,128)(2,1)S(1)}, bf16[72,512]{1,0:T(8,128)(2,1)S(1)}, u32[]{:S(2)}, u32[]{:S(2)}) collective-permute-start(bf16[72,512]{1,0:T(8,128)(2,1)S(1)} %get-tuple-element.65), channel_id=1, source_target_pairs={{0,4},{4,8},{8,12},{12,0},{1,5},{5,9},{9,13},{13,1},{2,6},{6,10},{... | collective-permute-start | bytes 221192 | tf_op jit(solution)/shard_map/ppermute | solution.py:20
  31.4 7.8 %collective-permute-start.5 = (bf16[64,512]{1,0:T(8,128)(2,1)S(1)}, bf16[64,512]{1,0:T(8,128)(2,1)S(1)}, u32[]{:S(2)}, u32[]{:S(2)}) collective-permute-start(bf16[64,512]{1,0:T(8,128)(2,1)S(1)} %get-tuple-element.71), channel_id=1, source_target_pairs={{0,12},{4,8},{8,4},{12,0},{1,13},{5,9},{9,5},{13,1},{2,14},{6,10},... | collective-permute-start | bytes 196616 | tf_op jit(solution)/shard_map/ppermute | solution.py:31
  35.2 7.8 %collective-permute-start.6 = (bf16[64,512]{1,0:T(8,128)(2,1)S(1)}, bf16[64,512]{1,0:T(8,128)(2,1)S(1)}, u32[]{:S(2)}, u32[]{:S(2)}) collective-permute-start(bf16[64,512]{1,0:T(8,128)(2,1)S(1)} %get-tuple-element.72), channel_id=1, source_target_pairs={{0,8},{4,12},{8,0},{12,4},{1,9},{5,13},{9,1},{13,5},{2,10},{6,14},... | collective-permute-start | bytes 196616 | tf_op jit(solution)/shard_map/ppermute | solution.py:31
  35.7 7.3 %collective-permute-start.7 = (bf16[64,512]{1,0:T(8,128)(2,1)S(1)}, bf16[64,512]{1,0:T(8,128)(2,1)S(1)}, u32[]{:S(2)}, u32[]{:S(2)}) collective-permute-start(bf16[64,512]{1,0:T(8,128)(2,1)S(1)} %get-tuple-element.73), channel_id=1, source_target_pairs={{0,4},{4,0},{8,12},{12,8},{1,5},{5,1},{9,13},{13,9},{2,6},{6,2},{1... | collective-permute-start | bytes 196616 | tf_op jit(solution)/shard_map/ppermute | solution.py:31
  43.2 8.4 %collective-permute-start.9 = (bf16[32,1664]{1,0:T(8,128)(2,1)S(1)}, bf16[32,1664]{1,0:T(8,128)(2,1)S(1)}, u32[]{:S(2)}, u32[]{:S(2)}) collective-permute-start(bf16[32,1664]{1,0:T(8,128)(2,1)S(1)} %get-tuple-element.77), channel_id=1, source_target_pairs={{0,12},{4,8},{8,4},{12,0},{1,13},{5,9},{9,5},{13,1},{2,14},{6,10},... | collective-permute-start | bytes 319496 | tf_op jit(solution)/shard_map/ppermute | solution.py:31
  45.7 8.8 %collective-permute-start.10 = (bf16[32,1664]{1,0:T(8,128)(2,1)S(1)}, bf16[32,1664]{1,0:T(8,128)(2,1)S(1)}, u32[]{:S(2)}, u32[]{:S(2)}) collective-permute-start(bf16[32,1664]{1,0:T(8,128)(2,1)S(1)} %get-tuple-element.78), channel_id=1, source_target_pairs={{0,8},{4,12},{8,0},{12,4},{1,9},{5,13},{9,1},{13,5},{2,10},{6,14},... | collective-permute-start | bytes 319496 | tf_op jit(solution)/shard_map/ppermute | solution.py:31
  45.7 8.8 %collective-permute-start.11 = (bf16[32,1664]{1,0:T(8,128)(2,1)S(1)}, bf16[32,1664]{1,0:T(8,128)(2,1)S(1)}, u32[]{:S(2)}, u32[]{:S(2)}) collective-permute-start(bf16[32,1664]{1,0:T(8,128)(2,1)S(1)} %get-tuple-element.79), channel_id=1, source_target_pairs={{0,4},{4,0},{8,12},{12,8},{1,5},{5,1},{9,13},{13,9},{2,6},{6,2},{1... | collective-permute-start | bytes 319496 | tf_op jit(solution)/shard_map/ppermute | solution.py:31
  47.7 3.9 %collective-permute-start.8 = (bf16[32,512]{1,0:T(8,128)(2,1)S(1)}, bf16[32,512]{1,0:T(8,128)(2,1)S(1)}, u32[]{:S(2)}, u32[]{:S(2)}) collective-permute-start(bf16[32,512]{1,0:T(8,128)(2,1)S(1)} %get-tuple-element.76), channel_id=1, source_target_pairs={{0,2},{1,3},{2,0},{3,1},{4,6},{5,7},{6,4},{7,5},{8,10},{9,11},{10,... | collective-permute-start | bytes 98312 | tf_op jit(solution)/shard_map/ppermute | solution.py:31
  54.6 8.4 %collective-permute-start.15 = (bf16[32,1536]{1,0:T(8,128)(2,1)S(1)}, bf16[32,1536]{1,0:T(8,128)(2,1)S(1)}, u32[]{:S(2)}, u32[]{:S(2)}) collective-permute-start(bf16[32,1536]{1,0:T(8,128)(2,1)S(1)} %get-tuple-element.82.rest_0_), channel_id=1, source_target_pairs={{0,12},{4,8},{8,4},{12,0},{1,13},{5,9},{9,5},{13,1},{2,14},{6,10},... | collective-permute-start | bytes 294920 | tf_op jit(solution)/shard_map/ppermute | solution.py:31
  56.4 9.0 %collective-permute-start.14 = (bf16[32,1536]{1,0:T(8,128)(2,1)S(1)}, bf16[32,1536]{1,0:T(8,128)(2,1)S(1)}, u32[]{:S(2)}, u32[]{:S(2)}) collective-permute-start(bf16[32,1536]{1,0:T(8,128)(2,1)S(1)} %get-tuple-element.82.rest_0_), channel_id=1, source_target_pairs={{0,8},{4,12},{8,0},{12,4},{1,9},{5,13},{9,1},{13,5},{2,10},{6,14},... | collective-permute-start | bytes 294920 | tf_op jit(solution)/shard_map/ppermute | solution.py:31
  56.4 9.0 %collective-permute-start.13 = (bf16[32,1536]{1,0:T(8,128)(2,1)S(1)}, bf16[32,1536]{1,0:T(8,128)(2,1)S(1)}, u32[]{:S(2)}, u32[]{:S(2)}) collective-permute-start(bf16[32,1536]{1,0:T(8,128)(2,1)S(1)} %get-tuple-element.82.rest_0_), channel_id=1, source_target_pairs={{0,4},{4,0},{8,12},{12,8},{1,5},{5,1},{9,13},{13,9},{2,6},{6,2},{1... | collective-permute-start | bytes 294920 | tf_op jit(solution)/shard_map/ppermute | solution.py:31
  59.1 3.9 %collective-permute-start.12 = (bf16[32,512]{1,0:T(8,128)(2,1)S(1)}, bf16[32,512]{1,0:T(8,128)(2,1)S(1)}, u32[]{:S(2)}, u32[]{:S(2)}) collective-permute-start(bf16[32,512]{1,0:T(8,128)(2,1)S(1)} %get-tuple-element.81.piece_q), channel_id=1, source_target_pairs={{0,2},{1,3},{2,0},{3,1},{4,6},{5,7},{6,4},{7,5},{8,10},{9,11},{10,... | collective-permute-start | bytes 98312 | tf_op jit(solution)/shard_map/ppermute | solution.py:31
  65.4 11.1 %collective-permute-start.16 = (bf16[128,1536]{1,0:T(8,128)(2,1)S(1)}, bf16[128,1536]{1,0:T(8,128)(2,1)S(1)}, u32[]{:S(2)}, u32[]{:S(2)}) collective-permute-start(bf16[128,1536]{1,0:T(8,128)(2,1)S(1)} %get-tuple-element.83.block_p), channel_id=1, source_target_pairs={{0,2},{1,3},{2,0},{3,1},{4,6},{5,7},{6,4},{7,5},{8,10},{9,11},{10,... | collective-permute-start | bytes 1179656 | tf_op jit(solution)/shard_map/ppermute | solution.py:31
  66.6 6.1 %collective-permute-start.19 = (bf16[64,512]{1,0:T(8,128)(2,1)S(1)}, bf16[64,512]{1,0:T(8,128)(2,1)S(1)}, u32[]{:S(2)}, u32[]{:S(2)}) collective-permute-start(bf16[64,512]{1,0:T(8,128)(2,1)S(1)} %get-tuple-element.84.rest_0_), channel_id=1, source_target_pairs={{0,12},{4,8},{8,4},{12,0},{1,13},{5,9},{9,5},{13,1},{2,14},{6,10},... | collective-permute-start | bytes 196616 | tf_op jit(solution)/shard_map/ppermute | solution.py:31
  68.6 6.2 %collective-permute-start.18 = (bf16[64,512]{1,0:T(8,128)(2,1)S(1)}, bf16[64,512]{1,0:T(8,128)(2,1)S(1)}, u32[]{:S(2)}, u32[]{:S(2)}) collective-permute-start(bf16[64,512]{1,0:T(8,128)(2,1)S(1)} %get-tuple-element.84.rest_0_), channel_id=1, source_target_pairs={{0,8},{4,12},{8,0},{12,4},{1,9},{5,13},{9,1},{13,5},{2,10},{6,14},... | collective-permute-start | bytes 196616 | tf_op jit(solution)/shard_map/ppermute | solution.py:31
  68.6 6.2 %collective-permute-start.17 = (bf16[64,512]{1,0:T(8,128)(2,1)S(1)}, bf16[64,512]{1,0:T(8,128)(2,1)S(1)}, u32[]{:S(2)}, u32[]{:S(2)}) collective-permute-start(bf16[64,512]{1,0:T(8,128)(2,1)S(1)} %get-tuple-element.84.rest_0_), channel_id=1, source_target_pairs={{0,4},{4,0},{8,12},{12,8},{1,5},{5,1},{9,13},{13,9},{2,6},{6,2},{1... | collective-permute-start | bytes 196616 | tf_op jit(solution)/shard_map/ppermute | solution.py:31
  77.0 4.0 %collective-permute-start.20 = (bf16[256,2048]{1,0:T(8,128)(2,1)S(1)}, bf16[256,2048]{1,0:T(8,128)(2,1)S(1)}, u32[]{:S(2)}, u32[]{:S(2)}) collective-permute-start(bf16[256,2048]{1,0:T(8,128)(2,1)S(1)} %get-tuple-element.85.half), channel_id=1, source_target_pairs={{0,1},{1,0},{2,3},{3,2},{4,5},{5,4},{6,7},{7,6},{8,9},{9,8},{10,11... | collective-permute-start | bytes 3145736 | tf_op jit(solution)/shard_map/ppermute | solution.py:31
  77.1 3.2 %collective-permute-start.23 = (f32[8,384]{1,0:T(8,128)S(1)}, f32[8,384]{1,0:T(8,128)S(1)}, u32[]{:S(2)}, u32[]{:S(2)}) collective-permute-start(f32[8,384]{1,0:T(8,128)S(1)} %get-tuple-element.86.row), channel_id=1, source_target_pairs={{0,17},{1,16},{2,19},{3,18},{16,1},{17,0},{18,3},{19,2},{4,21},{5,... | collective-permute-start | bytes 36872 | tf_op jit(solution)/shard_map/ppermute | solution.py:619
  77.2 3.9 %collective-permute-start.22 = (f32[8,384]{1,0:T(8,128)S(1)}, f32[8,384]{1,0:T(8,128)S(1)}, u32[]{:S(2)}, u32[]{:S(2)}) collective-permute-start(f32[8,384]{1,0:T(8,128)S(1)} %get-tuple-element.86.row), channel_id=1, source_target_pairs={{0,16},{16,0},{1,17},{17,1},{2,18},{18,2},{3,19},{19,3},{4,20},{20... | collective-permute-start | bytes 36872 | tf_op jit(solution)/shard_map/ppermute | solution.py:31
  79.2 1.8 %collective-permute-start.21 = (f32[8,384]{1,0:T(8,128)S(1)}, f32[8,384]{1,0:T(8,128)S(1)}, u32[]{:S(2)}, u32[]{:S(2)}) collective-permute-start(f32[8,384]{1,0:T(8,128)S(1)} %get-tuple-element.86.row), channel_id=1, source_target_pairs={{0,1},{1,0},{2,3},{3,2},{4,5},{5,4},{6,7},{7,6},{8,9},{9,8},{10,11... | collective-permute-start | bytes 36872 | tf_op jit(solution)/shard_map/ppermute | solution.py:31

commit v12 on v7

--- a/solution.py
+++ b/solution.py
@@ -372,7 +372,7 @@
     block_q[aligned((1 - y) * piece, piece), :] = other_q[...]
 
 
-def fifth_kernel(weight_qkv, gain, bias, block_p, other_p, *rest):
+def fifth_kernel(weight_qkv, own, bias, block_p, other_p, *rest):
     *parts_q, half, row = rest
     core, y, z = position()
     rows = half.shape[0]
@@ -387,6 +387,7 @@
     wide = half[:, :three].astype(F32)
     gain_half = jnp.sum(wide * weight_qkv[mine, :].astype(F32), axis=1, keepdims=True)
     gain_half = jnp.broadcast_to(gain_half, (rows, GROUP)).T[:8]
+    gain = own[own.shape[0] - 16 : own.shape[0] - 15, :]
     own_gain = jnp.where(core == 0, gain[:, :rows], gain[:, rows:])
     gain_half = gain_half / own_gain
     out = half[:, three:].astype(F32)
@@ -542,7 +543,7 @@
     back = from_behind(back, "lon", 1)
     entries = 2 * (4 * width * width + width + heads)
     if rows // 2 // lons % 16 == 0 and lons & (lons - 1) == 0:
-        grads = staged(keep, came, back, qkv_v, gains, lons, heads, entries)
+        grads = staged(keep, came, back, qkv_v, own, lons, heads, entries)
     else:
         grads = plain(keep, came, weight_qkv, gains, heads, entries)
     (final_grad,) = call(
@@ -556,7 +557,7 @@
     return (final_grad, *(grad[None] for grad in grads))
 
 
-def staged(keep, came, after, weight_qkv, gains, lons, heads, entries):
+def staged(keep, came, after, weight_qkv, own, lons, heads, entries):
     rows, wide = keep.shape
     width = 2 * rows
     wide_p = CUT + GROUP
@@ -612,7 +613,7 @@
     half, row = call(
         fifth_kernel,
         [shape((rows, 4 * width), BF16), shape((8, rows + GROUP), F32)],
-        operands=(weight_qkv, gains, bias, block_p, other_p, block_q, *others_q),
+        operands=(weight_qkv, own, bias, block_p, other_p, block_q, *others_q),
     )
     row_section = swapped(row, "section", 1)
     row_both = lax.ppermute(row, ("section", "lat"), across())

time: 81.5 us -> 81.5 us (level)
    unnamed x8 -> x6, local copies, waits for them, and re-layouts: 3.43 us -> 3.42 us
where the time goes in v12:
time: 81.5 us; the launch traced here: 81.2 us
  starting transfers between devices  30.9 us (38%)
  waiting for transfers between devices  30.8 us (38%)
  Pallas kernels  15.3 us (19%)
  local copies, waits for them, and re-layouts  3.42 us (4%)
    ppermute x20, starting transfers between devices, swapped(): return lax.ppermute(value, axis, [(i, i ^ bit) for i in range(count)])  23.1 us
    ppermute x20, waiting for transfers between devices, swapped(): return lax.ppermute(value, axis, [(i, i ^ bit) for i in range(count)])  19 us
    pallas_call x12, Pallas kernels, call(): pl.pallas_call(kernel, out_shape=list(outs), in_specs=[pl.BlockSpec(memor...  15.3 us
    ppermute x2, starting transfers between devices, from_behind(): lax.ppermute(value, axis, [(i, (i + by) % count) for i in range(count)])  6.45 us
    ppermute x1, waiting for transfers between devices, passed_along(): return lax.ppermute(block, axis, route)  5.93 us
    ppermute x2, waiting for transfers between devices, from_behind(): lax.ppermute(value, axis, [(i, (i + by) % count) for i in range(count)])  5.62 us
    unnamed x6, local copies, waits for them, and re-layouts  3.42 us
  transfers between devices with their start and end apart: 24, of which 13 were waited for; matrix products, arithmetic and copies ran while one was open for 0% of the time, Pallas kernels for 3%

profile of v12, /device:TPU:0, one launch (start us, length us, event | category | flops | bytes accessed | tf_op | source)
XLA Modules:
  0.0 81.2 jit_solution(1383605755554435685)
XLA Ops:
  0.6 1.9 %shard_map.110 = (f32[160,512]{1,0:T(8,128)}, bf16[160,512]{1,0:T(8,128)(2,1)}) custom-call(bf16[1,6,12,2,512]{4,3,2,1,0:T(2,128)(2,1)} %bitcast.12, bf16[1,6,12,2,512]{4,3,2,1,0:T(2,128)(2,1)} %bitcast.13, s32[6,12]{1,0:T(8,128)} %land.1, f32[1,512]{1,0:T(1,128)} %gain.1, f32[1,16]{1,0:T(1,128)} %bias.1), custom_call_target="tpu_custom_call" | custom-call | flops 100000000 | bytes 788832 | tf_op jit(solution)/shard_map/pallas_call | solution.py:47
  2.5 5.1 %collective-permute-start = (bf16[160,512]{1,0:T(8,128)(2,1)}, bf16[160,512]{1,0:T(8,128)(2,1)S(1)}, u32[]{:S(2)}, u32[]{:S(2)}) collective-permute-start(bf16[160,512]{1,0:T(8,128)(2,1)} %get-tuple-element.49), channel_id=1, source_target_pairs={{0,12},{4,0},{8,4},{12,8},{1,13},{5,1},{9,5},{13,9},{2,14},{6,2},{... | collective-permute-start | bytes 491528 | tf_op jit(solution)/shard_map/ppermute | solution.py:20
  7.6 0.0 copy-start
  7.6 1.0 %copy-done = f32[160,512]{1,0:T(8,128)S(1)} copy-done((f32[160,512]{1,0:T(8,128)S(1)}, f32[160,512]{1,0:T(8,128)}, u32[]{:S(2)}) %copy-start) | copy-done | bytes 327704
  8.6 0.0 copy-start.1
  8.6 1.4 %copy-done.1 = bf16[1,512,1536]{2,1,0:T(8,128)(2,1)S(1)} copy-done((bf16[1,512,1536]{2,1,0:T(8,128)(2,1)S(1)}, bf16[1,512,1536]{2,1,0:T(8,128)(2,1)}, u32[]{:S(2)}) %copy-start.1) | copy-done | bytes 1572888
  10.0 1.0 %copy-done.2 = bf16[1,512,512]{2,1,0:T(8,128)(2,1)S(1)} copy-done((bf16[1,512,512]{2,1,0:T(8,128)(2,1)S(1)}, bf16[1,512,512]{2,1,0:T(8,128)(2,1)}, u32[]{:S(2)}) %copy-start.2) | copy-done | bytes 524312
  11.1 0.6 shard_map.111
  11.7 0.0 collective-permute-done.rim
  11.7 4.7 %shard_map.112 = (bf16[144,512]{1,0:T(8,128)(2,1)S(1)}, bf16[144,512]{1,0:T(8,128)(2,1)S(1)}, bf16[512,144]{1,0:T(8,128)(2,1)S(1)}, bf16[144,1536]{1,0:T(8,128)(...) custom-call(f32[160,512]{1,0:T(8,128)S(1)} %copy-done, ...), custom_call_target="tpu_custom_call" | custom-call | flops 1000000000 | bytes 6299648 | tf_op jit(solution)/shard_map/pallas_call | solution.py:47
  16.5 1.3 %collective-permute-start.1 = (bf16[144,512]{1,0:T(8,128)(2,1)S(1)}, bf16[144,512]{1,0:T(8,128)(2,1)S(1)}, u32[]{:S(2)}, u32[]{:S(2)}) collective-permute-start(bf16[144,512]{1,0:T(8,128)(2,1)S(1)} %get-tuple-element.53), channel_id=1, source_target_pairs={{16,0},{17,1},{18,2},{19,3},{20,4},{21,5},{22,6},{23,7},{24,8},{25... | collective-permute-start | bytes 442376 | tf_op jit(solution)/shard_map/ppermute | solution.py:26
  17.8 5.9 %collective-permute-done.1.skip = bf16[144,512]{1,0:T(8,128)(2,1)S(1)} collective-permute-done((bf16[144,512]{1,0:T(8,128)(2,1)S(1)}, bf16[144,512]{1,0:T(8,128)(2,1)S(1)}, u32[]{:S(2)}, u32[]{:S(2)}) %collective-permute-start.1) | collective-permute-done | bytes 147488 | tf_op jit(solution)/shard_map/ppermute | solution.py:26
  23.7 3.0 %shard_map.113 = (bf16[144,512]{1,0:T(8,128)(2,1)S(1)}, bf16[144,1536]{1,0:T(8,128)(2,1)S(1)}, f32[8,128]{1,0:T(8,128)S(1)}, bf16[256,2176]{1,0:T(8,128)(2,1)S(1)}) custom-call(bf16[144,512]{1,0:T(8,128)(2,1)S(1)} %collective-permute-done.1.skip, bf16[144,512]{1,0:T(8,128)(2,1)S(1)} %get-tuple-element.54.cot, bf16[144,1536]{1,0:T(8,128)(2,1)S(1)} %get-tuple-element.55.qkv, ...), custom_call_target="tpu_custom_call" | custom-call | flops 1000000000 | bytes 4075520 | tf_op jit(solution)/shard_map/pallas_call | solution.py:47
  26.7 0.1 collective-permute-start.3
  26.8 0.8 shard_map.114
  27.6 1.9 %collective-permute-done.3.came = bf16[256,2176]{1,0:T(8,128)(2,1)S(1)} collective-permute-done((bf16[256,2176]{1,0:T(8,128)(2,1)S(1)}, bf16[256,2176]{1,0:T(8,128)(2,1)S(1)}, u32[]{:S(2)}, u32[]{:S(2)}) %collective-permute-start.3) | collective-permute-done | bytes 1114144 | tf_op jit(solution)/shard_map/ppermute | solution.py:31
  29.5 0.4 shard_map.116
  29.9 1.6 %collective-permute-start.4 = (bf16[128,1536]{1,0:T(8,128)(2,1)S(1)}, bf16[128,1536]{1,0:T(8,128)(2,1)S(1)}, u32[]{:S(2)}, u32[]{:S(2)}) collective-permute-start(bf16[128,1536]{1,0:T(8,128)(2,1)S(1)} %get-tuple-element.69), channel_id=1, source_target_pairs={{0,2},{1,3},{2,0},{3,1},{4,6},{5,7},{6,4},{7,5},{8,10},{9,11},{10,... | collective-permute-start | bytes 1179656 | tf_op jit(solution)/shard_map/ppermute | solution.py:31
  31.5 3.7 %collective-permute-start.5 = (bf16[64,640]{1,0:T(8,128)(2,1)S(1)}, bf16[64,640]{1,0:T(8,128)(2,1)S(1)}, u32[]{:S(2)}, u32[]{:S(2)}) collective-permute-start(bf16[64,640]{1,0:T(8,128)(2,1)S(1)} %get-tuple-element.71), channel_id=1, source_target_pairs={{0,12},{4,8},{8,4},{12,0},{1,13},{5,9},{9,5},{13,1},{2,14},{6,10},... | collective-permute-start | bytes 245768 | tf_op jit(solution)/shard_map/ppermute | solution.py:31
  35.2 0.0 collective-permute-start.6
  35.2 0.7 collective-permute-start.7
  35.9 1.3 %collective-permute-start.2 = (bf16[72,512]{1,0:T(8,128)(2,1)S(1)}, bf16[72,512]{1,0:T(8,128)(2,1)S(1)}, u32[]{:S(2)}, u32[]{:S(2)}) collective-permute-start(bf16[72,512]{1,0:T(8,128)(2,1)S(1)} %get-tuple-element.65), channel_id=1, source_target_pairs={{0,4},{4,8},{8,12},{12,0},{1,5},{5,9},{9,13},{13,1},{2,6},{6,10},{... | collective-permute-start | bytes 221192 | tf_op jit(solution)/shard_map/ppermute | solution.py:20
  37.2 5.6 %collective-permute-done.2.back.after = bf16[72,512]{1,0:T(8,128)(2,1)S(1)} collective-permute-done((bf16[72,512]{1,0:T(8,128)(2,1)S(1)}, bf16[72,512]{1,0:T(8,128)(2,1)S(1)}, u32[]{:S(2)}, u32[]{:S(2)}) %collective-permute-start.2) | collective-permute-done | bytes 73760 | tf_op jit(solution)/shard_map/ppermute | solution.py:20
  42.9 0.0 collective-permute-done.5.rest_0_
  42.9 0.0 collective-permute-done.6.rest_1_
  42.9 0.2 collective-permute-done.7.rest_2_
  43.1 0.0 collective-permute-done.4.came_p
  43.1 0.2 shard_map.117
  43.3 2.4 %collective-permute-start.9 = (bf16[32,1536]{1,0:T(8,128)(2,1)S(1)}, bf16[32,1536]{1,0:T(8,128)(2,1)S(1)}, u32[]{:S(2)}, u32[]{:S(2)}) collective-permute-start(bf16[32,1536]{1,0:T(8,128)(2,1)S(1)} %get-tuple-element.77), channel_id=1, source_target_pairs={{0,12},{4,8},{8,4},{12,0},{1,13},{5,9},{9,5},{13,1},{2,14},{6,10},... | collective-permute-start | bytes 294920 | tf_op jit(solution)/shard_map/ppermute | solution.py:31
  45.7 0.6 collective-permute-start.10
  46.3 1.4 %collective-permute-start.11 = (bf16[32,1536]{1,0:T(8,128)(2,1)S(1)}, bf16[32,1536]{1,0:T(8,128)(2,1)S(1)}, u32[]{:S(2)}, u32[]{:S(2)}) collective-permute-start(bf16[32,1536]{1,0:T(8,128)(2,1)S(1)} %get-tuple-element.79), channel_id=1, source_target_pairs={{0,4},{4,0},{8,12},{12,8},{1,5},{5,1},{9,13},{13,9},{2,6},{6,2},{1... | collective-permute-start | bytes 294920 | tf_op jit(solution)/shard_map/ppermute | solution.py:31
  47.7 0.5 collective-permute-start.8
  48.2 3.5 %collective-permute-done.8.came_q = bf16[32,640]{1,0:T(8,128)(2,1)S(1)} collective-permute-done((bf16[32,640]{1,0:T(8,128)(2,1)S(1)}, bf16[32,640]{1,0:T(8,128)(2,1)S(1)}, u32[]{:S(2)}, u32[]{:S(2)}) %collective-permute-start.8) | collective-permute-done | bytes 40992 | tf_op jit(solution)/shard_map/ppermute | solution.py:31
  51.7 0.0 collective-permute-done.9.rest_0_
  51.7 2.5 %collective-permute-done.10.rest_1_ = bf16[32,1536]{1,0:T(8,128)(2,1)S(1)} collective-permute-done((bf16[32,1536]{1,0:T(8,128)(2,1)S(1)}, bf16[32,1536]{1,0:T(8,128)(2,1)S(1)}, u32[]{:S(2)}, u32[]{:S(2)}) %collective-permute-start.10) | collective-permute-done | bytes 98336 | tf_op jit(solution)/shard_map/ppermute | solution.py:31
  54.3 0.0 collective-permute-done.11.rest_2_
  54.3 0.1 shard_map.118
  54.3 2.3 %collective-permute-start.15 = (bf16[32,1408]{1,0:T(8,128)(2,1)S(1)}, bf16[32,1408]{1,0:T(8,128)(2,1)S(1)}, u32[]{:S(2)}, u32[]{:S(2)}) collective-permute-start(bf16[32,1408]{1,0:T(8,128)(2,1)S(1)} %get-tuple-element.82.rest_0_), channel_id=1, source_target_pairs={{0,12},{4,8},{8,4},{12,0},{1,13},{5,9},{9,5},{13,1},{2,14},{6,10},... | collective-permute-start | bytes 270344 | tf_op jit(solution)/shard_map/ppermute | solution.py:31
  56.7 0.0 collective-permute-start.14
  56.7 2.1 %collective-permute-start.13 = (bf16[32,1408]{1,0:T(8,128)(2,1)S(1)}, bf16[32,1408]{1,0:T(8,128)(2,1)S(1)}, u32[]{:S(2)}, u32[]{:S(2)}) collective-permute-start(bf16[32,1408]{1,0:T(8,128)(2,1)S(1)} %get-tuple-element.82.rest_0_), channel_id=1, source_target_pairs={{0,4},{4,0},{8,12},{12,8},{1,5},{5,1},{9,13},{13,9},{2,6},{6,2},{1... | collective-permute-start | bytes 270344 | tf_op jit(solution)/shard_map/ppermute | solution.py:31
  58.8 0.5 collective-permute-start.12
  59.3 3.5 %collective-permute-done.12.other_q = bf16[32,640]{1,0:T(8,128)(2,1)S(1)} collective-permute-done((bf16[32,640]{1,0:T(8,128)(2,1)S(1)}, bf16[32,640]{1,0:T(8,128)(2,1)S(1)}, u32[]{:S(2)}, u32[]{:S(2)}) %collective-permute-start.12) | collective-permute-done | bytes 40992 | tf_op jit(solution)/shard_map/ppermute | solution.py:31
  62.8 0.0 collective-permute-done.15.rest_3_
  62.8 1.3 %collective-permute-done.14.rest_2_ = bf16[32,1408]{1,0:T(8,128)(2,1)S(1)} collective-permute-done((bf16[32,1408]{1,0:T(8,128)(2,1)S(1)}, bf16[32,1408]{1,0:T(8,128)(2,1)S(1)}, u32[]{:S(2)}, u32[]{:S(2)}) %collective-permute-start.14) | collective-permute-done | bytes 90144 | tf_op jit(solution)/shard_map/ppermute | solution.py:31
  64.1 0.0 collective-permute-done.13.rest_1_
  64.2 0.7 collective-permute-start.16
  64.9 1.6 %collective-permute-start.19 = (bf16[64,640]{1,0:T(8,128)(2,1)S(1)}, bf16[64,640]{1,0:T(8,128)(2,1)S(1)}, u32[]{:S(2)}, u32[]{:S(2)}) collective-permute-start(bf16[64,640]{1,0:T(8,128)(2,1)S(1)} %get-tuple-element.84.rest_0_), channel_id=1, source_target_pairs={{0,12},{4,8},{8,4},{12,0},{1,13},{5,9},{9,5},{13,1},{2,14},{6,10},... | collective-permute-start | bytes 245768 | tf_op jit(solution)/shard_map/ppermute | solution.py:31
  66.5 0.0 collective-permute-start.18
  66.5 2.7 %collective-permute-start.17 = (bf16[64,640]{1,0:T(8,128)(2,1)S(1)}, bf16[64,640]{1,0:T(8,128)(2,1)S(1)}, u32[]{:S(2)}, u32[]{:S(2)}) collective-permute-start(bf16[64,640]{1,0:T(8,128)(2,1)S(1)} %get-tuple-element.84.rest_0_), channel_id=1, source_target_pairs={{0,4},{4,0},{8,12},{12,8},{1,5},{5,1},{9,13},{13,9},{2,6},{6,2},{1... | collective-permute-start | bytes 245768 | tf_op jit(solution)/shard_map/ppermute | solution.py:31
  69.3 2.8 %collective-permute-done.19.rest_3_ = bf16[64,640]{1,0:T(8,128)(2,1)S(1)} collective-permute-done((bf16[64,640]{1,0:T(8,128)(2,1)S(1)}, bf16[64,640]{1,0:T(8,128)(2,1)S(1)}, u32[]{:S(2)}, u32[]{:S(2)}) %collective-permute-start.19) | collective-permute-done | bytes 81952 | tf_op jit(solution)/shard_map/ppermute | solution.py:31
  72.1 2.0 %collective-permute-done.18.rest_2_ = bf16[64,640]{1,0:T(8,128)(2,1)S(1)} collective-permute-done((bf16[64,640]{1,0:T(8,128)(2,1)S(1)}, bf16[64,640]{1,0:T(8,128)(2,1)S(1)}, u32[]{:S(2)}, u32[]{:S(2)}) %collective-permute-start.18) | collective-permute-done | bytes 81952 | tf_op jit(solution)/shard_map/ppermute | solution.py:31
  74.1 0.0 collective-permute-done.17.rest_1_
  74.1 0.4 collective-permute-done.16.other_p
  74.5 0.5 shard_map.120
  75.0 0.0 collective-permute-start.20
  75.0 0.1 collective-permute-start.23
  75.1 2.1 %collective-permute-start.22 = (f32[8,384]{1,0:T(8,128)S(1)}, f32[8,384]{1,0:T(8,128)S(1)}, u32[]{:S(2)}, u32[]{:S(2)}) collective-permute-start(f32[8,384]{1,0:T(8,128)S(1)} %get-tuple-element.86.row), channel_id=1, source_target_pairs={{0,16},{16,0},{1,17},{17,1},{2,18},{18,2},{3,19},{19,3},{4,20},{20... | collective-permute-start | bytes 36872 | tf_op jit(solution)/shard_map/ppermute | solution.py:31
  77.2 0.0 collective-permute-start.21
  77.2 0.8 shard_map.115
  77.9 0.3 collective-permute-done.23.row_both
  78.2 0.8 collective-permute-done.22.row_section
  79.0 0.0 collective-permute-done.21.row_core
  79.0 0.0 collective-permute-done.20.other
  79.0 2.3 %shard_map.121 = (f32[512,1536]{1,0:T(8,128)}, f32[512,512]{1,0:T(8,128)}, f32[1,512]{1,0:T(1,128)}, f32[1,16]{1,0:T(1,128)}) custom-call(bf16[256,2048]{1,0:T(8,128)(2,1)S(1)} %get-tuple-element.85.half, bf16[256,2048]{1,0:T(8,128)(2,1)S(1)} %collective-permute-done.20.other, f32[8,384]{1,0:T(8,128)S(1)} %get-tuple-element.86.row, ...), custom_call_target="tpu_custom_call" | custom-call | flops 100000000 | bytes 6346816 | tf_op jit(solution)/shard_map/pallas_call | solution.py:47
  (2 shorter events, 0.0 us)
Async XLA Ops:
  2.5 9.2 %collective-permute-start = (bf16[160,512]{1,0:T(8,128)(2,1)}, bf16[160,512]{1,0:T(8,128)(2,1)S(1)}, u32[]{:S(2)}, u32[]{:S(2)}) collective-permute-start(bf16[160,512]{1,0:T(8,128)(2,1)} %get-tuple-element.49), channel_id=1, source_target_pairs={{0,12},{4,0},{8,4},{12,8},{1,13},{5,1},{9,5},{13,9},{2,14},{6,2},{... | collective-permute-start | bytes 491528 | tf_op jit(solution)/shard_map/ppermute | solution.py:20
  7.6 1.0 %copy-start = (f32[160,512]{1,0:T(8,128)S(1)}, f32[160,512]{1,0:T(8,128)}, u32[]{:S(2)}) copy-start(f32[160,512]{1,0:T(8,128)} %get-tuple-element.48.after.own.params) | copy-start | bytes 983044
  8.6 1.4 %copy-start.1 = (bf16[1,512,1536]{2,1,0:T(8,128)(2,1)S(1)}, bf16[1,512,1536]{2,1,0:T(8,128)(2,1)}, u32[]{:S(2)}) copy-start(bf16[1,512,1536]{2,1,0:T(8,128)(2,1)} %param.11) | copy-start | bytes 4718596
  10.0 1.0 %copy-start.2 = (bf16[1,512,512]{2,1,0:T(8,128)(2,1)S(1)}, bf16[1,512,512]{2,1,0:T(8,128)(2,1)}, u32[]{:S(2)}) copy-start(bf16[1,512,512]{2,1,0:T(8,128)(2,1)} %param.12) | copy-start | bytes 1572868
  16.5 7.2 %collective-permute-start.1 = (bf16[144,512]{1,0:T(8,128)(2,1)S(1)}, bf16[144,512]{1,0:T(8,128)(2,1)S(1)}, u32[]{:S(2)}, u32[]{:S(2)}) collective-permute-start(bf16[144,512]{1,0:T(8,128)(2,1)S(1)} %get-tuple-element.53), channel_id=1, source_target_pairs={{16,0},{17,1},{18,2},{19,3},{20,4},{21,5},{22,6},{23,7},{24,8},{25... | collective-permute-start | bytes 442376 | tf_op jit(solution)/shard_map/ppermute | solution.py:26
  26.7 2.8 %collective-permute-start.3 = (bf16[256,2176]{1,0:T(8,128)(2,1)S(1)}, bf16[256,2176]{1,0:T(8,128)(2,1)S(1)}, u32[]{:S(2)}, u32[]{:S(2)}) collective-permute-start(bf16[256,2176]{1,0:T(8,128)(2,1)S(1)} %get-tuple-element.67), channel_id=1, source_target_pairs={{0,1},{1,0},{2,3},{3,2},{4,5},{5,4},{6,7},{7,6},{8,9},{9,8},{10,11... | collective-permute-start | bytes 3342344 | tf_op jit(solution)/shard_map/ppermute | solution.py:31
  29.9 13.2 %collective-permute-start.4 = (bf16[128,1536]{1,0:T(8,128)(2,1)S(1)}, bf16[128,1536]{1,0:T(8,128)(2,1)S(1)}, u32[]{:S(2)}, u32[]{:S(2)}) collective-permute-start(bf16[128,1536]{1,0:T(8,128)(2,1)S(1)} %get-tuple-element.69), channel_id=1, source_target_pairs={{0,2},{1,3},{2,0},{3,1},{4,6},{5,7},{6,4},{7,5},{8,10},{9,11},{10,... | collective-permute-start | bytes 1179656 | tf_op jit(solution)/shard_map/ppermute | solution.py:31
  31.5 11.4 %collective-permute-start.5 = (bf16[64,640]{1,0:T(8,128)(2,1)S(1)}, bf16[64,640]{1,0:T(8,128)(2,1)S(1)}, u32[]{:S(2)}, u32[]{:S(2)}) collective-permute-start(bf16[64,640]{1,0:T(8,128)(2,1)S(1)} %get-tuple-element.71), channel_id=1, source_target_pairs={{0,12},{4,8},{8,4},{12,0},{1,13},{5,9},{9,5},{13,1},{2,14},{6,10},... | collective-permute-start | bytes 245768 | tf_op jit(solution)/shard_map/ppermute | solution.py:31
  35.2 7.7 %collective-permute-start.6 = (bf16[64,640]{1,0:T(8,128)(2,1)S(1)}, bf16[64,640]{1,0:T(8,128)(2,1)S(1)}, u32[]{:S(2)}, u32[]{:S(2)}) collective-permute-start(bf16[64,640]{1,0:T(8,128)(2,1)S(1)} %get-tuple-element.72), channel_id=1, source_target_pairs={{0,8},{4,12},{8,0},{12,4},{1,9},{5,13},{9,1},{13,5},{2,10},{6,14},... | collective-permute-start | bytes 245768 | tf_op jit(solution)/shard_map/ppermute | solution.py:31
  35.2 7.9 %collective-permute-start.7 = (bf16[64,640]{1,0:T(8,128)(2,1)S(1)}, bf16[64,640]{1,0:T(8,128)(2,1)S(1)}, u32[]{:S(2)}, u32[]{:S(2)}) collective-permute-start(bf16[64,640]{1,0:T(8,128)(2,1)S(1)} %get-tuple-element.73), channel_id=1, source_target_pairs={{0,4},{4,0},{8,12},{12,8},{1,5},{5,1},{9,13},{13,9},{2,6},{6,2},{1... | collective-permute-start | bytes 245768 | tf_op jit(solution)/shard_map/ppermute | solution.py:31
  35.9 7.0 %collective-permute-start.2 = (bf16[72,512]{1,0:T(8,128)(2,1)S(1)}, bf16[72,512]{1,0:T(8,128)(2,1)S(1)}, u32[]{:S(2)}, u32[]{:S(2)}) collective-permute-start(bf16[72,512]{1,0:T(8,128)(2,1)S(1)} %get-tuple-element.65), channel_id=1, source_target_pairs={{0,4},{4,8},{8,12},{12,0},{1,5},{5,9},{9,13},{13,1},{2,6},{6,10},{... | collective-permute-start | bytes 221192 | tf_op jit(solution)/shard_map/ppermute | solution.py:20
  43.3 8.5 %collective-permute-start.9 = (bf16[32,1536]{1,0:T(8,128)(2,1)S(1)}, bf16[32,1536]{1,0:T(8,128)(2,1)S(1)}, u32[]{:S(2)}, u32[]{:S(2)}) collective-permute-start(bf16[32,1536]{1,0:T(8,128)(2,1)S(1)} %get-tuple-element.77), channel_id=1, source_target_pairs={{0,12},{4,8},{8,4},{12,0},{1,13},{5,9},{9,5},{13,1},{2,14},{6,10},... | collective-permute-start | bytes 294920 | tf_op jit(solution)/shard_map/ppermute | solution.py:31
  45.7 8.6 %collective-permute-start.10 = (bf16[32,1536]{1,0:T(8,128)(2,1)S(1)}, bf16[32,1536]{1,0:T(8,128)(2,1)S(1)}, u32[]{:S(2)}, u32[]{:S(2)}) collective-permute-start(bf16[32,1536]{1,0:T(8,128)(2,1)S(1)} %get-tuple-element.78), channel_id=1, source_target_pairs={{0,8},{4,12},{8,0},{12,4},{1,9},{5,13},{9,1},{13,5},{2,10},{6,14},... | collective-permute-start | bytes 294920 | tf_op jit(solution)/shard_map/ppermute | solution.py:31
  46.3 8.0 %collective-permute-start.11 = (bf16[32,1536]{1,0:T(8,128)(2,1)S(1)}, bf16[32,1536]{1,0:T(8,128)(2,1)S(1)}, u32[]{:S(2)}, u32[]{:S(2)}) collective-permute-start(bf16[32,1536]{1,0:T(8,128)(2,1)S(1)} %get-tuple-element.79), channel_id=1, source_target_pairs={{0,4},{4,0},{8,12},{12,8},{1,5},{5,1},{9,13},{13,9},{2,6},{6,2},{1... | collective-permute-start | bytes 294920 | tf_op jit(solution)/shard_map/ppermute | solution.py:31
  47.7 4.0 %collective-permute-start.8 = (bf16[32,640]{1,0:T(8,128)(2,1)S(1)}, bf16[32,640]{1,0:T(8,128)(2,1)S(1)}, u32[]{:S(2)}, u32[]{:S(2)}) collective-permute-start(bf16[32,640]{1,0:T(8,128)(2,1)S(1)} %get-tuple-element.76), channel_id=1, source_target_pairs={{0,2},{1,3},{2,0},{3,1},{4,6},{5,7},{6,4},{7,5},{8,10},{9,11},{10,... | collective-permute-start | bytes 122888 | tf_op jit(solution)/shard_map/ppermute | solution.py:31
  54.3 8.5 %collective-permute-start.15 = (bf16[32,1408]{1,0:T(8,128)(2,1)S(1)}, bf16[32,1408]{1,0:T(8,128)(2,1)S(1)}, u32[]{:S(2)}, u32[]{:S(2)}) collective-permute-start(bf16[32,1408]{1,0:T(8,128)(2,1)S(1)} %get-tuple-element.82.rest_0_), channel_id=1, source_target_pairs={{0,12},{4,8},{8,4},{12,0},{1,13},{5,9},{9,5},{13,1},{2,14},{6,10},... | collective-permute-start | bytes 270344 | tf_op jit(solution)/shard_map/ppermute | solution.py:31
  56.7 7.5 %collective-permute-start.14 = (bf16[32,1408]{1,0:T(8,128)(2,1)S(1)}, bf16[32,1408]{1,0:T(8,128)(2,1)S(1)}, u32[]{:S(2)}, u32[]{:S(2)}) collective-permute-start(bf16[32,1408]{1,0:T(8,128)(2,1)S(1)} %get-tuple-element.82.rest_0_), channel_id=1, source_target_pairs={{0,8},{4,12},{8,0},{12,4},{1,9},{5,13},{9,1},{13,5},{2,10},{6,14},... | collective-permute-start | bytes 270344 | tf_op jit(solution)/shard_map/ppermute | solution.py:31
  56.7 7.5 %collective-permute-start.13 = (bf16[32,1408]{1,0:T(8,128)(2,1)S(1)}, bf16[32,1408]{1,0:T(8,128)(2,1)S(1)}, u32[]{:S(2)}, u32[]{:S(2)}) collective-permute-start(bf16[32,1408]{1,0:T(8,128)(2,1)S(1)} %get-tuple-element.82.rest_0_), channel_id=1, source_target_pairs={{0,4},{4,0},{8,12},{12,8},{1,5},{5,1},{9,13},{13,9},{2,6},{6,2},{1... | collective-permute-start | bytes 270344 | tf_op jit(solution)/shard_map/ppermute | solution.py:31
  58.8 4.0 %collective-permute-start.12 = (bf16[32,640]{1,0:T(8,128)(2,1)S(1)}, bf16[32,640]{1,0:T(8,128)(2,1)S(1)}, u32[]{:S(2)}, u32[]{:S(2)}) collective-permute-start(bf16[32,640]{1,0:T(8,128)(2,1)S(1)} %get-tuple-element.81.piece_q), channel_id=1, source_target_pairs={{0,2},{1,3},{2,0},{3,1},{4,6},{5,7},{6,4},{7,5},{8,10},{9,11},{10,... | collective-permute-start | bytes 122888 | tf_op jit(solution)/shard_map/ppermute | solution.py:31
  64.2 10.3 %collective-permute-start.16 = (bf16[128,1408]{1,0:T(8,128)(2,1)S(1)}, bf16[128,1408]{1,0:T(8,128)(2,1)S(1)}, u32[]{:S(2)}, u32[]{:S(2)}) collective-permute-start(bf16[128,1408]{1,0:T(8,128)(2,1)S(1)} %get-tuple-element.83.block_p), channel_id=1, source_target_pairs={{0,2},{1,3},{2,0},{3,1},{4,6},{5,7},{6,4},{7,5},{8,10},{9,11},{10,... | collective-permute-start | bytes 1081352 | tf_op jit(solution)/shard_map/ppermute | solution.py:31
  64.9 7.2 %collective-permute-start.19 = (bf16[64,640]{1,0:T(8,128)(2,1)S(1)}, bf16[64,640]{1,0:T(8,128)(2,1)S(1)}, u32[]{:S(2)}, u32[]{:S(2)}) collective-permute-start(bf16[64,640]{1,0:T(8,128)(2,1)S(1)} %get-tuple-element.84.rest_0_), channel_id=1, source_target_pairs={{0,12},{4,8},{8,4},{12,0},{1,13},{5,9},{9,5},{13,1},{2,14},{6,10},... | collective-permute-start | bytes 245768 | tf_op jit(solution)/shard_map/ppermute | solution.py:31
  66.5 7.6 %collective-permute-start.18 = (bf16[64,640]{1,0:T(8,128)(2,1)S(1)}, bf16[64,640]{1,0:T(8,128)(2,1)S(1)}, u32[]{:S(2)}, u32[]{:S(2)}) collective-permute-start(bf16[64,640]{1,0:T(8,128)(2,1)S(1)} %get-tuple-element.84.rest_0_), channel_id=1, source_target_pairs={{0,8},{4,12},{8,0},{12,4},{1,9},{5,13},{9,1},{13,5},{2,10},{6,14},... | collective-permute-start | bytes 245768 | tf_op jit(solution)/shard_map/ppermute | solution.py:31
  66.5 7.6 %collective-permute-start.17 = (bf16[64,640]{1,0:T(8,128)(2,1)S(1)}, bf16[64,640]{1,0:T(8,128)(2,1)S(1)}, u32[]{:S(2)}, u32[]{:S(2)}) collective-permute-start(bf16[64,640]{1,0:T(8,128)(2,1)S(1)} %get-tuple-element.84.rest_0_), channel_id=1, source_target_pairs={{0,4},{4,0},{8,12},{12,8},{1,5},{5,1},{9,13},{13,9},{2,6},{6,2},{1... | collective-permute-start | bytes 245768 | tf_op jit(solution)/shard_map/ppermute | solution.py:31
  75.0 4.0 %collective-permute-start.20 = (bf16[256,2048]{1,0:T(8,128)(2,1)S(1)}, bf16[256,2048]{1,0:T(8,128)(2,1)S(1)}, u32[]{:S(2)}, u32[]{:S(2)}) collective-permute-start(bf16[256,2048]{1,0:T(8,128)(2,1)S(1)} %get-tuple-element.85.half), channel_id=1, source_target_pairs={{0,1},{1,0},{2,3},{3,2},{4,5},{5,4},{6,7},{7,6},{8,9},{9,8},{10,11... | collective-permute-start | bytes 3145736 | tf_op jit(solution)/shard_map/ppermute | solution.py:31
  75.0 3.2 %collective-permute-start.23 = (f32[8,384]{1,0:T(8,128)S(1)}, f32[8,384]{1,0:T(8,128)S(1)}, u32[]{:S(2)}, u32[]{:S(2)}) collective-permute-start(f32[8,384]{1,0:T(8,128)S(1)} %get-tuple-element.86.row), channel_id=1, source_target_pairs={{0,17},{1,16},{2,19},{3,18},{16,1},{17,0},{18,3},{19,2},{4,21},{5,... | collective-permute-start | bytes 36872 | tf_op jit(solution)/shard_map/ppermute | solution.py:619
  75.1 3.9 %collective-permute-start.22 = (f32[8,384]{1,0:T(8,128)S(1)}, f32[8,384]{1,0:T(8,128)S(1)}, u32[]{:S(2)}, u32[]{:S(2)}) collective-permute-start(f32[8,384]{1,0:T(8,128)S(1)} %get-tuple-element.86.row), channel_id=1, source_target_pairs={{0,16},{16,0},{1,17},{17,1},{2,18},{18,2},{3,19},{19,3},{4,20},{20... | collective-permute-start | bytes 36872 | tf_op jit(solution)/shard_map/ppermute | solution.py:31
  77.2 1.8 %collective-permute-start.21 = (f32[8,384]{1,0:T(8,128)S(1)}, f32[8,384]{1,0:T(8,128)S(1)}, u32[]{:S(2)}, u32[]{:S(2)}) collective-permute-start(f32[8,384]{1,0:T(8,128)S(1)} %get-tuple-element.86.row), channel_id=1, source_target_pairs={{0,1},{1,0},{2,3},{3,2},{4,5},{5,4},{6,7},{7,6},{8,9},{9,8},{10,11... | collective-permute-start | bytes 36872 | tf_op jit(solution)/shard_map/ppermute | solution.py:31

commit v13 on v9

--- a/solution.py
+++ b/solution.py
@@ -9,7 +9,7 @@
 
 SHIFT = 6
 GROUP = 128
-CUT = 1280
+CUT = 1408
 EPSILON = 1e-05
 F32 = jnp.float32
 BF16 = jnp.bfloat16
@@ -387,7 +387,7 @@
     block_q[aligned((1 - y) * piece, piece), :] = other_q[...]
 
 
-def fifth_kernel(weight_qkv, gain, bias, block_p, other_p, *rest):
+def fifth_kernel(weight_qkv, own, bias, block_p, other_p, *rest):
     *parts_q, half, row = rest
     core, y, z = position()
     rows = half.shape[0]
@@ -402,6 +402,7 @@
     wide = half[:, :three].astype(F32)
     gain_half = jnp.sum(wide * weight_qkv[mine, :].astype(F32), axis=1, keepdims=True)
     gain_half = jnp.broadcast_to(gain_half, (rows, GROUP)).T[:8]
+    gain = own[own.shape[0] - 16 : own.shape[0] - 15, :]
     own_gain = jnp.where(core == 0, gain[:, :rows], gain[:, rows:])
     gain_half = gain_half / own_gain
     out = half[:, three:].astype(F32)
@@ -561,7 +562,7 @@
     back = from_behind(back, "lon", 1)
     entries = 2 * (4 * width * width + width + heads)
     if rows // 2 // lons % 16 == 0 and lons & (lons - 1) == 0:
-        grads = staged(keep, came, back, qkv_v, gains, lons, heads, entries)
+        grads = staged(keep, came, back, qkv_v, own, lons, heads, entries)
     else:
         grads = plain(keep, came, weight_qkv, gains, heads, entries)
     (final_grad,) = call(
@@ -575,7 +576,7 @@
     return (final_grad, *(grad[None] for grad in grads))
 
 
-def staged(keep, came, after, weight_qkv, gains, lons, heads, entries):
+def staged(keep, came, after, weight_qkv, own, lons, heads, entries):
     rows, wide = keep.shape
     width = 2 * rows
     wide_p = CUT + GROUP
@@ -631,7 +632,7 @@
     half, row = call(
         fifth_kernel,
         [shape((rows, 4 * width), BF16), shape((8, rows + GROUP), F32)],
-        operands=(weight_qkv, gains, bias, block_p, other_p, block_q, *others_q),
+        operands=(weight_qkv, own, bias, block_p, other_p, block_q, *others_q),
     )
     row_section = swapped(row, "section", 1)
     row_both = lax.ppermute(row, ("section", "lat"), across())

time: 83.4 us -> 82.5 us (0.989)
  waiting for transfers between devices: 32.8 us -> 31.5 us
    ppermute x3, waiting for transfers between devices: 7.13 us -> 6.08 us  [from_behind(): lax.ppermute(value, axis, [(i, (i + by) % count) for i in range(count)])]
    unnamed x8 -> x6, local copies, waits for them, and re-layouts: 3.43 us -> 3.42 us
  transfers between devices with their start and end apart: 25 -> 25, of which waited for: 12 -> 13; matrix products, arithmetic and copies ran while one was open for 0% -> 0% of each run, Pallas kernels for 5% -> 6%
where the time goes in v13:
time: 82.5 us; the launch traced here: 82.3 us
  waiting for transfers between devices  31.5 us (38%)
  starting transfers between devices  30.9 us (37%)
  Pallas kernels  15.8 us (19%)
  local copies, waits for them, and re-layouts  3.42 us (4%)
    ppermute x20, starting transfers between devices, swapped(): return lax.ppermute(value, axis, [(i, i ^ bit) for i in range(count)])  23.3 us
    ppermute x20, waiting for transfers between devices, swapped(): return lax.ppermute(value, axis, [(i, i ^ bit) for i in range(count)])  19.4 us
    pallas_call x13, Pallas kernels, call(): pl.pallas_call(kernel, out_shape=list(outs), in_specs=[pl.BlockSpec(memor...  15.8 us
    ppermute x3, starting transfers between devices, from_behind(): lax.ppermute(value, axis, [(i, (i + by) % count) for i in range(count)])  6.23 us
    ppermute x3, waiting for transfers between devices, from_behind(): lax.ppermute(value, axis, [(i, (i + by) % count) for i in range(count)])  6.08 us
    ppermute x1, waiting for transfers between devices, passed_along(): return lax.ppermute(block, axis, route)  5.74 us
    unnamed x6, local copies, waits for them, and re-layouts  3.42 us
  transfers between devices with their start and end apart: 25, of which 13 were waited for; matrix products, arithmetic and copies ran while one was open for 0% of the time, Pallas kernels for 6%

profile of v13, /device:TPU:0, one launch (start us, length us, event | category | flops | bytes accessed | tf_op | source)
XLA Modules:
  0.0 82.3 jit_solution(15651558051677968055)
XLA Ops:
  0.6 1.9 %shard_map.110 = (f32[160,512]{1,0:T(8,128)}, bf16[80,512]{1,0:T(8,128)(2,1)}, bf16[80,512]{1,0:T(8,128)(2,1)}) custom-call(bf16[1,6,12,2,512]{4,3,2,1,0:T(2,128)(2,1)} %bitcast.12, bf16[1,6,12,2,512]{4,3,2,1,0:T(2,128)(2,1)} %bitcast.13, s32[6,12]{1,0:T(8,128)} %land.1, f32[1,512]{1,0:T(1,128)} %gain.1, f32[1,16]{1,0:T(1,128)} %bias.1), custom_call_target="tpu_custom_call" | custom-call | flops 100000000 | bytes 788832 | tf_op jit(solution)/shard_map/pallas_call | solution.py:47
  2.5 5.1 %collective-permute-start.1 = (bf16[80,512]{1,0:T(8,128)(2,1)}, bf16[80,512]{1,0:T(8,128)(2,1)S(1)}, u32[]{:S(2)}, u32[]{:S(2)}) collective-permute-start(bf16[80,512]{1,0:T(8,128)(2,1)} %get-tuple-element.51), channel_id=1, source_target_pairs={{0,12},{4,0},{8,4},{12,8},{1,13},{5,1},{9,5},{13,9},{2,14},{6,2},{... | collective-permute-start | bytes 245768 | tf_op jit(solution)/shard_map/ppermute | solution.py:20
  7.6 0.4 collective-permute-start
  8.1 1.0 %copy-done = f32[160,512]{1,0:T(8,128)S(1)} copy-done((f32[160,512]{1,0:T(8,128)S(1)}, f32[160,512]{1,0:T(8,128)}, u32[]{:S(2)}) %copy-start) | copy-done | bytes 327704
  9.1 1.4 %copy-done.1 = bf16[1,512,1536]{2,1,0:T(8,128)(2,1)S(1)} copy-done((bf16[1,512,1536]{2,1,0:T(8,128)(2,1)S(1)}, bf16[1,512,1536]{2,1,0:T(8,128)(2,1)}, u32[]{:S(2)}) %copy-start.1) | copy-done | bytes 1572888
  10.5 1.0 %copy-done.2 = bf16[1,512,512]{2,1,0:T(8,128)(2,1)S(1)} copy-done((bf16[1,512,512]{2,1,0:T(8,128)(2,1)S(1)}, bf16[1,512,512]{2,1,0:T(8,128)(2,1)}, u32[]{:S(2)}) %copy-start.2) | copy-done | bytes 524312
  11.5 0.6 shard_map.111
  12.1 0.0 collective-permute-done.1.rim
  12.2 2.4 %shard_map.112 = (bf16[512,144]{1,0:T(8,128)(2,1)S(1)}, bf16[144,1536]{1,0:T(8,128)(2,1)S(1)}, bf16[2304,144]{1,0:T(8,128)(2,1)S(1)}, bf16[512,144]{1,0:T(8,128)...) custom-call(f32[160,512]{1,0:T(8,128)S(1)} %copy-done, bf16[80,512]{1,0:T(8,128)(2,1)S(1)} %collective-permute-done.1.rim, ...), custom_call_target="tpu_custom_call" | custom-call | flops 1000000000 | bytes 3825664 | tf_op jit(solution)/shard_map/pallas_call | solution.py:47
  14.6 0.0 collective-permute-done.rim
  14.6 2.8 %shard_map.113 = (bf16[144,512]{1,0:T(8,128)(2,1)S(1)}, bf16[144,512]{1,0:T(8,128)(2,1)S(1)}) custom-call(f32[160,512]{1,0:T(8,128)S(1)} %copy-done, bf16[80,512]{1,0:T(8,128)(2,1)S(1)} %collective-permute-done.rim, bf16[144,1536]{1,0:T(8,128)(2,1)S(1)} %get-tuple-element.53.qkv, bf16[2304,144]{1,0:T(8,128)(2,1)S(1)} %get-tuple-element.54.probs, ...), custom_call_target="tpu_custom_call" | custom-call | flops 1000000000 | bytes 4349952 | tf_op jit(solution)/shard_map/pallas_call | solution.py:47
  17.4 1.3 %collective-permute-start.2 = (bf16[144,512]{1,0:T(8,128)(2,1)S(1)}, bf16[144,512]{1,0:T(8,128)(2,1)S(1)}, u32[]{:S(2)}, u32[]{:S(2)}) collective-permute-start(bf16[144,512]{1,0:T(8,128)(2,1)S(1)} %get-tuple-element.59), channel_id=1, source_target_pairs={{16,0},{17,1},{18,2},{19,3},{20,4},{21,5},{22,6},{23,7},{24,8},{25... | collective-permute-start | bytes 442376 | tf_op jit(solution)/shard_map/ppermute | solution.py:26
  18.7 5.7 %collective-permute-done.2.skip = bf16[144,512]{1,0:T(8,128)(2,1)S(1)} collective-permute-done((bf16[144,512]{1,0:T(8,128)(2,1)S(1)}, bf16[144,512]{1,0:T(8,128)(2,1)S(1)}, u32[]{:S(2)}, u32[]{:S(2)}) %collective-permute-start.2) | collective-permute-done | bytes 147488 | tf_op jit(solution)/shard_map/ppermute | solution.py:26
  24.4 3.0 %shard_map.114 = (bf16[144,512]{1,0:T(8,128)(2,1)S(1)}, bf16[144,1536]{1,0:T(8,128)(2,1)S(1)}, f32[8,128]{1,0:T(8,128)S(1)}, bf16[256,2176]{1,0:T(8,128)(2,1)S(1)}) custom-call(bf16[144,512]{1,0:T(8,128)(2,1)S(1)} %collective-permute-done.2.skip, bf16[144,512]{1,0:T(8,128)(2,1)S(1)} %get-tuple-element.60.cot, bf16[144,1536]{1,0:T(8,128)(2,1)S(1)} %get-tuple-element.53.qkv, ...), custom_call_target="tpu_custom_call" | custom-call | flops 1000000000 | bytes 4075520 | tf_op jit(solution)/shard_map/pallas_call | solution.py:47
  27.4 0.1 collective-permute-start.4
  27.5 0.8 shard_map.115
  28.3 1.9 %collective-permute-done.4.came = bf16[256,2176]{1,0:T(8,128)(2,1)S(1)} collective-permute-done((bf16[256,2176]{1,0:T(8,128)(2,1)S(1)}, bf16[256,2176]{1,0:T(8,128)(2,1)S(1)}, u32[]{:S(2)}, u32[]{:S(2)}) %collective-permute-start.4) | collective-permute-done | bytes 1114144 | tf_op jit(solution)/shard_map/ppermute | solution.py:31
  30.3 0.4 shard_map.117
  30.6 1.6 %collective-permute-start.5 = (bf16[128,1536]{1,0:T(8,128)(2,1)S(1)}, bf16[128,1536]{1,0:T(8,128)(2,1)S(1)}, u32[]{:S(2)}, u32[]{:S(2)}) collective-permute-start(bf16[128,1536]{1,0:T(8,128)(2,1)S(1)} %get-tuple-element.71), channel_id=1, source_target_pairs={{0,2},{1,3},{2,0},{3,1},{4,6},{5,7},{6,4},{7,5},{8,10},{9,11},{10,... | collective-permute-start | bytes 1179656 | tf_op jit(solution)/shard_map/ppermute | solution.py:31
  32.2 2.6 %collective-permute-start.6 = (bf16[64,640]{1,0:T(8,128)(2,1)S(1)}, bf16[64,640]{1,0:T(8,128)(2,1)S(1)}, u32[]{:S(2)}, u32[]{:S(2)}) collective-permute-start(bf16[64,640]{1,0:T(8,128)(2,1)S(1)} %get-tuple-element.73), channel_id=1, source_target_pairs={{0,12},{4,8},{8,4},{12,0},{1,13},{5,9},{9,5},{13,1},{2,14},{6,10},... | collective-permute-start | bytes 245768 | tf_op jit(solution)/shard_map/ppermute | solution.py:31
  34.8 0.5 collective-permute-start.7
  35.3 1.3 %collective-permute-start.8 = (bf16[64,640]{1,0:T(8,128)(2,1)S(1)}, bf16[64,640]{1,0:T(8,128)(2,1)S(1)}, u32[]{:S(2)}, u32[]{:S(2)}) collective-permute-start(bf16[64,640]{1,0:T(8,128)(2,1)S(1)} %get-tuple-element.75), channel_id=1, source_target_pairs={{0,4},{4,0},{8,12},{12,8},{1,5},{5,1},{9,13},{13,9},{2,6},{6,2},{1... | collective-permute-start | bytes 245768 | tf_op jit(solution)/shard_map/ppermute | solution.py:31
  36.6 0.7 collective-permute-start.3
  37.3 6.1 %collective-permute-done.3.back.after = bf16[72,512]{1,0:T(8,128)(2,1)S(1)} collective-permute-done((bf16[72,512]{1,0:T(8,128)(2,1)S(1)}, bf16[72,512]{1,0:T(8,128)(2,1)S(1)}, u32[]{:S(2)}, u32[]{:S(2)}) %collective-permute-start.3) | collective-permute-done | bytes 73760 | tf_op jit(solution)/shard_map/ppermute | solution.py:20
  43.4 0.0 collective-permute-done.6.rest_0_
  43.4 0.9 %collective-permute-done.7.rest_1_ = bf16[64,640]{1,0:T(8,128)(2,1)S(1)} collective-permute-done((bf16[64,640]{1,0:T(8,128)(2,1)S(1)}, bf16[64,640]{1,0:T(8,128)(2,1)S(1)}, u32[]{:S(2)}, u32[]{:S(2)}) %collective-permute-start.7) | collective-permute-done | bytes 81952 | tf_op jit(solution)/shard_map/ppermute | solution.py:31
  44.3 0.0 collective-permute-done.8.rest_2_
  44.3 0.0 collective-permute-done.5.came_p
  44.3 0.2 shard_map.118
  44.5 1.7 %collective-permute-start.10 = (bf16[32,1536]{1,0:T(8,128)(2,1)S(1)}, bf16[32,1536]{1,0:T(8,128)(2,1)S(1)}, u32[]{:S(2)}, u32[]{:S(2)}) collective-permute-start(bf16[32,1536]{1,0:T(8,128)(2,1)S(1)} %get-tuple-element.79), channel_id=1, source_target_pairs={{0,12},{4,8},{8,4},{12,0},{1,13},{5,9},{9,5},{13,1},{2,14},{6,10},... | collective-permute-start | bytes 294920 | tf_op jit(solution)/shard_map/ppermute | solution.py:31
  46.2 0.0 collective-permute-start.11
  46.2 2.8 %collective-permute-start.12 = (bf16[32,1536]{1,0:T(8,128)(2,1)S(1)}, bf16[32,1536]{1,0:T(8,128)(2,1)S(1)}, u32[]{:S(2)}, u32[]{:S(2)}) collective-permute-start(bf16[32,1536]{1,0:T(8,128)(2,1)S(1)} %get-tuple-element.81), channel_id=1, source_target_pairs={{0,4},{4,0},{8,12},{12,8},{1,5},{5,1},{9,13},{13,9},{2,6},{6,2},{1... | collective-permute-start | bytes 294920 | tf_op jit(solution)/shard_map/ppermute | solution.py:31
  49.0 0.5 collective-permute-start.9
  49.5 3.5 %collective-permute-done.9.came_q = bf16[32,640]{1,0:T(8,128)(2,1)S(1)} collective-permute-done((bf16[32,640]{1,0:T(8,128)(2,1)S(1)}, bf16[32,640]{1,0:T(8,128)(2,1)S(1)}, u32[]{:S(2)}, u32[]{:S(2)}) %collective-permute-start.9) | collective-permute-done | bytes 40992 | tf_op jit(solution)/shard_map/ppermute | solution.py:31
  53.0 0.0 collective-permute-done.10.rest_0_
  53.0 1.8 %collective-permute-done.11.rest_1_ = bf16[32,1536]{1,0:T(8,128)(2,1)S(1)} collective-permute-done((bf16[32,1536]{1,0:T(8,128)(2,1)S(1)}, bf16[32,1536]{1,0:T(8,128)(2,1)S(1)}, u32[]{:S(2)}, u32[]{:S(2)}) %collective-permute-start.11) | collective-permute-done | bytes 98336 | tf_op jit(solution)/shard_map/ppermute | solution.py:31
  54.8 0.0 collective-permute-done.12.rest_2_
  54.8 0.1 shard_map.119
  54.9 2.5 %collective-permute-start.16 = (bf16[32,1408]{1,0:T(8,128)(2,1)S(1)}, bf16[32,1408]{1,0:T(8,128)(2,1)S(1)}, u32[]{:S(2)}, u32[]{:S(2)}) collective-permute-start(bf16[32,1408]{1,0:T(8,128)(2,1)S(1)} %get-tuple-element.84.rest_0_), channel_id=1, source_target_pairs={{0,12},{4,8},{8,4},{12,0},{1,13},{5,9},{9,5},{13,1},{2,14},{6,10},... | collective-permute-start | bytes 270344 | tf_op jit(solution)/shard_map/ppermute | solution.py:31
  57.4 0.0 collective-permute-start.15
  57.4 2.0 %collective-permute-start.14 = (bf16[32,1408]{1,0:T(8,128)(2,1)S(1)}, bf16[32,1408]{1,0:T(8,128)(2,1)S(1)}, u32[]{:S(2)}, u32[]{:S(2)}) collective-permute-start(bf16[32,1408]{1,0:T(8,128)(2,1)S(1)} %get-tuple-element.84.rest_0_), channel_id=1, source_target_pairs={{0,4},{4,0},{8,12},{12,8},{1,5},{5,1},{9,13},{13,9},{2,6},{6,2},{1... | collective-permute-start | bytes 270344 | tf_op jit(solution)/shard_map/ppermute | solution.py:31
  59.3 0.8 collective-permute-start.13
  60.1 3.2 %collective-permute-done.13.other_q = bf16[32,640]{1,0:T(8,128)(2,1)S(1)} collective-permute-done((bf16[32,640]{1,0:T(8,128)(2,1)S(1)}, bf16[32,640]{1,0:T(8,128)(2,1)S(1)}, u32[]{:S(2)}, u32[]{:S(2)}) %collective-permute-start.13) | collective-permute-done | bytes 40992 | tf_op jit(solution)/shard_map/ppermute | solution.py:31
  63.3 0.0 collective-permute-done.16.rest_3_
  63.3 1.7 %collective-permute-done.15.rest_2_ = bf16[32,1408]{1,0:T(8,128)(2,1)S(1)} collective-permute-done((bf16[32,1408]{1,0:T(8,128)(2,1)S(1)}, bf16[32,1408]{1,0:T(8,128)(2,1)S(1)}, u32[]{:S(2)}, u32[]{:S(2)}) %collective-permute-start.15) | collective-permute-done | bytes 90144 | tf_op jit(solution)/shard_map/ppermute | solution.py:31
  65.1 0.0 collective-permute-done.14.rest_1_
  65.1 0.5 collective-permute-start.17
  65.7 2.0 %collective-permute-start.20 = (bf16[64,640]{1,0:T(8,128)(2,1)S(1)}, bf16[64,640]{1,0:T(8,128)(2,1)S(1)}, u32[]{:S(2)}, u32[]{:S(2)}) collective-permute-start(bf16[64,640]{1,0:T(8,128)(2,1)S(1)} %get-tuple-element.86.rest_0_), channel_id=1, source_target_pairs={{0,12},{4,8},{8,4},{12,0},{1,13},{5,9},{9,5},{13,1},{2,14},{6,10},... | collective-permute-start | bytes 245768 | tf_op jit(solution)/shard_map/ppermute | solution.py:31
  67.6 2.4 %collective-permute-start.18 = (bf16[64,640]{1,0:T(8,128)(2,1)S(1)}, bf16[64,640]{1,0:T(8,128)(2,1)S(1)}, u32[]{:S(2)}, u32[]{:S(2)}) collective-permute-start(bf16[64,640]{1,0:T(8,128)(2,1)S(1)} %get-tuple-element.86.rest_0_), channel_id=1, source_target_pairs={{0,4},{4,0},{8,12},{12,8},{1,5},{5,1},{9,13},{13,9},{2,6},{6,2},{1... | collective-permute-start | bytes 245768 | tf_op jit(solution)/shard_map/ppermute | solution.py:31
  70.1 2.8 %collective-permute-done.20.rest_3_ = bf16[64,640]{1,0:T(8,128)(2,1)S(1)} collective-permute-done((bf16[64,640]{1,0:T(8,128)(2,1)S(1)}, bf16[64,640]{1,0:T(8,128)(2,1)S(1)}, u32[]{:S(2)}, u32[]{:S(2)}) %collective-permute-start.20) | collective-permute-done | bytes 81952 | tf_op jit(solution)/shard_map/ppermute | solution.py:31
  72.9 2.2 %collective-permute-done.19.rest_2_ = bf16[64,640]{1,0:T(8,128)(2,1)S(1)} collective-permute-done((bf16[64,640]{1,0:T(8,128)(2,1)S(1)}, bf16[64,640]{1,0:T(8,128)(2,1)S(1)}, u32[]{:S(2)}, u32[]{:S(2)}) %collective-permute-start.19) | collective-permute-done | bytes 81952 | tf_op jit(solution)/shard_map/ppermute | solution.py:31
  75.1 0.0 collective-permute-done.18.rest_1_
  75.1 0.5 collective-permute-done.17.other_p
  75.5 0.5 shard_map.121
  76.0 0.0 collective-permute-start.21
  76.1 0.1 collective-permute-start.24
  76.1 2.1 %collective-permute-start.23 = (f32[8,384]{1,0:T(8,128)S(1)}, f32[8,384]{1,0:T(8,128)S(1)}, u32[]{:S(2)}, u32[]{:S(2)}) collective-permute-start(f32[8,384]{1,0:T(8,128)S(1)} %get-tuple-element.88.row), channel_id=1, source_target_pairs={{0,16},{16,0},{1,17},{17,1},{2,18},{18,2},{3,19},{19,3},{4,20},{20... | collective-permute-start | bytes 36872 | tf_op jit(solution)/shard_map/ppermute | solution.py:31
  78.2 0.0 collective-permute-start.22
  78.2 0.8 shard_map.116
  79.0 0.3 collective-permute-done.24.row_both
  79.3 0.8 collective-permute-done.23.row_section
  80.0 0.0 collective-permute-done.22.row_core
  80.0 0.0 collective-permute-done.21.other
  80.0 2.3 %shard_map.122 = (f32[512,1536]{1,0:T(8,128)}, f32[512,512]{1,0:T(8,128)}, f32[1,512]{1,0:T(1,128)}, f32[1,16]{1,0:T(1,128)}) custom-call(bf16[256,2048]{1,0:T(8,128)(2,1)S(1)} %get-tuple-element.87.half, bf16[256,2048]{1,0:T(8,128)(2,1)S(1)} %collective-permute-done.21.other, f32[8,384]{1,0:T(8,128)S(1)} %get-tuple-element.88.row, ...), custom_call_target="tpu_custom_call" | custom-call | flops 100000000 | bytes 6346816 | tf_op jit(solution)/shard_map/pallas_call | solution.py:47
  (5 shorter events, 0.1 us)
Async XLA Ops:
  2.5 9.6 %collective-permute-start.1 = (bf16[80,512]{1,0:T(8,128)(2,1)}, bf16[80,512]{1,0:T(8,128)(2,1)S(1)}, u32[]{:S(2)}, u32[]{:S(2)}) collective-permute-start(bf16[80,512]{1,0:T(8,128)(2,1)} %get-tuple-element.51), channel_id=1, source_target_pairs={{0,12},{4,0},{8,4},{12,8},{1,13},{5,1},{9,5},{13,9},{2,14},{6,2},{... | collective-permute-start | bytes 245768 | tf_op jit(solution)/shard_map/ppermute | solution.py:20
  7.6 6.9 %collective-permute-start = (bf16[80,512]{1,0:T(8,128)(2,1)}, bf16[80,512]{1,0:T(8,128)(2,1)S(1)}, u32[]{:S(2)}, u32[]{:S(2)}) collective-permute-start(bf16[80,512]{1,0:T(8,128)(2,1)} %get-tuple-element.50), channel_id=1, source_target_pairs={{0,12},{4,0},{8,4},{12,8},{1,13},{5,1},{9,5},{13,9},{2,14},{6,2},{... | collective-permute-start | bytes 245768 | tf_op jit(solution)/shard_map/ppermute | solution.py:20
  8.1 1.0 %copy-start = (f32[160,512]{1,0:T(8,128)S(1)}, f32[160,512]{1,0:T(8,128)}, u32[]{:S(2)}) copy-start(f32[160,512]{1,0:T(8,128)} %get-tuple-element.49.after.own.params) | copy-start | bytes 983044
  9.1 1.4 %copy-start.1 = (bf16[1,512,1536]{2,1,0:T(8,128)(2,1)S(1)}, bf16[1,512,1536]{2,1,0:T(8,128)(2,1)}, u32[]{:S(2)}) copy-start(bf16[1,512,1536]{2,1,0:T(8,128)(2,1)} %param.11) | copy-start | bytes 4718596
  10.5 1.0 %copy-start.2 = (bf16[1,512,512]{2,1,0:T(8,128)(2,1)S(1)}, bf16[1,512,512]{2,1,0:T(8,128)(2,1)}, u32[]{:S(2)}) copy-start(bf16[1,512,512]{2,1,0:T(8,128)(2,1)} %param.12) | copy-start | bytes 1572868
  17.4 7.0 %collective-permute-start.2 = (bf16[144,512]{1,0:T(8,128)(2,1)S(1)}, bf16[144,512]{1,0:T(8,128)(2,1)S(1)}, u32[]{:S(2)}, u32[]{:S(2)}) collective-permute-start(bf16[144,512]{1,0:T(8,128)(2,1)S(1)} %get-tuple-element.59), channel_id=1, source_target_pairs={{16,0},{17,1},{18,2},{19,3},{20,4},{21,5},{22,6},{23,7},{24,8},{25... | collective-permute-start | bytes 442376 | tf_op jit(solution)/shard_map/ppermute | solution.py:26
  27.4 2.8 %collective-permute-start.4 = (bf16[256,2176]{1,0:T(8,128)(2,1)S(1)}, bf16[256,2176]{1,0:T(8,128)(2,1)S(1)}, u32[]{:S(2)}, u32[]{:S(2)}) collective-permute-start(bf16[256,2176]{1,0:T(8,128)(2,1)S(1)} %get-tuple-element.69), channel_id=1, source_target_pairs={{0,1},{1,0},{2,3},{3,2},{4,5},{5,4},{6,7},{7,6},{8,9},{9,8},{10,11... | collective-permute-start | bytes 3342344 | tf_op jit(solution)/shard_map/ppermute | solution.py:31
  30.6 13.7 %collective-permute-start.5 = (bf16[128,1536]{1,0:T(8,128)(2,1)S(1)}, bf16[128,1536]{1,0:T(8,128)(2,1)S(1)}, u32[]{:S(2)}, u32[]{:S(2)}) collective-permute-start(bf16[128,1536]{1,0:T(8,128)(2,1)S(1)} %get-tuple-element.71), channel_id=1, source_target_pairs={{0,2},{1,3},{2,0},{3,1},{4,6},{5,7},{6,4},{7,5},{8,10},{9,11},{10,... | collective-permute-start | bytes 1179656 | tf_op jit(solution)/shard_map/ppermute | solution.py:31
  32.2 11.1 %collective-permute-start.6 = (bf16[64,640]{1,0:T(8,128)(2,1)S(1)}, bf16[64,640]{1,0:T(8,128)(2,1)S(1)}, u32[]{:S(2)}, u32[]{:S(2)}) collective-permute-start(bf16[64,640]{1,0:T(8,128)(2,1)S(1)} %get-tuple-element.73), channel_id=1, source_target_pairs={{0,12},{4,8},{8,4},{12,0},{1,13},{5,9},{9,5},{13,1},{2,14},{6,10},... | collective-permute-start | bytes 245768 | tf_op jit(solution)/shard_map/ppermute | solution.py:31
  34.8 9.5 %collective-permute-start.7 = (bf16[64,640]{1,0:T(8,128)(2,1)S(1)}, bf16[64,640]{1,0:T(8,128)(2,1)S(1)}, u32[]{:S(2)}, u32[]{:S(2)}) collective-permute-start(bf16[64,640]{1,0:T(8,128)(2,1)S(1)} %get-tuple-element.74), channel_id=1, source_target_pairs={{0,8},{4,12},{8,0},{12,4},{1,9},{5,13},{9,1},{13,5},{2,10},{6,14},... | collective-permute-start | bytes 245768 | tf_op jit(solution)/shard_map/ppermute | solution.py:31
  35.3 9.0 %collective-permute-start.8 = (bf16[64,640]{1,0:T(8,128)(2,1)S(1)}, bf16[64,640]{1,0:T(8,128)(2,1)S(1)}, u32[]{:S(2)}, u32[]{:S(2)}) collective-permute-start(bf16[64,640]{1,0:T(8,128)(2,1)S(1)} %get-tuple-element.75), channel_id=1, source_target_pairs={{0,4},{4,0},{8,12},{12,8},{1,5},{5,1},{9,13},{13,9},{2,6},{6,2},{1... | collective-permute-start | bytes 245768 | tf_op jit(solution)/shard_map/ppermute | solution.py:31
  36.6 6.7 %collective-permute-start.3 = (bf16[72,512]{1,0:T(8,128)(2,1)S(1)}, bf16[72,512]{1,0:T(8,128)(2,1)S(1)}, u32[]{:S(2)}, u32[]{:S(2)}) collective-permute-start(bf16[72,512]{1,0:T(8,128)(2,1)S(1)} %get-tuple-element.67), channel_id=1, source_target_pairs={{0,4},{4,8},{8,12},{12,0},{1,5},{5,9},{9,13},{13,1},{2,6},{6,10},{... | collective-permute-start | bytes 221192 | tf_op jit(solution)/shard_map/ppermute | solution.py:20
  44.5 8.5 %collective-permute-start.10 = (bf16[32,1536]{1,0:T(8,128)(2,1)S(1)}, bf16[32,1536]{1,0:T(8,128)(2,1)S(1)}, u32[]{:S(2)}, u32[]{:S(2)}) collective-permute-start(bf16[32,1536]{1,0:T(8,128)(2,1)S(1)} %get-tuple-element.79), channel_id=1, source_target_pairs={{0,12},{4,8},{8,4},{12,0},{1,13},{5,9},{9,5},{13,1},{2,14},{6,10},... | collective-permute-start | bytes 294920 | tf_op jit(solution)/shard_map/ppermute | solution.py:31
  46.2 8.6 %collective-permute-start.11 = (bf16[32,1536]{1,0:T(8,128)(2,1)S(1)}, bf16[32,1536]{1,0:T(8,128)(2,1)S(1)}, u32[]{:S(2)}, u32[]{:S(2)}) collective-permute-start(bf16[32,1536]{1,0:T(8,128)(2,1)S(1)} %get-tuple-element.80), channel_id=1, source_target_pairs={{0,8},{4,12},{8,0},{12,4},{1,9},{5,13},{9,1},{13,5},{2,10},{6,14},... | collective-permute-start | bytes 294920 | tf_op jit(solution)/shard_map/ppermute | solution.py:31
  46.2 8.6 %collective-permute-start.12 = (bf16[32,1536]{1,0:T(8,128)(2,1)S(1)}, bf16[32,1536]{1,0:T(8,128)(2,1)S(1)}, u32[]{:S(2)}, u32[]{:S(2)}) collective-permute-start(bf16[32,1536]{1,0:T(8,128)(2,1)S(1)} %get-tuple-element.81), channel_id=1, source_target_pairs={{0,4},{4,0},{8,12},{12,8},{1,5},{5,1},{9,13},{13,9},{2,6},{6,2},{1... | collective-permute-start | bytes 294920 | tf_op jit(solution)/shard_map/ppermute | solution.py:31
  49.0 4.0 %collective-permute-start.9 = (bf16[32,640]{1,0:T(8,128)(2,1)S(1)}, bf16[32,640]{1,0:T(8,128)(2,1)S(1)}, u32[]{:S(2)}, u32[]{:S(2)}) collective-permute-start(bf16[32,640]{1,0:T(8,128)(2,1)S(1)} %get-tuple-element.78), channel_id=1, source_target_pairs={{0,2},{1,3},{2,0},{3,1},{4,6},{5,7},{6,4},{7,5},{8,10},{9,11},{10,... | collective-permute-start | bytes 122888 | tf_op jit(solution)/shard_map/ppermute | solution.py:31
  54.9 8.5 %collective-permute-start.16 = (bf16[32,1408]{1,0:T(8,128)(2,1)S(1)}, bf16[32,1408]{1,0:T(8,128)(2,1)S(1)}, u32[]{:S(2)}, u32[]{:S(2)}) collective-permute-start(bf16[32,1408]{1,0:T(8,128)(2,1)S(1)} %get-tuple-element.84.rest_0_), channel_id=1, source_target_pairs={{0,12},{4,8},{8,4},{12,0},{1,13},{5,9},{9,5},{13,1},{2,14},{6,10},... | collective-permute-start | bytes 270344 | tf_op jit(solution)/shard_map/ppermute | solution.py:31
  57.4 7.7 %collective-permute-start.15 = (bf16[32,1408]{1,0:T(8,128)(2,1)S(1)}, bf16[32,1408]{1,0:T(8,128)(2,1)S(1)}, u32[]{:S(2)}, u32[]{:S(2)}) collective-permute-start(bf16[32,1408]{1,0:T(8,128)(2,1)S(1)} %get-tuple-element.84.rest_0_), channel_id=1, source_target_pairs={{0,8},{4,12},{8,0},{12,4},{1,9},{5,13},{9,1},{13,5},{2,10},{6,14},... | collective-permute-start | bytes 270344 | tf_op jit(solution)/shard_map/ppermute | solution.py:31
  57.4 7.7 %collective-permute-start.14 = (bf16[32,1408]{1,0:T(8,128)(2,1)S(1)}, bf16[32,1408]{1,0:T(8,128)(2,1)S(1)}, u32[]{:S(2)}, u32[]{:S(2)}) collective-permute-start(bf16[32,1408]{1,0:T(8,128)(2,1)S(1)} %get-tuple-element.84.rest_0_), channel_id=1, source_target_pairs={{0,4},{4,0},{8,12},{12,8},{1,5},{5,1},{9,13},{13,9},{2,6},{6,2},{1... | collective-permute-start | bytes 270344 | tf_op jit(solution)/shard_map/ppermute | solution.py:31
  59.3 4.0 %collective-permute-start.13 = (bf16[32,640]{1,0:T(8,128)(2,1)S(1)}, bf16[32,640]{1,0:T(8,128)(2,1)S(1)}, u32[]{:S(2)}, u32[]{:S(2)}) collective-permute-start(bf16[32,640]{1,0:T(8,128)(2,1)S(1)} %get-tuple-element.83.piece_q), channel_id=1, source_target_pairs={{0,2},{1,3},{2,0},{3,1},{4,6},{5,7},{6,4},{7,5},{8,10},{9,11},{10,... | collective-permute-start | bytes 122888 | tf_op jit(solution)/shard_map/ppermute | solution.py:31
  65.1 10.4 %collective-permute-start.17 = (bf16[128,1408]{1,0:T(8,128)(2,1)S(1)}, bf16[128,1408]{1,0:T(8,128)(2,1)S(1)}, u32[]{:S(2)}, u32[]{:S(2)}) collective-permute-start(bf16[128,1408]{1,0:T(8,128)(2,1)S(1)} %get-tuple-element.85.block_p), channel_id=1, source_target_pairs={{0,2},{1,3},{2,0},{3,1},{4,6},{5,7},{6,4},{7,5},{8,10},{9,11},{10,... | collective-permute-start | bytes 1081352 | tf_op jit(solution)/shard_map/ppermute | solution.py:31
  65.7 7.2 %collective-permute-start.20 = (bf16[64,640]{1,0:T(8,128)(2,1)S(1)}, bf16[64,640]{1,0:T(8,128)(2,1)S(1)}, u32[]{:S(2)}, u32[]{:S(2)}) collective-permute-start(bf16[64,640]{1,0:T(8,128)(2,1)S(1)} %get-tuple-element.86.rest_0_), channel_id=1, source_target_pairs={{0,12},{4,8},{8,4},{12,0},{1,13},{5,9},{9,5},{13,1},{2,14},{6,10},... | collective-permute-start | bytes 245768 | tf_op jit(solution)/shard_map/ppermute | solution.py:31
  67.6 7.4 %collective-permute-start.19 = (bf16[64,640]{1,0:T(8,128)(2,1)S(1)}, bf16[64,640]{1,0:T(8,128)(2,1)S(1)}, u32[]{:S(2)}, u32[]{:S(2)}) collective-permute-start(bf16[64,640]{1,0:T(8,128)(2,1)S(1)} %get-tuple-element.86.rest_0_), channel_id=1, source_target_pairs={{0,8},{4,12},{8,0},{12,4},{1,9},{5,13},{9,1},{13,5},{2,10},{6,14},... | collective-permute-start | bytes 245768 | tf_op jit(solution)/shard_map/ppermute | solution.py:31
  67.6 7.4 %collective-permute-start.18 = (bf16[64,640]{1,0:T(8,128)(2,1)S(1)}, bf16[64,640]{1,0:T(8,128)(2,1)S(1)}, u32[]{:S(2)}, u32[]{:S(2)}) collective-permute-start(bf16[64,640]{1,0:T(8,128)(2,1)S(1)} %get-tuple-element.86.rest_0_), channel_id=1, source_target_pairs={{0,4},{4,0},{8,12},{12,8},{1,5},{5,1},{9,13},{13,9},{2,6},{6,2},{1... | collective-permute-start | bytes 245768 | tf_op jit(solution)/shard_map/ppermute | solution.py:31
  76.0 4.0 %collective-permute-start.21 = (bf16[256,2048]{1,0:T(8,128)(2,1)S(1)}, bf16[256,2048]{1,0:T(8,128)(2,1)S(1)}, u32[]{:S(2)}, u32[]{:S(2)}) collective-permute-start(bf16[256,2048]{1,0:T(8,128)(2,1)S(1)} %get-tuple-element.87.half), channel_id=1, source_target_pairs={{0,1},{1,0},{2,3},{3,2},{4,5},{5,4},{6,7},{7,6},{8,9},{9,8},{10,11... | collective-permute-start | bytes 3145736 | tf_op jit(solution)/shard_map/ppermute | solution.py:31
  76.1 3.2 %collective-permute-start.24 = (f32[8,384]{1,0:T(8,128)S(1)}, f32[8,384]{1,0:T(8,128)S(1)}, u32[]{:S(2)}, u32[]{:S(2)}) collective-permute-start(f32[8,384]{1,0:T(8,128)S(1)} %get-tuple-element.88.row), channel_id=1, source_target_pairs={{0,17},{1,16},{2,19},{3,18},{16,1},{17,0},{18,3},{19,2},{4,21},{5,... | collective-permute-start | bytes 36872 | tf_op jit(solution)/shard_map/ppermute | solution.py:638
  76.1 3.9 %collective-permute-start.23 = (f32[8,384]{1,0:T(8,128)S(1)}, f32[8,384]{1,0:T(8,128)S(1)}, u32[]{:S(2)}, u32[]{:S(2)}) collective-permute-start(f32[8,384]{1,0:T(8,128)S(1)} %get-tuple-element.88.row), channel_id=1, source_target_pairs={{0,16},{16,0},{1,17},{17,1},{2,18},{18,2},{3,19},{19,3},{4,20},{20... | collective-permute-start | bytes 36872 | tf_op jit(solution)/shard_map/ppermute | solution.py:31
  78.2 1.8 %collective-permute-start.22 = (f32[8,384]{1,0:T(8,128)S(1)}, f32[8,384]{1,0:T(8,128)S(1)}, u32[]{:S(2)}, u32[]{:S(2)}) collective-permute-start(f32[8,384]{1,0:T(8,128)S(1)} %get-tuple-element.88.row), channel_id=1, source_target_pairs={{0,1},{1,0},{2,3},{3,2},{4,5},{5,4},{6,7},{7,6},{8,9},{9,8},{10,11... | collective-permute-start | bytes 36872 | tf_op jit(solution)/shard_map/ppermute | solution.py:31

commit v14 on v12

--- a/solution.py
+++ b/solution.py
@@ -205,7 +205,7 @@
 def forward_kernel(
     own, rim, weight_qkv, weight_t, weight_out,
     skip, cot, normed_t, qkv, probs_b, attended_t, extra, normed_out,
-    probs, queries_t, keys_t, values_t, grad_proj,
+    queries_t, keys_t, values_t, grad_proj,
     *, heads, lats, cols,
 ):
     width = own.shape[1]
@@ -249,14 +249,13 @@
             block = block + params[1:2, head : head + 1] * land
             block = jnp.exp(block - jnp.max(block, axis=0, keepdims=True))
             weights = block * (1.0 / jnp.sum(block, axis=0, keepdims=True))
-            probs[head * count : (head + 1) * count, :] = weights
             weights_b = weights.astype(BF16)
             probs_b[head * count : (head + 1) * count, :] = weights_b
             out = dot(values_t[head * size : (head + 1) * size, :], weights_b)
             attended_t[head * size : (head + 1) * size, :] = out.astype(BF16)
     grad_out = jnp.concatenate([mine[half:], came[half : 2 * half]], axis=0)
     cot[...] = grad_out.astype(BF16)
-    back_through(cot[...], probs, probs_b, qkv, keys_t, weight_out, grad_proj, size, None)
+    back_through(cot[...], probs_b, probs_b, qkv, keys_t, weight_out, grad_proj, size, None)
     skip[...] = (
         through_norm(grad_proj[...], weight_t, gain, normed, inverse) + grad_out
     ).astype(BF16)
@@ -503,7 +502,6 @@
             shape((count, width), F32),
         ],
         scratch=[
-            vmem((heads * count, count), F32),
             vmem((width, count), BF16),
             vmem((width, count), BF16),
             vmem((width, count), BF16),

time: 81.5 us -> 81.6 us (level)
  no operation moved by 1% of the time
where the time goes in v14:
time: 81.6 us; the launch traced here: 81.3 us
  starting transfers between devices  30.9 us (38%)
  waiting for transfers between devices  30.8 us (38%)
  Pallas kernels  15.4 us (19%)
  local copies, waits for them, and re-layouts  3.42 us (4%)
    ppermute x20, starting transfers between devices, swapped(): return lax.ppermute(value, axis, [(i, i ^ bit) for i in range(count)])  23.1 us
    ppermute x20, waiting for transfers between devices, swapped(): return lax.ppermute(value, axis, [(i, i ^ bit) for i in range(count)])  19 us
    pallas_call x12, Pallas kernels, call(): pl.pallas_call(kernel, out_shape=list(outs), in_specs=[pl.BlockSpec(memor...  15.4 us
    ppermute x2, starting transfers between devices, from_behind(): lax.ppermute(value, axis, [(i, (i + by) % count) for i in range(count)])  6.44 us
    ppermute x1, waiting for transfers between devices, passed_along(): return lax.ppermute(block, axis, route)  5.93 us
    ppermute x2, waiting for transfers between devices, from_behind(): lax.ppermute(value, axis, [(i, (i + by) % count) for i in range(count)])  5.62 us
    unnamed x6, local copies, waits for them, and re-layouts  3.42 us
  transfers between devices with their start and end apart: 24, of which 13 were waited for; matrix products, arithmetic and copies ran while one was open for 0% of the time, Pallas kernels for 3%

profile of v14, /device:TPU:0, one launch (start us, length us, event | category | flops | bytes accessed | tf_op | source)
XLA Modules:
  0.0 81.3 jit_solution(18127900958333606128)
XLA Ops:
  0.6 1.9 %shard_map.110 = (f32[160,512]{1,0:T(8,128)}, bf16[160,512]{1,0:T(8,128)(2,1)}) custom-call(bf16[1,6,12,2,512]{4,3,2,1,0:T(2,128)(2,1)} %bitcast.12, bf16[1,6,12,2,512]{4,3,2,1,0:T(2,128)(2,1)} %bitcast.13, s32[6,12]{1,0:T(8,128)} %land.1, f32[1,512]{1,0:T(1,128)} %gain.1, f32[1,16]{1,0:T(1,128)} %bias.1), custom_call_target="tpu_custom_call" | custom-call | flops 100000000 | bytes 788832 | tf_op jit(solution)/shard_map/pallas_call | solution.py:47
  2.5 5.1 %collective-permute-start = (bf16[160,512]{1,0:T(8,128)(2,1)}, bf16[160,512]{1,0:T(8,128)(2,1)S(1)}, u32[]{:S(2)}, u32[]{:S(2)}) collective-permute-start(bf16[160,512]{1,0:T(8,128)(2,1)} %get-tuple-element.49), channel_id=1, source_target_pairs={{0,12},{4,0},{8,4},{12,8},{1,13},{5,1},{9,5},{13,9},{2,14},{6,2},{... | collective-permute-start | bytes 491528 | tf_op jit(solution)/shard_map/ppermute | solution.py:20
  7.6 0.0 copy-start
  7.6 1.0 %copy-done = f32[160,512]{1,0:T(8,128)S(1)} copy-done((f32[160,512]{1,0:T(8,128)S(1)}, f32[160,512]{1,0:T(8,128)}, u32[]{:S(2)}) %copy-start) | copy-done | bytes 327704
  8.6 0.0 copy-start.1
  8.6 1.4 %copy-done.1 = bf16[1,512,1536]{2,1,0:T(8,128)(2,1)S(1)} copy-done((bf16[1,512,1536]{2,1,0:T(8,128)(2,1)S(1)}, bf16[1,512,1536]{2,1,0:T(8,128)(2,1)}, u32[]{:S(2)}) %copy-start.1) | copy-done | bytes 1572888
  10.0 1.0 %copy-done.2 = bf16[1,512,512]{2,1,0:T(8,128)(2,1)S(1)} copy-done((bf16[1,512,512]{2,1,0:T(8,128)(2,1)S(1)}, bf16[1,512,512]{2,1,0:T(8,128)(2,1)}, u32[]{:S(2)}) %copy-start.2) | copy-done | bytes 524312
  11.1 0.6 shard_map.111
  11.7 0.0 collective-permute-done.rim
  11.7 4.8 %shard_map.112 = (bf16[144,512]{1,0:T(8,128)(2,1)S(1)}, bf16[144,512]{1,0:T(8,128)(2,1)S(1)}, bf16[512,144]{1,0:T(8,128)(2,1)S(1)}, bf16[144,1536]{1,0:T(8,128)(...) custom-call(f32[160,512]{1,0:T(8,128)S(1)} %copy-done, ...), custom_call_target="tpu_custom_call" | custom-call | flops 1000000000 | bytes 6299648 | tf_op jit(solution)/shard_map/pallas_call | solution.py:47
  16.5 1.3 %collective-permute-start.1 = (bf16[144,512]{1,0:T(8,128)(2,1)S(1)}, bf16[144,512]{1,0:T(8,128)(2,1)S(1)}, u32[]{:S(2)}, u32[]{:S(2)}) collective-permute-start(bf16[144,512]{1,0:T(8,128)(2,1)S(1)} %get-tuple-element.53), channel_id=1, source_target_pairs={{16,0},{17,1},{18,2},{19,3},{20,4},{21,5},{22,6},{23,7},{24,8},{25... | collective-permute-start | bytes 442376 | tf_op jit(solution)/shard_map/ppermute | solution.py:26
  17.8 5.9 %collective-permute-done.1.skip = bf16[144,512]{1,0:T(8,128)(2,1)S(1)} collective-permute-done((bf16[144,512]{1,0:T(8,128)(2,1)S(1)}, bf16[144,512]{1,0:T(8,128)(2,1)S(1)}, u32[]{:S(2)}, u32[]{:S(2)}) %collective-permute-start.1) | collective-permute-done | bytes 147488 | tf_op jit(solution)/shard_map/ppermute | solution.py:26
  23.8 3.0 %shard_map.113 = (bf16[144,512]{1,0:T(8,128)(2,1)S(1)}, bf16[144,1536]{1,0:T(8,128)(2,1)S(1)}, f32[8,128]{1,0:T(8,128)S(1)}, bf16[256,2176]{1,0:T(8,128)(2,1)S(1)}) custom-call(bf16[144,512]{1,0:T(8,128)(2,1)S(1)} %collective-permute-done.1.skip, bf16[144,512]{1,0:T(8,128)(2,1)S(1)} %get-tuple-element.54.cot, bf16[144,1536]{1,0:T(8,128)(2,1)S(1)} %get-tuple-element.55.qkv, ...), custom_call_target="tpu_custom_call" | custom-call | flops 1000000000 | bytes 4075520 | tf_op jit(solution)/shard_map/pallas_call | solution.py:47
  26.8 0.1 collective-permute-start.3
  26.9 0.8 shard_map.114
  27.7 1.9 %collective-permute-done.3.came = bf16[256,2176]{1,0:T(8,128)(2,1)S(1)} collective-permute-done((bf16[256,2176]{1,0:T(8,128)(2,1)S(1)}, bf16[256,2176]{1,0:T(8,128)(2,1)S(1)}, u32[]{:S(2)}, u32[]{:S(2)}) %collective-permute-start.3) | collective-permute-done | bytes 1114144 | tf_op jit(solution)/shard_map/ppermute | solution.py:31
  29.6 0.4 shard_map.116
  30.0 1.6 %collective-permute-start.4 = (bf16[128,1536]{1,0:T(8,128)(2,1)S(1)}, bf16[128,1536]{1,0:T(8,128)(2,1)S(1)}, u32[]{:S(2)}, u32[]{:S(2)}) collective-permute-start(bf16[128,1536]{1,0:T(8,128)(2,1)S(1)} %get-tuple-element.69), channel_id=1, source_target_pairs={{0,2},{1,3},{2,0},{3,1},{4,6},{5,7},{6,4},{7,5},{8,10},{9,11},{10,... | collective-permute-start | bytes 1179656 | tf_op jit(solution)/shard_map/ppermute | solution.py:31
  31.6 3.7 %collective-permute-start.5 = (bf16[64,640]{1,0:T(8,128)(2,1)S(1)}, bf16[64,640]{1,0:T(8,128)(2,1)S(1)}, u32[]{:S(2)}, u32[]{:S(2)}) collective-permute-start(bf16[64,640]{1,0:T(8,128)(2,1)S(1)} %get-tuple-element.71), channel_id=1, source_target_pairs={{0,12},{4,8},{8,4},{12,0},{1,13},{5,9},{9,5},{13,1},{2,14},{6,10},... | collective-permute-start | bytes 245768 | tf_op jit(solution)/shard_map/ppermute | solution.py:31
  35.3 0.0 collective-permute-start.6
  35.3 0.7 collective-permute-start.7
  36.0 1.3 %collective-permute-start.2 = (bf16[72,512]{1,0:T(8,128)(2,1)S(1)}, bf16[72,512]{1,0:T(8,128)(2,1)S(1)}, u32[]{:S(2)}, u32[]{:S(2)}) collective-permute-start(bf16[72,512]{1,0:T(8,128)(2,1)S(1)} %get-tuple-element.65), channel_id=1, source_target_pairs={{0,4},{4,8},{8,12},{12,0},{1,5},{5,9},{9,13},{13,1},{2,6},{6,10},{... | collective-permute-start | bytes 221192 | tf_op jit(solution)/shard_map/ppermute | solution.py:20
  37.3 5.6 %collective-permute-done.2.back.after = bf16[72,512]{1,0:T(8,128)(2,1)S(1)} collective-permute-done((bf16[72,512]{1,0:T(8,128)(2,1)S(1)}, bf16[72,512]{1,0:T(8,128)(2,1)S(1)}, u32[]{:S(2)}, u32[]{:S(2)}) %collective-permute-start.2) | collective-permute-done | bytes 73760 | tf_op jit(solution)/shard_map/ppermute | solution.py:20
  42.9 0.0 collective-permute-done.5.rest_0_
  42.9 0.0 collective-permute-done.6.rest_1_
  42.9 0.2 collective-permute-done.7.rest_2_
  43.2 0.0 collective-permute-done.4.came_p
  43.2 0.2 shard_map.117
  43.4 2.4 %collective-permute-start.9 = (bf16[32,1536]{1,0:T(8,128)(2,1)S(1)}, bf16[32,1536]{1,0:T(8,128)(2,1)S(1)}, u32[]{:S(2)}, u32[]{:S(2)}) collective-permute-start(bf16[32,1536]{1,0:T(8,128)(2,1)S(1)} %get-tuple-element.77), channel_id=1, source_target_pairs={{0,12},{4,8},{8,4},{12,0},{1,13},{5,9},{9,5},{13,1},{2,14},{6,10},... | collective-permute-start | bytes 294920 | tf_op jit(solution)/shard_map/ppermute | solution.py:31
  45.8 0.6 collective-permute-start.10
  46.4 1.4 %collective-permute-start.11 = (bf16[32,1536]{1,0:T(8,128)(2,1)S(1)}, bf16[32,1536]{1,0:T(8,128)(2,1)S(1)}, u32[]{:S(2)}, u32[]{:S(2)}) collective-permute-start(bf16[32,1536]{1,0:T(8,128)(2,1)S(1)} %get-tuple-element.79), channel_id=1, source_target_pairs={{0,4},{4,0},{8,12},{12,8},{1,5},{5,1},{9,13},{13,9},{2,6},{6,2},{1... | collective-permute-start | bytes 294920 | tf_op jit(solution)/shard_map/ppermute | solution.py:31
  47.8 0.5 collective-permute-start.8
  48.3 3.5 %collective-permute-done.8.came_q = bf16[32,640]{1,0:T(8,128)(2,1)S(1)} collective-permute-done((bf16[32,640]{1,0:T(8,128)(2,1)S(1)}, bf16[32,640]{1,0:T(8,128)(2,1)S(1)}, u32[]{:S(2)}, u32[]{:S(2)}) %collective-permute-start.8) | collective-permute-done | bytes 40992 | tf_op jit(solution)/shard_map/ppermute | solution.py:31
  51.8 0.0 collective-permute-done.9.rest_0_
  51.8 2.5 %collective-permute-done.10.rest_1_ = bf16[32,1536]{1,0:T(8,128)(2,1)S(1)} collective-permute-done((bf16[32,1536]{1,0:T(8,128)(2,1)S(1)}, bf16[32,1536]{1,0:T(8,128)(2,1)S(1)}, u32[]{:S(2)}, u32[]{:S(2)}) %collective-permute-start.10) | collective-permute-done | bytes 98336 | tf_op jit(solution)/shard_map/ppermute | solution.py:31
  54.3 0.0 collective-permute-done.11.rest_2_
  54.3 0.1 shard_map.118
  54.4 2.3 %collective-permute-start.15 = (bf16[32,1408]{1,0:T(8,128)(2,1)S(1)}, bf16[32,1408]{1,0:T(8,128)(2,1)S(1)}, u32[]{:S(2)}, u32[]{:S(2)}) collective-permute-start(bf16[32,1408]{1,0:T(8,128)(2,1)S(1)} %get-tuple-element.82.rest_0_), channel_id=1, source_target_pairs={{0,12},{4,8},{8,4},{12,0},{1,13},{5,9},{9,5},{13,1},{2,14},{6,10},... | collective-permute-start | bytes 270344 | tf_op jit(solution)/shard_map/ppermute | solution.py:31
  56.7 0.0 collective-permute-start.14
  56.7 2.1 %collective-permute-start.13 = (bf16[32,1408]{1,0:T(8,128)(2,1)S(1)}, bf16[32,1408]{1,0:T(8,128)(2,1)S(1)}, u32[]{:S(2)}, u32[]{:S(2)}) collective-permute-start(bf16[32,1408]{1,0:T(8,128)(2,1)S(1)} %get-tuple-element.82.rest_0_), channel_id=1, source_target_pairs={{0,4},{4,0},{8,12},{12,8},{1,5},{5,1},{9,13},{13,9},{2,6},{6,2},{1... | collective-permute-start | bytes 270344 | tf_op jit(solution)/shard_map/ppermute | solution.py:31
  58.9 0.5 collective-permute-start.12
  59.4 3.5 %collective-permute-done.12.other_q = bf16[32,640]{1,0:T(8,128)(2,1)S(1)} collective-permute-done((bf16[32,640]{1,0:T(8,128)(2,1)S(1)}, bf16[32,640]{1,0:T(8,128)(2,1)S(1)}, u32[]{:S(2)}, u32[]{:S(2)}) %collective-permute-start.12) | collective-permute-done | bytes 40992 | tf_op jit(solution)/shard_map/ppermute | solution.py:31
  62.9 0.0 collective-permute-done.15.rest_3_
  62.9 1.3 %collective-permute-done.14.rest_2_ = bf16[32,1408]{1,0:T(8,128)(2,1)S(1)} collective-permute-done((bf16[32,1408]{1,0:T(8,128)(2,1)S(1)}, bf16[32,1408]{1,0:T(8,128)(2,1)S(1)}, u32[]{:S(2)}, u32[]{:S(2)}) %collective-permute-start.14) | collective-permute-done | bytes 90144 | tf_op jit(solution)/shard_map/ppermute | solution.py:31
  64.2 0.0 collective-permute-done.13.rest_1_
  64.3 0.7 collective-permute-start.16
  65.0 1.7 %collective-permute-start.19 = (bf16[64,640]{1,0:T(8,128)(2,1)S(1)}, bf16[64,640]{1,0:T(8,128)(2,1)S(1)}, u32[]{:S(2)}, u32[]{:S(2)}) collective-permute-start(bf16[64,640]{1,0:T(8,128)(2,1)S(1)} %get-tuple-element.84.rest_0_), channel_id=1, source_target_pairs={{0,12},{4,8},{8,4},{12,0},{1,13},{5,9},{9,5},{13,1},{2,14},{6,10},... | collective-permute-start | bytes 245768 | tf_op jit(solution)/shard_map/ppermute | solution.py:31
  66.6 0.0 collective-permute-start.18
  66.6 2.7 %collective-permute-start.17 = (bf16[64,640]{1,0:T(8,128)(2,1)S(1)}, bf16[64,640]{1,0:T(8,128)(2,1)S(1)}, u32[]{:S(2)}, u32[]{:S(2)}) collective-permute-start(bf16[64,640]{1,0:T(8,128)(2,1)S(1)} %get-tuple-element.84.rest_0_), channel_id=1, source_target_pairs={{0,4},{4,0},{8,12},{12,8},{1,5},{5,1},{9,13},{13,9},{2,6},{6,2},{1... | collective-permute-start | bytes 245768 | tf_op jit(solution)/shard_map/ppermute | solution.py:31
  69.4 2.8 %collective-permute-done.19.rest_3_ = bf16[64,640]{1,0:T(8,128)(2,1)S(1)} collective-permute-done((bf16[64,640]{1,0:T(8,128)(2,1)S(1)}, bf16[64,640]{1,0:T(8,128)(2,1)S(1)}, u32[]{:S(2)}, u32[]{:S(2)}) %collective-permute-start.19) | collective-permute-done | bytes 81952 | tf_op jit(solution)/shard_map/ppermute | solution.py:31
  72.2 2.0 %collective-permute-done.18.rest_2_ = bf16[64,640]{1,0:T(8,128)(2,1)S(1)} collective-permute-done((bf16[64,640]{1,0:T(8,128)(2,1)S(1)}, bf16[64,640]{1,0:T(8,128)(2,1)S(1)}, u32[]{:S(2)}, u32[]{:S(2)}) %collective-permute-start.18) | collective-permute-done | bytes 81952 | tf_op jit(solution)/shard_map/ppermute | solution.py:31
  74.2 0.0 collective-permute-done.17.rest_1_
  74.2 0.4 collective-permute-done.16.other_p
  74.6 0.5 shard_map.120
  75.1 0.0 collective-permute-start.20
  75.1 0.1 collective-permute-start.23
  75.2 2.1 %collective-permute-start.22 = (f32[8,384]{1,0:T(8,128)S(1)}, f32[8,384]{1,0:T(8,128)S(1)}, u32[]{:S(2)}, u32[]{:S(2)}) collective-permute-start(f32[8,384]{1,0:T(8,128)S(1)} %get-tuple-element.86.row), channel_id=1, source_target_pairs={{0,16},{16,0},{1,17},{17,1},{2,18},{18,2},{3,19},{19,3},{4,20},{20... | collective-permute-start | bytes 36872 | tf_op jit(solution)/shard_map/ppermute | solution.py:31
  77.2 0.0 collective-permute-start.21
  77.2 0.8 shard_map.115
  78.0 0.3 collective-permute-done.23.row_both
  78.3 0.8 collective-permute-done.22.row_section
  79.0 0.0 collective-permute-done.21.row_core
  79.0 0.0 collective-permute-done.20.other
  79.0 2.3 %shard_map.121 = (f32[512,1536]{1,0:T(8,128)}, f32[512,512]{1,0:T(8,128)}, f32[1,512]{1,0:T(1,128)}, f32[1,16]{1,0:T(1,128)}) custom-call(bf16[256,2048]{1,0:T(8,128)(2,1)S(1)} %get-tuple-element.85.half, bf16[256,2048]{1,0:T(8,128)(2,1)S(1)} %collective-permute-done.20.other, f32[8,384]{1,0:T(8,128)S(1)} %get-tuple-element.86.row, ...), custom_call_target="tpu_custom_call" | custom-call | flops 100000000 | bytes 6346816 | tf_op jit(solution)/shard_map/pallas_call | solution.py:47
  (2 shorter events, 0.0 us)
Async XLA Ops:
  2.5 9.2 %collective-permute-start = (bf16[160,512]{1,0:T(8,128)(2,1)}, bf16[160,512]{1,0:T(8,128)(2,1)S(1)}, u32[]{:S(2)}, u32[]{:S(2)}) collective-permute-start(bf16[160,512]{1,0:T(8,128)(2,1)} %get-tuple-element.49), channel_id=1, source_target_pairs={{0,12},{4,0},{8,4},{12,8},{1,13},{5,1},{9,5},{13,9},{2,14},{6,2},{... | collective-permute-start | bytes 491528 | tf_op jit(solution)/shard_map/ppermute | solution.py:20
  7.6 1.0 %copy-start = (f32[160,512]{1,0:T(8,128)S(1)}, f32[160,512]{1,0:T(8,128)}, u32[]{:S(2)}) copy-start(f32[160,512]{1,0:T(8,128)} %get-tuple-element.48.after.own.params) | copy-start | bytes 983044
  8.6 1.4 %copy-start.1 = (bf16[1,512,1536]{2,1,0:T(8,128)(2,1)S(1)}, bf16[1,512,1536]{2,1,0:T(8,128)(2,1)}, u32[]{:S(2)}) copy-start(bf16[1,512,1536]{2,1,0:T(8,128)(2,1)} %param.11) | copy-start | bytes 4718596
  10.0 1.0 %copy-start.2 = (bf16[1,512,512]{2,1,0:T(8,128)(2,1)S(1)}, bf16[1,512,512]{2,1,0:T(8,128)(2,1)}, u32[]{:S(2)}) copy-start(bf16[1,512,512]{2,1,0:T(8,128)(2,1)} %param.12) | copy-start | bytes 1572868
  16.5 7.2 %collective-permute-start.1 = (bf16[144,512]{1,0:T(8,128)(2,1)S(1)}, bf16[144,512]{1,0:T(8,128)(2,1)S(1)}, u32[]{:S(2)}, u32[]{:S(2)}) collective-permute-start(bf16[144,512]{1,0:T(8,128)(2,1)S(1)} %get-tuple-element.53), channel_id=1, source_target_pairs={{16,0},{17,1},{18,2},{19,3},{20,4},{21,5},{22,6},{23,7},{24,8},{25... | collective-permute-start | bytes 442376 | tf_op jit(solution)/shard_map/ppermute | solution.py:26
  26.8 2.8 %collective-permute-start.3 = (bf16[256,2176]{1,0:T(8,128)(2,1)S(1)}, bf16[256,2176]{1,0:T(8,128)(2,1)S(1)}, u32[]{:S(2)}, u32[]{:S(2)}) collective-permute-start(bf16[256,2176]{1,0:T(8,128)(2,1)S(1)} %get-tuple-element.67), channel_id=1, source_target_pairs={{0,1},{1,0},{2,3},{3,2},{4,5},{5,4},{6,7},{7,6},{8,9},{9,8},{10,11... | collective-permute-start | bytes 3342344 | tf_op jit(solution)/shard_map/ppermute | solution.py:31
  30.0 13.2 %collective-permute-start.4 = (bf16[128,1536]{1,0:T(8,128)(2,1)S(1)}, bf16[128,1536]{1,0:T(8,128)(2,1)S(1)}, u32[]{:S(2)}, u32[]{:S(2)}) collective-permute-start(bf16[128,1536]{1,0:T(8,128)(2,1)S(1)} %get-tuple-element.69), channel_id=1, source_target_pairs={{0,2},{1,3},{2,0},{3,1},{4,6},{5,7},{6,4},{7,5},{8,10},{9,11},{10,... | collective-permute-start | bytes 1179656 | tf_op jit(solution)/shard_map/ppermute | solution.py:31
  31.6 11.4 %collective-permute-start.5 = (bf16[64,640]{1,0:T(8,128)(2,1)S(1)}, bf16[64,640]{1,0:T(8,128)(2,1)S(1)}, u32[]{:S(2)}, u32[]{:S(2)}) collective-permute-start(bf16[64,640]{1,0:T(8,128)(2,1)S(1)} %get-tuple-element.71), channel_id=1, source_target_pairs={{0,12},{4,8},{8,4},{12,0},{1,13},{5,9},{9,5},{13,1},{2,14},{6,10},... | collective-permute-start | bytes 245768 | tf_op jit(solution)/shard_map/ppermute | solution.py:31
  35.3 7.7 %collective-permute-start.6 = (bf16[64,640]{1,0:T(8,128)(2,1)S(1)}, bf16[64,640]{1,0:T(8,128)(2,1)S(1)}, u32[]{:S(2)}, u32[]{:S(2)}) collective-permute-start(bf16[64,640]{1,0:T(8,128)(2,1)S(1)} %get-tuple-element.72), channel_id=1, source_target_pairs={{0,8},{4,12},{8,0},{12,4},{1,9},{5,13},{9,1},{13,5},{2,10},{6,14},... | collective-permute-start | bytes 245768 | tf_op jit(solution)/shard_map/ppermute | solution.py:31
  35.3 7.9 %collective-permute-start.7 = (bf16[64,640]{1,0:T(8,128)(2,1)S(1)}, bf16[64,640]{1,0:T(8,128)(2,1)S(1)}, u32[]{:S(2)}, u32[]{:S(2)}) collective-permute-start(bf16[64,640]{1,0:T(8,128)(2,1)S(1)} %get-tuple-element.73), channel_id=1, source_target_pairs={{0,4},{4,0},{8,12},{12,8},{1,5},{5,1},{9,13},{13,9},{2,6},{6,2},{1... | collective-permute-start | bytes 245768 | tf_op jit(solution)/shard_map/ppermute | solution.py:31
  36.0 7.0 %collective-permute-start.2 = (bf16[72,512]{1,0:T(8,128)(2,1)S(1)}, bf16[72,512]{1,0:T(8,128)(2,1)S(1)}, u32[]{:S(2)}, u32[]{:S(2)}) collective-permute-start(bf16[72,512]{1,0:T(8,128)(2,1)S(1)} %get-tuple-element.65), channel_id=1, source_target_pairs={{0,4},{4,8},{8,12},{12,0},{1,5},{5,9},{9,13},{13,1},{2,6},{6,10},{... | collective-permute-start | bytes 221192 | tf_op jit(solution)/shard_map/ppermute | solution.py:20
  43.4 8.5 %collective-permute-start.9 = (bf16[32,1536]{1,0:T(8,128)(2,1)S(1)}, bf16[32,1536]{1,0:T(8,128)(2,1)S(1)}, u32[]{:S(2)}, u32[]{:S(2)}) collective-permute-start(bf16[32,1536]{1,0:T(8,128)(2,1)S(1)} %get-tuple-element.77), channel_id=1, source_target_pairs={{0,12},{4,8},{8,4},{12,0},{1,13},{5,9},{9,5},{13,1},{2,14},{6,10},... | collective-permute-start | bytes 294920 | tf_op jit(solution)/shard_map/ppermute | solution.py:31
  45.8 8.6 %collective-permute-start.10 = (bf16[32,1536]{1,0:T(8,128)(2,1)S(1)}, bf16[32,1536]{1,0:T(8,128)(2,1)S(1)}, u32[]{:S(2)}, u32[]{:S(2)}) collective-permute-start(bf16[32,1536]{1,0:T(8,128)(2,1)S(1)} %get-tuple-element.78), channel_id=1, source_target_pairs={{0,8},{4,12},{8,0},{12,4},{1,9},{5,13},{9,1},{13,5},{2,10},{6,14},... | collective-permute-start | bytes 294920 | tf_op jit(solution)/shard_map/ppermute | solution.py:31
  46.4 8.0 %collective-permute-start.11 = (bf16[32,1536]{1,0:T(8,128)(2,1)S(1)}, bf16[32,1536]{1,0:T(8,128)(2,1)S(1)}, u32[]{:S(2)}, u32[]{:S(2)}) collective-permute-start(bf16[32,1536]{1,0:T(8,128)(2,1)S(1)} %get-tuple-element.79), channel_id=1, source_target_pairs={{0,4},{4,0},{8,12},{12,8},{1,5},{5,1},{9,13},{13,9},{2,6},{6,2},{1... | collective-permute-start | bytes 294920 | tf_op jit(solution)/shard_map/ppermute | solution.py:31
  47.8 4.0 %collective-permute-start.8 = (bf16[32,640]{1,0:T(8,128)(2,1)S(1)}, bf16[32,640]{1,0:T(8,128)(2,1)S(1)}, u32[]{:S(2)}, u32[]{:S(2)}) collective-permute-start(bf16[32,640]{1,0:T(8,128)(2,1)S(1)} %get-tuple-element.76), channel_id=1, source_target_pairs={{0,2},{1,3},{2,0},{3,1},{4,6},{5,7},{6,4},{7,5},{8,10},{9,11},{10,... | collective-permute-start | bytes 122888 | tf_op jit(solution)/shard_map/ppermute | solution.py:31
  54.4 8.5 %collective-permute-start.15 = (bf16[32,1408]{1,0:T(8,128)(2,1)S(1)}, bf16[32,1408]{1,0:T(8,128)(2,1)S(1)}, u32[]{:S(2)}, u32[]{:S(2)}) collective-permute-start(bf16[32,1408]{1,0:T(8,128)(2,1)S(1)} %get-tuple-element.82.rest_0_), channel_id=1, source_target_pairs={{0,12},{4,8},{8,4},{12,0},{1,13},{5,9},{9,5},{13,1},{2,14},{6,10},... | collective-permute-start | bytes 270344 | tf_op jit(solution)/shard_map/ppermute | solution.py:31
  56.7 7.5 %collective-permute-start.14 = (bf16[32,1408]{1,0:T(8,128)(2,1)S(1)}, bf16[32,1408]{1,0:T(8,128)(2,1)S(1)}, u32[]{:S(2)}, u32[]{:S(2)}) collective-permute-start(bf16[32,1408]{1,0:T(8,128)(2,1)S(1)} %get-tuple-element.82.rest_0_), channel_id=1, source_target_pairs={{0,8},{4,12},{8,0},{12,4},{1,9},{5,13},{9,1},{13,5},{2,10},{6,14},... | collective-permute-start | bytes 270344 | tf_op jit(solution)/shard_map/ppermute | solution.py:31
  56.7 7.5 %collective-permute-start.13 = (bf16[32,1408]{1,0:T(8,128)(2,1)S(1)}, bf16[32,1408]{1,0:T(8,128)(2,1)S(1)}, u32[]{:S(2)}, u32[]{:S(2)}) collective-permute-start(bf16[32,1408]{1,0:T(8,128)(2,1)S(1)} %get-tuple-element.82.rest_0_), channel_id=1, source_target_pairs={{0,4},{4,0},{8,12},{12,8},{1,5},{5,1},{9,13},{13,9},{2,6},{6,2},{1... | collective-permute-start | bytes 270344 | tf_op jit(solution)/shard_map/ppermute | solution.py:31
  58.9 4.0 %collective-permute-start.12 = (bf16[32,640]{1,0:T(8,128)(2,1)S(1)}, bf16[32,640]{1,0:T(8,128)(2,1)S(1)}, u32[]{:S(2)}, u32[]{:S(2)}) collective-permute-start(bf16[32,640]{1,0:T(8,128)(2,1)S(1)} %get-tuple-element.81.piece_q), channel_id=1, source_target_pairs={{0,2},{1,3},{2,0},{3,1},{4,6},{5,7},{6,4},{7,5},{8,10},{9,11},{10,... | collective-permute-start | bytes 122888 | tf_op jit(solution)/shard_map/ppermute | solution.py:31
  64.3 10.3 %collective-permute-start.16 = (bf16[128,1408]{1,0:T(8,128)(2,1)S(1)}, bf16[128,1408]{1,0:T(8,128)(2,1)S(1)}, u32[]{:S(2)}, u32[]{:S(2)}) collective-permute-start(bf16[128,1408]{1,0:T(8,128)(2,1)S(1)} %get-tuple-element.83.block_p), channel_id=1, source_target_pairs={{0,2},{1,3},{2,0},{3,1},{4,6},{5,7},{6,4},{7,5},{8,10},{9,11},{10,... | collective-permute-start | bytes 1081352 | tf_op jit(solution)/shard_map/ppermute | solution.py:31
  65.0 7.2 %collective-permute-start.19 = (bf16[64,640]{1,0:T(8,128)(2,1)S(1)}, bf16[64,640]{1,0:T(8,128)(2,1)S(1)}, u32[]{:S(2)}, u32[]{:S(2)}) collective-permute-start(bf16[64,640]{1,0:T(8,128)(2,1)S(1)} %get-tuple-element.84.rest_0_), channel_id=1, source_target_pairs={{0,12},{4,8},{8,4},{12,0},{1,13},{5,9},{9,5},{13,1},{2,14},{6,10},... | collective-permute-start | bytes 245768 | tf_op jit(solution)/shard_map/ppermute | solution.py:31
  66.6 7.6 %collective-permute-start.18 = (bf16[64,640]{1,0:T(8,128)(2,1)S(1)}, bf16[64,640]{1,0:T(8,128)(2,1)S(1)}, u32[]{:S(2)}, u32[]{:S(2)}) collective-permute-start(bf16[64,640]{1,0:T(8,128)(2,1)S(1)} %get-tuple-element.84.rest_0_), channel_id=1, source_target_pairs={{0,8},{4,12},{8,0},{12,4},{1,9},{5,13},{9,1},{13,5},{2,10},{6,14},... | collective-permute-start | bytes 245768 | tf_op jit(solution)/shard_map/ppermute | solution.py:31
  66.6 7.6 %collective-permute-start.17 = (bf16[64,640]{1,0:T(8,128)(2,1)S(1)}, bf16[64,640]{1,0:T(8,128)(2,1)S(1)}, u32[]{:S(2)}, u32[]{:S(2)}) collective-permute-start(bf16[64,640]{1,0:T(8,128)(2,1)S(1)} %get-tuple-element.84.rest_0_), channel_id=1, source_target_pairs={{0,4},{4,0},{8,12},{12,8},{1,5},{5,1},{9,13},{13,9},{2,6},{6,2},{1... | collective-permute-start | bytes 245768 | tf_op jit(solution)/shard_map/ppermute | solution.py:31
  75.1 4.0 %collective-permute-start.20 = (bf16[256,2048]{1,0:T(8,128)(2,1)S(1)}, bf16[256,2048]{1,0:T(8,128)(2,1)S(1)}, u32[]{:S(2)}, u32[]{:S(2)}) collective-permute-start(bf16[256,2048]{1,0:T(8,128)(2,1)S(1)} %get-tuple-element.85.half), channel_id=1, source_target_pairs={{0,1},{1,0},{2,3},{3,2},{4,5},{5,4},{6,7},{7,6},{8,9},{9,8},{10,11... | collective-permute-start | bytes 3145736 | tf_op jit(solution)/shard_map/ppermute | solution.py:31
  75.1 3.2 %collective-permute-start.23 = (f32[8,384]{1,0:T(8,128)S(1)}, f32[8,384]{1,0:T(8,128)S(1)}, u32[]{:S(2)}, u32[]{:S(2)}) collective-permute-start(f32[8,384]{1,0:T(8,128)S(1)} %get-tuple-element.86.row), channel_id=1, source_target_pairs={{0,17},{1,16},{2,19},{3,18},{16,1},{17,0},{18,3},{19,2},{4,21},{5,... | collective-permute-start | bytes 36872 | tf_op jit(solution)/shard_map/ppermute | solution.py:617
  75.2 3.9 %collective-permute-start.22 = (f32[8,384]{1,0:T(8,128)S(1)}, f32[8,384]{1,0:T(8,128)S(1)}, u32[]{:S(2)}, u32[]{:S(2)}) collective-permute-start(f32[8,384]{1,0:T(8,128)S(1)} %get-tuple-element.86.row), channel_id=1, source_target_pairs={{0,16},{16,0},{1,17},{17,1},{2,18},{18,2},{3,19},{19,3},{4,20},{20... | collective-permute-start | bytes 36872 | tf_op jit(solution)/shard_map/ppermute | solution.py:31
  77.2 1.8 %collective-permute-start.21 = (f32[8,384]{1,0:T(8,128)S(1)}, f32[8,384]{1,0:T(8,128)S(1)}, u32[]{:S(2)}, u32[]{:S(2)}) collective-permute-start(f32[8,384]{1,0:T(8,128)S(1)} %get-tuple-element.86.row), channel_id=1, source_target_pairs={{0,1},{1,0},{2,3},{3,2},{4,5},{5,4},{6,7},{7,6},{8,9},{9,8},{10,11... | collective-permute-start | bytes 36872 | tf_op jit(solution)/shard_map/ppermute | solution.py:31
